TPU v7x, 32 devices: a whole 2x2x4 slice. The times are simulated.
32 devices in a mesh: kv: 16 (over z, x, core), tp: 2 (over y).
Axes of the slice: x: 2, y: 2, z: 4, core: 2. Of those that a mesh axis runs over, the one named last changes fastest.
Arguments:
- queries: bfloat16 [128, 7168], P('kv', 'tp'), may hold values from -30 to 30
- new_keys: bfloat16 [128, 7168], P('kv', 'tp'), may hold values from -6 to 6
- new_values: bfloat16 [128, 7168], P('kv', 'tp'), may hold values from -6 to 6
- keys: bfloat16 [6144, 7168], P('kv', 'tp'), may hold values from -8 to 8
- values: bfloat16 [6144, 7168], P('kv', 'tp'), may hold values from -6 to 6
- slot_request: int32 [6144], P('kv'), may hold values from 0 to 127, as said below
- slot_valid: int32 [6144], P('kv'), may hold values from 0 to 1, as said below
- out_weight: bfloat16 [7168, 7168], P('tp', 'kv'), may hold values from -0.0625 to 0.0625
- out_bias: bfloat16 [7168], P('kv'), may hold values from -3 to 3
- residual: bfloat16 [128, 7168], P('tp', 'kv'), may hold values from -6 to 6
Outputs:
- layer_out: bfloat16 [128, 7168], P('tp', 'kv')
Inputs may be any that keep to these rules, and one draw needn't show every extreme that they name: `slot_request`: slots come in pages of 16 consecutive slots owned by one request; a request's pages are consecutive and may span several holders; every request owns at least one page and at most 130 pages, and one request owns exactly 130. `slot_valid`: only the last page of each request has empty slots, and that page holds at least one cached token in its first slot.
All inputs are finite; a program needn't handle non-finite values.
Results may differ from a plain program's by a relative error of at most 0.0033.
Values may be sent and summed in bfloat16 or wider, within the bound.
No kernel may reach another device: no remote copies, remote signals or barrier semaphores. Data moves between devices by JAX's collectives and lax.ppermute only.
A program may use at most 64 MiB of HBM per device.

v0:
```python
import math

import jax
import jax.numpy as jnp
from jax import lax
from jax.sharding import PartitionSpec as P

HD = 128


floor_score = -1e30


def settle(x):
    return lax.optimization_barrier(x.astype(jnp.bfloat16)).astype(jnp.float32)


def normalize(numer, denom, head_count):
    row_total = numer.shape[0]
    quotient = numer.reshape(row_total, head_count, HD) / denom[:, :, None]
    return quotient.reshape(row_total, head_count * HD).astype(jnp.bfloat16)


def on_device(
    queries,
    new_keys,
    new_values,
    keys,
    values,
    slot_request,
    slot_valid,
    out_weight,
    out_bias,
    residual,
):
    head_count = queries.shape[1] // HD
    score_scale = 1.0 / math.sqrt(HD)
    own_rows = queries.shape[0]
    first_row = lax.axis_index("kv") * own_rows
    every_query = lax.all_gather(queries, "kv", axis=0, tiled=True)
    request_count = every_query.shape[0]
    slot_count = keys.shape[0]
    picked = jnp.take(every_query, slot_request, axis=0).reshape(slot_count, head_count, HD)
    scores = (
        jnp.einsum(
            "shd,shd->sh",
            picked,
            keys.reshape(slot_count, head_count, HD),
            preferred_element_type=jnp.float32,
        )
        * score_scale
    )
    live_slot = (slot_valid == 1)[:, None]
    masked = jnp.where(live_slot, scores, floor_score)
    self_scores = (
        jnp.einsum(
            "rhd,rhd->rh",
            queries.reshape(own_rows, head_count, HD),
            new_keys.reshape(own_rows, head_count, HD),
            preferred_element_type=jnp.float32,
        )
        * score_scale
    )
    local_top = (
        jnp.full((request_count, head_count), floor_score, jnp.float32).at[slot_request].max(masked)
    )
    own_top = jnp.maximum(lax.dynamic_slice_in_dim(local_top, first_row, own_rows, 0), self_scores)
    local_top = lax.dynamic_update_slice_in_dim(local_top, own_top, first_row, 0)
    row_top = lax.pmax(local_top, "kv")
    slot_weight = settle(
        jnp.where(live_slot, jnp.exp(masked - jnp.take(row_top, slot_request, axis=0)), 0.0)
    )
    weighted = slot_weight[:, :, None] * values.reshape(slot_count, head_count, HD).astype(
        jnp.float32
    )
    numer_local = jax.ops.segment_sum(
        weighted.reshape(slot_count, head_count * HD), slot_request, num_segments=request_count
    )
    denom_local = jax.ops.segment_sum(slot_weight, slot_request, num_segments=request_count)
    self_weight = settle(
        jnp.exp(self_scores - lax.dynamic_slice_in_dim(row_top, first_row, own_rows, 0))
    )
    self_numer = (
        self_weight[:, :, None] * new_values.reshape(own_rows, head_count, HD).astype(jnp.float32)
    ).reshape(own_rows, head_count * HD)
    numer_local = lax.dynamic_update_slice_in_dim(
        numer_local,
        lax.dynamic_slice_in_dim(numer_local, first_row, own_rows, 0) + self_numer,
        first_row,
        0,
    )
    denom_local = lax.dynamic_update_slice_in_dim(
        denom_local,
        lax.dynamic_slice_in_dim(denom_local, first_row, own_rows, 0) + self_weight,
        first_row,
        0,
    )
    numer, denom = lax.psum((numer_local, denom_local), "kv")
    attended = normalize(numer, denom, head_count)
    projected = lax.psum_scatter(
        jnp.dot(attended, out_weight, preferred_element_type=jnp.float32),
        "tp",
        scatter_dimension=0,
        tiled=True,
    )
    total = residual.astype(jnp.float32) + projected + out_bias.astype(jnp.float32)[None, :]
    return total.astype(jnp.bfloat16)


def solution(mesh):
    placed = (
        P("kv", "tp"),
        P("kv", "tp"),
        P("kv", "tp"),
        P("kv", "tp"),
        P("kv", "tp"),
        P("kv"),
        P("kv"),
        P("tp", "kv"),
        P("kv"),
        P("tp", "kv"),
    )
    return jax.shard_map(
        on_device, mesh=mesh, in_specs=placed, out_specs=P("tp", "kv"), check_vma=False
    )
```

profile of v0, /device:TPU:0, one launch (start us, length us, event | category | flops | bytes accessed | tf_op | source)
XLA Modules:
  0.0 268.9 jit_solution(10539537003695489412)
XLA Ops:
  6.5 0.0 copy-start
  6.5 0.0 all-reduce.2.cloned.1.call-start
  6.5 0.8 compare_select_fusion
  7.4 27.5 %all_gather.3 = bf16[128,3584]{1,0:T(8,128)(2,1)} all-gather(bf16[8,3584]{1,0:T(8,128)(2,1)} %param.10), channel_id=1, replica_groups=mesh['kv'=16,'tp'=2] {'kv'}, dimensions={0}, use_global_device_ids=true | all-gather | bytes 974848 | tf_op jit(solution)/shard_map/all_gather | solution.py:40
  34.9 8.9 %gather_fusion = bf16[384,3584]{1,0:T(8,128)(2,1)} fusion(bf16[128,3584]{1,0:T(8,128)(2,1)} %all_gather.3, s32[1024]{0:T(1024)S(1)} %pad_clamp_fusion), kind=kCustom, calls=%fused_computation | custom fusion | bytes 5506560 | tf_op jit(solution)/shard_map/jit(_take)/gather | solution.py:43
  43.8 0.0 copy-start.5
  43.8 0.0 copy-start.7
  43.8 4.5 %copy.12 = bf16[384,3584]{0,1:T(8,128)(2,1)} copy(bf16[384,3584]{1,0:T(8,128)(2,1)} %gather_fusion) | data formatting | bytes 5505024 | tf_op jit(solution)/shard_map/jit(_take)/gather | solution.py:43
  48.3 0.0 copy-done.5
  48.3 0.0 copy-done.7
  48.3 0.0 copy-start.6
  48.3 4.5 %copy.13 = bf16[384,3584]{0,1:T(8,128)(2,1)} copy(bf16[384,3584]{1,0:T(8,128)(2,1)} %param.13) | data formatting | bytes 5505024 | tf_op args[3]
  52.8 0.0 copy-start.2
  52.8 3.7 %fusion = f32[384,28]{0,1:T(8,128)S(1)} fusion(bf16[384,28,128]{0,2,1:T(8,128)(2,1)} %bitcast.17, bf16[384,28,128]{0,2,1:T(8,128)(2,1)} %bitcast.16, pred[384]{0:T(512)(128)(4,1)S(1)} %get-tuple-element.5), kind=kLoop, calls=%fused_computation.7 | loop fusion | flops 6870528 | bytes 5548416
  56.5 0.1 copy.24
  56.7 0.0 copy-done.2
  56.7 0.9 fusion.7
  57.6 0.1 copy.29
  57.7 0.0 copy-done.6
  57.7 3.3 %scatter_custom_fusion = f32[128,28]{1,0:T(8,128)S(1)} fusion(s32[384]{0:T(512)S(1)} %compare_select_fusion, f32[384,28]{1,0:T(8,128)S(1)} %copy.24, f32[]{:T(128)} %constant.27.clone.1, f32[]{:T(128)} %constant.20.clone.1, pred[384]{0:T(512)(128)(4,1)S(1)} %get-tuple-element.6), kind=kCustom, calls=%fused_computation.14 | custom fusion | flops 32256 | bytes 212992 | tf_op jit(solution)/shard_map/scatter-max | solution.py:65
  61.0 58.0 %pmax.7 = f32[128,28]{1,0:T(8,128)S(1)} all-reduce(f32[128,28]{1,0:T(8,128)S(1)} %maximum_dynamic-update-slice_fusion), channel_id=1, replica_groups=mesh['kv'=16,'tp'=2] {'kv'}, use_global_device_ids=true, to_apply=%region_1.2 | all-reduce | flops 3584 | bytes 28672 | tf_op jit(solution)/shard_map/pmax | solution.py:69
  119.0 1.6 gather_fusion.1
  120.6 1.7 select_convert_fusion
  122.3 1.0 copy.14
  123.3 4.5 %copy.15 = bf16[384,3584]{0,1:T(8,128)(2,1)} copy(bf16[384,3584]{1,0:T(8,128)(2,1)} %param.14) | data formatting | bytes 5505024 | tf_op args[4]
  127.9 4.5 %bitcast_multiply_fusion = f32[384,3584]{0,1:T(8,128)} fusion(bf16[384,3584]{0,1:T(8,128)(2,1)} %copy.15, f32[384,28]{0,1:T(8,128)S(1)} %copy.14), kind=kLoop, calls=%fused_computation.5 | loop fusion | flops 2752512 | bytes 8300544 | tf_op jit(solution)/shard_map/mul | solution.py:73
  132.4 0.0 copy-start.4
  132.4 6.2 %copy.16 = f32[384,3584]{1,0:T(8,128)} copy(f32[384,3584]{0,1:T(8,128)} %bitcast_multiply_fusion) | data formatting | bytes 11010048 | tf_op jit(solution)/shard_map/mul | solution.py:73
  138.6 0.1 copy.17
  138.7 11.0 %scatter_custom_fusion.1 = f32[128,3584]{1,0:T(8,128)} fusion(s32[384]{0:T(512)S(1)} %copy-done.5, f32[384,3584]{1,0:T(8,128)} %copy.16, f32[]{:T(128)} %constant.14.clone.1), kind=kCustom, calls=%fused_computation.10 | custom fusion | flops 1376256 | bytes 1835520 | tf_op jit(solution)/shard_map/scatter-add | solution.py:76
  149.7 0.0 copy-done.4
  149.7 1.6 fusion.6
  151.3 0.0 all-reduce.2.cloned.1.call-update
  151.3 0.0 reduce-scatter.2.cloned.1.call-start
  151.4 0.0 copy-done.1
  151.4 3.2 %scatter_custom_fusion.2 = f32[128,28]{1,0:T(8,128)S(1)} fusion(s32[384]{0:T(512)S(1)} %copy-done.5, bf16[384,28]{1,0:T(8,128)(2,1)S(1)} %copy-done.1, f32[]{:T(128)} %constant.14.clone.1), kind=kCustom, calls=%fused_computation.24 | custom fusion | flops 21504 | bytes 112644 | tf_op jit(solution)/shard_map/scatter-add | solution.py:79
  154.6 58.2 %psum.15 = f32[128,28]{1,0:T(8,128)S(1)} all-reduce(f32[128,28]{1,0:T(8,128)S(1)} %add_dynamic-update-slice_fusion), channel_id=1, replica_groups=mesh['kv'=16,'tp'=2] {'kv'}, use_global_device_ids=true, to_apply=%region_5.6 | all-reduce | flops 3584 | bytes 28672 | tf_op jit(solution)/shard_map/psum | solution.py:98
  212.8 0.1 copy.18
  212.9 1.4 div.11
  214.3 2.8 %copy.19 = f32[128,3584]{1,0:T(8,128)} copy(f32[128,3584]{0,1:T(8,128)} %bitcast.18) | data formatting | bytes 3670016 | tf_op jit(solution)/shard_map/div | solution.py:20
  217.1 28.6 %all-reduce.2.cloned.1.call-done = f32[128,3584]{1,0:T(8,128)} async-done(((f32[128,3584]{1,0:T(8,128)}), f32[128,3584]{1,0:T(8,128)}) %all-reduce.2.cloned.1.call-update) | async-done | bytes 1835024 | tf_op jit(solution)/shard_map/psum | solution.py:98
  245.7 0.0 copy-done
  245.7 3.9 %fusion.1 = f32[128,448]{1,0:T(8,128)} fusion(bf16[3584,448]{0,1:T(8,128)(2,1)S(1)} %copy-done, f32[128,3584]{1,0:T(8,128)} %all-reduce.2.cloned.1.call-done, f32[128,3584]{1,0:T(8,128)} %copy.19), kind=kOutput, calls=%fused_computation.9 | convolution fusion | flops 411959296 | bytes 7110656 | tf_op jit(solution)/shard_map/dot_general | solution.py:101
  249.5 0.0 reduce-scatter.2.cloned.1.call-update
  249.6 0.0 copy-done.8
  249.6 11.0 %reduce-scatter.2.cloned.1.call-done = f32[64,448]{1,0:T(8,128)} async-done(((f32[128,448]{1,0:T(8,128)}), f32[64,448]{1,0:T(8,128)}) %reduce-scatter.2.cloned.1.call-update) | async-done | bytes 114704 | tf_op jit(solution)/shard_map/reduce_scatter | solution.py:100
  260.6 0.0 copy-done.3
  260.6 1.6 add_convert_fusion
  (9 shorter events, 0.1 us)
Async XLA Ops:
  6.5 239.1 %copy-start = (bf16[3584,448]{0,1:T(8,128)(2,1)S(1)}, bf16[3584,448]{0,1:T(8,128)(2,1)}, u32[]{:S(2)}) copy-start(bf16[3584,448]{0,1:T(8,128)(2,1)} %param.17) | copy-start | bytes 9633796
  6.5 239.1 %all-reduce.2.cloned.1.call-start = ((), (), s32[]{:S(2)}) async-start(), calls=%async_computation.1 | async-start | bytes 3670016 | tf_op jit(solution)/shard_map/psum | solution.py:98
  43.8 4.5 %copy-start.5 = (s32[384]{0:T(512)S(1)}, s32[384]{0:T(512)}, u32[]{:S(2)}) copy-start(s32[384]{0:T(512)} %param.15) | copy-start | bytes 4612
  43.8 4.5 %copy-start.7 = (s32[384]{0:T(512)S(1)}, s32[384]{0:T(512)}, u32[]{:S(2)}) copy-start(s32[384]{0:T(512)} %param.16) | copy-start | bytes 4612
  48.3 9.4 %copy-start.6 = (pred[384]{0:T(512)(128)(4,1)}, pred[384]{0:T(512)(128)(4,1)S(1)}, u32[]{:S(2)}) copy-start(pred[384]{0:T(512)(128)(4,1)S(1)} %get-tuple-element.6) | copy-start | bytes 1156
  52.8 3.8 %copy-start.2 = (bf16[8,3584]{1,0:T(8,128)(2,1)S(1)}, bf16[8,3584]{1,0:T(8,128)(2,1)}, u32[]{:S(2)}) copy-start(bf16[8,3584]{1,0:T(8,128)(2,1)} %param.10) | copy-start | bytes 172036
  132.4 17.3 %copy-start.4 = (bf16[8,3584]{1,0:T(8,128)(2,1)S(1)}, bf16[8,3584]{1,0:T(8,128)(2,1)}, u32[]{:S(2)}) copy-start(bf16[8,3584]{1,0:T(8,128)(2,1)} %param.12) | copy-start | bytes 172036
  138.6 12.8 %copy-start.1 = (bf16[384,28]{1,0:T(8,128)(2,1)S(1)}, bf16[384,28]{1,0:T(8,128)(2,1)}, u32[]{:S(2)}) copy-start(bf16[384,28]{1,0:T(8,128)(2,1)} %select_convert_fusion) | copy-start | bytes 64516
  151.3 109.2 %reduce-scatter.2.cloned.1.call-start = ((), (), s32[]{:S(2)}) async-start(), calls=%async_computation.2 | async-start | bytes 393216 | tf_op jit(solution)/shard_map/reduce_scatter | solution.py:100
  217.1 32.5 %copy-start.8 = (bf16[448]{0:T(512)(128)(2,1)S(1)}, bf16[448]{0:T(512)(128)(2,1)}, u32[]{:S(2)}) copy-start(bf16[448]{0:T(512)(128)(2,1)} %param.18) | copy-start | bytes 2692
  217.1 43.5 %copy-start.3 = (bf16[64,448]{1,0:T(8,128)(2,1)S(1)}, bf16[64,448]{1,0:T(8,128)(2,1)}, u32[]{:S(2)}) copy-start(bf16[64,448]{1,0:T(8,128)(2,1)} %param.19) | copy-start | bytes 172036
Sparse Core Ops, SparseCore 0:
  151.5 94.1 all-reduce.1
  249.7 10.8 reduce-scatter.1
where the time goes:
time: 270 us; the launch traced here: 269 us
  blocking collectives  144 us (53%)
  waiting for transfers between devices  39.6 us (15%)
  local copies, waits for them, and re-layouts  35.8 us (13%)
  other arithmetic  32.4 us (12%)
  between operations  13.5 us (5%)
  matrix products  3.85 us (1%)
    psum x1, blocking collectives, on_device(): numer, denom = lax.psum((numer_local, denom_local), 'kv')  58.2 us
    pmax x1, blocking collectives, on_device(): row_top = lax.pmax(local_top, 'kv')  58 us
    psum x1, waiting for transfers between devices, on_device(): numer, denom = lax.psum((numer_local, denom_local), 'kv')  28.6 us
    all_gather x1, blocking collectives, on_device(): every_query = lax.all_gather(queries, 'kv', axis=0, tiled=True)  27.5 us
    gather x2, local copies, waits for them, and re-layouts, on_device(): jnp.take(every_query, slot_request, axis=0)  13.4 us
    scatter-add x1, other arithmetic, on_device(): jax.ops.segment_sum(weighted.reshape(slot_count, head_count * HD), slot_r...  11 us
    reduce_scatter x1, waiting for transfers between devices, on_device(): lax.psum_scatter(jnp.dot(attended, out_weight, preferred_element_type=jnp...  11 us
    unnamed x20, local copies, waits for them, and re-layouts  9.08 us
  transfers between devices with their start and end apart: 2, of which 2 were waited for; matrix products, arithmetic and copies ran while one was open for 3% of the time, Pallas kernels for 0%

commit v1 on v0

v1 whole, which is shorter than its diff:
```python
import functools
import math

import jax
import jax.numpy as jnp
from jax import lax
from jax.experimental import pallas as pl
from jax.experimental.pallas import tpu as pltpu
from jax.sharding import PartitionSpec as P

HD = 128
PAGE = 16
OUTER = 4
LANES = 128
STAT = 32

floor_score = -1e30
f32 = jnp.float32
bf16 = jnp.bfloat16
WHOLE = pl.BlockSpec(memory_space=pltpu.VMEM)
SCALARS = pl.BlockSpec(memory_space=pltpu.SMEM)


def params(megabytes=48):
    return pltpu.CompilerParams(vmem_limit_bytes=megabytes * 1024 * 1024)


def offset_of(block, mid):
    core = block // (mid * OUTER)
    middle = (block // OUTER) % mid
    return core + 2 * middle + 2 * mid * (block % OUTER)


def place_of(offset, mid):
    core = offset % 2
    middle = (offset // 2) % mid
    return (core * mid + middle) * OUTER + offset // (2 * mid)


def prep_kernel(mid, own_rows, ids, request, valid, queries, new_keys, pick, mask, own_top):
    rows, slots = mask.shape
    row = lax.broadcasted_iota(jnp.int32, (rows, slots), 0)
    lane = lax.broadcasted_iota(jnp.int32, (rows, slots), 1)
    owners = jnp.broadcast_to(request[...], (rows, slots))
    mine = jnp.sum(jnp.where(lane == row * PAGE, owners, 0), axis=1, keepdims=True)
    before = jnp.sum(jnp.where(lane == row * PAGE - PAGE, owners, 0), axis=1, keepdims=True)
    page = lax.broadcasted_iota(jnp.int32, (rows, 1), 0)
    first = ((page == 0) | (mine != before)) & (page < slots // PAGE)
    live = (owners == mine) & first & (jnp.broadcast_to(valid[...], (rows, slots)) == 1)
    mask[...] = jnp.where(live, 1.0, 0.0)
    place = lax.broadcasted_iota(jnp.int32, pick.shape, 1)
    owner = lax.bitwise_xor(offset_of(place // own_rows, mid), ids[0])
    named = owner * own_rows + place % own_rows
    pick[...] = jnp.where((named == mine) & first, 1.0, 0.0).astype(bf16)
    heads = queries.shape[1] // HD
    where = lax.broadcasted_iota(jnp.int32, own_top.shape, 1)
    top = jnp.zeros(own_top.shape, f32)
    for head in range(heads):
        cut = slice(head * HD, (head + 1) * HD)
        score = jnp.sum(
            queries[:, cut].astype(f32) * new_keys[:, cut].astype(f32), axis=1, keepdims=True
        ) * (1.0 / math.sqrt(HD))
        top = jnp.where(where == head, score, top)
    own_top[...] = top


def split_top(top):
    lane = lax.broadcasted_iota(jnp.int32, top.shape, 1)
    top = jnp.where(lane < STAT, top, 0.0)
    high = top.astype(bf16).astype(f32)
    rest = top - high
    middle = rest.astype(bf16).astype(f32)
    low = rest - middle
    return high + pltpu.roll(middle, STAT, 1) + pltpu.roll(low, 2 * STAT, 1)


def join_top(stat):
    return (stat + pltpu.roll(stat, LANES - STAT, 1)) + pltpu.roll(stat, LANES - 2 * STAT, 1)


def attend_kernel(group, pick, mask, near, far, keys, values, keep, send, tops):
    step = pl.program_id(0)
    rows = pick.shape[0]
    half = near.shape[0]
    total = 2 * half
    chosen = jnp.dot(
        pick[:, :half], near[...], preferred_element_type=f32
    ) + jnp.dot(pick[:, half:], far[...], preferred_element_type=f32)
    chosen = chosen.astype(bf16)
    live = mask[...] > 0.0
    lane = lax.broadcasted_iota(jnp.int32, (rows, LANES), 1)

    @pl.when(step == 0)
    def _():
        tops[...] = jnp.zeros_like(tops)

    top_all = tops[...]
    found = []
    for head in range(group):
        cut = slice(head * HD, (head + 1) * HD)
        score = lax.dot_general(
            chosen[:, cut], keys[:, cut], (((1,), (1,)), ((), ())), preferred_element_type=f32
        ) * (1.0 / math.sqrt(HD))
        score = jnp.where(live, score, floor_score)
        top = jnp.max(score, axis=1, keepdims=True)
        weight = jnp.where(live, jnp.exp(score - top), 0.0).astype(bf16)
        denom = jnp.sum(weight.astype(f32), axis=1, keepdims=True)
        denom = jnp.where(denom > 0.0, denom, 1.0)
        numer = jnp.dot(weight, values[:, cut], preferred_element_type=f32)
        found.append((numer / denom).astype(bf16))
        top_all = jnp.where(lane == step * group + head, top + jnp.log(denom), top_all)
    tops[...] = top_all
    spread = functools.partial(
        lax.dot_general, dimension_numbers=(((0,), (0,)), ((), ())), preferred_element_type=f32
    )
    dense = spread(pick[...], jnp.concatenate(found, axis=1)).astype(bf16)
    columns = pl.ds(pl.multiple_of(step * group * HD, HD), group * HD)
    keep[:, columns] = dense[:half]
    send[:, columns] = dense[half:]

    @pl.when(step == pl.num_programs(0) - 1)
    def _():
        stat = jnp.where(lane == LANES - 1, 1.0, split_top(tops[...])).astype(bf16)
        wide = spread(pick[...], stat)
        place = lax.broadcasted_iota(jnp.int32, (total, LANES), 1)
        absent = wide[:, LANES - 1 :] == 0.0
        wide = jnp.where(absent & (place < STAT), floor_score, wide).astype(bf16)
        start = keep.shape[1] - LANES
        keep[:, start:] = wide[:half]
        send[:, start:] = wide[half:]


def merge(parts, tops):
    best = functools.reduce(jnp.maximum, tops)
    weights = [jnp.exp(top - best) for top in tops]
    total = functools.reduce(jnp.add, weights)
    shares = [weight / total for weight in weights]

    def head_of(head):
        terms = [
            share[:, head : head + 1] * part(head) for share, part in zip(shares, parts)
        ]
        return functools.reduce(jnp.add, terms)

    return head_of, best + jnp.log(total)


def part_of(ref):
    return lambda head: ref[:, head * HD : (head + 1) * HD].astype(f32)


def top_of(ref):
    return join_top(ref[:, ref.shape[1] - LANES :].astype(f32))


def merge_kernel(count, *refs):
    ins, outs = refs[:count], refs[count:]
    heads = ins[0].shape[1] // HD - 1
    rows = outs[0].shape[0]
    head_of, top = merge([part_of(ref) for ref in ins], [top_of(ref) for ref in ins])
    for head in range(heads + 1):
        cut = slice(head * HD, (head + 1) * HD)
        block = head_of(head) if head < heads else split_top(top)
        for at, out in enumerate(outs):
            out[:, cut] = block[at * rows : (at + 1) * rows].astype(bf16)


def last_kernel(count, *refs):
    ins = refs[:count]
    new_values, own_top, out = refs[count:]
    head_of, _ = merge(
        [part_of(ref) for ref in ins] + [part_of(new_values)],
        [top_of(ref) for ref in ins] + [own_top[...]],
    )
    for head in range(out.shape[1] // HD):
        out[:, head * HD : (head + 1) * HD] = head_of(head).astype(bf16)


def project_kernel(mid, own_rows, ids, *refs):
    count = len(refs) - 1
    acc = refs[-1]
    places = [at for at in range(count) if refs[at].dtype == f32]
    ins, weight, outs = refs[: places[0] - 1], refs[places[0] - 1], refs[places[0] : count]
    step = pl.program_id(0)

    @pl.when(step == 0)
    def _():
        acc[...] = jnp.zeros_like(acc)

    at = 0
    for ref in ins:
        rows = ref.shape[0]
        acc[at : at + rows, :] += jnp.dot(ref[...], weight[...], preferred_element_type=f32)
        at += rows

    @pl.when(step == pl.num_programs(0) - 1)
    def _():
        blocks = outs[0].shape[0] // own_rows
        for distance, out in enumerate(outs):
            side = lax.bitwise_xor(ids[1], distance)
            for block in range(blocks):
                offset = lax.bitwise_xor(side * blocks + block, ids[0])
                start = pl.multiple_of(place_of(offset, mid) * own_rows, own_rows)
                out[block * own_rows : (block + 1) * own_rows, :] = acc[pl.ds(start, own_rows), :]


def hop(x, axis, count, distance):
    return lax.ppermute(x, axis, [(i, i ^ distance) for i in range(count)])


def on_device(
    kv_count,
    tp_count,
    queries,
    new_keys,
    new_values,
    keys,
    values,
    slot_request,
    slot_valid,
    out_weight,
    out_bias,
    residual,
):
    own_rows, width = queries.shape
    heads = width // HD
    slots = keys.shape[0]
    mid = kv_count // (2 * OUTER)
    requests = kv_count * own_rows
    rows = -(-(slots // PAGE) // 16) * 16
    group = 7 if heads % 7 == 0 else 1
    columns = out_weight.shape[1]
    wide = width + LANES
    ids = jnp.stack([lax.axis_index("kv"), lax.axis_index("tp")]).astype(jnp.int32)
    kv_hop = lambda x, distance: hop(x, "kv", kv_count, distance)

    def gather(block):
        line = jnp.concatenate(
            [block] + [kv_hop(block, 2 * mid * far) for far in range(1, OUTER)], axis=0
        )
        lines = [line] + [kv_hop(line, 2 * near) for near in range(1, mid)]
        return lines, [kv_hop(each, 1) for each in lines]

    pick, mask, own_top = pl.pallas_call(
        functools.partial(prep_kernel, mid, own_rows),
        out_shape=(
            jax.ShapeDtypeStruct((rows, requests), bf16),
            jax.ShapeDtypeStruct((rows, slots), f32),
            jax.ShapeDtypeStruct((own_rows, LANES), f32),
        ),
        in_specs=[SCALARS] + [WHOLE] * 4,
        out_specs=(WHOLE,) * 3,
        compiler_params=params(),
        name="prep",
    )(ids, slot_request.reshape(1, slots), slot_valid.reshape(1, slots), queries, new_keys)

    near, far = gather(queries)
    near = jnp.concatenate(near, axis=0)
    far = jnp.concatenate(far, axis=0)
    half = requests // 2
    fixed = lambda shape: pl.BlockSpec(shape, lambda step: (0, 0))
    moving = lambda height: pl.BlockSpec((height, group * HD), lambda step: (0, step))
    keep, send = pl.pallas_call(
        functools.partial(attend_kernel, group),
        grid=(heads // group,),
        out_shape=(jax.ShapeDtypeStruct((half, wide), bf16),) * 2,
        in_specs=[
            fixed((rows, requests)),
            fixed((rows, slots)),
            moving(half),
            moving(half),
            moving(slots),
            moving(slots),
        ],
        out_specs=(fixed((half, wide)),) * 2,
        scratch_shapes=[pltpu.VMEM((rows, LANES), f32)],
        compiler_params=params(),
        name="attend",
    )(pick, mask, near, far, keys, values)

    def merged(ins, count):
        size = ins[0].shape[0] // count
        return pl.pallas_call(
            functools.partial(merge_kernel, len(ins)),
            out_shape=(jax.ShapeDtypeStruct((size, wide), bf16),) * count,
            in_specs=[WHOLE] * len(ins),
            out_specs=(WHOLE,) * count,
            compiler_params=params(),
            name="merge",
        )(*ins)

    blocks = merged([keep, kv_hop(send, 1)], mid)
    blocks = merged(
        [blocks[0]] + [kv_hop(blocks[near], 2 * near) for near in range(1, mid)], OUTER
    )
    ins = [blocks[0]] + [kv_hop(blocks[far], 2 * mid * far) for far in range(1, OUTER)]
    attended = pl.pallas_call(
        functools.partial(last_kernel, len(ins)),
        out_shape=jax.ShapeDtypeStruct((own_rows, width), bf16),
        in_specs=[WHOLE] * (len(ins) + 2),
        out_specs=WHOLE,
        compiler_params=params(),
        name="last",
    )(*ins, new_values, own_top)

    near, far = gather(attended)
    tall = requests // tp_count
    deep = 4 if heads % 4 == 0 else 7 if heads % 7 == 0 else 1
    ins = near + far
    outs = project(ids, ins, out_weight, mid, own_rows, deep, tall)
    total = outs[0]
    for distance in range(1, tp_count):
        total = total + hop(outs[distance], "tp", tp_count, distance)
    total = total + residual.astype(f32) + out_bias.astype(f32)[None, :]
    return total.astype(bf16)


def project(ids, ins, out_weight, mid, own_rows, deep, tall):
    columns = out_weight.shape[1]
    depth = out_weight.shape[0]
    requests = sum(each.shape[0] for each in ins)
    return pl.pallas_call(
        functools.partial(project_kernel, mid, own_rows),
        grid=(depth // (deep * HD),),
        out_shape=(jax.ShapeDtypeStruct((tall, columns), f32),) * (requests // tall),
        in_specs=[SCALARS]
        + [pl.BlockSpec((each.shape[0], deep * HD), lambda step: (0, step)) for each in ins]
        + [pl.BlockSpec((deep * HD, columns), lambda step: (step, 0))],
        out_specs=(pl.BlockSpec((tall, columns), lambda step: (0, 0)),) * (requests // tall),
        scratch_shapes=[pltpu.VMEM((requests, columns), f32)],
        compiler_params=params(),
        name="project",
    )(ids, *ins, out_weight)


def solution(mesh):
    placed = (
        P("kv", "tp"),
        P("kv", "tp"),
        P("kv", "tp"),
        P("kv", "tp"),
        P("kv", "tp"),
        P("kv"),
        P("kv"),
        P("tp", "kv"),
        P("kv"),
        P("tp", "kv"),
    )
    return jax.shard_map(
        functools.partial(on_device, mesh.shape["kv"], mesh.shape["tp"]),
        mesh=mesh,
        in_specs=placed,
        out_specs=P("tp", "kv"),
        check_vma=False,
    )
```

time: 270 us -> 84 us (0.31)
  blocking collectives: 144 us -> 0 us
  other arithmetic: 32.4 us -> 0.79 us
  local copies, waits for them, and re-layouts: 35.8 us -> 13.5 us
  starting transfers between devices: 0.04 us -> 21.1 us
  Pallas kernels: 0 us -> 16.7 us
  between operations: 13.5 us -> 0.11 us
  waiting for transfers between devices: 39.6 us -> 31.3 us
  matrix products: 3.85 us -> 0 us
    psum x1 -> x0, blocking collectives: 58.2 us -> none  [on_device(): numer, denom = lax.psum((numer_local, denom_local), 'kv')]
    pmax x1 -> x0, blocking collectives: 58 us -> none  [on_device(): row_top = lax.pmax(local_top, 'kv')]
    ppermute x0 -> x18, waiting for transfers between devices: none -> 31.3 us  [hop(): return lax.ppermute(x, axis, [(i, i ^ distance) for i in range(count)])]
    psum x1 -> x0, waiting for transfers between devices: 28.6 us -> none  [on_device(): numer, denom = lax.psum((numer_local, denom_local), 'kv')]
    all_gather x1 -> x0, blocking collectives: 27.5 us -> none  [on_device(): every_query = lax.all_gather(queries, 'kv', axis=0, tiled=True)]
    ppermute x0 -> x18, starting transfers between devices: none -> 21.1 us  [hop(): return lax.ppermute(x, axis, [(i, i ^ distance) for i in range(count)])]
    pallas_call x0 -> x6, Pallas kernels: none -> 16.7 us  [the longest x1 10.3 us: on_device(): pl.pallas_call(functools.partial(attend_kernel, group), grid=(heads // gr...]
    gather x3 -> x0, local copies, waits for them, and re-layouts: 15 us -> none  [the longest x2 13.4 us: on_device(): jnp.take(every_query, slot_request, axis=0)]
  transfers between devices with their start and end apart: 2 -> 18, of which waited for: 2 -> 13; matrix products, arithmetic and copies ran while one was open for 3% -> 10% of each run, Pallas kernels for 0% -> 1%
where the time goes in v1:
time: 84 us; the launch traced here: 83.4 us
  waiting for transfers between devices  31.3 us (37%)
  starting transfers between devices  21.1 us (25%)
  Pallas kernels  16.7 us (20%)
  local copies, waits for them, and re-layouts  13.5 us (16%)
    ppermute x18, waiting for transfers between devices, hop(): return lax.ppermute(x, axis, [(i, i ^ distance) for i in range(count)])  31.3 us
    ppermute x18, starting transfers between devices, hop(): return lax.ppermute(x, axis, [(i, i ^ distance) for i in range(count)])  21.1 us
    unnamed x18, local copies, waits for them, and re-layouts  12.1 us
    pallas_call x1, Pallas kernels, on_device(): pl.pallas_call(functools.partial(attend_kernel, group), grid=(heads // gr...  10.3 us
    pallas_call x1, Pallas kernels, project(): pl.pallas_call(functools.partial(project_kernel, mid, own_rows), grid=(de...  4.18 us
  transfers between devices with their start and end apart: 18, of which 13 were waited for; matrix products, arithmetic and copies ran while one was open for 10% of the time, Pallas kernels for 1%

profile of v1, /device:TPU:0, one launch (start us, length us, event | category | flops | bytes accessed | tf_op | source)
XLA Modules:
  0.0 83.4 jit_solution(14280097912039391124)
XLA Ops:
  0.0 3.0 %collective-permute-start = (bf16[8,3584]{1,0:T(8,128)(2,1)}, bf16[8,3584]{1,0:T(8,128)(2,1)S(1)}, u32[]{:S(2)}, u32[]{:S(2)}) collective-permute-start(bf16[8,3584]{1,0:T(8,128)(2,1)} %queries.1), channel_id=1, source_target_pairs={{0,8},{2,10},{4,12},{6,14},{8,0},{10,2},{12,4},{14,6},{16,24},{18,... | collective-permute-start | bytes 172040 | tf_op jit(solution)/shard_map/ppermute | solution.py:208
  3.0 2.6 %collective-permute-start.1 = (bf16[8,3584]{1,0:T(8,128)(2,1)}, bf16[8,3584]{1,0:T(8,128)(2,1)S(1)}, u32[]{:S(2)}, u32[]{:S(2)}) collective-permute-start(bf16[8,3584]{1,0:T(8,128)(2,1)} %queries.1), channel_id=1, source_target_pairs={{0,16},{2,18},{4,20},{6,22},{8,24},{10,26},{12,28},{14,30},{16,0},... | collective-permute-start | bytes 172040 | tf_op jit(solution)/shard_map/ppermute | solution.py:208
  5.6 0.9 %constant_dynamic-update-slice_fusion.3 = (bf16[32,3584]{1,0:T(8,128)(2,1)S(1)}, bf16[64,3584]{1,0:T(8,128)(2,1)S(1)}) fusion(bf16[8,3584]{1,0:T(8,128)(2,1)} %queries.1), kind=kLoop, calls=%fused_computation.6 | loop fusion | bytes 172032
  6.5 0.0 collective-permute-done
  6.5 2.9 %collective-permute-done.1 = bf16[8,3584]{1,0:T(8,128)(2,1)S(1)} collective-permute-done((bf16[8,3584]{1,0:T(8,128)(2,1)}, bf16[8,3584]{1,0:T(8,128)(2,1)S(1)}, u32[]{:S(2)}, u32[]{:S(2)}) %collective-permute-start.1) | collective-permute-done | bytes 57376 | tf_op jit(solution)/shard_map/ppermute | solution.py:208
  9.4 2.4 %collective-permute-done.2 = bf16[8,3584]{1,0:T(8,128)(2,1)S(1)} collective-permute-done((bf16[8,3584]{1,0:T(8,128)(2,1)}, bf16[8,3584]{1,0:T(8,128)(2,1)S(1)}, u32[]{:S(2)}, u32[]{:S(2)}) %collective-permute-start.2) | collective-permute-done | bytes 57376 | tf_op jit(solution)/shard_map/ppermute | solution.py:208
  11.8 1.6 %collective-permute-start.3 = (bf16[32,3584]{1,0:T(8,128)(2,1)S(1)}, bf16[32,3584]{1,0:T(8,128)(2,1)S(1)}, u32[]{:S(2)}, u32[]{:S(2)}) collective-permute-start(bf16[32,3584]{1,0:T(8,128)(2,1)S(1)} %get-tuple-element.31), channel_id=1, source_target_pairs={{0,4},{2,6},{4,0},{6,2},{8,12},{10,14},{12,8},{14,10},{16,20},{18,... | collective-permute-start | bytes 688136 | tf_op jit(solution)/shard_map/ppermute | solution.py:208
  13.4 0.7 reshape.7.request
  14.1 0.7 reshape.8.valid
  14.7 0.1 pad_add_fusion.ids
  14.8 0.8 copy-done.2
  15.6 0.8 copy-done.3
  16.5 0.7 prep.1
  17.1 0.1 collective-permute-start.4
  17.2 0.7 collective-permute-done.3
  17.9 0.0 collective-permute-start.5
  17.9 0.7 collective-permute-done.4
  18.7 0.7 collective-permute-done.5
  19.4 0.0 copy-start.1
  19.4 1.8 %copy-done.1 = bf16[384,3584]{1,0:T(8,128)(2,1)S(1)} copy-done((bf16[384,3584]{1,0:T(8,128)(2,1)S(1)}, bf16[384,3584]{1,0:T(8,128)(2,1)}, u32[]{:S(2)}) %copy-start.1) | copy-done | bytes 2752536
  21.2 10.3 %attend.1 = (bf16[64,3712]{1,0:T(8,128)(2,1)S(1)}, bf16[64,3712]{1,0:T(8,128)(2,1)S(1)}) custom-call(bf16[32,128]{1,0:T(8,128)(2,1)S(1)} %get-tuple-element.18.pick, f32[32,384]{1,0:T(8,128)S(1)} %get-tuple-element.19.mask, bf16[64,3584]{1,0:T(8,128)(2,1)S(1)} %constant_dynamic-update-slice_fusion.4.near, bf16[64,3584]{1,0:T(8,128)(2,1)S(1)} %pad_maximum_fusion.far, ...), custom_call_target="tpu_custom_call" | custom-call | tf_op jit(solution)/shard_map/attend/pallas_call | solution.py:263
  31.5 0.2 collective-permute-start.6
  31.7 1.7 %collective-permute-done.6.refs_1_ = bf16[64,3712]{1,0:T(8,128)(2,1)S(1)} collective-permute-done((bf16[64,3712]{1,0:T(8,128)(2,1)S(1)}, bf16[64,3712]{1,0:T(8,128)(2,1)S(1)}, u32[]{:S(2)}, u32[]{:S(2)}) %collective-permute-start.6) | collective-permute-done | bytes 475168 | tf_op jit(solution)/shard_map/ppermute | solution.py:208
  33.4 0.7 merge.2
  34.1 1.6 %collective-permute-start.7 = (bf16[32,3712]{1,0:T(8,128)(2,1)S(1)}, bf16[32,3712]{1,0:T(8,128)(2,1)S(1)}, u32[]{:S(2)}, u32[]{:S(2)}) collective-permute-start(bf16[32,3712]{1,0:T(8,128)(2,1)S(1)} %get-tuple-element.23), channel_id=1, source_target_pairs={{0,4},{2,6},{4,0},{6,2},{8,12},{10,14},{12,8},{14,10},{16,20},{18,... | collective-permute-start | bytes 712712 | tf_op jit(solution)/shard_map/ppermute | solution.py:208
  35.7 6.3 %collective-permute-done.7.refs_1_ = bf16[32,3712]{1,0:T(8,128)(2,1)S(1)} collective-permute-done((bf16[32,3712]{1,0:T(8,128)(2,1)S(1)}, bf16[32,3712]{1,0:T(8,128)(2,1)S(1)}, u32[]{:S(2)}, u32[]{:S(2)}) %collective-permute-start.7) | collective-permute-done | bytes 237600 | tf_op jit(solution)/shard_map/ppermute | solution.py:208
  42.0 0.4 merge.3
  42.5 1.4 %collective-permute-start.10 = (bf16[8,3712]{1,0:T(8,128)(2,1)S(1)}, bf16[8,3712]{1,0:T(8,128)(2,1)S(1)}, u32[]{:S(2)}, u32[]{:S(2)}) collective-permute-start(bf16[8,3712]{1,0:T(8,128)(2,1)S(1)} %get-tuple-element.27), channel_id=1, source_target_pairs={{0,24},{2,26},{4,28},{6,30},{8,16},{10,18},{12,20},{14,22},{16,8},... | collective-permute-start | bytes 178184 | tf_op jit(solution)/shard_map/ppermute | solution.py:208
  43.8 0.4 collective-permute-start.8
  44.2 2.7 %collective-permute-start.9 = (bf16[8,3712]{1,0:T(8,128)(2,1)S(1)}, bf16[8,3712]{1,0:T(8,128)(2,1)S(1)}, u32[]{:S(2)}, u32[]{:S(2)}) collective-permute-start(bf16[8,3712]{1,0:T(8,128)(2,1)S(1)} %get-tuple-element.26), channel_id=1, source_target_pairs={{0,16},{2,18},{4,20},{6,22},{8,24},{10,26},{12,28},{14,30},{16,0},... | collective-permute-start | bytes 178184 | tf_op jit(solution)/shard_map/ppermute | solution.py:208
  46.9 1.9 %collective-permute-done.10.refs_3_ = bf16[8,3712]{1,0:T(8,128)(2,1)S(1)} collective-permute-done((bf16[8,3712]{1,0:T(8,128)(2,1)S(1)}, bf16[8,3712]{1,0:T(8,128)(2,1)S(1)}, u32[]{:S(2)}, u32[]{:S(2)}) %collective-permute-start.10) | collective-permute-done | bytes 59424 | tf_op jit(solution)/shard_map/ppermute | solution.py:208
  48.8 0.0 collective-permute-done.8.refs_1_
  48.8 0.6 collective-permute-done.9.refs_2_
  49.4 0.4 last.1
  49.8 1.6 %collective-permute-start.11 = (bf16[8,3584]{1,0:T(8,128)(2,1)S(1)}, bf16[8,3584]{1,0:T(8,128)(2,1)S(1)}, u32[]{:S(2)}, u32[]{:S(2)}) collective-permute-start(bf16[8,3584]{1,0:T(8,128)(2,1)S(1)} %last.1), channel_id=1, source_target_pairs={{0,8},{2,10},{4,12},{6,14},{8,0},{10,2},{12,4},{14,6},{16,24},{18,... | collective-permute-start | bytes 172040 | tf_op jit(solution)/shard_map/ppermute | solution.py:208
  51.4 1.3 %collective-permute-start.12 = (bf16[8,3584]{1,0:T(8,128)(2,1)S(1)}, bf16[8,3584]{1,0:T(8,128)(2,1)S(1)}, u32[]{:S(2)}, u32[]{:S(2)}) collective-permute-start(bf16[8,3584]{1,0:T(8,128)(2,1)S(1)} %last.1), channel_id=1, source_target_pairs={{0,16},{2,18},{4,20},{6,22},{8,24},{10,26},{12,28},{14,30},{16,0},... | collective-permute-start | bytes 172040 | tf_op jit(solution)/shard_map/ppermute | solution.py:208
  52.7 1.6 %collective-permute-start.13 = (bf16[8,3584]{1,0:T(8,128)(2,1)S(1)}, bf16[8,3584]{1,0:T(8,128)(2,1)S(1)}, u32[]{:S(2)}, u32[]{:S(2)}) collective-permute-start(bf16[8,3584]{1,0:T(8,128)(2,1)S(1)} %last.1), channel_id=1, source_target_pairs={{0,24},{2,26},{4,28},{6,30},{8,16},{10,18},{12,20},{14,22},{16,8},... | collective-permute-start | bytes 172040 | tf_op jit(solution)/shard_map/ppermute | solution.py:208
  54.3 0.0 collective-permute-done.11
  54.3 2.8 %collective-permute-done.12 = bf16[8,3584]{1,0:T(8,128)(2,1)S(1)} collective-permute-done((bf16[8,3584]{1,0:T(8,128)(2,1)S(1)}, bf16[8,3584]{1,0:T(8,128)(2,1)S(1)}, u32[]{:S(2)}, u32[]{:S(2)}) %collective-permute-start.12) | collective-permute-done | bytes 57376 | tf_op jit(solution)/shard_map/ppermute | solution.py:208
  57.1 1.6 %collective-permute-done.13 = bf16[8,3584]{1,0:T(8,128)(2,1)S(1)} collective-permute-done((bf16[8,3584]{1,0:T(8,128)(2,1)S(1)}, bf16[8,3584]{1,0:T(8,128)(2,1)S(1)}, u32[]{:S(2)}, u32[]{:S(2)}) %collective-permute-start.13) | collective-permute-done | bytes 57376 | tf_op jit(solution)/shard_map/ppermute | solution.py:208
  58.7 1.6 %collective-permute-start.14 = (bf16[32,3584]{1,0:T(8,128)(2,1)S(1)}, bf16[32,3584]{1,0:T(8,128)(2,1)S(1)}, u32[]{:S(2)}, u32[]{:S(2)}) collective-permute-start(bf16[32,3584]{1,0:T(8,128)(2,1)S(1)} %pad_maximum_fusion.1.refs_0_), channel_id=1, source_target_pairs={{0,4},{2,6},{4,0},{6,2},{8,12},{10,14},{12,8},{14,10},{16,20},{18,... | collective-permute-start | bytes 688136 | tf_op jit(solution)/shard_map/ppermute | solution.py:208
  60.3 4.5 %collective-permute-done.14.refs_1_ = bf16[32,3584]{1,0:T(8,128)(2,1)S(1)} collective-permute-done((bf16[32,3584]{1,0:T(8,128)(2,1)S(1)}, bf16[32,3584]{1,0:T(8,128)(2,1)S(1)}, u32[]{:S(2)}, u32[]{:S(2)}) %collective-permute-start.14) | collective-permute-done | bytes 229408 | tf_op jit(solution)/shard_map/ppermute | solution.py:208
  64.8 5.7 %copy.11.refs_4_ = bf16[3584,448]{1,0:T(8,128)(2,1)} copy(bf16[3584,448]{0,1:T(8,128)(2,1)} %param.17) | data formatting | bytes 6422528 | tf_op args[7]
  70.6 2.0 %copy-done = bf16[3584,448]{1,0:T(8,128)(2,1)S(1)} copy-done((bf16[3584,448]{1,0:T(8,128)(2,1)S(1)}, bf16[3584,448]{1,0:T(8,128)(2,1)}, u32[]{:S(2)}) %copy-start) | copy-done | bytes 3211288
  72.6 4.2 %project.1 = (f32[64,448]{1,0:T(8,128)S(1)}, f32[64,448]{1,0:T(8,128)S(1)}) custom-call(s32[2]{0:T(128)S(1)} %pad_add_fusion.ids, bf16[32,3584]{1,0:T(8,128)(2,1)S(1)} %pad_maximum_fusion.1.refs_0_, bf16[32,3584]{1,0:T(8,128)(2,1)S(1)} %collective-permute-done.14.refs_1_, bf16[32,3584]{1,0:T(8,128)(2,1)S(1)} %collective-permute-done.15.refs_2_, ...), custom_call_target="tpu_custom_call" | custom-call | tf_op jit(solution)/shard_map/project/pallas_call | solution.py:322
  76.8 1.6 %collective-permute-start.17 = (f32[64,448]{1,0:T(8,128)S(1)}, f32[64,448]{1,0:T(8,128)S(1)}, u32[]{:S(2)}, u32[]{:S(2)}) collective-permute-start(f32[64,448]{1,0:T(8,128)S(1)} %get-tuple-element.30), channel_id=1, source_target_pairs={{0,1},{1,0},{2,3},{3,2},{4,5},{5,4},{6,7},{7,6},{8,9},{9,8},{10,11... | collective-permute-start | bytes 344072 | tf_op jit(solution)/shard_map/ppermute | solution.py:208
  78.4 4.4 %collective-permute-done.17 = f32[64,448]{1,0:T(8,128)S(1)} collective-permute-done((f32[64,448]{1,0:T(8,128)S(1)}, f32[64,448]{1,0:T(8,128)S(1)}, u32[]{:S(2)}, u32[]{:S(2)}) %collective-permute-start.17) | collective-permute-done | bytes 114720 | tf_op jit(solution)/shard_map/ppermute | solution.py:208
  82.8 0.7 add_convert_fusion
  (21 shorter events, 0.1 us)
Async XLA Ops:
  0.0 6.5 %collective-permute-start = (bf16[8,3584]{1,0:T(8,128)(2,1)}, bf16[8,3584]{1,0:T(8,128)(2,1)S(1)}, u32[]{:S(2)}, u32[]{:S(2)}) collective-permute-start(bf16[8,3584]{1,0:T(8,128)(2,1)} %queries.1), channel_id=1, source_target_pairs={{0,8},{2,10},{4,12},{6,14},{8,0},{10,2},{12,4},{14,6},{16,24},{18,... | collective-permute-start | bytes 172040 | tf_op jit(solution)/shard_map/ppermute | solution.py:208
  3.0 6.4 %collective-permute-start.1 = (bf16[8,3584]{1,0:T(8,128)(2,1)}, bf16[8,3584]{1,0:T(8,128)(2,1)S(1)}, u32[]{:S(2)}, u32[]{:S(2)}) collective-permute-start(bf16[8,3584]{1,0:T(8,128)(2,1)} %queries.1), channel_id=1, source_target_pairs={{0,16},{2,18},{4,20},{6,22},{8,24},{10,26},{12,28},{14,30},{16,0},... | collective-permute-start | bytes 172040 | tf_op jit(solution)/shard_map/ppermute | solution.py:208
  5.6 6.2 %collective-permute-start.2 = (bf16[8,3584]{1,0:T(8,128)(2,1)}, bf16[8,3584]{1,0:T(8,128)(2,1)S(1)}, u32[]{:S(2)}, u32[]{:S(2)}) collective-permute-start(bf16[8,3584]{1,0:T(8,128)(2,1)} %queries.1), channel_id=1, source_target_pairs={{0,24},{2,26},{4,28},{6,30},{8,16},{10,18},{12,20},{14,22},{16,8},... | collective-permute-start | bytes 172040 | tf_op jit(solution)/shard_map/ppermute | solution.py:208
  11.8 6.1 %collective-permute-start.3 = (bf16[32,3584]{1,0:T(8,128)(2,1)S(1)}, bf16[32,3584]{1,0:T(8,128)(2,1)S(1)}, u32[]{:S(2)}, u32[]{:S(2)}) collective-permute-start(bf16[32,3584]{1,0:T(8,128)(2,1)S(1)} %get-tuple-element.31), channel_id=1, source_target_pairs={{0,4},{2,6},{4,0},{6,2},{8,12},{10,14},{12,8},{14,10},{16,20},{18,... | collective-permute-start | bytes 688136 | tf_op jit(solution)/shard_map/ppermute | solution.py:208
  14.8 0.8 copy-start.2
  15.6 0.8 copy-start.3
  17.1 1.6 %collective-permute-start.4 = (bf16[32,3584]{1,0:T(8,128)(2,1)S(1)}, bf16[32,3584]{1,0:T(8,128)(2,1)S(1)}, u32[]{:S(2)}, u32[]{:S(2)}) collective-permute-start(bf16[32,3584]{1,0:T(8,128)(2,1)S(1)} %get-tuple-element.31), channel_id=1, source_target_pairs={{0,2},{2,0},{4,6},{6,4},{8,10},{10,8},{12,14},{14,12},{16,18},{18,... | collective-permute-start | bytes 688136 | tf_op jit(solution)/shard_map/ppermute | solution.py:208
  17.9 1.5 %collective-permute-start.5 = (bf16[32,3584]{1,0:T(8,128)(2,1)S(1)}, bf16[32,3584]{1,0:T(8,128)(2,1)S(1)}, u32[]{:S(2)}, u32[]{:S(2)}) collective-permute-start(bf16[32,3584]{1,0:T(8,128)(2,1)S(1)} %collective-permute-done.3), channel_id=1, source_target_pairs={{0,2},{2,0},{4,6},{6,4},{8,10},{10,8},{12,14},{14,12},{16,18},{18,... | collective-permute-start | bytes 688136 | tf_op jit(solution)/shard_map/ppermute | solution.py:208
  19.4 1.8 %copy-start.1 = (bf16[384,3584]{1,0:T(8,128)(2,1)S(1)}, bf16[384,3584]{1,0:T(8,128)(2,1)}, u32[]{:S(2)}) copy-start(bf16[384,3584]{1,0:T(8,128)(2,1)} %keys.1) | copy-start | bytes 8257540
  21.2 28.2 %copy-start.4 = (bf16[8,3584]{1,0:T(8,128)(2,1)S(1)}, bf16[8,3584]{1,0:T(8,128)(2,1)}, u32[]{:S(2)}) copy-start(bf16[8,3584]{1,0:T(8,128)(2,1)} %refs_4_.2) | copy-start | bytes 172036
  31.5 1.9 %collective-permute-start.6 = (bf16[64,3712]{1,0:T(8,128)(2,1)S(1)}, bf16[64,3712]{1,0:T(8,128)(2,1)S(1)}, u32[]{:S(2)}, u32[]{:S(2)}) collective-permute-start(bf16[64,3712]{1,0:T(8,128)(2,1)S(1)} %get-tuple-element.21), channel_id=1, source_target_pairs={{0,2},{2,0},{4,6},{6,4},{8,10},{10,8},{12,14},{14,12},{16,18},{18,... | collective-permute-start | bytes 1425416 | tf_op jit(solution)/shard_map/ppermute | solution.py:208
  34.1 7.9 %collective-permute-start.7 = (bf16[32,3712]{1,0:T(8,128)(2,1)S(1)}, bf16[32,3712]{1,0:T(8,128)(2,1)S(1)}, u32[]{:S(2)}, u32[]{:S(2)}) collective-permute-start(bf16[32,3712]{1,0:T(8,128)(2,1)S(1)} %get-tuple-element.23), channel_id=1, source_target_pairs={{0,4},{2,6},{4,0},{6,2},{8,12},{10,14},{12,8},{14,10},{16,20},{18,... | collective-permute-start | bytes 712712 | tf_op jit(solution)/shard_map/ppermute | solution.py:208
  42.5 6.3 %collective-permute-start.10 = (bf16[8,3712]{1,0:T(8,128)(2,1)S(1)}, bf16[8,3712]{1,0:T(8,128)(2,1)S(1)}, u32[]{:S(2)}, u32[]{:S(2)}) collective-permute-start(bf16[8,3712]{1,0:T(8,128)(2,1)S(1)} %get-tuple-element.27), channel_id=1, source_target_pairs={{0,24},{2,26},{4,28},{6,30},{8,16},{10,18},{12,20},{14,22},{16,8},... | collective-permute-start | bytes 178184 | tf_op jit(solution)/shard_map/ppermute | solution.py:208
  43.8 5.0 %collective-permute-start.8 = (bf16[8,3712]{1,0:T(8,128)(2,1)S(1)}, bf16[8,3712]{1,0:T(8,128)(2,1)S(1)}, u32[]{:S(2)}, u32[]{:S(2)}) collective-permute-start(bf16[8,3712]{1,0:T(8,128)(2,1)S(1)} %get-tuple-element.25), channel_id=1, source_target_pairs={{0,8},{2,10},{4,12},{6,14},{8,0},{10,2},{12,4},{14,6},{16,24},{18,... | collective-permute-start | bytes 178184 | tf_op jit(solution)/shard_map/ppermute | solution.py:208
  44.2 5.2 %collective-permute-start.9 = (bf16[8,3712]{1,0:T(8,128)(2,1)S(1)}, bf16[8,3712]{1,0:T(8,128)(2,1)S(1)}, u32[]{:S(2)}, u32[]{:S(2)}) collective-permute-start(bf16[8,3712]{1,0:T(8,128)(2,1)S(1)} %get-tuple-element.26), channel_id=1, source_target_pairs={{0,16},{2,18},{4,20},{6,22},{8,24},{10,26},{12,28},{14,30},{16,0},... | collective-permute-start | bytes 178184 | tf_op jit(solution)/shard_map/ppermute | solution.py:208
  49.8 4.5 %collective-permute-start.11 = (bf16[8,3584]{1,0:T(8,128)(2,1)S(1)}, bf16[8,3584]{1,0:T(8,128)(2,1)S(1)}, u32[]{:S(2)}, u32[]{:S(2)}) collective-permute-start(bf16[8,3584]{1,0:T(8,128)(2,1)S(1)} %last.1), channel_id=1, source_target_pairs={{0,8},{2,10},{4,12},{6,14},{8,0},{10,2},{12,4},{14,6},{16,24},{18,... | collective-permute-start | bytes 172040 | tf_op jit(solution)/shard_map/ppermute | solution.py:208
  51.4 5.7 %collective-permute-start.12 = (bf16[8,3584]{1,0:T(8,128)(2,1)S(1)}, bf16[8,3584]{1,0:T(8,128)(2,1)S(1)}, u32[]{:S(2)}, u32[]{:S(2)}) collective-permute-start(bf16[8,3584]{1,0:T(8,128)(2,1)S(1)} %last.1), channel_id=1, source_target_pairs={{0,16},{2,18},{4,20},{6,22},{8,24},{10,26},{12,28},{14,30},{16,0},... | collective-permute-start | bytes 172040 | tf_op jit(solution)/shard_map/ppermute | solution.py:208
  52.7 6.0 %collective-permute-start.13 = (bf16[8,3584]{1,0:T(8,128)(2,1)S(1)}, bf16[8,3584]{1,0:T(8,128)(2,1)S(1)}, u32[]{:S(2)}, u32[]{:S(2)}) collective-permute-start(bf16[8,3584]{1,0:T(8,128)(2,1)S(1)} %last.1), channel_id=1, source_target_pairs={{0,24},{2,26},{4,28},{6,30},{8,16},{10,18},{12,20},{14,22},{16,8},... | collective-permute-start | bytes 172040 | tf_op jit(solution)/shard_map/ppermute | solution.py:208
  58.7 6.1 %collective-permute-start.14 = (bf16[32,3584]{1,0:T(8,128)(2,1)S(1)}, bf16[32,3584]{1,0:T(8,128)(2,1)S(1)}, u32[]{:S(2)}, u32[]{:S(2)}) collective-permute-start(bf16[32,3584]{1,0:T(8,128)(2,1)S(1)} %pad_maximum_fusion.1.refs_0_), channel_id=1, source_target_pairs={{0,4},{2,6},{4,0},{6,2},{8,12},{10,14},{12,8},{14,10},{16,20},{18,... | collective-permute-start | bytes 688136 | tf_op jit(solution)/shard_map/ppermute | solution.py:208
  60.3 10.3 %collective-permute-start.15 = (bf16[32,3584]{1,0:T(8,128)(2,1)S(1)}, bf16[32,3584]{1,0:T(8,128)(2,1)S(1)}, u32[]{:S(2)}, u32[]{:S(2)}) collective-permute-start(bf16[32,3584]{1,0:T(8,128)(2,1)S(1)} %pad_maximum_fusion.1.refs_0_), channel_id=1, source_target_pairs={{0,2},{2,0},{4,6},{6,4},{8,10},{10,8},{12,14},{14,12},{16,18},{18,... | collective-permute-start | bytes 688136 | tf_op jit(solution)/shard_map/ppermute | solution.py:208
  64.8 5.8 %collective-permute-start.16 = (bf16[32,3584]{1,0:T(8,128)(2,1)S(1)}, bf16[32,3584]{1,0:T(8,128)(2,1)S(1)}, u32[]{:S(2)}, u32[]{:S(2)}) collective-permute-start(bf16[32,3584]{1,0:T(8,128)(2,1)S(1)} %collective-permute-done.14.refs_1_), channel_id=1, source_target_pairs={{0,2},{2,0},{4,6},{6,4},{8,10},{10,8},{12,14},{14,12},{16,18},{18,... | collective-permute-start | bytes 688136 | tf_op jit(solution)/shard_map/ppermute | solution.py:208
  64.8 13.6 %copy-start.6 = (bf16[448]{0:T(512)(128)(2,1)S(1)}, bf16[448]{0:T(512)(128)(2,1)}, u32[]{:S(2)}) copy-start(bf16[448]{0:T(512)(128)(2,1)} %param.18) | copy-start | bytes 2692
  64.8 18.0 %copy-start.5 = (bf16[64,448]{1,0:T(8,128)(2,1)S(1)}, bf16[64,448]{1,0:T(8,128)(2,1)}, u32[]{:S(2)}) copy-start(bf16[64,448]{1,0:T(8,128)(2,1)} %param.19) | copy-start | bytes 172036
  70.6 2.0 %copy-start = (bf16[3584,448]{1,0:T(8,128)(2,1)S(1)}, bf16[3584,448]{1,0:T(8,128)(2,1)}, u32[]{:S(2)}) copy-start(bf16[3584,448]{1,0:T(8,128)(2,1)} %copy.11.refs_4_) | copy-start | bytes 9633796
  76.8 6.0 %collective-permute-start.17 = (f32[64,448]{1,0:T(8,128)S(1)}, f32[64,448]{1,0:T(8,128)S(1)}, u32[]{:S(2)}, u32[]{:S(2)}) collective-permute-start(f32[64,448]{1,0:T(8,128)S(1)} %get-tuple-element.30), channel_id=1, source_target_pairs={{0,1},{1,0},{2,3},{3,2},{4,5},{5,4},{6,7},{7,6},{8,9},{9,8},{10,11... | collective-permute-start | bytes 344072 | tf_op jit(solution)/shard_map/ppermute | solution.py:208

commit v2 on v1

v2 whole, which is shorter than its diff:
```python
import functools
import math

import jax
import jax.numpy as jnp
from jax import lax
from jax.experimental import pallas as pl
from jax.experimental.pallas import tpu as pltpu
from jax.sharding import PartitionSpec as P

HD = 128
PAGE = 16
OUTER = 4
LANES = 128
STAT = 32

floor_score = -1e30
PACK_US = 5
f32 = jnp.float32
bf16 = jnp.bfloat16
WHOLE = pl.BlockSpec(memory_space=pltpu.VMEM)
SCALARS = pl.BlockSpec(memory_space=pltpu.SMEM)
ANY = pl.BlockSpec(memory_space=pl.ANY)


def params(megabytes=24):
    return pltpu.CompilerParams(vmem_limit_bytes=megabytes * 1024 * 1024)


def offset_of(block, mid):
    core = block // (mid * OUTER)
    middle = (block // OUTER) % mid
    return core + 2 * middle + 2 * mid * (OUTER - 1 - block % OUTER)


def place_of(offset, mid):
    core = offset % 2
    middle = (offset // 2) % mid
    return (core * mid + middle) * OUTER + OUTER - 1 - offset // (2 * mid)


def prep_kernel(
    mid, own_rows, ids, request, valid, queries, new_keys, pick, mask, own_top
):
    rows, slots = mask.shape
    row = lax.broadcasted_iota(jnp.int32, (rows, slots), 0)
    lane = lax.broadcasted_iota(jnp.int32, (rows, slots), 1)
    owners = jnp.broadcast_to(request[...], (rows, slots))
    mine = jnp.sum(jnp.where(lane == row * PAGE, owners, 0), axis=1, keepdims=True)
    before = jnp.sum(jnp.where(lane == row * PAGE - PAGE, owners, 0), axis=1, keepdims=True)
    page = lax.broadcasted_iota(jnp.int32, (rows, 1), 0)
    first = ((page == 0) | (mine != before)) & (page < slots // PAGE)
    live = (owners == mine) & first & (jnp.broadcast_to(valid[...], (rows, slots)) == 1)
    mask[...] = jnp.where(live, 1.0, 0.0)
    place = lax.broadcasted_iota(jnp.int32, pick.shape, 1)
    owner = lax.bitwise_xor(offset_of(place // own_rows, mid), ids[0])
    named = owner * own_rows + place % own_rows
    pick[...] = jnp.where((named == mine) & first, 1.0, 0.0).astype(bf16)
    heads = queries.shape[1] // HD
    where = lax.broadcasted_iota(jnp.int32, own_top.shape, 1)
    top = jnp.zeros(own_top.shape, f32)
    for head in range(heads):
        cut = slice(head * HD, (head + 1) * HD)
        score = jnp.sum(
            queries[:, cut].astype(f32) * new_keys[:, cut].astype(f32), axis=1, keepdims=True
        ) * (1.0 / math.sqrt(HD))
        top = jnp.where(where == head, score, top)
    own_top[...] = top


def split_top(top):
    lane = lax.broadcasted_iota(jnp.int32, top.shape, 1)
    top = jnp.where(lane < STAT, top, 0.0)
    high = top.astype(bf16).astype(f32)
    rest = top - high
    middle = rest.astype(bf16).astype(f32)
    low = rest - middle
    return high + pltpu.roll(middle, STAT, 1) + pltpu.roll(low, 2 * STAT, 1)


def join_top(stat):
    return (stat + pltpu.roll(stat, LANES - STAT, 1)) + pltpu.roll(stat, LANES - 2 * STAT, 1)


def stacked(refs):
    return jnp.concatenate([ref[...].astype(f32) for ref in refs], axis=0)


def pack_kernel(count, tail, *refs):
    outs = refs[len(refs) - 1 - tail :]
    rows = stacked(refs[:count]).astype(bf16)
    outs[0][...] = rows
    if tail:
        outs[1][...] = rows[: outs[1].shape[0]]


def attend_kernel(count, pick, mask, keys, values, *refs):
    blocks, (keep, send) = refs[:count], refs[count:]
    rows = pick.shape[0]
    heads = keys.shape[1] // HD
    half = keep.shape[0]
    lane = lax.broadcasted_iota(jnp.int32, (rows, LANES), 1)
    live = mask[...] > 0.0
    chosen = jnp.dot(pick[...], stacked(blocks).astype(bf16), preferred_element_type=f32)
    zero = jnp.zeros((rows, HD), f32)
    sets = [tuple(range(at, min(at + 2, heads))) for at in range(0, heads, 2)]
    cuts = [slice(each[0] * HD, (each[-1] + 1) * HD) for each in sets]

    def diagonal(each):
        bands = [
            jnp.concatenate(
                [chosen[:, head * HD : (head + 1) * HD] if other == head else zero for other in each],
                axis=1,
            )
            for head in each
        ]
        return jnp.concatenate(bands, axis=0).astype(bf16)

    scores = [
        lax.dot_general(
            diagonal(each), keys[:, cut], (((1,), (1,)), ((), ())), preferred_element_type=f32
        )
        for each, cut in zip(sets, cuts)
    ]
    tops = jnp.zeros((rows, LANES), f32)
    weights, denoms = [], []
    for each, score in zip(sets, scores):
        wide = jnp.concatenate([live] * len(each), axis=0)
        score = jnp.where(wide, score * (1.0 / math.sqrt(HD)), floor_score)
        top = jnp.max(score, axis=1, keepdims=True)
        weight = jnp.where(wide, jnp.exp(score - top), 0.0).astype(bf16)
        denom = jnp.sum(weight.astype(f32), axis=1, keepdims=True)
        denom = jnp.where(denom > 0.0, denom, 1.0)
        weights.append(weight)
        denoms.append(denom)
        for at, head in enumerate(each):
            part = slice(at * rows, (at + 1) * rows)
            tops = jnp.where(lane == head, top[part] + jnp.log(denom[part]), tops)
    found = []
    for each, cut, weight, denom in zip(sets, cuts, weights, denoms):
        numer = jnp.dot(weight, values[:, cut], preferred_element_type=f32) / denom
        for at in range(len(each)):
            found.append(numer[at * rows : (at + 1) * rows, at * HD : (at + 1) * HD])
    spread = functools.partial(
        lax.dot_general, dimension_numbers=(((0,), (0,)), ((), ())), preferred_element_type=f32
    )
    dense = spread(pick[...], jnp.concatenate(found, axis=1).astype(bf16)).astype(bf16)
    stat = jnp.where(lane == LANES - 1, 1.0, split_top(tops)).astype(bf16)
    stat = spread(pick[...], stat)
    place = lax.broadcasted_iota(jnp.int32, stat.shape, 1)
    absent = stat[:, LANES - 1 :] == 0.0
    stat = jnp.where(absent & (place < STAT), floor_score, stat).astype(bf16)
    for out, part in ((keep, slice(0, half)), (send, slice(half, 2 * half))):
        out[:, : heads * HD] = dense[part]
        out[:, heads * HD :] = stat[part]


def merge(parts, tops):
    best = functools.reduce(jnp.maximum, tops)
    weights = [jnp.exp(top - best) for top in tops]
    total = functools.reduce(jnp.add, weights)
    shares = [weight / total for weight in weights]

    def head_of(head):
        terms = [
            share[:, head : head + 1] * part(head) for share, part in zip(shares, parts)
        ]
        return functools.reduce(jnp.add, terms)

    return head_of, best + jnp.log(total)


def part_of(ref):
    return lambda head: ref[:, head * HD : (head + 1) * HD].astype(f32)


def top_of(ref):
    return join_top(ref[:, ref.shape[1] - LANES :].astype(f32))


def merge_kernel(count, *refs):
    ins, outs = refs[:count], refs[count:]
    heads = ins[0].shape[1] // HD - 1
    rows = outs[0].shape[0]
    head_of, top = merge([part_of(ref) for ref in ins], [top_of(ref) for ref in ins])
    for head in range(heads + 1):
        cut = slice(head * HD, (head + 1) * HD)
        block = head_of(head) if head < heads else split_top(top)
        for at, out in enumerate(outs):
            out[:, cut] = block[at * rows : (at + 1) * rows].astype(bf16)


def last_kernel(count, *refs):
    ins = refs[:count]
    new_values, own_top, out = refs[count:]
    head_of, _ = merge(
        [part_of(ref) for ref in ins] + [part_of(new_values)],
        [top_of(ref) for ref in ins] + [own_top[...]],
    )
    for head in range(out.shape[1] // HD):
        out[:, head * HD : (head + 1) * HD] = head_of(head).astype(bf16)


def by_weight(blocks, weight):
    return lax.dot_general(
        stacked(blocks).astype(bf16), weight[...], (((1,), (1,)), ((), ())), preferred_element_type=f32
    )


def project_kernel(mid, own_rows, count, ids, *refs):
    blocks, weight, outs, acc = refs[:count], refs[count], refs[count + 1 : -1], refs[-1]
    acc[...] = by_weight(blocks, weight)
    owners = outs[0].shape[0] // own_rows
    for distance, out in enumerate(outs):
        side = lax.bitwise_xor(ids[1], distance)
        for at in range(owners):
            offset = lax.bitwise_xor(side * owners + at, ids[0])
            start = pl.multiple_of(place_of(offset, mid) * own_rows, own_rows)
            out[at * own_rows : (at + 1) * own_rows, :] = acc[pl.ds(start, own_rows), :]


def part_kernel(mid, nears, own_rows, count, ids, *refs):
    blocks, weight, outs, acc = refs[:count], refs[count], refs[count + 1 : -1], refs[-1]
    acc[...] = by_weight(blocks, weight)
    outers = outs[0].shape[0] // (own_rows * 2 * len(nears))
    for distance, out in enumerate(outs):
        side = lax.bitwise_xor(ids[1], distance)
        for at in range(len(nears) * outers * 2):
            near, outer, core = at // (2 * outers), side * outers + (at // 2) % outers, at % 2
            place = lax.bitwise_xor(core, ids[0] % 2) * len(nears) + near
            place = place * OUTER + OUTER - 1 - lax.bitwise_xor(outer, ids[0] // (2 * mid))
            start = pl.multiple_of(place * own_rows, own_rows)
            out[at * own_rows : (at + 1) * own_rows, :] = acc[pl.ds(start, own_rows), :]


def add_part(total, part, mid, nears, own_rows, ids):
    outers = part.shape[0] // (own_rows * 2 * len(nears))
    for at in range(len(nears) * outers * 2):
        near, outer, core = at // (2 * outers), (at // 2) % outers, at % 2
        middle = lax.bitwise_xor((ids[0] // 2) % mid, nears[near])
        start = pl.multiple_of(((outer * mid + middle) * 2 + core) * own_rows, own_rows)
        total[pl.ds(start, own_rows), :] += part[at * own_rows : (at + 1) * own_rows]


def base_kernel(mid, own_rows, ids, kept, residual, bias, total):
    total[...] = residual[...].astype(f32) + bias[...].astype(f32)
    add_part(total, kept[...], mid, (0,), own_rows, ids)


def final_kernel(mid, nears, own_rows, ids, base, early, kept, received, out, total):
    total[...] = base[...]
    add_part(total, early[...], mid, (0,), own_rows, ids)
    add_part(total, kept[...] + received[...], mid, nears, own_rows, ids)
    out[...] = total[...].astype(bf16)


def hop(x, axis, count, distance):
    return lax.ppermute(x, axis, [(i, i ^ distance) for i in range(count)])


def on_device(
    kv_count,
    tp_count,
    queries,
    new_keys,
    new_values,
    keys,
    values,
    slot_request,
    slot_valid,
    out_weight,
    out_bias,
    residual,
):
    own_rows, width = queries.shape
    slots = keys.shape[0]
    mid = kv_count // (2 * OUTER)
    requests = kv_count * own_rows
    rows = -(-(slots // PAGE) // 16) * 16
    wide = width + LANES
    ids = jnp.stack([lax.axis_index("kv"), lax.axis_index("tp")]).astype(jnp.int32)
    kv_hop = lambda x, distance: hop(x, "kv", kv_count, distance)
    shaped = jax.ShapeDtypeStruct

    def call(kernel, shapes, scratch, name, *operands, spec=lambda at: WHOLE, us=1):
        single = not isinstance(shapes, tuple)
        return pl.pallas_call(
            kernel,
            out_shape=shapes,
            in_specs=[SCALARS if x is ids else spec(at) for at, x in enumerate(operands)],
            out_specs=WHOLE if single else (WHOLE,) * len(shapes),
            scratch_shapes=scratch,
            compiler_params=params(),
            cost_estimate=pl.CostEstimate(
                flops=0, bytes_accessed=int(us * 3.5e6), transcendentals=0
            ),
            name=name,
        )(*operands)

    def pack(parts, head, after):
        height = sum(x.shape[0] for x in parts)
        shapes = [shaped((rows, width), bf16) for rows in (height, head) if rows]
        return call(
            functools.partial(pack_kernel, len(parts), len(shapes) - 1),
            tuple(shapes),
            [],
            "pack",
            *parts,
            *after,
            spec=lambda at: WHOLE if at < len(parts) else ANY,
            us=PACK_US,
        )

    def gather(block, before, between):
        outer = {far: kv_hop(block, 2 * mid * far) for far in (3, 2, 1)}
        own = {near: kv_hop(block, 2 * near) for near in range(1, mid)}
        near_all, pair = pack([outer[3], outer[2], outer[1], block], 2 * own_rows, [*own.values(), *before])
        near_other = kv_hop(near_all, 1)
        far = []
        for near in range(1, mid):
            far += [kv_hop(pair, 2 * near), kv_hop(outer[1], 2 * near), own[near]]
        after, kept = between(near_all, near_other)
        (far_all,) = pack(far, 0, after)
        return near_all, far_all, near_other, kv_hop(far_all, 1), kept

    pick, mask, own_top = call(
        functools.partial(prep_kernel, mid, own_rows),
        (
            shaped((rows, requests), bf16),
            shaped((rows, slots), f32),
            shaped((own_rows, LANES), f32),
        ),
        [],
        "prep",
        ids,
        slot_request.reshape(1, slots),
        slot_valid.reshape(1, slots),
        queries,
        new_keys,
    )
    *blocks, _ = gather(queries, [keys], lambda near_all, near_other: ([pick, values], None))
    half = requests // 2
    keep, send = call(
        functools.partial(attend_kernel, len(blocks)),
        (shaped((half, wide), bf16),) * 2,
        [],
        "attend",
        pick,
        mask,
        keys,
        values,
        *blocks,
    )

    def merged(ins, count):
        size = ins[0].shape[0] // count
        return call(
            functools.partial(merge_kernel, len(ins)),
            (shaped((size, wide), bf16),) * count,
            [],
            "merge",
            *ins,
        )

    blocks = merged([keep, kv_hop(send, 1)], 2 * mid)
    outer = []
    for at in (0, 1):
        there = [kv_hop(blocks[2 * near + at], 2 * near) for near in range(1, mid)]
        outer += merged([blocks[at]] + there, 2)
    ins = [outer[3]] + [kv_hop(outer[OUTER - 1 - far], 2 * mid * far) for far in (3, 2, 1)]
    attended = call(
        functools.partial(last_kernel, len(ins)),
        shaped((own_rows, width), bf16),
        [],
        "last",
        *ins,
        new_values,
        own_top,
    )

    weight = out_weight.T
    columns = out_weight.shape[1]

    def projected(kernel, blocks, nears):
        height = 2 * OUTER * nears * own_rows
        return call(
            functools.partial(kernel, own_rows, len(blocks)),
            (shaped((height // tp_count, columns), f32),) * tp_count,
            [pltpu.VMEM((height, columns), f32)],
            "project",
            ids,
            *blocks,
            weight,
        )

    tp_hop = lambda x, distance: hop(x, "tp", tp_count, distance)
    sets = ((0,), tuple(range(1, mid)))
    if tp_count == 2 and (kv_count // tp_count) % (2 * mid) == 0:

        def early(near_all, near_other):
            part = functools.partial(part_kernel, mid, sets[0])
            kept, sent = projected(part, [near_all, near_other], 1)
            base = call(
                functools.partial(base_kernel, mid, own_rows),
                shaped(residual.shape, f32),
                [],
                "base",
                ids,
                kept,
                residual,
                out_bias.reshape(1, columns),
            )
            return [base], [base, tp_hop(sent, 1)]

        _, far_all, _, far_other, parts = gather(attended, [], early)
        part = functools.partial(part_kernel, mid, sets[1])
        kept, sent = projected(part, [far_all, far_other], mid - 1)
        return call(
            functools.partial(final_kernel, mid, sets[1], own_rows),
            shaped(residual.shape, bf16),
            [pltpu.VMEM(residual.shape, f32)],
            "final",
            ids,
            *parts,
            kept,
            tp_hop(sent, 1),
        )
    *blocks, _ = gather(attended, [], lambda near_all, near_other: ([], None))
    outs = projected(functools.partial(project_kernel, mid), blocks, mid)
    total = outs[0]
    for distance in range(1, tp_count):
        total = total + tp_hop(outs[distance], distance)
    total = total + residual.astype(f32) + out_bias.astype(f32)[None, :]
    return total.astype(bf16)


def solution(mesh):
    placed = (
        P("kv", "tp"),
        P("kv", "tp"),
        P("kv", "tp"),
        P("kv", "tp"),
        P("kv", "tp"),
        P("kv"),
        P("kv"),
        P("tp", "kv"),
        P("kv"),
        P("tp", "kv"),
    )
    return jax.shard_map(
        functools.partial(on_device, mesh.shape["kv"], mesh.shape["tp"]),
        mesh=mesh,
        in_specs=placed,
        out_specs=P("tp", "kv"),
        check_vma=False,
    )
```

time: 84 us -> 68.6 us (0.82)
  local copies, waits for them, and re-layouts: 13.5 us -> 4.62 us
  Pallas kernels: 16.7 us -> 9.39 us
  starting transfers between devices: 21.1 us -> 26.7 us
  waiting for transfers between devices: 31.3 us -> 27.3 us
    unnamed x18 -> x26, local copies, waits for them, and re-layouts: 12.1 us -> 4.61 us
    pallas_call x6 -> x14, Pallas kernels: 16.7 us -> 9.39 us  [call(): pl.pallas_call(kernel, out_shape=shapes, in_specs=[SCALARS if x is ids el...]
    ppermute x18 -> x24, starting transfers between devices: 21.1 us -> 26.7 us  [hop(): return lax.ppermute(x, axis, [(i, i ^ distance) for i in range(count)])]
    ppermute x18 -> x24, waiting for transfers between devices: 31.3 us -> 27.3 us  [hop(): return lax.ppermute(x, axis, [(i, i ^ distance) for i in range(count)])]
  transfers between devices with their start and end apart: 18 -> 24, of which waited for: 13 -> 14; matrix products, arithmetic and copies ran while one was open for 10% -> 0% of each run, Pallas kernels for 1% -> 7%
where the time goes in v2:
time: 68.6 us; the launch traced here: 68.3 us
  waiting for transfers between devices  27.3 us (40%)
  starting transfers between devices  26.7 us (39%)
  Pallas kernels  9.39 us (14%)
  local copies, waits for them, and re-layouts  4.62 us (7%)
    ppermute x24, waiting for transfers between devices, hop(): return lax.ppermute(x, axis, [(i, i ^ distance) for i in range(count)])  27.3 us
    ppermute x24, starting transfers between devices, hop(): return lax.ppermute(x, axis, [(i, i ^ distance) for i in range(count)])  26.7 us
    pallas_call x14, Pallas kernels, call(): pl.pallas_call(kernel, out_shape=shapes, in_specs=[SCALARS if x is ids el...  9.39 us
    unnamed x26, local copies, waits for them, and re-layouts  4.61 us
  transfers between devices with their start and end apart: 24, of which 14 were waited for; matrix products, arithmetic and copies ran while one was open for 0% of the time, Pallas kernels for 7%

profile of v2, /device:TPU:0, one launch (start us, length us, event | category | flops | bytes accessed | tf_op | source)
XLA Modules:
  0.0 68.3 jit_solution(2902795435453931545)
XLA Ops:
  0.0 3.0 %collective-permute-start.2 = (bf16[8,3584]{1,0:T(8,128)(2,1)}, bf16[8,3584]{1,0:T(8,128)(2,1)S(1)}, u32[]{:S(2)}, u32[]{:S(2)}) collective-permute-start(bf16[8,3584]{1,0:T(8,128)(2,1)} %refs_3_.1), channel_id=1, source_target_pairs={{0,8},{2,10},{4,12},{6,14},{8,0},{10,2},{12,4},{14,6},{16,24},{18,... | collective-permute-start | bytes 172040 | tf_op jit(solution)/shard_map/ppermute | solution.py:258
  3.0 1.5 %collective-permute-start.3 = (bf16[8,3584]{1,0:T(8,128)(2,1)}, bf16[8,3584]{1,0:T(8,128)(2,1)S(1)}, u32[]{:S(2)}, u32[]{:S(2)}) collective-permute-start(bf16[8,3584]{1,0:T(8,128)(2,1)} %refs_3_.1), channel_id=1, source_target_pairs={{0,4},{2,6},{4,0},{6,2},{8,12},{10,14},{12,8},{14,10},{16,20},{18,... | collective-permute-start | bytes 172040 | tf_op jit(solution)/shard_map/ppermute | solution.py:258
  4.5 2.5 %collective-permute-start = (bf16[8,3584]{1,0:T(8,128)(2,1)}, bf16[8,3584]{1,0:T(8,128)(2,1)S(1)}, u32[]{:S(2)}, u32[]{:S(2)}) collective-permute-start(bf16[8,3584]{1,0:T(8,128)(2,1)} %refs_3_.1), channel_id=1, source_target_pairs={{0,24},{2,26},{4,28},{6,30},{8,16},{10,18},{12,20},{14,22},{16,8},... | collective-permute-start | bytes 172040 | tf_op jit(solution)/shard_map/ppermute | solution.py:258
  7.0 0.1 collective-permute-start.1
  7.1 0.3 collective-permute-done.3.refs_4_.refs_2_
  7.4 3.7 %collective-permute-done.refs_0_ = bf16[8,3584]{1,0:T(8,128)(2,1)S(1)} collective-permute-done((bf16[8,3584]{1,0:T(8,128)(2,1)}, bf16[8,3584]{1,0:T(8,128)(2,1)S(1)}, u32[]{:S(2)}, u32[]{:S(2)}) %collective-permute-start) | collective-permute-done | bytes 57376 | tf_op jit(solution)/shard_map/ppermute | solution.py:258
  11.1 1.8 %collective-permute-done.1.refs_1_ = bf16[8,3584]{1,0:T(8,128)(2,1)S(1)} collective-permute-done((bf16[8,3584]{1,0:T(8,128)(2,1)}, bf16[8,3584]{1,0:T(8,128)(2,1)S(1)}, u32[]{:S(2)}, u32[]{:S(2)}) %collective-permute-start.1) | collective-permute-done | bytes 57376 | tf_op jit(solution)/shard_map/ppermute | solution.py:258
  12.9 1.8 %copy-done.1 = bf16[384,3584]{1,0:T(8,128)(2,1)S(1)} copy-done((bf16[384,3584]{1,0:T(8,128)(2,1)S(1)}, bf16[384,3584]{1,0:T(8,128)(2,1)}, u32[]{:S(2)}) %copy-start.1) | copy-done | bytes 2752536
  14.7 0.8 %copy-done.5 = bf16[8,3584]{1,0:T(8,128)(2,1)S(1)} copy-done((bf16[8,3584]{1,0:T(8,128)(2,1)S(1)}, bf16[8,3584]{1,0:T(8,128)(2,1)}, u32[]{:S(2)}) %copy-start.5) | copy-done | bytes 57368
  15.5 0.6 collective-permute-start.4
  16.2 1.5 %collective-permute-start.5 = (bf16[8,3584]{1,0:T(8,128)(2,1)S(1)}, bf16[8,3584]{1,0:T(8,128)(2,1)S(1)}, u32[]{:S(2)}, u32[]{:S(2)}) collective-permute-start(bf16[8,3584]{1,0:T(8,128)(2,1)S(1)} %collective-permute-done.2.refs_2_), channel_id=1, source_target_pairs={{0,4},{2,6},{4,0},{6,2},{8,12},{10,14},{12,8},{14,10},{16,20},{18,... | collective-permute-start | bytes 172040 | tf_op jit(solution)/shard_map/ppermute | solution.py:258
  17.7 0.1 pad_add_fusion.ids
  17.8 0.7 prep.1
  18.5 0.1 collective-permute-start.6
  18.5 2.5 %collective-permute-done.5.refs_1_ = bf16[8,3584]{1,0:T(8,128)(2,1)S(1)} collective-permute-done((bf16[8,3584]{1,0:T(8,128)(2,1)S(1)}, bf16[8,3584]{1,0:T(8,128)(2,1)S(1)}, u32[]{:S(2)}, u32[]{:S(2)}) %collective-permute-start.5) | collective-permute-done | bytes 57376 | tf_op jit(solution)/shard_map/ppermute | solution.py:258
  21.0 1.8 %copy-done.3 = bf16[384,3584]{1,0:T(8,128)(2,1)S(1)} copy-done((bf16[384,3584]{1,0:T(8,128)(2,1)S(1)}, bf16[384,3584]{1,0:T(8,128)(2,1)}, u32[]{:S(2)}) %copy-start.3) | copy-done | bytes 2752536
  22.9 1.5 %collective-permute-done.7.refs_3_ = bf16[32,3584]{1,0:T(8,128)(2,1)S(1)} collective-permute-done((bf16[32,3584]{1,0:T(8,128)(2,1)S(1)}, bf16[32,3584]{1,0:T(8,128)(2,1)S(1)}, u32[]{:S(2)}, u32[]{:S(2)}) %collective-permute-start.7) | collective-permute-done | bytes 229408 | tf_op jit(solution)/shard_map/ppermute | solution.py:258
  24.4 0.2 copy-done.4
  24.6 2.0 %attend.1 = (bf16[64,3712]{1,0:T(8,128)(2,1)S(1)}, bf16[64,3712]{1,0:T(8,128)(2,1)S(1)}) custom-call(bf16[32,128]{1,0:T(8,128)(2,1)S(1)} %get-tuple-element.26.refs_3_.pick, f32[32,384]{1,0:T(8,128)S(1)} %get-tuple-element.27.mask, bf16[384,3584]{1,0:T(8,128)(2,1)S(1)} %copy-done.2, bf16[384,3584]{1,0:T(8,128)(2,1)S(1)} %copy-done.4, ...), custom_call_target="tpu_custom_call" | custom-call | bytes 3500000 | tf_op jit(solution)/shard_map/attend/pallas_call | solution.py:287
  26.6 1.8 %collective-permute-done.8.refs_1_ = bf16[64,3712]{1,0:T(8,128)(2,1)S(1)} collective-permute-done((bf16[64,3712]{1,0:T(8,128)(2,1)S(1)}, bf16[64,3712]{1,0:T(8,128)(2,1)S(1)}, u32[]{:S(2)}, u32[]{:S(2)}) %collective-permute-start.8) | collective-permute-done | bytes 475168 | tf_op jit(solution)/shard_map/ppermute | solution.py:258
  28.5 0.7 %merge.3 = (bf16[16,3712]{1,0:T(8,128)(2,1)S(1)}, bf16[16,3712]{1,0:T(8,128)(2,1)S(1)}, bf16[16,3712]{1,0:T(8,128)(2,1)S(1)}, bf16[16,3712]{1,0:T(8,128)(2,1)S(1)}) custom-call(bf16[64,3712]{1,0:T(8,128)(2,1)S(1)} %get-tuple-element.30.refs_0_, bf16[64,3712]{1,0:T(8,128)(2,1)S(1)} %collective-permute-done.8.refs_1_), custom_call_target="tpu_custom_call" | custom-call | bytes 3500000 | tf_op jit(solution)/shard_map/merge/pallas_call | solution.py:287
  29.2 0.9 %collective-permute-start.10 = (bf16[16,3712]{1,0:T(8,128)(2,1)S(1)}, bf16[16,3712]{1,0:T(8,128)(2,1)S(1)}, u32[]{:S(2)}, u32[]{:S(2)}) collective-permute-start(bf16[16,3712]{1,0:T(8,128)(2,1)S(1)} %get-tuple-element.36), channel_id=1, source_target_pairs={{0,4},{2,6},{4,0},{6,2},{8,12},{10,14},{12,8},{14,10},{16,20},{18,... | collective-permute-start | bytes 356360 | tf_op jit(solution)/shard_map/ppermute | solution.py:258
  30.1 1.2 %collective-permute-start.9 = (bf16[16,3712]{1,0:T(8,128)(2,1)S(1)}, bf16[16,3712]{1,0:T(8,128)(2,1)S(1)}, u32[]{:S(2)}, u32[]{:S(2)}) collective-permute-start(bf16[16,3712]{1,0:T(8,128)(2,1)S(1)} %get-tuple-element.33), channel_id=1, source_target_pairs={{0,4},{2,6},{4,0},{6,2},{8,12},{10,14},{12,8},{14,10},{16,20},{18,... | collective-permute-start | bytes 356360 | tf_op jit(solution)/shard_map/ppermute | solution.py:258
  31.3 4.0 %collective-permute-done.10.refs_1_ = bf16[16,3712]{1,0:T(8,128)(2,1)S(1)} collective-permute-done((bf16[16,3712]{1,0:T(8,128)(2,1)S(1)}, bf16[16,3712]{1,0:T(8,128)(2,1)S(1)}, u32[]{:S(2)}, u32[]{:S(2)}) %collective-permute-start.10) | collective-permute-done | bytes 118816 | tf_op jit(solution)/shard_map/ppermute | solution.py:258
  35.3 0.3 merge.5
  35.6 2.3 %collective-permute-start.11 = (bf16[8,3712]{1,0:T(8,128)(2,1)S(1)}, bf16[8,3712]{1,0:T(8,128)(2,1)S(1)}, u32[]{:S(2)}, u32[]{:S(2)}) collective-permute-start(bf16[8,3712]{1,0:T(8,128)(2,1)S(1)} %get-tuple-element.37), channel_id=1, source_target_pairs={{0,24},{2,26},{4,28},{6,30},{8,16},{10,18},{12,20},{14,22},{16,8},... | collective-permute-start | bytes 178184 | tf_op jit(solution)/shard_map/ppermute | solution.py:258
  38.0 0.3 merge.4
  38.3 2.2 %collective-permute-start.13 = (bf16[8,3712]{1,0:T(8,128)(2,1)S(1)}, bf16[8,3712]{1,0:T(8,128)(2,1)S(1)}, u32[]{:S(2)}, u32[]{:S(2)}) collective-permute-start(bf16[8,3712]{1,0:T(8,128)(2,1)S(1)} %get-tuple-element.39), channel_id=1, source_target_pairs={{0,8},{2,10},{4,12},{6,14},{8,0},{10,2},{12,4},{14,6},{16,24},{18,... | collective-permute-start | bytes 178184 | tf_op jit(solution)/shard_map/ppermute | solution.py:258
  40.5 1.6 %collective-permute-done.11.refs_1_ = bf16[8,3712]{1,0:T(8,128)(2,1)S(1)} collective-permute-done((bf16[8,3712]{1,0:T(8,128)(2,1)S(1)}, bf16[8,3712]{1,0:T(8,128)(2,1)S(1)}, u32[]{:S(2)}, u32[]{:S(2)}) %collective-permute-start.11) | collective-permute-done | bytes 59424 | tf_op jit(solution)/shard_map/ppermute | solution.py:258
  42.1 1.4 %collective-permute-done.12.refs_2_ = bf16[8,3712]{1,0:T(8,128)(2,1)S(1)} collective-permute-done((bf16[8,3712]{1,0:T(8,128)(2,1)S(1)}, bf16[8,3712]{1,0:T(8,128)(2,1)S(1)}, u32[]{:S(2)}, u32[]{:S(2)}) %collective-permute-start.12) | collective-permute-done | bytes 59424 | tf_op jit(solution)/shard_map/ppermute | solution.py:258
  43.6 0.4 last.1.refs_3_
  43.9 2.1 %collective-permute-start.14 = (bf16[8,3584]{1,0:T(8,128)(2,1)S(1)}, bf16[8,3584]{1,0:T(8,128)(2,1)S(1)}, u32[]{:S(2)}, u32[]{:S(2)}) collective-permute-start(bf16[8,3584]{1,0:T(8,128)(2,1)S(1)} %last.1.refs_3_), channel_id=1, source_target_pairs={{0,24},{2,26},{4,28},{6,30},{8,16},{10,18},{12,20},{14,22},{16,8},... | collective-permute-start | bytes 172040 | tf_op jit(solution)/shard_map/ppermute | solution.py:258
  46.0 0.6 collective-permute-start.15
  46.6 1.8 %collective-permute-start.16 = (bf16[8,3584]{1,0:T(8,128)(2,1)S(1)}, bf16[8,3584]{1,0:T(8,128)(2,1)S(1)}, u32[]{:S(2)}, u32[]{:S(2)}) collective-permute-start(bf16[8,3584]{1,0:T(8,128)(2,1)S(1)} %last.1.refs_3_), channel_id=1, source_target_pairs={{0,8},{2,10},{4,12},{6,14},{8,0},{10,2},{12,4},{14,6},{16,24},{18,... | collective-permute-start | bytes 172040 | tf_op jit(solution)/shard_map/ppermute | solution.py:258
  48.4 0.9 %collective-permute-start.17 = (bf16[8,3584]{1,0:T(8,128)(2,1)S(1)}, bf16[8,3584]{1,0:T(8,128)(2,1)S(1)}, u32[]{:S(2)}, u32[]{:S(2)}) collective-permute-start(bf16[8,3584]{1,0:T(8,128)(2,1)S(1)} %last.1.refs_3_), channel_id=1, source_target_pairs={{0,4},{2,6},{4,0},{6,2},{8,12},{10,14},{12,8},{14,10},{16,20},{18,... | collective-permute-start | bytes 172040 | tf_op jit(solution)/shard_map/ppermute | solution.py:258
  49.3 0.7 %collective-permute-done.14.refs_0_ = bf16[8,3584]{1,0:T(8,128)(2,1)S(1)} collective-permute-done((bf16[8,3584]{1,0:T(8,128)(2,1)S(1)}, bf16[8,3584]{1,0:T(8,128)(2,1)S(1)}, u32[]{:S(2)}, u32[]{:S(2)}) %collective-permute-start.14) | collective-permute-done | bytes 57376 | tf_op jit(solution)/shard_map/ppermute | solution.py:258
  50.0 1.7 %collective-permute-done.15.refs_1_ = bf16[8,3584]{1,0:T(8,128)(2,1)S(1)} collective-permute-done((bf16[8,3584]{1,0:T(8,128)(2,1)S(1)}, bf16[8,3584]{1,0:T(8,128)(2,1)S(1)}, u32[]{:S(2)}, u32[]{:S(2)}) %collective-permute-start.15) | collective-permute-done | bytes 57376 | tf_op jit(solution)/shard_map/ppermute | solution.py:258
  51.6 0.9 %collective-permute-done.17.refs_4_.refs_2_ = bf16[8,3584]{1,0:T(8,128)(2,1)S(1)} collective-permute-done((bf16[8,3584]{1,0:T(8,128)(2,1)S(1)}, bf16[8,3584]{1,0:T(8,128)(2,1)S(1)}, u32[]{:S(2)}, u32[]{:S(2)}) %collective-permute-start.17) | collective-permute-done | bytes 57376 | tf_op jit(solution)/shard_map/ppermute | solution.py:258
  52.7 0.9 %collective-permute-start.20 = (bf16[16,3584]{1,0:T(8,128)(2,1)S(1)}, bf16[16,3584]{1,0:T(8,128)(2,1)S(1)}, u32[]{:S(2)}, u32[]{:S(2)}) collective-permute-start(bf16[16,3584]{1,0:T(8,128)(2,1)S(1)} %get-tuple-element.44), channel_id=1, source_target_pairs={{0,4},{2,6},{4,0},{6,2},{8,12},{10,14},{12,8},{14,10},{16,20},{18,... | collective-permute-start | bytes 344072 | tf_op jit(solution)/shard_map/ppermute | solution.py:258
  53.6 1.2 %collective-permute-start.21 = (bf16[8,3584]{1,0:T(8,128)(2,1)S(1)}, bf16[8,3584]{1,0:T(8,128)(2,1)S(1)}, u32[]{:S(2)}, u32[]{:S(2)}) collective-permute-start(bf16[8,3584]{1,0:T(8,128)(2,1)S(1)} %collective-permute-done.16.refs_2_), channel_id=1, source_target_pairs={{0,4},{2,6},{4,0},{6,2},{8,12},{10,14},{12,8},{14,10},{16,20},{18,... | collective-permute-start | bytes 172040 | tf_op jit(solution)/shard_map/ppermute | solution.py:258
  54.8 1.6 %project.2 = (f32[32,448]{1,0:T(8,128)S(1)}, f32[32,448]{1,0:T(8,128)S(1)}) custom-call(s32[2]{0:T(128)S(1)} %pad_add_fusion.ids, bf16[32,3584]{1,0:T(8,128)(2,1)S(1)} %get-tuple-element.41.refs_0_, bf16[32,3584]{1,0:T(8,128)(2,1)S(1)} %collective-permute-done.18.refs_1_, bf16[448,3584]{1,0:T(8,128)(2,1)S(1)} %bitcast.3), custom_call_target="tpu_custom_call" | custom-call | bytes 3500000 | tf_op jit(solution)/shard_map/project/pallas_call | solution.py:287
  56.4 0.6 base.1.refs_3_
  57.0 2.5 %collective-permute-done.21.refs_1_ = bf16[8,3584]{1,0:T(8,128)(2,1)S(1)} collective-permute-done((bf16[8,3584]{1,0:T(8,128)(2,1)S(1)}, bf16[8,3584]{1,0:T(8,128)(2,1)S(1)}, u32[]{:S(2)}, u32[]{:S(2)}) %collective-permute-start.21) | collective-permute-done | bytes 57376 | tf_op jit(solution)/shard_map/ppermute | solution.py:258
  59.6 1.6 %collective-permute-start.19 = (f32[32,448]{1,0:T(8,128)S(1)}, f32[32,448]{1,0:T(8,128)S(1)}, u32[]{:S(2)}, u32[]{:S(2)}) collective-permute-start(f32[32,448]{1,0:T(8,128)S(1)} %get-tuple-element.43), channel_id=1, source_target_pairs={{0,1},{1,0},{2,3},{3,2},{4,5},{5,4},{6,7},{7,6},{8,9},{9,8},{10,11... | collective-permute-start | bytes 172040 | tf_op jit(solution)/shard_map/ppermute | solution.py:258
  61.2 1.6 %project.3 = (f32[32,448]{1,0:T(8,128)S(1)}, f32[32,448]{1,0:T(8,128)S(1)}) custom-call(s32[2]{0:T(128)S(1)} %pad_add_fusion.ids, bf16[32,3584]{1,0:T(8,128)(2,1)S(1)} %pack.7.refs_0_, bf16[32,3584]{1,0:T(8,128)(2,1)S(1)} %collective-permute-done.22.refs_1_, bf16[448,3584]{1,0:T(8,128)(2,1)S(1)} %bitcast.4), custom_call_target="tpu_custom_call" | custom-call | bytes 3500000 | tf_op jit(solution)/shard_map/project/pallas_call | solution.py:287
  62.8 1.5 %collective-permute-start.23 = (f32[32,448]{1,0:T(8,128)S(1)}, f32[32,448]{1,0:T(8,128)S(1)}, u32[]{:S(2)}, u32[]{:S(2)}) collective-permute-start(f32[32,448]{1,0:T(8,128)S(1)} %get-tuple-element.46), channel_id=1, source_target_pairs={{0,1},{1,0},{2,3},{3,2},{4,5},{5,4},{6,7},{7,6},{8,9},{9,8},{10,11... | collective-permute-start | bytes 172040 | tf_op jit(solution)/shard_map/ppermute | solution.py:258
  64.2 2.9 %collective-permute-done.23.received = f32[32,448]{1,0:T(8,128)S(1)} collective-permute-done((f32[32,448]{1,0:T(8,128)S(1)}, f32[32,448]{1,0:T(8,128)S(1)}, u32[]{:S(2)}, u32[]{:S(2)}) %collective-permute-start.23) | collective-permute-done | bytes 57376 | tf_op jit(solution)/shard_map/ppermute | solution.py:258
  67.1 1.2 %final.1 = bf16[64,448]{1,0:T(8,128)(2,1)} custom-call(s32[2]{0:T(128)S(1)} %pad_add_fusion.ids, f32[64,448]{1,0:T(8,128)S(1)} %base.1.refs_3_, f32[32,448]{1,0:T(8,128)S(1)} %collective-permute-done.19.early, f32[32,448]{1,0:T(8,128)S(1)} %get-tuple-element.45.kept, f32[32,448]{1,0:T(8,128)S(1)} %collective-permute-done.23.received), custom_call_target="tpu_custom_call" | custom-call | bytes 3500000 | tf_op jit(solution)/shard_map/final/pallas_call | solution.py:287
  (44 shorter events, 0.4 us)
Async XLA Ops:
  0.0 7.1 %collective-permute-start.2 = (bf16[8,3584]{1,0:T(8,128)(2,1)}, bf16[8,3584]{1,0:T(8,128)(2,1)S(1)}, u32[]{:S(2)}, u32[]{:S(2)}) collective-permute-start(bf16[8,3584]{1,0:T(8,128)(2,1)} %refs_3_.1), channel_id=1, source_target_pairs={{0,8},{2,10},{4,12},{6,14},{8,0},{10,2},{12,4},{14,6},{16,24},{18,... | collective-permute-start | bytes 172040 | tf_op jit(solution)/shard_map/ppermute | solution.py:258
  3.0 4.4 %collective-permute-start.3 = (bf16[8,3584]{1,0:T(8,128)(2,1)}, bf16[8,3584]{1,0:T(8,128)(2,1)S(1)}, u32[]{:S(2)}, u32[]{:S(2)}) collective-permute-start(bf16[8,3584]{1,0:T(8,128)(2,1)} %refs_3_.1), channel_id=1, source_target_pairs={{0,4},{2,6},{4,0},{6,2},{8,12},{10,14},{12,8},{14,10},{16,20},{18,... | collective-permute-start | bytes 172040 | tf_op jit(solution)/shard_map/ppermute | solution.py:258
  4.5 6.6 %collective-permute-start = (bf16[8,3584]{1,0:T(8,128)(2,1)}, bf16[8,3584]{1,0:T(8,128)(2,1)S(1)}, u32[]{:S(2)}, u32[]{:S(2)}) collective-permute-start(bf16[8,3584]{1,0:T(8,128)(2,1)} %refs_3_.1), channel_id=1, source_target_pairs={{0,24},{2,26},{4,28},{6,30},{8,16},{10,18},{12,20},{14,22},{16,8},... | collective-permute-start | bytes 172040 | tf_op jit(solution)/shard_map/ppermute | solution.py:258
  7.0 5.9 %collective-permute-start.1 = (bf16[8,3584]{1,0:T(8,128)(2,1)}, bf16[8,3584]{1,0:T(8,128)(2,1)S(1)}, u32[]{:S(2)}, u32[]{:S(2)}) collective-permute-start(bf16[8,3584]{1,0:T(8,128)(2,1)} %refs_3_.1), channel_id=1, source_target_pairs={{0,16},{2,18},{4,20},{6,22},{8,24},{10,26},{12,28},{14,30},{16,0},... | collective-permute-start | bytes 172040 | tf_op jit(solution)/shard_map/ppermute | solution.py:258
  12.9 1.8 %copy-start.1 = (bf16[384,3584]{1,0:T(8,128)(2,1)S(1)}, bf16[384,3584]{1,0:T(8,128)(2,1)}, u32[]{:S(2)}) copy-start(bf16[384,3584]{1,0:T(8,128)(2,1)} %keys.1) | copy-start | bytes 8257540
  14.7 0.8 %copy-start.5 = (bf16[8,3584]{1,0:T(8,128)(2,1)S(1)}, bf16[8,3584]{1,0:T(8,128)(2,1)}, u32[]{:S(2)}) copy-start(bf16[8,3584]{1,0:T(8,128)(2,1)} %refs_3_.1) | copy-start | bytes 172036
  15.5 0.7 %copy-start.10 = (s32[384]{0:T(512)S(1)}, s32[384]{0:T(512)}, u32[]{:S(2)}) copy-start(s32[384]{0:T(512)} %param.16) | copy-start | bytes 4612
  15.5 0.7 %copy-start.11 = (s32[384]{0:T(512)S(1)}, s32[384]{0:T(512)}, u32[]{:S(2)}) copy-start(s32[384]{0:T(512)} %param.15) | copy-start | bytes 4612
  15.5 2.3 %copy-start.6 = (bf16[8,3584]{1,0:T(8,128)(2,1)S(1)}, bf16[8,3584]{1,0:T(8,128)(2,1)}, u32[]{:S(2)}) copy-start(bf16[8,3584]{1,0:T(8,128)(2,1)} %refs_3_.1) | copy-start | bytes 172036
  15.5 2.3 %copy-start.8 = (bf16[8,3584]{1,0:T(8,128)(2,1)S(1)}, bf16[8,3584]{1,0:T(8,128)(2,1)}, u32[]{:S(2)}) copy-start(bf16[8,3584]{1,0:T(8,128)(2,1)} %new_keys.1) | copy-start | bytes 172036
  15.5 8.9 %copy-start.2 = (bf16[384,3584]{1,0:T(8,128)(2,1)S(1)}, bf16[384,3584]{1,0:T(8,128)(2,1)}, u32[]{:S(2)}) copy-start(bf16[384,3584]{1,0:T(8,128)(2,1)} %keys.1) | copy-start | bytes 8257540
  15.5 5.5 %collective-permute-start.4 = (bf16[16,3584]{1,0:T(8,128)(2,1)S(1)}, bf16[16,3584]{1,0:T(8,128)(2,1)S(1)}, u32[]{:S(2)}, u32[]{:S(2)}) collective-permute-start(bf16[16,3584]{1,0:T(8,128)(2,1)S(1)} %get-tuple-element.29), channel_id=1, source_target_pairs={{0,4},{2,6},{4,0},{6,2},{8,12},{10,14},{12,8},{14,10},{16,20},{18,... | collective-permute-start | bytes 344072 | tf_op jit(solution)/shard_map/ppermute | solution.py:258
  16.2 4.8 %collective-permute-start.5 = (bf16[8,3584]{1,0:T(8,128)(2,1)S(1)}, bf16[8,3584]{1,0:T(8,128)(2,1)S(1)}, u32[]{:S(2)}, u32[]{:S(2)}) collective-permute-start(bf16[8,3584]{1,0:T(8,128)(2,1)S(1)} %collective-permute-done.2.refs_2_), channel_id=1, source_target_pairs={{0,4},{2,6},{4,0},{6,2},{8,12},{10,14},{12,8},{14,10},{16,20},{18,... | collective-permute-start | bytes 172040 | tf_op jit(solution)/shard_map/ppermute | solution.py:258
  18.5 4.4 %collective-permute-start.6 = (bf16[32,3584]{1,0:T(8,128)(2,1)S(1)}, bf16[32,3584]{1,0:T(8,128)(2,1)S(1)}, u32[]{:S(2)}, u32[]{:S(2)}) collective-permute-start(bf16[32,3584]{1,0:T(8,128)(2,1)S(1)} %get-tuple-element.28.refs_0_), channel_id=1, source_target_pairs={{0,2},{2,0},{4,6},{6,4},{8,10},{10,8},{12,14},{14,12},{16,18},{18,... | collective-permute-start | bytes 688136 | tf_op jit(solution)/shard_map/ppermute | solution.py:258
  21.0 1.8 %copy-start.3 = (bf16[384,3584]{1,0:T(8,128)(2,1)S(1)}, bf16[384,3584]{1,0:T(8,128)(2,1)}, u32[]{:S(2)}) copy-start(bf16[384,3584]{1,0:T(8,128)(2,1)} %values.1) | copy-start | bytes 8257540
  22.8 1.8 %copy-start.4 = (bf16[384,3584]{1,0:T(8,128)(2,1)S(1)}, bf16[384,3584]{1,0:T(8,128)(2,1)}, u32[]{:S(2)}) copy-start(bf16[384,3584]{1,0:T(8,128)(2,1)} %values.1) | copy-start | bytes 8257540
  22.8 1.6 %collective-permute-start.7 = (bf16[32,3584]{1,0:T(8,128)(2,1)S(1)}, bf16[32,3584]{1,0:T(8,128)(2,1)S(1)}, u32[]{:S(2)}, u32[]{:S(2)}) collective-permute-start(bf16[32,3584]{1,0:T(8,128)(2,1)S(1)} %pack.5.refs_1_), channel_id=1, source_target_pairs={{0,2},{2,0},{4,6},{6,4},{8,10},{10,8},{12,14},{14,12},{16,18},{18,... | collective-permute-start | bytes 688136 | tf_op jit(solution)/shard_map/ppermute | solution.py:258
  24.6 19.0 %copy-start.9 = (bf16[8,3584]{1,0:T(8,128)(2,1)S(1)}, bf16[8,3584]{1,0:T(8,128)(2,1)}, u32[]{:S(2)}) copy-start(bf16[8,3584]{1,0:T(8,128)(2,1)} %refs_4_.3) | copy-start | bytes 172036
  24.6 30.2 %copy-start.12 = (bf16[448]{0:T(512)(128)(2,1)S(1)}, bf16[448]{0:T(512)(128)(2,1)}, u32[]{:S(2)}) copy-start(bf16[448]{0:T(512)(128)(2,1)} %param.18) | copy-start | bytes 2692
  24.6 30.2 %copy-start = (bf16[3584,448]{0,1:T(8,128)(2,1)S(1)}, bf16[3584,448]{0,1:T(8,128)(2,1)}, u32[]{:S(2)}) copy-start(bf16[3584,448]{0,1:T(8,128)(2,1)} %param.17) | copy-start | bytes 9633796
  26.6 1.9 %collective-permute-start.8 = (bf16[64,3712]{1,0:T(8,128)(2,1)S(1)}, bf16[64,3712]{1,0:T(8,128)(2,1)S(1)}, u32[]{:S(2)}, u32[]{:S(2)}) collective-permute-start(bf16[64,3712]{1,0:T(8,128)(2,1)S(1)} %get-tuple-element.31), channel_id=1, source_target_pairs={{0,2},{2,0},{4,6},{6,4},{8,10},{10,8},{12,14},{14,12},{16,18},{18,... | collective-permute-start | bytes 1425416 | tf_op jit(solution)/shard_map/ppermute | solution.py:258
  28.5 27.9 %copy-start.7 = (bf16[64,448]{1,0:T(8,128)(2,1)S(1)}, bf16[64,448]{1,0:T(8,128)(2,1)}, u32[]{:S(2)}) copy-start(bf16[64,448]{1,0:T(8,128)(2,1)} %residual.1) | copy-start | bytes 172036
  29.2 6.1 %collective-permute-start.10 = (bf16[16,3712]{1,0:T(8,128)(2,1)S(1)}, bf16[16,3712]{1,0:T(8,128)(2,1)S(1)}, u32[]{:S(2)}, u32[]{:S(2)}) collective-permute-start(bf16[16,3712]{1,0:T(8,128)(2,1)S(1)} %get-tuple-element.36), channel_id=1, source_target_pairs={{0,4},{2,6},{4,0},{6,2},{8,12},{10,14},{12,8},{14,10},{16,20},{18,... | collective-permute-start | bytes 356360 | tf_op jit(solution)/shard_map/ppermute | solution.py:258
  30.1 7.9 %collective-permute-start.9 = (bf16[16,3712]{1,0:T(8,128)(2,1)S(1)}, bf16[16,3712]{1,0:T(8,128)(2,1)S(1)}, u32[]{:S(2)}, u32[]{:S(2)}) collective-permute-start(bf16[16,3712]{1,0:T(8,128)(2,1)S(1)} %get-tuple-element.33), channel_id=1, source_target_pairs={{0,4},{2,6},{4,0},{6,2},{8,12},{10,14},{12,8},{14,10},{16,20},{18,... | collective-permute-start | bytes 356360 | tf_op jit(solution)/shard_map/ppermute | solution.py:258
  35.6 6.5 %collective-permute-start.11 = (bf16[8,3712]{1,0:T(8,128)(2,1)S(1)}, bf16[8,3712]{1,0:T(8,128)(2,1)S(1)}, u32[]{:S(2)}, u32[]{:S(2)}) collective-permute-start(bf16[8,3712]{1,0:T(8,128)(2,1)S(1)} %get-tuple-element.37), channel_id=1, source_target_pairs={{0,24},{2,26},{4,28},{6,30},{8,16},{10,18},{12,20},{14,22},{16,8},... | collective-permute-start | bytes 178184 | tf_op jit(solution)/shard_map/ppermute | solution.py:258
  38.0 5.6 %collective-permute-start.12 = (bf16[8,3712]{1,0:T(8,128)(2,1)S(1)}, bf16[8,3712]{1,0:T(8,128)(2,1)S(1)}, u32[]{:S(2)}, u32[]{:S(2)}) collective-permute-start(bf16[8,3712]{1,0:T(8,128)(2,1)S(1)} %get-tuple-element.38), channel_id=1, source_target_pairs={{0,16},{2,18},{4,20},{6,22},{8,24},{10,26},{12,28},{14,30},{16,0},... | collective-permute-start | bytes 178184 | tf_op jit(solution)/shard_map/ppermute | solution.py:258
  38.3 5.2 %collective-permute-start.13 = (bf16[8,3712]{1,0:T(8,128)(2,1)S(1)}, bf16[8,3712]{1,0:T(8,128)(2,1)S(1)}, u32[]{:S(2)}, u32[]{:S(2)}) collective-permute-start(bf16[8,3712]{1,0:T(8,128)(2,1)S(1)} %get-tuple-element.39), channel_id=1, source_target_pairs={{0,8},{2,10},{4,12},{6,14},{8,0},{10,2},{12,4},{14,6},{16,24},{18,... | collective-permute-start | bytes 178184 | tf_op jit(solution)/shard_map/ppermute | solution.py:258
  43.9 6.0 %collective-permute-start.14 = (bf16[8,3584]{1,0:T(8,128)(2,1)S(1)}, bf16[8,3584]{1,0:T(8,128)(2,1)S(1)}, u32[]{:S(2)}, u32[]{:S(2)}) collective-permute-start(bf16[8,3584]{1,0:T(8,128)(2,1)S(1)} %last.1.refs_3_), channel_id=1, source_target_pairs={{0,24},{2,26},{4,28},{6,30},{8,16},{10,18},{12,20},{14,22},{16,8},... | collective-permute-start | bytes 172040 | tf_op jit(solution)/shard_map/ppermute | solution.py:258
  46.0 5.6 %collective-permute-start.15 = (bf16[8,3584]{1,0:T(8,128)(2,1)S(1)}, bf16[8,3584]{1,0:T(8,128)(2,1)S(1)}, u32[]{:S(2)}, u32[]{:S(2)}) collective-permute-start(bf16[8,3584]{1,0:T(8,128)(2,1)S(1)} %last.1.refs_3_), channel_id=1, source_target_pairs={{0,16},{2,18},{4,20},{6,22},{8,24},{10,26},{12,28},{14,30},{16,0},... | collective-permute-start | bytes 172040 | tf_op jit(solution)/shard_map/ppermute | solution.py:258
  46.6 5.1 %collective-permute-start.16 = (bf16[8,3584]{1,0:T(8,128)(2,1)S(1)}, bf16[8,3584]{1,0:T(8,128)(2,1)S(1)}, u32[]{:S(2)}, u32[]{:S(2)}) collective-permute-start(bf16[8,3584]{1,0:T(8,128)(2,1)S(1)} %last.1.refs_3_), channel_id=1, source_target_pairs={{0,8},{2,10},{4,12},{6,14},{8,0},{10,2},{12,4},{14,6},{16,24},{18,... | collective-permute-start | bytes 172040 | tf_op jit(solution)/shard_map/ppermute | solution.py:258
  48.4 4.2 %collective-permute-start.17 = (bf16[8,3584]{1,0:T(8,128)(2,1)S(1)}, bf16[8,3584]{1,0:T(8,128)(2,1)S(1)}, u32[]{:S(2)}, u32[]{:S(2)}) collective-permute-start(bf16[8,3584]{1,0:T(8,128)(2,1)S(1)} %last.1.refs_3_), channel_id=1, source_target_pairs={{0,4},{2,6},{4,0},{6,2},{8,12},{10,14},{12,8},{14,10},{16,20},{18,... | collective-permute-start | bytes 172040 | tf_op jit(solution)/shard_map/ppermute | solution.py:258
  52.6 2.2 %collective-permute-start.18 = (bf16[32,3584]{1,0:T(8,128)(2,1)S(1)}, bf16[32,3584]{1,0:T(8,128)(2,1)S(1)}, u32[]{:S(2)}, u32[]{:S(2)}) collective-permute-start(bf16[32,3584]{1,0:T(8,128)(2,1)S(1)} %get-tuple-element.41.refs_0_), channel_id=1, source_target_pairs={{0,2},{2,0},{4,6},{6,4},{8,10},{10,8},{12,14},{14,12},{16,18},{18,... | collective-permute-start | bytes 688136 | tf_op jit(solution)/shard_map/ppermute | solution.py:258
  52.7 6.8 %collective-permute-start.20 = (bf16[16,3584]{1,0:T(8,128)(2,1)S(1)}, bf16[16,3584]{1,0:T(8,128)(2,1)S(1)}, u32[]{:S(2)}, u32[]{:S(2)}) collective-permute-start(bf16[16,3584]{1,0:T(8,128)(2,1)S(1)} %get-tuple-element.44), channel_id=1, source_target_pairs={{0,4},{2,6},{4,0},{6,2},{8,12},{10,14},{12,8},{14,10},{16,20},{18,... | collective-permute-start | bytes 344072 | tf_op jit(solution)/shard_map/ppermute | solution.py:258
  53.6 5.9 %collective-permute-start.21 = (bf16[8,3584]{1,0:T(8,128)(2,1)S(1)}, bf16[8,3584]{1,0:T(8,128)(2,1)S(1)}, u32[]{:S(2)}, u32[]{:S(2)}) collective-permute-start(bf16[8,3584]{1,0:T(8,128)(2,1)S(1)} %collective-permute-done.16.refs_2_), channel_id=1, source_target_pairs={{0,4},{2,6},{4,0},{6,2},{8,12},{10,14},{12,8},{14,10},{16,20},{18,... | collective-permute-start | bytes 172040 | tf_op jit(solution)/shard_map/ppermute | solution.py:258
  59.5 1.7 %collective-permute-start.22 = (bf16[32,3584]{1,0:T(8,128)(2,1)S(1)}, bf16[32,3584]{1,0:T(8,128)(2,1)S(1)}, u32[]{:S(2)}, u32[]{:S(2)}) collective-permute-start(bf16[32,3584]{1,0:T(8,128)(2,1)S(1)} %pack.7.refs_0_), channel_id=1, source_target_pairs={{0,2},{2,0},{4,6},{6,4},{8,10},{10,8},{12,14},{14,12},{16,18},{18,... | collective-permute-start | bytes 688136 | tf_op jit(solution)/shard_map/ppermute | solution.py:258
  59.6 4.7 %collective-permute-start.19 = (f32[32,448]{1,0:T(8,128)S(1)}, f32[32,448]{1,0:T(8,128)S(1)}, u32[]{:S(2)}, u32[]{:S(2)}) collective-permute-start(f32[32,448]{1,0:T(8,128)S(1)} %get-tuple-element.43), channel_id=1, source_target_pairs={{0,1},{1,0},{2,3},{3,2},{4,5},{5,4},{6,7},{7,6},{8,9},{9,8},{10,11... | collective-permute-start | bytes 172040 | tf_op jit(solution)/shard_map/ppermute | solution.py:258
  62.8 4.3 %collective-permute-start.23 = (f32[32,448]{1,0:T(8,128)S(1)}, f32[32,448]{1,0:T(8,128)S(1)}, u32[]{:S(2)}, u32[]{:S(2)}) collective-permute-start(f32[32,448]{1,0:T(8,128)S(1)} %get-tuple-element.46), channel_id=1, source_target_pairs={{0,1},{1,0},{2,3},{3,2},{4,5},{5,4},{6,7},{7,6},{8,9},{9,8},{10,11... | collective-permute-start | bytes 172040 | tf_op jit(solution)/shard_map/ppermute | solution.py:258

commit v3 on v2

--- a/solution.py
+++ b/solution.py
@@ -15,11 +15,10 @@
 STAT = 32
 
 floor_score = -1e30
-PACK_US = 5
+SENT = jnp.bfloat16
 f32 = jnp.float32
 bf16 = jnp.bfloat16
 WHOLE = pl.BlockSpec(memory_space=pltpu.VMEM)
-SCALARS = pl.BlockSpec(memory_space=pltpu.SMEM)
 ANY = pl.BlockSpec(memory_space=pl.ANY)
 
 
@@ -39,9 +38,7 @@
     return (core * mid + middle) * OUTER + OUTER - 1 - offset // (2 * mid)
 
 
-def prep_kernel(
-    mid, own_rows, ids, request, valid, queries, new_keys, pick, mask, own_top
-):
+def prep_kernel(mid, own_rows, request, valid, queries, new_keys, pick, mask, own_top, held):
     rows, slots = mask.shape
     row = lax.broadcasted_iota(jnp.int32, (rows, slots), 0)
     lane = lax.broadcasted_iota(jnp.int32, (rows, slots), 1)
@@ -53,7 +50,7 @@
     live = (owners == mine) & first & (jnp.broadcast_to(valid[...], (rows, slots)) == 1)
     mask[...] = jnp.where(live, 1.0, 0.0)
     place = lax.broadcasted_iota(jnp.int32, pick.shape, 1)
-    owner = lax.bitwise_xor(offset_of(place // own_rows, mid), ids[0])
+    owner = lax.bitwise_xor(offset_of(place // own_rows, mid), lax.axis_index("kv"))
     named = owner * own_rows + place % own_rows
     pick[...] = jnp.where((named == mine) & first, 1.0, 0.0).astype(bf16)
     heads = queries.shape[1] // HD
@@ -66,6 +63,7 @@
         ) * (1.0 / math.sqrt(HD))
         top = jnp.where(where == head, score, top)
     own_top[...] = top
+    held[...] = queries[...]
 
 
 def split_top(top):
@@ -86,12 +84,12 @@
     return jnp.concatenate([ref[...].astype(f32) for ref in refs], axis=0)
 
 
-def pack_kernel(count, tail, *refs):
-    outs = refs[len(refs) - 1 - tail :]
-    rows = stacked(refs[:count]).astype(bf16)
-    outs[0][...] = rows
-    if tail:
-        outs[1][...] = rows[: outs[1].shape[0]]
+def pack_kernel(count, *refs):
+    refs[-1][...] = stacked(refs[:count]).astype(bf16)
+
+
+def ready_kernel(*refs):
+    refs[-1][...] = jnp.zeros_like(refs[-1])
 
 
 def attend_kernel(count, pick, mask, keys, values, *refs):
@@ -201,57 +199,35 @@
         out[:, head * HD : (head + 1) * HD] = head_of(head).astype(bf16)
 
 
-def by_weight(blocks, weight):
-    return lax.dot_general(
-        stacked(blocks).astype(bf16), weight[...], (((1,), (1,)), ((), ())), preferred_element_type=f32
-    )
-
-
-def project_kernel(mid, own_rows, count, ids, *refs):
+def project_kernel(mid, own_rows, count, *refs):
     blocks, weight, outs, acc = refs[:count], refs[count], refs[count + 1 : -1], refs[-1]
-    acc[...] = by_weight(blocks, weight)
+    acc[...] = lax.dot_general(
+        stacked(blocks).astype(bf16),
+        weight[...],
+        (((1,), (1,)), ((), ())),
+        preferred_element_type=f32,
+    )
+    here = lax.axis_index("kv")
     owners = outs[0].shape[0] // own_rows
     for distance, out in enumerate(outs):
-        side = lax.bitwise_xor(ids[1], distance)
+        side = lax.bitwise_xor(lax.axis_index("tp"), distance)
+        rows = []
         for at in range(owners):
-            offset = lax.bitwise_xor(side * owners + at, ids[0])
+            offset = lax.bitwise_xor(side * owners + at, here)
             start = pl.multiple_of(place_of(offset, mid) * own_rows, own_rows)
-            out[at * own_rows : (at + 1) * own_rows, :] = acc[pl.ds(start, own_rows), :]
-
-
-def part_kernel(mid, nears, own_rows, count, ids, *refs):
-    blocks, weight, outs, acc = refs[:count], refs[count], refs[count + 1 : -1], refs[-1]
-    acc[...] = by_weight(blocks, weight)
-    outers = outs[0].shape[0] // (own_rows * 2 * len(nears))
-    for distance, out in enumerate(outs):
-        side = lax.bitwise_xor(ids[1], distance)
-        for at in range(len(nears) * outers * 2):
-            near, outer, core = at // (2 * outers), side * outers + (at // 2) % outers, at % 2
-            place = lax.bitwise_xor(core, ids[0] % 2) * len(nears) + near
-            place = place * OUTER + OUTER - 1 - lax.bitwise_xor(outer, ids[0] // (2 * mid))
-            start = pl.multiple_of(place * own_rows, own_rows)
-            out[at * own_rows : (at + 1) * own_rows, :] = acc[pl.ds(start, own_rows), :]
-
-
-def add_part(total, part, mid, nears, own_rows, ids):
-    outers = part.shape[0] // (own_rows * 2 * len(nears))
-    for at in range(len(nears) * outers * 2):
-        near, outer, core = at // (2 * outers), (at // 2) % outers, at % 2
-        middle = lax.bitwise_xor((ids[0] // 2) % mid, nears[near])
-        start = pl.multiple_of(((outer * mid + middle) * 2 + core) * own_rows, own_rows)
-        total[pl.ds(start, own_rows), :] += part[at * own_rows : (at + 1) * own_rows]
-
-
-def base_kernel(mid, own_rows, ids, kept, residual, bias, total):
-    total[...] = residual[...].astype(f32) + bias[...].astype(f32)
-    add_part(total, kept[...], mid, (0,), own_rows, ids)
-
-
-def final_kernel(mid, nears, own_rows, ids, base, early, kept, received, out, total):
-    total[...] = base[...]
-    add_part(total, early[...], mid, (0,), own_rows, ids)
-    add_part(total, kept[...] + received[...], mid, nears, own_rows, ids)
-    out[...] = total[...].astype(bf16)
+            rows.append(acc[pl.ds(start, own_rows), :])
+        out[...] = jnp.concatenate(rows, axis=0).astype(out.dtype)
+
+
+def base_kernel(kept, residual, bias, total):
+    total[...] = kept[...] + residual[...].astype(f32) + bias[...].astype(f32)
+
+
+def final_kernel(total, *refs):
+    value = total[...]
+    for part in refs[:-1]:
+        value = value + part[...].astype(f32)
+    refs[-1][...] = value.astype(bf16)
 
 
 def hop(x, axis, count, distance):
@@ -278,67 +254,57 @@
     requests = kv_count * own_rows
     rows = -(-(slots // PAGE) // 16) * 16
     wide = width + LANES
-    ids = jnp.stack([lax.axis_index("kv"), lax.axis_index("tp")]).astype(jnp.int32)
     kv_hop = lambda x, distance: hop(x, "kv", kv_count, distance)
     shaped = jax.ShapeDtypeStruct
 
-    def call(kernel, shapes, scratch, name, *operands, spec=lambda at: WHOLE, us=1):
+    def call(kernel, shapes, scratch, name, *operands, spec=lambda at: WHOLE):
         single = not isinstance(shapes, tuple)
         return pl.pallas_call(
             kernel,
             out_shape=shapes,
-            in_specs=[SCALARS if x is ids else spec(at) for at, x in enumerate(operands)],
+            in_specs=[spec(at) for at in range(len(operands))],
             out_specs=WHOLE if single else (WHOLE,) * len(shapes),
             scratch_shapes=scratch,
             compiler_params=params(),
-            cost_estimate=pl.CostEstimate(
-                flops=0, bytes_accessed=int(us * 3.5e6), transcendentals=0
-            ),
             name=name,
         )(*operands)
 
-    def pack(parts, head, after):
-        height = sum(x.shape[0] for x in parts)
-        shapes = [shaped((rows, width), bf16) for rows in (height, head) if rows]
+    def pack(parts, after):
         return call(
-            functools.partial(pack_kernel, len(parts), len(shapes) - 1),
-            tuple(shapes),
+            functools.partial(pack_kernel, len(parts)),
+            shaped((sum(x.shape[0] for x in parts), width), bf16),
             [],
             "pack",
             *parts,
             *after,
             spec=lambda at: WHOLE if at < len(parts) else ANY,
-            us=PACK_US,
         )
 
-    def gather(block, before, between):
-        outer = {far: kv_hop(block, 2 * mid * far) for far in (3, 2, 1)}
-        own = {near: kv_hop(block, 2 * near) for near in range(1, mid)}
-        near_all, pair = pack([outer[3], outer[2], outer[1], block], 2 * own_rows, [*own.values(), *before])
-        near_other = kv_hop(near_all, 1)
-        far = []
-        for near in range(1, mid):
-            far += [kv_hop(pair, 2 * near), kv_hop(outer[1], 2 * near), own[near]]
-        after, kept = between(near_all, near_other)
-        (far_all,) = pack(far, 0, after)
-        return near_all, far_all, near_other, kv_hop(far_all, 1), kept
-
-    pick, mask, own_top = call(
+    def gather(block, last, before, after):
+        near = pack([kv_hop(block, 2 * mid * far) for far in (3, 2, 1)] + [last], before)
+        far = [kv_hop(near, 2 * middle) for middle in range(1, mid)]
+        if after:
+            far = [pack(far, after)]
+        line = [near] + far
+        return line + [kv_hop(x, 1) for x in line]
+
+    pick, mask, own_top, held = call(
         functools.partial(prep_kernel, mid, own_rows),
         (
             shaped((rows, requests), bf16),
             shaped((rows, slots), f32),
             shaped((own_rows, LANES), f32),
+            shaped(queries.shape, bf16),
         ),
         [],
         "prep",
-        ids,
         slot_request.reshape(1, slots),
         slot_valid.reshape(1, slots),
         queries,
         new_keys,
     )
-    *blocks, _ = gather(queries, [keys], lambda near_all, near_other: ([pick, values], None))
+    ready = call(ready_kernel, shaped((8, LANES), f32), [], "ready", keys, values, spec=lambda at: ANY)
+    blocks = gather(queries, held, [pick], [ready])
     half = requests // 2
     keep, send = call(
         functools.partial(attend_kernel, len(blocks)),
@@ -378,60 +344,22 @@
         own_top,
     )
 
-    weight = out_weight.T
+    blocks = gather(attended, attended, [], [])
     columns = out_weight.shape[1]
-
-    def projected(kernel, blocks, nears):
-        height = 2 * OUTER * nears * own_rows
-        return call(
-            functools.partial(kernel, own_rows, len(blocks)),
-            (shaped((height // tp_count, columns), f32),) * tp_count,
-            [pltpu.VMEM((height, columns), f32)],
-            "project",
-            ids,
-            *blocks,
-            weight,
-        )
-
-    tp_hop = lambda x, distance: hop(x, "tp", tp_count, distance)
-    sets = ((0,), tuple(range(1, mid)))
-    if tp_count == 2 and (kv_count // tp_count) % (2 * mid) == 0:
-
-        def early(near_all, near_other):
-            part = functools.partial(part_kernel, mid, sets[0])
-            kept, sent = projected(part, [near_all, near_other], 1)
-            base = call(
-                functools.partial(base_kernel, mid, own_rows),
-                shaped(residual.shape, f32),
-                [],
-                "base",
-                ids,
-                kept,
-                residual,
-                out_bias.reshape(1, columns),
-            )
-            return [base], [base, tp_hop(sent, 1)]
-
-        _, far_all, _, far_other, parts = gather(attended, [], early)
-        part = functools.partial(part_kernel, mid, sets[1])
-        kept, sent = projected(part, [far_all, far_other], mid - 1)
-        return call(
-            functools.partial(final_kernel, mid, sets[1], own_rows),
-            shaped(residual.shape, bf16),
-            [pltpu.VMEM(residual.shape, f32)],
-            "final",
-            ids,
-            *parts,
-            kept,
-            tp_hop(sent, 1),
-        )
-    *blocks, _ = gather(attended, [], lambda near_all, near_other: ([], None))
-    outs = projected(functools.partial(project_kernel, mid), blocks, mid)
-    total = outs[0]
-    for distance in range(1, tp_count):
-        total = total + tp_hop(outs[distance], distance)
-    total = total + residual.astype(f32) + out_bias.astype(f32)[None, :]
-    return total.astype(bf16)
+    shape = (requests // tp_count, columns)
+    kept, *sent = call(
+        functools.partial(project_kernel, mid, own_rows, len(blocks)),
+        (shaped(shape, f32),) + (shaped(shape, SENT),) * (tp_count - 1),
+        [pltpu.VMEM((requests, columns), f32)],
+        "project",
+        *blocks,
+        out_weight.T,
+    )
+    received = [hop(x, "tp", tp_count, at + 1) for at, x in enumerate(sent)]
+    total = call(
+        base_kernel, shaped(shape, f32), [], "base", kept, residual, out_bias.reshape(1, columns)
+    )
+    return call(final_kernel, shaped(shape, bf16), [], "final", total, *received)
 
 
 def solution(mesh):

time: 68.6 us -> 59.6 us (0.87)
  starting transfers between devices: 26.7 us -> 20.8 us
  Pallas kernels: 9.39 us -> 5.72 us
  local copies, waits for them, and re-layouts: 4.62 us -> 6.58 us
  waiting for transfers between devices: 27.3 us -> 26.1 us
    ppermute x24 -> x19, starting transfers between devices: 26.7 us -> 20.8 us  [hop(): return lax.ppermute(x, axis, [(i, i ^ distance) for i in range(count)])]
    pallas_call x14 -> x13, Pallas kernels: 9.39 us -> 5.72 us  [call(): pl.pallas_call(kernel, out_shape=shapes, in_specs=[spec(at) for at in ran...]
    ppermute x24 -> x19, waiting for transfers between devices: 27.3 us -> 26.1 us  [hop(): return lax.ppermute(x, axis, [(i, i ^ distance) for i in range(count)])]
    unnamed x26 -> x18, local copies, waits for them, and re-layouts: 4.61 us -> 5.21 us
  transfers between devices with their start and end apart: 24 -> 19, of which waited for: 14 -> 13; matrix products, arithmetic and copies ran while one was open for 0% -> 2% of each run, Pallas kernels for 7% -> 1%
where the time goes in v3:
time: 59.6 us; the launch traced here: 59.3 us
  waiting for transfers between devices  26.1 us (44%)
  starting transfers between devices  20.8 us (35%)
  local copies, waits for them, and re-layouts  6.58 us (11%)
  Pallas kernels  5.72 us (10%)
    ppermute x19, waiting for transfers between devices, hop(): return lax.ppermute(x, axis, [(i, i ^ distance) for i in range(count)])  26.1 us
    ppermute x19, starting transfers between devices, hop(): return lax.ppermute(x, axis, [(i, i ^ distance) for i in range(count)])  20.8 us
    pallas_call x13, Pallas kernels, call(): pl.pallas_call(kernel, out_shape=shapes, in_specs=[spec(at) for at in ran...  5.72 us
    unnamed x18, local copies, waits for them, and re-layouts  5.21 us
  transfers between devices with their start and end apart: 19, of which 13 were waited for; matrix products, arithmetic and copies ran while one was open for 2% of the time, Pallas kernels for 1%

profile of v3, /device:TPU:0, one launch (start us, length us, event | category | flops | bytes accessed | tf_op | source)
XLA Modules:
  0.0 59.3 jit_solution(1004935805226020843)
XLA Ops:
  0.0 5.0 %collective-permute-start = (bf16[8,3584]{1,0:T(8,128)(2,1)}, bf16[8,3584]{1,0:T(8,128)(2,1)S(1)}, u32[]{:S(2)}, u32[]{:S(2)}) collective-permute-start(bf16[8,3584]{1,0:T(8,128)(2,1)} %queries.1), channel_id=1, source_target_pairs={{0,24},{2,26},{4,28},{6,30},{8,16},{10,18},{12,20},{14,22},{16,8},... | collective-permute-start | bytes 172040 | tf_op jit(solution)/shard_map/ppermute | solution.py:234
  5.0 0.0 collective-permute-start.1
  5.1 0.6 collective-permute-start.2
  5.6 0.7 %reshape.10.valid = s32[1,384]{1,0:T(1,128)S(1)} reshape(s32[384]{0:T(512)} %param.16) | data formatting | bytes 3072 | tf_op jit(solution)/shard_map/reshape | solution.py:302
  6.3 0.7 %reshape.9.request = s32[1,384]{1,0:T(1,128)S(1)} reshape(s32[384]{0:T(512)} %param.15) | data formatting | bytes 3072 | tf_op jit(solution)/shard_map/reshape | solution.py:301
  7.0 0.8 %copy-done.5 = bf16[8,3584]{1,0:T(8,128)(2,1)S(1)} copy-done((bf16[8,3584]{1,0:T(8,128)(2,1)S(1)}, bf16[8,3584]{1,0:T(8,128)(2,1)}, u32[]{:S(2)}) %copy-start.5) | copy-done | bytes 57368
  7.8 0.8 %copy-done.6 = bf16[8,3584]{1,0:T(8,128)(2,1)S(1)} copy-done((bf16[8,3584]{1,0:T(8,128)(2,1)S(1)}, bf16[8,3584]{1,0:T(8,128)(2,1)}, u32[]{:S(2)}) %copy-start.6) | copy-done | bytes 57368
  8.6 0.1 prep.1
  8.8 1.6 %collective-permute-done.1.refs_1_ = bf16[8,3584]{1,0:T(8,128)(2,1)S(1)} collective-permute-done((bf16[8,3584]{1,0:T(8,128)(2,1)}, bf16[8,3584]{1,0:T(8,128)(2,1)S(1)}, u32[]{:S(2)}, u32[]{:S(2)}) %collective-permute-start.1) | collective-permute-done | bytes 57376 | tf_op jit(solution)/shard_map/ppermute | solution.py:234
  10.3 0.0 collective-permute-done.2.refs_2_
  10.4 1.6 %collective-permute-start.3 = (bf16[32,3584]{1,0:T(8,128)(2,1)S(1)}, bf16[32,3584]{1,0:T(8,128)(2,1)S(1)}, u32[]{:S(2)}, u32[]{:S(2)}) collective-permute-start(bf16[32,3584]{1,0:T(8,128)(2,1)S(1)} %pack.3.refs_0_), channel_id=1, source_target_pairs={{0,4},{2,6},{4,0},{6,2},{8,12},{10,14},{12,8},{14,10},{16,20},{18,... | collective-permute-start | bytes 688136 | tf_op jit(solution)/shard_map/ppermute | solution.py:234
  11.9 1.8 %copy-done = bf16[384,3584]{1,0:T(8,128)(2,1)S(1)} copy-done((bf16[384,3584]{1,0:T(8,128)(2,1)S(1)}, bf16[384,3584]{1,0:T(8,128)(2,1)}, u32[]{:S(2)}) %copy-start) | copy-done | bytes 2752536
  13.7 1.8 %copy-done.2 = bf16[384,3584]{1,0:T(8,128)(2,1)S(1)} copy-done((bf16[384,3584]{1,0:T(8,128)(2,1)S(1)}, bf16[384,3584]{1,0:T(8,128)(2,1)}, u32[]{:S(2)}) %copy-start.2) | copy-done | bytes 2752536
  15.5 1.6 %collective-permute-done.3.refs_0_ = bf16[32,3584]{1,0:T(8,128)(2,1)S(1)} collective-permute-done((bf16[32,3584]{1,0:T(8,128)(2,1)S(1)}, bf16[32,3584]{1,0:T(8,128)(2,1)S(1)}, u32[]{:S(2)}, u32[]{:S(2)}) %collective-permute-start.3) | collective-permute-done | bytes 229408 | tf_op jit(solution)/shard_map/ppermute | solution.py:234
  17.1 0.1 collective-permute-start.5
  17.2 1.5 %collective-permute-done.5.refs_3_ = bf16[32,3584]{1,0:T(8,128)(2,1)S(1)} collective-permute-done((bf16[32,3584]{1,0:T(8,128)(2,1)S(1)}, bf16[32,3584]{1,0:T(8,128)(2,1)S(1)}, u32[]{:S(2)}, u32[]{:S(2)}) %collective-permute-start.5) | collective-permute-done | bytes 229408 | tf_op jit(solution)/shard_map/ppermute | solution.py:234
  18.6 2.0 %attend.1 = (bf16[64,3712]{1,0:T(8,128)(2,1)S(1)}, bf16[64,3712]{1,0:T(8,128)(2,1)S(1)}) custom-call(bf16[32,128]{1,0:T(8,128)(2,1)S(1)} %get-tuple-element.21.refs_4_.pick, f32[32,384]{1,0:T(8,128)S(1)} %get-tuple-element.22.mask, bf16[384,3584]{1,0:T(8,128)(2,1)S(1)} %copy-done.1, bf16[384,3584]{1,0:T(8,128)(2,1)S(1)} %copy-done.2, ...), custom_call_target="tpu_custom_call" | custom-call | tf_op jit(solution)/shard_map/attend/pallas_call | solution.py:262
  20.6 0.2 collective-permute-start.6
  20.8 1.7 %collective-permute-done.6.refs_1_ = bf16[64,3712]{1,0:T(8,128)(2,1)S(1)} collective-permute-done((bf16[64,3712]{1,0:T(8,128)(2,1)S(1)}, bf16[64,3712]{1,0:T(8,128)(2,1)S(1)}, u32[]{:S(2)}, u32[]{:S(2)}) %collective-permute-start.6) | collective-permute-done | bytes 475168 | tf_op jit(solution)/shard_map/ppermute | solution.py:234
  22.5 0.7 %merge.3 = (bf16[16,3712]{1,0:T(8,128)(2,1)S(1)}, bf16[16,3712]{1,0:T(8,128)(2,1)S(1)}, bf16[16,3712]{1,0:T(8,128)(2,1)S(1)}, bf16[16,3712]{1,0:T(8,128)(2,1)S(1)}) custom-call(bf16[64,3712]{1,0:T(8,128)(2,1)S(1)} %get-tuple-element.24.refs_0_, bf16[64,3712]{1,0:T(8,128)(2,1)S(1)} %collective-permute-done.6.refs_1_), custom_call_target="tpu_custom_call" | custom-call | tf_op jit(solution)/shard_map/merge/pallas_call | solution.py:262
  23.2 0.0 copy-start.8
  23.2 0.0 copy-start.4
  23.3 1.6 %collective-permute-start.8 = (bf16[16,3712]{1,0:T(8,128)(2,1)S(1)}, bf16[16,3712]{1,0:T(8,128)(2,1)S(1)}, u32[]{:S(2)}, u32[]{:S(2)}) collective-permute-start(bf16[16,3712]{1,0:T(8,128)(2,1)S(1)} %get-tuple-element.30), channel_id=1, source_target_pairs={{0,4},{2,6},{4,0},{6,2},{8,12},{10,14},{12,8},{14,10},{16,20},{18,... | collective-permute-start | bytes 356360 | tf_op jit(solution)/shard_map/ppermute | solution.py:234
  24.9 0.4 collective-permute-start.7
  25.4 4.0 %collective-permute-done.8.refs_1_ = bf16[16,3712]{1,0:T(8,128)(2,1)S(1)} collective-permute-done((bf16[16,3712]{1,0:T(8,128)(2,1)S(1)}, bf16[16,3712]{1,0:T(8,128)(2,1)S(1)}, u32[]{:S(2)}, u32[]{:S(2)}) %collective-permute-start.8) | collective-permute-done | bytes 118816 | tf_op jit(solution)/shard_map/ppermute | solution.py:234
  29.4 0.3 merge.5
  29.7 1.5 %collective-permute-start.10 = (bf16[8,3712]{1,0:T(8,128)(2,1)S(1)}, bf16[8,3712]{1,0:T(8,128)(2,1)S(1)}, u32[]{:S(2)}, u32[]{:S(2)}) collective-permute-start(bf16[8,3712]{1,0:T(8,128)(2,1)S(1)} %get-tuple-element.32), channel_id=1, source_target_pairs={{0,16},{2,18},{4,20},{6,22},{8,24},{10,26},{12,28},{14,30},{16,0},... | collective-permute-start | bytes 178184 | tf_op jit(solution)/shard_map/ppermute | solution.py:234
  31.2 1.6 %collective-permute-start.9 = (bf16[8,3712]{1,0:T(8,128)(2,1)S(1)}, bf16[8,3712]{1,0:T(8,128)(2,1)S(1)}, u32[]{:S(2)}, u32[]{:S(2)}) collective-permute-start(bf16[8,3712]{1,0:T(8,128)(2,1)S(1)} %get-tuple-element.31), channel_id=1, source_target_pairs={{0,24},{2,26},{4,28},{6,30},{8,16},{10,18},{12,20},{14,22},{16,8},... | collective-permute-start | bytes 178184 | tf_op jit(solution)/shard_map/ppermute | solution.py:234
  32.8 0.0 collective-permute-done.7.refs_1_
  32.8 0.3 merge.4
  33.1 0.5 collective-permute-start.11
  33.7 2.1 %collective-permute-done.10.refs_2_ = bf16[8,3712]{1,0:T(8,128)(2,1)S(1)} collective-permute-done((bf16[8,3712]{1,0:T(8,128)(2,1)S(1)}, bf16[8,3712]{1,0:T(8,128)(2,1)S(1)}, u32[]{:S(2)}, u32[]{:S(2)}) %collective-permute-start.10) | collective-permute-done | bytes 59424 | tf_op jit(solution)/shard_map/ppermute | solution.py:234
  35.7 1.5 %collective-permute-done.9.refs_1_ = bf16[8,3712]{1,0:T(8,128)(2,1)S(1)} collective-permute-done((bf16[8,3712]{1,0:T(8,128)(2,1)S(1)}, bf16[8,3712]{1,0:T(8,128)(2,1)S(1)}, u32[]{:S(2)}, u32[]{:S(2)}) %collective-permute-start.9) | collective-permute-done | bytes 59424 | tf_op jit(solution)/shard_map/ppermute | solution.py:234
  37.2 0.6 collective-permute-done.11.refs_3_
  37.8 0.4 last.1.refs_3_
  38.2 1.8 %collective-permute-start.12 = (bf16[8,3584]{1,0:T(8,128)(2,1)S(1)}, bf16[8,3584]{1,0:T(8,128)(2,1)S(1)}, u32[]{:S(2)}, u32[]{:S(2)}) collective-permute-start(bf16[8,3584]{1,0:T(8,128)(2,1)S(1)} %last.1.refs_3_), channel_id=1, source_target_pairs={{0,24},{2,26},{4,28},{6,30},{8,16},{10,18},{12,20},{14,22},{16,8},... | collective-permute-start | bytes 172040 | tf_op jit(solution)/shard_map/ppermute | solution.py:234
  40.1 2.6 %collective-permute-start.14 = (bf16[8,3584]{1,0:T(8,128)(2,1)S(1)}, bf16[8,3584]{1,0:T(8,128)(2,1)S(1)}, u32[]{:S(2)}, u32[]{:S(2)}) collective-permute-start(bf16[8,3584]{1,0:T(8,128)(2,1)S(1)} %last.1.refs_3_), channel_id=1, source_target_pairs={{0,8},{2,10},{4,12},{6,14},{8,0},{10,2},{12,4},{14,6},{16,24},{18,... | collective-permute-start | bytes 172040 | tf_op jit(solution)/shard_map/ppermute | solution.py:234
  42.7 1.6 %collective-permute-done.12.refs_0_ = bf16[8,3584]{1,0:T(8,128)(2,1)S(1)} collective-permute-done((bf16[8,3584]{1,0:T(8,128)(2,1)S(1)}, bf16[8,3584]{1,0:T(8,128)(2,1)S(1)}, u32[]{:S(2)}, u32[]{:S(2)}) %collective-permute-start.12) | collective-permute-done | bytes 57376 | tf_op jit(solution)/shard_map/ppermute | solution.py:234
  44.2 1.2 %collective-permute-done.13.refs_1_ = bf16[8,3584]{1,0:T(8,128)(2,1)S(1)} collective-permute-done((bf16[8,3584]{1,0:T(8,128)(2,1)S(1)}, bf16[8,3584]{1,0:T(8,128)(2,1)S(1)}, u32[]{:S(2)}, u32[]{:S(2)}) %collective-permute-start.13) | collective-permute-done | bytes 57376 | tf_op jit(solution)/shard_map/ppermute | solution.py:234
  45.5 0.0 collective-permute-done.14.refs_2_
  45.5 1.6 %collective-permute-start.15 = (bf16[32,3584]{1,0:T(8,128)(2,1)S(1)}, bf16[32,3584]{1,0:T(8,128)(2,1)S(1)}, u32[]{:S(2)}, u32[]{:S(2)}) collective-permute-start(bf16[32,3584]{1,0:T(8,128)(2,1)S(1)} %pack.5.refs_0_), channel_id=1, source_target_pairs={{0,4},{2,6},{4,0},{6,2},{8,12},{10,14},{12,8},{14,10},{16,20},{18,... | collective-permute-start | bytes 688136 | tf_op jit(solution)/shard_map/ppermute | solution.py:234
  47.1 0.0 collective-permute-start.16
  47.1 4.5 %collective-permute-done.15.refs_1_ = bf16[32,3584]{1,0:T(8,128)(2,1)S(1)} collective-permute-done((bf16[32,3584]{1,0:T(8,128)(2,1)S(1)}, bf16[32,3584]{1,0:T(8,128)(2,1)S(1)}, u32[]{:S(2)}, u32[]{:S(2)}) %collective-permute-start.15) | collective-permute-done | bytes 229408 | tf_op jit(solution)/shard_map/ppermute | solution.py:234
  51.6 1.5 %collective-permute-done.17.refs_3_ = bf16[32,3584]{1,0:T(8,128)(2,1)S(1)} collective-permute-done((bf16[32,3584]{1,0:T(8,128)(2,1)S(1)}, bf16[32,3584]{1,0:T(8,128)(2,1)S(1)}, u32[]{:S(2)}, u32[]{:S(2)}) %collective-permute-start.17) | collective-permute-done | bytes 229408 | tf_op jit(solution)/shard_map/ppermute | solution.py:234
  53.1 1.2 %project.1 = (f32[64,448]{1,0:T(8,128)S(1)}, bf16[64,448]{1,0:T(8,128)(2,1)S(1)}) custom-call(bf16[32,3584]{1,0:T(8,128)(2,1)S(1)} %pack.5.refs_0_, bf16[32,3584]{1,0:T(8,128)(2,1)S(1)} %collective-permute-done.15.refs_1_, bf16[32,3584]{1,0:T(8,128)(2,1)S(1)} %collective-permute-done.16.refs_2_, bf16[32,3584]{1,0:T(8,128)(2,1)S(1)} %collective-permute-done.17.refs_3_, ...), custom_call_target="tpu_custom_call" | custom-call | tf_op jit(solution)/shard_map/project/pallas_call | solution.py:262
  54.3 1.6 %collective-permute-start.18 = (bf16[64,448]{1,0:T(8,128)(2,1)S(1)}, bf16[64,448]{1,0:T(8,128)(2,1)S(1)}, u32[]{:S(2)}, u32[]{:S(2)}) collective-permute-start(bf16[64,448]{1,0:T(8,128)(2,1)S(1)} %get-tuple-element.36), channel_id=1, source_target_pairs={{0,1},{1,0},{2,3},{3,2},{4,5},{5,4},{6,7},{7,6},{8,9},{9,8},{10,11... | collective-permute-start | bytes 172040 | tf_op jit(solution)/shard_map/ppermute | solution.py:234
  55.9 2.7 %collective-permute-done.18.refs_0_ = bf16[64,448]{1,0:T(8,128)(2,1)S(1)} collective-permute-done((bf16[64,448]{1,0:T(8,128)(2,1)S(1)}, bf16[64,448]{1,0:T(8,128)(2,1)S(1)}, u32[]{:S(2)}, u32[]{:S(2)}) %collective-permute-start.18) | collective-permute-done | bytes 57376 | tf_op jit(solution)/shard_map/ppermute | solution.py:234
  58.6 0.6 %final.1 = bf16[64,448]{1,0:T(8,128)(2,1)} custom-call(f32[64,448]{1,0:T(8,128)S(1)} %base.1.total, bf16[64,448]{1,0:T(8,128)(2,1)S(1)} %collective-permute-done.18.refs_0_), custom_call_target="tpu_custom_call" | custom-call | tf_op jit(solution)/shard_map/final/pallas_call | solution.py:262
  (24 shorter events, 0.1 us)
Async XLA Ops:
  0.0 8.8 %collective-permute-start = (bf16[8,3584]{1,0:T(8,128)(2,1)}, bf16[8,3584]{1,0:T(8,128)(2,1)S(1)}, u32[]{:S(2)}, u32[]{:S(2)}) collective-permute-start(bf16[8,3584]{1,0:T(8,128)(2,1)} %queries.1), channel_id=1, source_target_pairs={{0,24},{2,26},{4,28},{6,30},{8,16},{10,18},{12,20},{14,22},{16,8},... | collective-permute-start | bytes 172040 | tf_op jit(solution)/shard_map/ppermute | solution.py:234
  5.0 5.3 %collective-permute-start.1 = (bf16[8,3584]{1,0:T(8,128)(2,1)}, bf16[8,3584]{1,0:T(8,128)(2,1)S(1)}, u32[]{:S(2)}, u32[]{:S(2)}) collective-permute-start(bf16[8,3584]{1,0:T(8,128)(2,1)} %queries.1), channel_id=1, source_target_pairs={{0,16},{2,18},{4,20},{6,22},{8,24},{10,26},{12,28},{14,30},{16,0},... | collective-permute-start | bytes 172040 | tf_op jit(solution)/shard_map/ppermute | solution.py:234
  5.1 5.3 %collective-permute-start.2 = (bf16[8,3584]{1,0:T(8,128)(2,1)}, bf16[8,3584]{1,0:T(8,128)(2,1)S(1)}, u32[]{:S(2)}, u32[]{:S(2)}) collective-permute-start(bf16[8,3584]{1,0:T(8,128)(2,1)} %queries.1), channel_id=1, source_target_pairs={{0,8},{2,10},{4,12},{6,14},{8,0},{10,2},{12,4},{14,6},{16,24},{18,... | collective-permute-start | bytes 172040 | tf_op jit(solution)/shard_map/ppermute | solution.py:234
  7.0 0.8 %copy-start.5 = (bf16[8,3584]{1,0:T(8,128)(2,1)S(1)}, bf16[8,3584]{1,0:T(8,128)(2,1)}, u32[]{:S(2)}) copy-start(bf16[8,3584]{1,0:T(8,128)(2,1)} %new_keys.1) | copy-start | bytes 172036
  7.8 0.8 %copy-start.6 = (bf16[8,3584]{1,0:T(8,128)(2,1)S(1)}, bf16[8,3584]{1,0:T(8,128)(2,1)}, u32[]{:S(2)}) copy-start(bf16[8,3584]{1,0:T(8,128)(2,1)} %queries.1) | copy-start | bytes 172036
  10.4 6.7 %collective-permute-start.3 = (bf16[32,3584]{1,0:T(8,128)(2,1)S(1)}, bf16[32,3584]{1,0:T(8,128)(2,1)S(1)}, u32[]{:S(2)}, u32[]{:S(2)}) collective-permute-start(bf16[32,3584]{1,0:T(8,128)(2,1)S(1)} %pack.3.refs_0_), channel_id=1, source_target_pairs={{0,4},{2,6},{4,0},{6,2},{8,12},{10,14},{12,8},{14,10},{16,20},{18,... | collective-permute-start | bytes 688136 | tf_op jit(solution)/shard_map/ppermute | solution.py:234
  11.9 1.8 %copy-start = (bf16[384,3584]{1,0:T(8,128)(2,1)S(1)}, bf16[384,3584]{1,0:T(8,128)(2,1)}, u32[]{:S(2)}) copy-start(bf16[384,3584]{1,0:T(8,128)(2,1)} %keys.1) | copy-start | bytes 8257540
  13.7 1.8 %copy-start.2 = (bf16[384,3584]{1,0:T(8,128)(2,1)S(1)}, bf16[384,3584]{1,0:T(8,128)(2,1)}, u32[]{:S(2)}) copy-start(bf16[384,3584]{1,0:T(8,128)(2,1)} %values.1) | copy-start | bytes 8257540
  15.5 3.1 %copy-start.1 = (bf16[384,3584]{1,0:T(8,128)(2,1)S(1)}, bf16[384,3584]{1,0:T(8,128)(2,1)}, u32[]{:S(2)}) copy-start(bf16[384,3584]{1,0:T(8,128)(2,1)} %keys.1) | copy-start | bytes 8257540
  15.5 1.7 %collective-permute-start.4 = (bf16[32,3584]{1,0:T(8,128)(2,1)S(1)}, bf16[32,3584]{1,0:T(8,128)(2,1)S(1)}, u32[]{:S(2)}, u32[]{:S(2)}) collective-permute-start(bf16[32,3584]{1,0:T(8,128)(2,1)S(1)} %pack.3.refs_0_), channel_id=1, source_target_pairs={{0,2},{2,0},{4,6},{6,4},{8,10},{10,8},{12,14},{14,12},{16,18},{18,... | collective-permute-start | bytes 688136 | tf_op jit(solution)/shard_map/ppermute | solution.py:234
  17.1 1.6 %collective-permute-start.5 = (bf16[32,3584]{1,0:T(8,128)(2,1)S(1)}, bf16[32,3584]{1,0:T(8,128)(2,1)S(1)}, u32[]{:S(2)}, u32[]{:S(2)}) collective-permute-start(bf16[32,3584]{1,0:T(8,128)(2,1)S(1)} %pack.4.refs_1_), channel_id=1, source_target_pairs={{0,2},{2,0},{4,6},{6,4},{8,10},{10,8},{12,14},{14,12},{16,18},{18,... | collective-permute-start | bytes 688136 | tf_op jit(solution)/shard_map/ppermute | solution.py:234
  18.6 19.2 %copy-start.7 = (bf16[8,3584]{1,0:T(8,128)(2,1)S(1)}, bf16[8,3584]{1,0:T(8,128)(2,1)}, u32[]{:S(2)}) copy-start(bf16[8,3584]{1,0:T(8,128)(2,1)} %refs_4_.1) | copy-start | bytes 172036
  18.6 34.4 %copy-start.3 = (bf16[3584,448]{0,1:T(8,128)(2,1)S(1)}, bf16[3584,448]{0,1:T(8,128)(2,1)}, u32[]{:S(2)}) copy-start(bf16[3584,448]{0,1:T(8,128)(2,1)} %param.17) | copy-start | bytes 9633796
  20.6 1.9 %collective-permute-start.6 = (bf16[64,3712]{1,0:T(8,128)(2,1)S(1)}, bf16[64,3712]{1,0:T(8,128)(2,1)S(1)}, u32[]{:S(2)}, u32[]{:S(2)}) collective-permute-start(bf16[64,3712]{1,0:T(8,128)(2,1)S(1)} %get-tuple-element.25), channel_id=1, source_target_pairs={{0,2},{2,0},{4,6},{6,4},{8,10},{10,8},{12,14},{14,12},{16,18},{18,... | collective-permute-start | bytes 1425416 | tf_op jit(solution)/shard_map/ppermute | solution.py:234
  23.2 32.6 %copy-start.8 = (bf16[448]{0:T(512)(128)(2,1)S(1)}, bf16[448]{0:T(512)(128)(2,1)}, u32[]{:S(2)}) copy-start(bf16[448]{0:T(512)(128)(2,1)} %param.18) | copy-start | bytes 2692
  23.2 32.6 %copy-start.4 = (bf16[64,448]{1,0:T(8,128)(2,1)S(1)}, bf16[64,448]{1,0:T(8,128)(2,1)}, u32[]{:S(2)}) copy-start(bf16[64,448]{1,0:T(8,128)(2,1)} %residual.1) | copy-start | bytes 172036
  23.3 6.1 %collective-permute-start.8 = (bf16[16,3712]{1,0:T(8,128)(2,1)S(1)}, bf16[16,3712]{1,0:T(8,128)(2,1)S(1)}, u32[]{:S(2)}, u32[]{:S(2)}) collective-permute-start(bf16[16,3712]{1,0:T(8,128)(2,1)S(1)} %get-tuple-element.30), channel_id=1, source_target_pairs={{0,4},{2,6},{4,0},{6,2},{8,12},{10,14},{12,8},{14,10},{16,20},{18,... | collective-permute-start | bytes 356360 | tf_op jit(solution)/shard_map/ppermute | solution.py:234
  24.9 7.9 %collective-permute-start.7 = (bf16[16,3712]{1,0:T(8,128)(2,1)S(1)}, bf16[16,3712]{1,0:T(8,128)(2,1)S(1)}, u32[]{:S(2)}, u32[]{:S(2)}) collective-permute-start(bf16[16,3712]{1,0:T(8,128)(2,1)S(1)} %get-tuple-element.27), channel_id=1, source_target_pairs={{0,4},{2,6},{4,0},{6,2},{8,12},{10,14},{12,8},{14,10},{16,20},{18,... | collective-permute-start | bytes 356360 | tf_op jit(solution)/shard_map/ppermute | solution.py:234
  29.7 6.0 %collective-permute-start.10 = (bf16[8,3712]{1,0:T(8,128)(2,1)S(1)}, bf16[8,3712]{1,0:T(8,128)(2,1)S(1)}, u32[]{:S(2)}, u32[]{:S(2)}) collective-permute-start(bf16[8,3712]{1,0:T(8,128)(2,1)S(1)} %get-tuple-element.32), channel_id=1, source_target_pairs={{0,16},{2,18},{4,20},{6,22},{8,24},{10,26},{12,28},{14,30},{16,0},... | collective-permute-start | bytes 178184 | tf_op jit(solution)/shard_map/ppermute | solution.py:234
  31.2 6.0 %collective-permute-start.9 = (bf16[8,3712]{1,0:T(8,128)(2,1)S(1)}, bf16[8,3712]{1,0:T(8,128)(2,1)S(1)}, u32[]{:S(2)}, u32[]{:S(2)}) collective-permute-start(bf16[8,3712]{1,0:T(8,128)(2,1)S(1)} %get-tuple-element.31), channel_id=1, source_target_pairs={{0,24},{2,26},{4,28},{6,30},{8,16},{10,18},{12,20},{14,22},{16,8},... | collective-permute-start | bytes 178184 | tf_op jit(solution)/shard_map/ppermute | solution.py:234
  33.1 4.7 %collective-permute-start.11 = (bf16[8,3712]{1,0:T(8,128)(2,1)S(1)}, bf16[8,3712]{1,0:T(8,128)(2,1)S(1)}, u32[]{:S(2)}, u32[]{:S(2)}) collective-permute-start(bf16[8,3712]{1,0:T(8,128)(2,1)S(1)} %get-tuple-element.33), channel_id=1, source_target_pairs={{0,8},{2,10},{4,12},{6,14},{8,0},{10,2},{12,4},{14,6},{16,24},{18,... | collective-permute-start | bytes 178184 | tf_op jit(solution)/shard_map/ppermute | solution.py:234
  38.2 6.0 %collective-permute-start.12 = (bf16[8,3584]{1,0:T(8,128)(2,1)S(1)}, bf16[8,3584]{1,0:T(8,128)(2,1)S(1)}, u32[]{:S(2)}, u32[]{:S(2)}) collective-permute-start(bf16[8,3584]{1,0:T(8,128)(2,1)S(1)} %last.1.refs_3_), channel_id=1, source_target_pairs={{0,24},{2,26},{4,28},{6,30},{8,16},{10,18},{12,20},{14,22},{16,8},... | collective-permute-start | bytes 172040 | tf_op jit(solution)/shard_map/ppermute | solution.py:234
  40.1 5.4 %collective-permute-start.13 = (bf16[8,3584]{1,0:T(8,128)(2,1)S(1)}, bf16[8,3584]{1,0:T(8,128)(2,1)S(1)}, u32[]{:S(2)}, u32[]{:S(2)}) collective-permute-start(bf16[8,3584]{1,0:T(8,128)(2,1)S(1)} %last.1.refs_3_), channel_id=1, source_target_pairs={{0,16},{2,18},{4,20},{6,22},{8,24},{10,26},{12,28},{14,30},{16,0},... | collective-permute-start | bytes 172040 | tf_op jit(solution)/shard_map/ppermute | solution.py:234
  40.1 5.4 %collective-permute-start.14 = (bf16[8,3584]{1,0:T(8,128)(2,1)S(1)}, bf16[8,3584]{1,0:T(8,128)(2,1)S(1)}, u32[]{:S(2)}, u32[]{:S(2)}) collective-permute-start(bf16[8,3584]{1,0:T(8,128)(2,1)S(1)} %last.1.refs_3_), channel_id=1, source_target_pairs={{0,8},{2,10},{4,12},{6,14},{8,0},{10,2},{12,4},{14,6},{16,24},{18,... | collective-permute-start | bytes 172040 | tf_op jit(solution)/shard_map/ppermute | solution.py:234
  45.5 6.1 %collective-permute-start.15 = (bf16[32,3584]{1,0:T(8,128)(2,1)S(1)}, bf16[32,3584]{1,0:T(8,128)(2,1)S(1)}, u32[]{:S(2)}, u32[]{:S(2)}) collective-permute-start(bf16[32,3584]{1,0:T(8,128)(2,1)S(1)} %pack.5.refs_0_), channel_id=1, source_target_pairs={{0,4},{2,6},{4,0},{6,2},{8,12},{10,14},{12,8},{14,10},{16,20},{18,... | collective-permute-start | bytes 688136 | tf_op jit(solution)/shard_map/ppermute | solution.py:234
  47.1 4.5 %collective-permute-start.16 = (bf16[32,3584]{1,0:T(8,128)(2,1)S(1)}, bf16[32,3584]{1,0:T(8,128)(2,1)S(1)}, u32[]{:S(2)}, u32[]{:S(2)}) collective-permute-start(bf16[32,3584]{1,0:T(8,128)(2,1)S(1)} %pack.5.refs_0_), channel_id=1, source_target_pairs={{0,2},{2,0},{4,6},{6,4},{8,10},{10,8},{12,14},{14,12},{16,18},{18,... | collective-permute-start | bytes 688136 | tf_op jit(solution)/shard_map/ppermute | solution.py:234
  51.6 1.5 %collective-permute-start.17 = (bf16[32,3584]{1,0:T(8,128)(2,1)S(1)}, bf16[32,3584]{1,0:T(8,128)(2,1)S(1)}, u32[]{:S(2)}, u32[]{:S(2)}) collective-permute-start(bf16[32,3584]{1,0:T(8,128)(2,1)S(1)} %collective-permute-done.15.refs_1_), channel_id=1, source_target_pairs={{0,2},{2,0},{4,6},{6,4},{8,10},{10,8},{12,14},{14,12},{16,18},{18,... | collective-permute-start | bytes 688136 | tf_op jit(solution)/shard_map/ppermute | solution.py:234
  54.3 4.3 %collective-permute-start.18 = (bf16[64,448]{1,0:T(8,128)(2,1)S(1)}, bf16[64,448]{1,0:T(8,128)(2,1)S(1)}, u32[]{:S(2)}, u32[]{:S(2)}) collective-permute-start(bf16[64,448]{1,0:T(8,128)(2,1)S(1)} %get-tuple-element.36), channel_id=1, source_target_pairs={{0,1},{1,0},{2,3},{3,2},{4,5},{5,4},{6,7},{7,6},{8,9},{9,8},{10,11... | collective-permute-start | bytes 172040 | tf_op jit(solution)/shard_map/ppermute | solution.py:234

commit v4 on v3

--- a/solution.py
+++ b/solution.py
@@ -16,6 +16,8 @@
 
 floor_score = -1e30
 SENT = jnp.bfloat16
+GATHER_DIRECT = 1
+REDUCE_DIRECT = 3
 f32 = jnp.float32
 bf16 = jnp.bfloat16
 WHOLE = pl.BlockSpec(memory_space=pltpu.VMEM)
@@ -26,19 +28,39 @@
     return pltpu.CompilerParams(vmem_limit_bytes=megabytes * 1024 * 1024)
 
 
-def offset_of(block, mid):
-    core = block // (mid * OUTER)
-    middle = (block // OUTER) % mid
-    return core + 2 * middle + 2 * mid * (OUTER - 1 - block % OUTER)
-
-
-def place_of(offset, mid):
-    core = offset % 2
-    middle = (offset // 2) % mid
-    return (core * mid + middle) * OUTER + OUTER - 1 - offset // (2 * mid)
-
-
-def prep_kernel(mid, own_rows, request, valid, queries, new_keys, pick, mask, own_top, held):
+def relayed(direct):
+    return [far for far in (3, 2, 1) if far != direct]
+
+
+def gather_order(mid, direct):
+    lines = [[(far, 0) for far in relayed(direct) + [0, direct]]]
+    lines[0] += [(direct, middle) for middle in range(1, mid)]
+    lines += [[(far, middle) for far in relayed(direct) + [0]] for middle in range(1, mid)]
+    return [
+        core + 2 * middle + 2 * mid * far
+        for core in (0, 1)
+        for line in lines
+        for far, middle in line
+    ]
+
+
+def reduce_order(mid, direct):
+    return [
+        core + 2 * middle + 2 * mid * far
+        for core in (0, 1)
+        for middle in range(mid)
+        for far in relayed(direct) + [0, direct]
+    ]
+
+
+def request_at(place, order, own_rows):
+    distance = jnp.zeros_like(place)
+    for at, value in enumerate(order):
+        distance = jnp.where(place // own_rows == at, value, distance)
+    return lax.bitwise_xor(distance, lax.axis_index("kv")) * own_rows + place % own_rows
+
+
+def prep_kernel(mid, own_rows, request, valid, pick, spread, mask):
     rows, slots = mask.shape
     row = lax.broadcasted_iota(jnp.int32, (rows, slots), 0)
     lane = lax.broadcasted_iota(jnp.int32, (rows, slots), 1)
@@ -50,20 +72,22 @@
     live = (owners == mine) & first & (jnp.broadcast_to(valid[...], (rows, slots)) == 1)
     mask[...] = jnp.where(live, 1.0, 0.0)
     place = lax.broadcasted_iota(jnp.int32, pick.shape, 1)
-    owner = lax.bitwise_xor(offset_of(place // own_rows, mid), lax.axis_index("kv"))
-    named = owner * own_rows + place % own_rows
-    pick[...] = jnp.where((named == mine) & first, 1.0, 0.0).astype(bf16)
-    heads = queries.shape[1] // HD
+    orders = (gather_order(mid, GATHER_DIRECT), reduce_order(mid, REDUCE_DIRECT))
+    for out, order in zip((pick, spread), orders):
+        named = request_at(place, order, own_rows)
+        out[...] = jnp.where((named == mine) & first, 1.0, 0.0).astype(bf16)
+
+
+def own_kernel(queries, new_keys, own_top):
     where = lax.broadcasted_iota(jnp.int32, own_top.shape, 1)
     top = jnp.zeros(own_top.shape, f32)
-    for head in range(heads):
+    for head in range(queries.shape[1] // HD):
         cut = slice(head * HD, (head + 1) * HD)
         score = jnp.sum(
             queries[:, cut].astype(f32) * new_keys[:, cut].astype(f32), axis=1, keepdims=True
         ) * (1.0 / math.sqrt(HD))
         top = jnp.where(where == head, score, top)
     own_top[...] = top
-    held[...] = queries[...]
 
 
 def split_top(top):
@@ -88,15 +112,18 @@
     refs[-1][...] = stacked(refs[:count]).astype(bf16)
 
 
+def hold_kernel(queries, held):
+    held[...] = queries[...]
+
+
 def ready_kernel(*refs):
     refs[-1][...] = jnp.zeros_like(refs[-1])
 
 
-def attend_kernel(count, pick, mask, keys, values, *refs):
-    blocks, (keep, send) = refs[:count], refs[count:]
+def attend_kernel(count, pick, spread_to, mask, keys, values, *refs):
+    blocks, outs = refs[:count], refs[count:]
     rows = pick.shape[0]
     heads = keys.shape[1] // HD
-    half = keep.shape[0]
     lane = lax.broadcasted_iota(jnp.int32, (rows, LANES), 1)
     live = mask[...] > 0.0
     chosen = jnp.dot(pick[...], stacked(blocks).astype(bf16), preferred_element_type=f32)
@@ -142,13 +169,15 @@
     spread = functools.partial(
         lax.dot_general, dimension_numbers=(((0,), (0,)), ((), ())), preferred_element_type=f32
     )
-    dense = spread(pick[...], jnp.concatenate(found, axis=1).astype(bf16)).astype(bf16)
+    dense = spread(spread_to[...], jnp.concatenate(found, axis=1).astype(bf16)).astype(bf16)
     stat = jnp.where(lane == LANES - 1, 1.0, split_top(tops)).astype(bf16)
-    stat = spread(pick[...], stat)
+    stat = spread(spread_to[...], stat)
     place = lax.broadcasted_iota(jnp.int32, stat.shape, 1)
     absent = stat[:, LANES - 1 :] == 0.0
     stat = jnp.where(absent & (place < STAT), floor_score, stat).astype(bf16)
-    for out, part in ((keep, slice(0, half)), (send, slice(half, 2 * half))):
+    size = outs[0].shape[0]
+    for at, out in enumerate(outs):
+        part = slice(at * size, (at + 1) * size)
         out[:, : heads * HD] = dense[part]
         out[:, heads * HD :] = stat[part]
 
@@ -168,32 +197,37 @@
     return head_of, best + jnp.log(total)
 
 
-def part_of(ref):
-    return lambda head: ref[:, head * HD : (head + 1) * HD].astype(f32)
-
-
-def top_of(ref):
-    return join_top(ref[:, ref.shape[1] - LANES :].astype(f32))
+def part_of(ref, start, rows):
+    return lambda head: ref[:, head * HD : (head + 1) * HD].astype(f32)[start : start + rows]
+
+
+def top_of(ref, start, rows):
+    return join_top(ref[:, ref.shape[1] - LANES :].astype(f32)[start : start + rows])
 
 
 def merge_kernel(count, *refs):
     ins, outs = refs[:count], refs[count:]
     heads = ins[0].shape[1] // HD - 1
-    rows = outs[0].shape[0]
-    head_of, top = merge([part_of(ref) for ref in ins], [top_of(ref) for ref in ins])
+    rows = sum(out.shape[0] for out in outs)
+    head_of, top = merge(
+        [part_of(ref, 0, rows) for ref in ins], [top_of(ref, 0, rows) for ref in ins]
+    )
     for head in range(heads + 1):
         cut = slice(head * HD, (head + 1) * HD)
         block = head_of(head) if head < heads else split_top(top)
-        for at, out in enumerate(outs):
-            out[:, cut] = block[at * rows : (at + 1) * rows].astype(bf16)
+        at = 0
+        for out in outs:
+            out[:, cut] = block[at : at + out.shape[0]].astype(bf16)
+            at += out.shape[0]
 
 
 def last_kernel(count, *refs):
     ins = refs[:count]
     new_values, own_top, out = refs[count:]
+    rows = out.shape[0]
     head_of, _ = merge(
-        [part_of(ref) for ref in ins] + [part_of(new_values)],
-        [top_of(ref) for ref in ins] + [own_top[...]],
+        [part_of(ref, ref.shape[0] - rows, rows) for ref in ins] + [part_of(new_values, 0, rows)],
+        [top_of(ref, ref.shape[0] - rows, rows) for ref in ins] + [own_top[...]],
     )
     for head in range(out.shape[1] // HD):
         out[:, head * HD : (head + 1) * HD] = head_of(head).astype(bf16)
@@ -201,22 +235,20 @@
 
 def project_kernel(mid, own_rows, count, *refs):
     blocks, weight, outs, acc = refs[:count], refs[count], refs[count + 1 : -1], refs[-1]
-    acc[...] = lax.dot_general(
+    product = lax.dot_general(
         stacked(blocks).astype(bf16),
         weight[...],
         (((1,), (1,)), ((), ())),
         preferred_element_type=f32,
     )
-    here = lax.axis_index("kv")
-    owners = outs[0].shape[0] // own_rows
+    for at, distance in enumerate(gather_order(mid, GATHER_DIRECT)):
+        owner = lax.bitwise_xor(lax.axis_index("kv"), distance)
+        start = pl.multiple_of(owner * own_rows, own_rows)
+        acc[pl.ds(start, own_rows), :] = product[at * own_rows : (at + 1) * own_rows]
     for distance, out in enumerate(outs):
+        rows = out.shape[0]
         side = lax.bitwise_xor(lax.axis_index("tp"), distance)
-        rows = []
-        for at in range(owners):
-            offset = lax.bitwise_xor(side * owners + at, here)
-            start = pl.multiple_of(place_of(offset, mid) * own_rows, own_rows)
-            rows.append(acc[pl.ds(start, own_rows), :])
-        out[...] = jnp.concatenate(rows, axis=0).astype(out.dtype)
+        out[...] = acc[pl.ds(pl.multiple_of(side * rows, rows), rows), :].astype(out.dtype)
 
 
 def base_kernel(kept, residual, bias, total):
@@ -269,7 +301,7 @@
             name=name,
         )(*operands)
 
-    def pack(parts, after):
+    def pack(parts, *after):
         return call(
             functools.partial(pack_kernel, len(parts)),
             shaped((sum(x.shape[0] for x in parts), width), bf16),
@@ -280,60 +312,70 @@
             spec=lambda at: WHOLE if at < len(parts) else ANY,
         )
 
-    def gather(block, last, before, after):
-        near = pack([kv_hop(block, 2 * mid * far) for far in (3, 2, 1)] + [last], before)
-        far = [kv_hop(near, 2 * middle) for middle in range(1, mid)]
+    def gather(block, own, before, after):
+        outer = {far: kv_hop(block, 2 * mid * far) for far in (3, 2, 1)}
+        across = [
+            kv_hop(block, 2 * middle + 2 * mid * GATHER_DIRECT) for middle in range(1, mid)
+        ]
+        relay = pack([outer[far] for far in relayed(GATHER_DIRECT)] + [own], *before)
+        near = pack([relay, outer[GATHER_DIRECT], *across])
+        far = [kv_hop(relay, 2 * middle) for middle in range(1, mid)]
         if after:
-            far = [pack(far, after)]
+            far = [pack(far, *after)]
         line = [near] + far
         return line + [kv_hop(x, 1) for x in line]
 
-    pick, mask, own_top, held = call(
+    pick, spread_to, mask = call(
         functools.partial(prep_kernel, mid, own_rows),
         (
             shaped((rows, requests), bf16),
+            shaped((rows, requests), bf16),
             shaped((rows, slots), f32),
-            shaped((own_rows, LANES), f32),
-            shaped(queries.shape, bf16),
         ),
         [],
         "prep",
         slot_request.reshape(1, slots),
         slot_valid.reshape(1, slots),
-        queries,
-        new_keys,
-    )
-    ready = call(ready_kernel, shaped((8, LANES), f32), [], "ready", keys, values, spec=lambda at: ANY)
-    blocks = gather(queries, held, [pick], [ready])
-    half = requests // 2
-    keep, send = call(
+    )
+    held = call(hold_kernel, shaped(queries.shape, bf16), [], "hold", queries)
+    own_top = call(own_kernel, shaped((own_rows, LANES), f32), [], "own", held, new_keys)
+    ready = [
+        call(ready_kernel, shaped((8, LANES), f32), [], "ready", x, spec=lambda at: ANY)
+        for x in (keys, values)
+    ]
+    blocks = gather(queries, held, [ready[0]], [ready[1], pick, own_top])
+    size = OUTER * own_rows
+    outs = call(
         functools.partial(attend_kernel, len(blocks)),
-        (shaped((half, wide), bf16),) * 2,
+        (shaped((size, wide), bf16),) * (2 * mid),
         [],
         "attend",
         pick,
+        spread_to,
         mask,
         keys,
         values,
         *blocks,
     )
 
-    def merged(ins, count):
-        size = ins[0].shape[0] // count
+    def merged(ins, *heights):
         return call(
             functools.partial(merge_kernel, len(ins)),
-            (shaped((size, wide), bf16),) * count,
+            tuple(shaped((height * own_rows, wide), bf16) for height in heights),
             [],
             "merge",
             *ins,
         )
 
-    blocks = merged([keep, kv_hop(send, 1)], 2 * mid)
-    outer = []
-    for at in (0, 1):
-        there = [kv_hop(blocks[2 * near + at], 2 * near) for near in range(1, mid)]
-        outer += merged([blocks[at]] + there, 2)
-    ins = [outer[3]] + [kv_hop(outer[OUTER - 1 - far], 2 * mid * far) for far in (3, 2, 1)]
+    relays, ins = [], []
+    for middle in range(1, mid):
+        relay, straight = merged([outs[middle], kv_hop(outs[mid + middle], 1)], 3, 1)
+        relays.append(kv_hop(relay, 2 * middle))
+        ins.append(kv_hop(straight, 2 * middle + 2 * mid * REDUCE_DIRECT))
+    *pair, own, straight = merged([outs[0], kv_hop(outs[mid], 1)], 2, 1, 1)
+    pair = merged(pair + relays, 1, 1)
+    ins += [own, *relays, kv_hop(straight, 2 * mid * REDUCE_DIRECT)]
+    ins += [kv_hop(x, 2 * mid * far) for x, far in zip(pair, relayed(REDUCE_DIRECT))]
     attended = call(
         functools.partial(last_kernel, len(ins)),
         shaped((own_rows, width), bf16),

time: 59.6 us -> 57 us (0.956)
  starting transfers between devices: 20.8 us -> 25 us
  local copies, waits for them, and re-layouts: 6.58 us -> 2.71 us
  waiting for transfers between devices: 26.1 us -> 23.2 us
    ppermute x19 -> x22, starting transfers between devices: 20.8 us -> 25 us  [hop(): return lax.ppermute(x, axis, [(i, i ^ distance) for i in range(count)])]
    ppermute x19 -> x22, waiting for transfers between devices: 26.1 us -> 23.2 us  [hop(): return lax.ppermute(x, axis, [(i, i ^ distance) for i in range(count)])]
    unnamed x18 -> x22, local copies, waits for them, and re-layouts: 5.21 us -> 2.7 us
    reshape x1, local copies, waits for them, and re-layouts: 0.68 us -> 0.01 us  [on_device(): slot_request.reshape(1, slots)]
    reshape x1, local copies, waits for them, and re-layouts: 0.68 us -> 0.01 us  [on_device(): slot_valid.reshape(1, slots)]
    pallas_call x13 -> x18, Pallas kernels: 5.72 us -> 5.69 us  [call(): pl.pallas_call(kernel, out_shape=shapes, in_specs=[spec(at) for at in ran...]
  transfers between devices with their start and end apart: 19 -> 22, of which waited for: 13 -> 14; matrix products, arithmetic and copies ran while one was open for 2% -> 0% of each run, Pallas kernels for 1% -> 3%
where the time goes in v4:
time: 57 us; the launch traced here: 56.8 us
  starting transfers between devices  25 us (44%)
  waiting for transfers between devices  23.2 us (41%)
  Pallas kernels  5.69 us (10%)
  local copies, waits for them, and re-layouts  2.71 us (5%)
    ppermute x22, starting transfers between devices, hop(): return lax.ppermute(x, axis, [(i, i ^ distance) for i in range(count)])  25 us
    ppermute x22, waiting for transfers between devices, hop(): return lax.ppermute(x, axis, [(i, i ^ distance) for i in range(count)])  23.2 us
    pallas_call x18, Pallas kernels, call(): pl.pallas_call(kernel, out_shape=shapes, in_specs=[spec(at) for at in ran...  5.69 us
    unnamed x22, local copies, waits for them, and re-layouts  2.7 us
  transfers between devices with their start and end apart: 22, of which 14 were waited for; matrix products, arithmetic and copies ran while one was open for 0% of the time, Pallas kernels for 3%

profile of v4, /device:TPU:0, one launch (start us, length us, event | category | flops | bytes accessed | tf_op | source)
XLA Modules:
  0.0 56.8 jit_solution(16282540082244021174)
XLA Ops:
  0.0 5.0 %collective-permute-start = (bf16[8,3584]{1,0:T(8,128)(2,1)}, bf16[8,3584]{1,0:T(8,128)(2,1)S(1)}, u32[]{:S(2)}, u32[]{:S(2)}) collective-permute-start(bf16[8,3584]{1,0:T(8,128)(2,1)} %queries.1), channel_id=1, source_target_pairs={{0,24},{2,26},{4,28},{6,30},{8,16},{10,18},{12,20},{14,22},{16,8},... | collective-permute-start | bytes 172040 | tf_op jit(solution)/shard_map/ppermute | solution.py:266
  5.0 0.0 collective-permute-start.1
  5.1 0.6 collective-permute-start.2
  5.6 2.4 %collective-permute-start.3 = (bf16[8,3584]{1,0:T(8,128)(2,1)}, bf16[8,3584]{1,0:T(8,128)(2,1)S(1)}, u32[]{:S(2)}, u32[]{:S(2)}) collective-permute-start(bf16[8,3584]{1,0:T(8,128)(2,1)} %queries.1), channel_id=1, source_target_pairs={{0,12},{2,14},{4,8},{6,10},{8,4},{10,6},{12,0},{14,2},{16,28},{18,... | collective-permute-start | bytes 172040 | tf_op jit(solution)/shard_map/ppermute | solution.py:266
  8.0 0.9 %copy-done.6 = bf16[8,3584]{1,0:T(8,128)(2,1)S(1)} copy-done((bf16[8,3584]{1,0:T(8,128)(2,1)S(1)}, bf16[8,3584]{1,0:T(8,128)(2,1)}, u32[]{:S(2)}) %copy-start.6) | copy-done | bytes 57368
  8.9 0.0 copy-start
  8.9 1.8 %copy-done = bf16[384,3584]{1,0:T(8,128)(2,1)S(1)} copy-done((bf16[384,3584]{1,0:T(8,128)(2,1)S(1)}, bf16[384,3584]{1,0:T(8,128)(2,1)}, u32[]{:S(2)}) %copy-start) | copy-done | bytes 2752536
  10.7 0.0 collective-permute-done.1.refs_1_
  10.7 1.2 %collective-permute-start.4 = (bf16[24,3584]{1,0:T(8,128)(2,1)S(1)}, bf16[24,3584]{1,0:T(8,128)(2,1)S(1)}, u32[]{:S(2)}, u32[]{:S(2)}) collective-permute-start(bf16[24,3584]{1,0:T(8,128)(2,1)S(1)} %pack.5.refs_0_), channel_id=1, source_target_pairs={{0,4},{2,6},{4,0},{6,2},{8,12},{10,14},{12,8},{14,10},{16,20},{18,... | collective-permute-start | bytes 516104 | tf_op jit(solution)/shard_map/ppermute | solution.py:266
  11.9 0.0 collective-permute-done.2.refs_1_
  11.9 0.4 collective-permute-done.3.refs_2_
  12.3 0.1 collective-permute-start.5
  12.5 0.1 own.1.refs_3_.refs_7_
  12.6 0.1 prep.1
  12.7 3.5 %collective-permute-done.4.refs_0_ = bf16[24,3584]{1,0:T(8,128)(2,1)S(1)} collective-permute-done((bf16[24,3584]{1,0:T(8,128)(2,1)S(1)}, bf16[24,3584]{1,0:T(8,128)(2,1)S(1)}, u32[]{:S(2)}, u32[]{:S(2)}) %collective-permute-start.4) | collective-permute-done | bytes 172064 | tf_op jit(solution)/shard_map/ppermute | solution.py:266
  16.2 0.1 collective-permute-start.6
  16.3 1.4 %collective-permute-done.6.refs_3_ = bf16[24,3584]{1,0:T(8,128)(2,1)S(1)} collective-permute-done((bf16[24,3584]{1,0:T(8,128)(2,1)S(1)}, bf16[24,3584]{1,0:T(8,128)(2,1)S(1)}, u32[]{:S(2)}, u32[]{:S(2)}) %collective-permute-start.6) | collective-permute-done | bytes 172064 | tf_op jit(solution)/shard_map/ppermute | solution.py:266
  17.7 2.0 %attend.1 = (bf16[32,3712]{1,0:T(8,128)(2,1)S(1)}, bf16[32,3712]{1,0:T(8,128)(2,1)S(1)}, bf16[32,3712]{1,0:T(8,128)(2,1)S(1)}, bf16[32,3712]{1,0:T(8,128)(2,1)S(1)}) custom-call(bf16[32,128]{1,0:T(8,128)(2,1)S(1)} %get-tuple-element.21.refs_2_.pick, bf16[32,128]{1,0:T(8,128)(2,1)S(1)} %get-tuple-element.22.spread_to, f32[32,384]{1,0:T(8,128)S(1)} %get-tuple-element.23.mask, ...), custom_call_target="tpu_custom_call" | custom-call | tf_op jit(solution)/shard_map/attend/pallas_call | solution.py:294
  19.7 0.2 collective-permute-start.7
  19.9 0.4 collective-permute-start.9
  20.3 1.0 %collective-permute-done.7.refs_1_ = bf16[32,3712]{1,0:T(8,128)(2,1)S(1)} collective-permute-done((bf16[32,3712]{1,0:T(8,128)(2,1)S(1)}, bf16[32,3712]{1,0:T(8,128)(2,1)S(1)}, u32[]{:S(2)}, u32[]{:S(2)}) %collective-permute-start.7) | collective-permute-done | bytes 237600 | tf_op jit(solution)/shard_map/ppermute | solution.py:266
  21.3 0.5 merge.3
  21.7 1.3 %collective-permute-start.10 = (bf16[24,3712]{1,0:T(8,128)(2,1)S(1)}, bf16[24,3712]{1,0:T(8,128)(2,1)S(1)}, u32[]{:S(2)}, u32[]{:S(2)}) collective-permute-start(bf16[24,3712]{1,0:T(8,128)(2,1)S(1)} %get-tuple-element.30), channel_id=1, source_target_pairs={{0,4},{2,6},{4,0},{6,2},{8,12},{10,14},{12,8},{14,10},{16,20},{18,... | collective-permute-start | bytes 534536 | tf_op jit(solution)/shard_map/ppermute | solution.py:266
  23.0 0.4 merge.4
  23.4 2.5 %collective-permute-start.11 = (bf16[8,3712]{1,0:T(8,128)(2,1)S(1)}, bf16[8,3712]{1,0:T(8,128)(2,1)S(1)}, u32[]{:S(2)}, u32[]{:S(2)}) collective-permute-start(bf16[8,3712]{1,0:T(8,128)(2,1)S(1)} %get-tuple-element.31), channel_id=1, source_target_pairs={{0,24},{2,26},{4,28},{6,30},{8,16},{10,18},{12,20},{14,22},{16,8},... | collective-permute-start | bytes 178184 | tf_op jit(solution)/shard_map/ppermute | solution.py:266
  25.9 1.7 %collective-permute-start.8 = (bf16[8,3712]{1,0:T(8,128)(2,1)S(1)}, bf16[8,3712]{1,0:T(8,128)(2,1)S(1)}, u32[]{:S(2)}, u32[]{:S(2)}) collective-permute-start(bf16[8,3712]{1,0:T(8,128)(2,1)S(1)} %get-tuple-element.26), channel_id=1, source_target_pairs={{0,28},{2,30},{4,24},{6,26},{8,20},{10,22},{12,16},{14,18},{16,12}... | collective-permute-start | bytes 178184 | tf_op jit(solution)/shard_map/ppermute | solution.py:266
  27.6 0.7 %collective-permute-done.10.refs_1_.refs_2_ = bf16[24,3712]{1,0:T(8,128)(2,1)S(1)} collective-permute-done((bf16[24,3712]{1,0:T(8,128)(2,1)S(1)}, bf16[24,3712]{1,0:T(8,128)(2,1)S(1)}, u32[]{:S(2)}, u32[]{:S(2)}) %collective-permute-start.10) | collective-permute-done | bytes 178208 | tf_op jit(solution)/shard_map/ppermute | solution.py:266
  28.3 0.3 merge.5
  28.7 3.0 %collective-permute-start.12 = (bf16[8,3712]{1,0:T(8,128)(2,1)S(1)}, bf16[8,3712]{1,0:T(8,128)(2,1)S(1)}, u32[]{:S(2)}, u32[]{:S(2)}) collective-permute-start(bf16[8,3712]{1,0:T(8,128)(2,1)S(1)} %get-tuple-element.33), channel_id=1, source_target_pairs={{0,16},{2,18},{4,20},{6,22},{8,24},{10,26},{12,28},{14,30},{16,0},... | collective-permute-start | bytes 178184 | tf_op jit(solution)/shard_map/ppermute | solution.py:266
  31.7 1.7 %collective-permute-done.8.refs_0_ = bf16[8,3712]{1,0:T(8,128)(2,1)S(1)} collective-permute-done((bf16[8,3712]{1,0:T(8,128)(2,1)S(1)}, bf16[8,3712]{1,0:T(8,128)(2,1)S(1)}, u32[]{:S(2)}, u32[]{:S(2)}) %collective-permute-start.8) | collective-permute-done | bytes 59424 | tf_op jit(solution)/shard_map/ppermute | solution.py:266
  33.4 1.3 %collective-permute-done.12.refs_4_ = bf16[8,3712]{1,0:T(8,128)(2,1)S(1)} collective-permute-done((bf16[8,3712]{1,0:T(8,128)(2,1)S(1)}, bf16[8,3712]{1,0:T(8,128)(2,1)S(1)}, u32[]{:S(2)}, u32[]{:S(2)}) %collective-permute-start.12) | collective-permute-done | bytes 59424 | tf_op jit(solution)/shard_map/ppermute | solution.py:266
  34.7 1.2 %collective-permute-done.13.refs_5_ = bf16[8,3712]{1,0:T(8,128)(2,1)S(1)} collective-permute-done((bf16[8,3712]{1,0:T(8,128)(2,1)S(1)}, bf16[8,3712]{1,0:T(8,128)(2,1)S(1)}, u32[]{:S(2)}, u32[]{:S(2)}) %collective-permute-start.13) | collective-permute-done | bytes 59424 | tf_op jit(solution)/shard_map/ppermute | solution.py:266
  35.9 0.4 last.1.refs_2_
  36.3 1.1 %collective-permute-start.14 = (bf16[8,3584]{1,0:T(8,128)(2,1)S(1)}, bf16[8,3584]{1,0:T(8,128)(2,1)S(1)}, u32[]{:S(2)}, u32[]{:S(2)}) collective-permute-start(bf16[8,3584]{1,0:T(8,128)(2,1)S(1)} %last.1.refs_2_), channel_id=1, source_target_pairs={{0,24},{2,26},{4,28},{6,30},{8,16},{10,18},{12,20},{14,22},{16,8},... | collective-permute-start | bytes 172040 | tf_op jit(solution)/shard_map/ppermute | solution.py:266
  37.5 1.0 %collective-permute-start.15 = (bf16[8,3584]{1,0:T(8,128)(2,1)S(1)}, bf16[8,3584]{1,0:T(8,128)(2,1)S(1)}, u32[]{:S(2)}, u32[]{:S(2)}) collective-permute-start(bf16[8,3584]{1,0:T(8,128)(2,1)S(1)} %last.1.refs_2_), channel_id=1, source_target_pairs={{0,16},{2,18},{4,20},{6,22},{8,24},{10,26},{12,28},{14,30},{16,0},... | collective-permute-start | bytes 172040 | tf_op jit(solution)/shard_map/ppermute | solution.py:266
  38.5 2.3 %collective-permute-start.16 = (bf16[8,3584]{1,0:T(8,128)(2,1)S(1)}, bf16[8,3584]{1,0:T(8,128)(2,1)S(1)}, u32[]{:S(2)}, u32[]{:S(2)}) collective-permute-start(bf16[8,3584]{1,0:T(8,128)(2,1)S(1)} %last.1.refs_2_), channel_id=1, source_target_pairs={{0,8},{2,10},{4,12},{6,14},{8,0},{10,2},{12,4},{14,6},{16,24},{18,... | collective-permute-start | bytes 172040 | tf_op jit(solution)/shard_map/ppermute | solution.py:266
  40.8 0.2 collective-permute-start.17
  41.0 2.0 %collective-permute-done.14.refs_0_ = bf16[8,3584]{1,0:T(8,128)(2,1)S(1)} collective-permute-done((bf16[8,3584]{1,0:T(8,128)(2,1)S(1)}, bf16[8,3584]{1,0:T(8,128)(2,1)S(1)}, u32[]{:S(2)}, u32[]{:S(2)}) %collective-permute-start.14) | collective-permute-done | bytes 57376 | tf_op jit(solution)/shard_map/ppermute | solution.py:266
  43.0 0.8 %collective-permute-done.15.refs_1_ = bf16[8,3584]{1,0:T(8,128)(2,1)S(1)} collective-permute-done((bf16[8,3584]{1,0:T(8,128)(2,1)S(1)}, bf16[8,3584]{1,0:T(8,128)(2,1)S(1)}, u32[]{:S(2)}, u32[]{:S(2)}) %collective-permute-start.15) | collective-permute-done | bytes 57376 | tf_op jit(solution)/shard_map/ppermute | solution.py:266
  43.8 0.4 collective-permute-start.18
  44.2 1.7 %collective-permute-done.17.refs_2_ = bf16[8,3584]{1,0:T(8,128)(2,1)S(1)} collective-permute-done((bf16[8,3584]{1,0:T(8,128)(2,1)S(1)}, bf16[8,3584]{1,0:T(8,128)(2,1)S(1)}, u32[]{:S(2)}, u32[]{:S(2)}) %collective-permute-start.17) | collective-permute-done | bytes 57376 | tf_op jit(solution)/shard_map/ppermute | solution.py:266
  46.0 0.1 collective-permute-start.19
  46.1 3.3 %collective-permute-done.18.refs_1_ = bf16[24,3584]{1,0:T(8,128)(2,1)S(1)} collective-permute-done((bf16[24,3584]{1,0:T(8,128)(2,1)S(1)}, bf16[24,3584]{1,0:T(8,128)(2,1)S(1)}, u32[]{:S(2)}, u32[]{:S(2)}) %collective-permute-start.18) | collective-permute-done | bytes 172064 | tf_op jit(solution)/shard_map/ppermute | solution.py:266
  49.3 1.4 %collective-permute-done.20.refs_3_ = bf16[24,3584]{1,0:T(8,128)(2,1)S(1)} collective-permute-done((bf16[24,3584]{1,0:T(8,128)(2,1)S(1)}, bf16[24,3584]{1,0:T(8,128)(2,1)S(1)}, u32[]{:S(2)}, u32[]{:S(2)}) %collective-permute-start.20) | collective-permute-done | bytes 172064 | tf_op jit(solution)/shard_map/ppermute | solution.py:266
  50.7 1.1 %project.1 = (f32[64,448]{1,0:T(8,128)S(1)}, bf16[64,448]{1,0:T(8,128)(2,1)S(1)}) custom-call(bf16[40,3584]{1,0:T(8,128)(2,1)S(1)} %pack.9.refs_0_, bf16[24,3584]{1,0:T(8,128)(2,1)S(1)} %collective-permute-done.18.refs_1_, bf16[40,3584]{1,0:T(8,128)(2,1)S(1)} %collective-permute-done.19.refs_2_, bf16[24,3584]{1,0:T(8,128)(2,1)S(1)} %collective-permute-done.20.refs_3_, ...), custom_call_target="tpu_custom_call" | custom-call | tf_op jit(solution)/shard_map/project/pallas_call | solution.py:294
  51.8 1.6 %collective-permute-start.21 = (bf16[64,448]{1,0:T(8,128)(2,1)S(1)}, bf16[64,448]{1,0:T(8,128)(2,1)S(1)}, u32[]{:S(2)}, u32[]{:S(2)}) collective-permute-start(bf16[64,448]{1,0:T(8,128)(2,1)S(1)} %get-tuple-element.36), channel_id=1, source_target_pairs={{0,1},{1,0},{2,3},{3,2},{4,5},{5,4},{6,7},{7,6},{8,9},{9,8},{10,11... | collective-permute-start | bytes 172040 | tf_op jit(solution)/shard_map/ppermute | solution.py:266
  53.4 2.7 %collective-permute-done.21.refs_0_ = bf16[64,448]{1,0:T(8,128)(2,1)S(1)} collective-permute-done((bf16[64,448]{1,0:T(8,128)(2,1)S(1)}, bf16[64,448]{1,0:T(8,128)(2,1)S(1)}, u32[]{:S(2)}, u32[]{:S(2)}) %collective-permute-start.21) | collective-permute-done | bytes 57376 | tf_op jit(solution)/shard_map/ppermute | solution.py:266
  56.2 0.6 %final.1 = bf16[64,448]{1,0:T(8,128)(2,1)} custom-call(f32[64,448]{1,0:T(8,128)S(1)} %base.1.total, bf16[64,448]{1,0:T(8,128)(2,1)S(1)} %collective-permute-done.21.refs_0_), custom_call_target="tpu_custom_call" | custom-call | tf_op jit(solution)/shard_map/final/pallas_call | solution.py:294
  (39 shorter events, 0.2 us)
Async XLA Ops:
  0.0 10.7 %collective-permute-start = (bf16[8,3584]{1,0:T(8,128)(2,1)}, bf16[8,3584]{1,0:T(8,128)(2,1)S(1)}, u32[]{:S(2)}, u32[]{:S(2)}) collective-permute-start(bf16[8,3584]{1,0:T(8,128)(2,1)} %queries.1), channel_id=1, source_target_pairs={{0,24},{2,26},{4,28},{6,30},{8,16},{10,18},{12,20},{14,22},{16,8},... | collective-permute-start | bytes 172040 | tf_op jit(solution)/shard_map/ppermute | solution.py:266
  5.0 5.7 %collective-permute-start.1 = (bf16[8,3584]{1,0:T(8,128)(2,1)}, bf16[8,3584]{1,0:T(8,128)(2,1)S(1)}, u32[]{:S(2)}, u32[]{:S(2)}) collective-permute-start(bf16[8,3584]{1,0:T(8,128)(2,1)} %queries.1), channel_id=1, source_target_pairs={{0,16},{2,18},{4,20},{6,22},{8,24},{10,26},{12,28},{14,30},{16,0},... | collective-permute-start | bytes 172040 | tf_op jit(solution)/shard_map/ppermute | solution.py:266
  5.1 6.9 %collective-permute-start.2 = (bf16[8,3584]{1,0:T(8,128)(2,1)}, bf16[8,3584]{1,0:T(8,128)(2,1)S(1)}, u32[]{:S(2)}, u32[]{:S(2)}) collective-permute-start(bf16[8,3584]{1,0:T(8,128)(2,1)} %queries.1), channel_id=1, source_target_pairs={{0,8},{2,10},{4,12},{6,14},{8,0},{10,2},{12,4},{14,6},{16,24},{18,... | collective-permute-start | bytes 172040 | tf_op jit(solution)/shard_map/ppermute | solution.py:266
  5.6 6.7 %collective-permute-start.3 = (bf16[8,3584]{1,0:T(8,128)(2,1)}, bf16[8,3584]{1,0:T(8,128)(2,1)S(1)}, u32[]{:S(2)}, u32[]{:S(2)}) collective-permute-start(bf16[8,3584]{1,0:T(8,128)(2,1)} %queries.1), channel_id=1, source_target_pairs={{0,12},{2,14},{4,8},{6,10},{8,4},{10,6},{12,0},{14,2},{16,28},{18,... | collective-permute-start | bytes 172040 | tf_op jit(solution)/shard_map/ppermute | solution.py:266
  8.0 0.9 %copy-start.6 = (bf16[8,3584]{1,0:T(8,128)(2,1)S(1)}, bf16[8,3584]{1,0:T(8,128)(2,1)}, u32[]{:S(2)}) copy-start(bf16[8,3584]{1,0:T(8,128)(2,1)} %queries.1) | copy-start | bytes 172036
  8.9 3.6 %copy-start.8 = (s32[384]{0:T(512)S(1)}, s32[384]{0:T(512)}, u32[]{:S(2)}) copy-start(s32[384]{0:T(512)} %param.16) | copy-start | bytes 4612
  8.9 3.6 %copy-start.9 = (s32[384]{0:T(512)S(1)}, s32[384]{0:T(512)}, u32[]{:S(2)}) copy-start(s32[384]{0:T(512)} %param.15) | copy-start | bytes 4612
  8.9 3.6 %copy-start.7 = (bf16[8,3584]{1,0:T(8,128)(2,1)S(1)}, bf16[8,3584]{1,0:T(8,128)(2,1)}, u32[]{:S(2)}) copy-start(bf16[8,3584]{1,0:T(8,128)(2,1)} %new_keys.1) | copy-start | bytes 172036
  8.9 1.8 %copy-start = (bf16[384,3584]{1,0:T(8,128)(2,1)S(1)}, bf16[384,3584]{1,0:T(8,128)(2,1)}, u32[]{:S(2)}) copy-start(bf16[384,3584]{1,0:T(8,128)(2,1)} %keys.1) | copy-start | bytes 8257540
  10.7 1.9 %copy-start.2 = (bf16[384,3584]{1,0:T(8,128)(2,1)S(1)}, bf16[384,3584]{1,0:T(8,128)(2,1)}, u32[]{:S(2)}) copy-start(bf16[384,3584]{1,0:T(8,128)(2,1)} %values.1) | copy-start | bytes 8257540
  10.7 7.0 %copy-start.1 = (bf16[384,3584]{1,0:T(8,128)(2,1)S(1)}, bf16[384,3584]{1,0:T(8,128)(2,1)}, u32[]{:S(2)}) copy-start(bf16[384,3584]{1,0:T(8,128)(2,1)} %keys.1) | copy-start | bytes 8257540
  10.7 5.5 %collective-permute-start.4 = (bf16[24,3584]{1,0:T(8,128)(2,1)S(1)}, bf16[24,3584]{1,0:T(8,128)(2,1)S(1)}, u32[]{:S(2)}, u32[]{:S(2)}) collective-permute-start(bf16[24,3584]{1,0:T(8,128)(2,1)S(1)} %pack.5.refs_0_), channel_id=1, source_target_pairs={{0,4},{2,6},{4,0},{6,2},{8,12},{10,14},{12,8},{14,10},{16,20},{18,... | collective-permute-start | bytes 516104 | tf_op jit(solution)/shard_map/ppermute | solution.py:266
  12.3 4.0 %collective-permute-start.5 = (bf16[40,3584]{1,0:T(8,128)(2,1)S(1)}, bf16[40,3584]{1,0:T(8,128)(2,1)S(1)}, u32[]{:S(2)}, u32[]{:S(2)}) collective-permute-start(bf16[40,3584]{1,0:T(8,128)(2,1)S(1)} %pack.6.refs_0_), channel_id=1, source_target_pairs={{0,2},{2,0},{4,6},{6,4},{8,10},{10,8},{12,14},{14,12},{16,18},{18,... | collective-permute-start | bytes 860168 | tf_op jit(solution)/shard_map/ppermute | solution.py:266
  16.2 1.5 %collective-permute-start.6 = (bf16[24,3584]{1,0:T(8,128)(2,1)S(1)}, bf16[24,3584]{1,0:T(8,128)(2,1)S(1)}, u32[]{:S(2)}, u32[]{:S(2)}) collective-permute-start(bf16[24,3584]{1,0:T(8,128)(2,1)S(1)} %pack.7.refs_1_), channel_id=1, source_target_pairs={{0,2},{2,0},{4,6},{6,4},{8,10},{10,8},{12,14},{14,12},{16,18},{18,... | collective-permute-start | bytes 516104 | tf_op jit(solution)/shard_map/ppermute | solution.py:266
  17.7 18.2 %copy-start.5 = (bf16[8,3584]{1,0:T(8,128)(2,1)S(1)}, bf16[8,3584]{1,0:T(8,128)(2,1)}, u32[]{:S(2)}) copy-start(bf16[8,3584]{1,0:T(8,128)(2,1)} %refs_6_.1) | copy-start | bytes 172036
  17.7 33.0 %copy-start.3 = (bf16[3584,448]{0,1:T(8,128)(2,1)S(1)}, bf16[3584,448]{0,1:T(8,128)(2,1)}, u32[]{:S(2)}) copy-start(bf16[3584,448]{0,1:T(8,128)(2,1)} %param.17) | copy-start | bytes 9633796
  19.7 1.6 %collective-permute-start.7 = (bf16[32,3712]{1,0:T(8,128)(2,1)S(1)}, bf16[32,3712]{1,0:T(8,128)(2,1)S(1)}, u32[]{:S(2)}, u32[]{:S(2)}) collective-permute-start(bf16[32,3712]{1,0:T(8,128)(2,1)S(1)} %get-tuple-element.25), channel_id=1, source_target_pairs={{0,2},{2,0},{4,6},{6,4},{8,10},{10,8},{12,14},{14,12},{16,18},{18,... | collective-permute-start | bytes 712712 | tf_op jit(solution)/shard_map/ppermute | solution.py:266
  19.9 3.1 %collective-permute-start.9 = (bf16[32,3712]{1,0:T(8,128)(2,1)S(1)}, bf16[32,3712]{1,0:T(8,128)(2,1)S(1)}, u32[]{:S(2)}, u32[]{:S(2)}) collective-permute-start(bf16[32,3712]{1,0:T(8,128)(2,1)S(1)} %get-tuple-element.28), channel_id=1, source_target_pairs={{0,2},{2,0},{4,6},{6,4},{8,10},{10,8},{12,14},{14,12},{16,18},{18,... | collective-permute-start | bytes 712712 | tf_op jit(solution)/shard_map/ppermute | solution.py:266
  21.7 6.6 %collective-permute-start.10 = (bf16[24,3712]{1,0:T(8,128)(2,1)S(1)}, bf16[24,3712]{1,0:T(8,128)(2,1)S(1)}, u32[]{:S(2)}, u32[]{:S(2)}) collective-permute-start(bf16[24,3712]{1,0:T(8,128)(2,1)S(1)} %get-tuple-element.30), channel_id=1, source_target_pairs={{0,4},{2,6},{4,0},{6,2},{8,12},{10,14},{12,8},{14,10},{16,20},{18,... | collective-permute-start | bytes 534536 | tf_op jit(solution)/shard_map/ppermute | solution.py:266
  23.4 8.3 %collective-permute-start.11 = (bf16[8,3712]{1,0:T(8,128)(2,1)S(1)}, bf16[8,3712]{1,0:T(8,128)(2,1)S(1)}, u32[]{:S(2)}, u32[]{:S(2)}) collective-permute-start(bf16[8,3712]{1,0:T(8,128)(2,1)S(1)} %get-tuple-element.31), channel_id=1, source_target_pairs={{0,24},{2,26},{4,28},{6,30},{8,16},{10,18},{12,20},{14,22},{16,8},... | collective-permute-start | bytes 178184 | tf_op jit(solution)/shard_map/ppermute | solution.py:266
  25.9 7.5 %collective-permute-start.8 = (bf16[8,3712]{1,0:T(8,128)(2,1)S(1)}, bf16[8,3712]{1,0:T(8,128)(2,1)S(1)}, u32[]{:S(2)}, u32[]{:S(2)}) collective-permute-start(bf16[8,3712]{1,0:T(8,128)(2,1)S(1)} %get-tuple-element.26), channel_id=1, source_target_pairs={{0,28},{2,30},{4,24},{6,26},{8,20},{10,22},{12,16},{14,18},{16,12}... | collective-permute-start | bytes 178184 | tf_op jit(solution)/shard_map/ppermute | solution.py:266
  28.7 6.1 %collective-permute-start.12 = (bf16[8,3712]{1,0:T(8,128)(2,1)S(1)}, bf16[8,3712]{1,0:T(8,128)(2,1)S(1)}, u32[]{:S(2)}, u32[]{:S(2)}) collective-permute-start(bf16[8,3712]{1,0:T(8,128)(2,1)S(1)} %get-tuple-element.33), channel_id=1, source_target_pairs={{0,16},{2,18},{4,20},{6,22},{8,24},{10,26},{12,28},{14,30},{16,0},... | collective-permute-start | bytes 178184 | tf_op jit(solution)/shard_map/ppermute | solution.py:266
  31.7 4.2 %collective-permute-start.13 = (bf16[8,3712]{1,0:T(8,128)(2,1)S(1)}, bf16[8,3712]{1,0:T(8,128)(2,1)S(1)}, u32[]{:S(2)}, u32[]{:S(2)}) collective-permute-start(bf16[8,3712]{1,0:T(8,128)(2,1)S(1)} %get-tuple-element.34), channel_id=1, source_target_pairs={{0,8},{2,10},{4,12},{6,14},{8,0},{10,2},{12,4},{14,6},{16,24},{18,... | collective-permute-start | bytes 178184 | tf_op jit(solution)/shard_map/ppermute | solution.py:266
  35.9 17.5 %copy-start.10 = (bf16[448]{0:T(512)(128)(2,1)S(1)}, bf16[448]{0:T(512)(128)(2,1)}, u32[]{:S(2)}) copy-start(bf16[448]{0:T(512)(128)(2,1)} %param.18) | copy-start | bytes 2692
  35.9 17.5 %copy-start.4 = (bf16[64,448]{1,0:T(8,128)(2,1)S(1)}, bf16[64,448]{1,0:T(8,128)(2,1)}, u32[]{:S(2)}) copy-start(bf16[64,448]{1,0:T(8,128)(2,1)} %residual.1) | copy-start | bytes 172036
  36.3 6.7 %collective-permute-start.14 = (bf16[8,3584]{1,0:T(8,128)(2,1)S(1)}, bf16[8,3584]{1,0:T(8,128)(2,1)S(1)}, u32[]{:S(2)}, u32[]{:S(2)}) collective-permute-start(bf16[8,3584]{1,0:T(8,128)(2,1)S(1)} %last.1.refs_2_), channel_id=1, source_target_pairs={{0,24},{2,26},{4,28},{6,30},{8,16},{10,18},{12,20},{14,22},{16,8},... | collective-permute-start | bytes 172040 | tf_op jit(solution)/shard_map/ppermute | solution.py:266
  37.5 6.4 %collective-permute-start.15 = (bf16[8,3584]{1,0:T(8,128)(2,1)S(1)}, bf16[8,3584]{1,0:T(8,128)(2,1)S(1)}, u32[]{:S(2)}, u32[]{:S(2)}) collective-permute-start(bf16[8,3584]{1,0:T(8,128)(2,1)S(1)} %last.1.refs_2_), channel_id=1, source_target_pairs={{0,16},{2,18},{4,20},{6,22},{8,24},{10,26},{12,28},{14,30},{16,0},... | collective-permute-start | bytes 172040 | tf_op jit(solution)/shard_map/ppermute | solution.py:266
  38.5 5.7 %collective-permute-start.16 = (bf16[8,3584]{1,0:T(8,128)(2,1)S(1)}, bf16[8,3584]{1,0:T(8,128)(2,1)S(1)}, u32[]{:S(2)}, u32[]{:S(2)}) collective-permute-start(bf16[8,3584]{1,0:T(8,128)(2,1)S(1)} %last.1.refs_2_), channel_id=1, source_target_pairs={{0,8},{2,10},{4,12},{6,14},{8,0},{10,2},{12,4},{14,6},{16,24},{18,... | collective-permute-start | bytes 172040 | tf_op jit(solution)/shard_map/ppermute | solution.py:266
  40.8 5.2 %collective-permute-start.17 = (bf16[8,3584]{1,0:T(8,128)(2,1)S(1)}, bf16[8,3584]{1,0:T(8,128)(2,1)S(1)}, u32[]{:S(2)}, u32[]{:S(2)}) collective-permute-start(bf16[8,3584]{1,0:T(8,128)(2,1)S(1)} %last.1.refs_2_), channel_id=1, source_target_pairs={{0,12},{2,14},{4,8},{6,10},{8,4},{10,6},{12,0},{14,2},{16,28},{18,... | collective-permute-start | bytes 172040 | tf_op jit(solution)/shard_map/ppermute | solution.py:266
  43.8 5.5 %collective-permute-start.18 = (bf16[24,3584]{1,0:T(8,128)(2,1)S(1)}, bf16[24,3584]{1,0:T(8,128)(2,1)S(1)}, u32[]{:S(2)}, u32[]{:S(2)}) collective-permute-start(bf16[24,3584]{1,0:T(8,128)(2,1)S(1)} %pack.8.refs_0_), channel_id=1, source_target_pairs={{0,4},{2,6},{4,0},{6,2},{8,12},{10,14},{12,8},{14,10},{16,20},{18,... | collective-permute-start | bytes 516104 | tf_op jit(solution)/shard_map/ppermute | solution.py:266
  46.0 3.3 %collective-permute-start.19 = (bf16[40,3584]{1,0:T(8,128)(2,1)S(1)}, bf16[40,3584]{1,0:T(8,128)(2,1)S(1)}, u32[]{:S(2)}, u32[]{:S(2)}) collective-permute-start(bf16[40,3584]{1,0:T(8,128)(2,1)S(1)} %pack.9.refs_0_), channel_id=1, source_target_pairs={{0,2},{2,0},{4,6},{6,4},{8,10},{10,8},{12,14},{14,12},{16,18},{18,... | collective-permute-start | bytes 860168 | tf_op jit(solution)/shard_map/ppermute | solution.py:266
  49.3 1.4 %collective-permute-start.20 = (bf16[24,3584]{1,0:T(8,128)(2,1)S(1)}, bf16[24,3584]{1,0:T(8,128)(2,1)S(1)}, u32[]{:S(2)}, u32[]{:S(2)}) collective-permute-start(bf16[24,3584]{1,0:T(8,128)(2,1)S(1)} %collective-permute-done.18.refs_1_), channel_id=1, source_target_pairs={{0,2},{2,0},{4,6},{6,4},{8,10},{10,8},{12,14},{14,12},{16,18},{18,... | collective-permute-start | bytes 516104 | tf_op jit(solution)/shard_map/ppermute | solution.py:266
  51.8 4.3 %collective-permute-start.21 = (bf16[64,448]{1,0:T(8,128)(2,1)S(1)}, bf16[64,448]{1,0:T(8,128)(2,1)S(1)}, u32[]{:S(2)}, u32[]{:S(2)}) collective-permute-start(bf16[64,448]{1,0:T(8,128)(2,1)S(1)} %get-tuple-element.36), channel_id=1, source_target_pairs={{0,1},{1,0},{2,3},{3,2},{4,5},{5,4},{6,7},{7,6},{8,9},{9,8},{10,11... | collective-permute-start | bytes 172040 | tf_op jit(solution)/shard_map/ppermute | solution.py:266

commit v5 on v4

--- a/solution.py
+++ b/solution.py
@@ -16,8 +16,9 @@
 
 floor_score = -1e30
 SENT = jnp.bfloat16
-GATHER_DIRECT = 1
-REDUCE_DIRECT = 3
+QUERY_ORDER = (3, 2, 1)
+REDUCE_ORDER = (2, 1, 3)
+RESULT_ORDER = (3, 2, 1)
 f32 = jnp.float32
 bf16 = jnp.bfloat16
 WHOLE = pl.BlockSpec(memory_space=pltpu.VMEM)
@@ -28,14 +29,14 @@
     return pltpu.CompilerParams(vmem_limit_bytes=megabytes * 1024 * 1024)
 
 
-def relayed(direct):
-    return [far for far in (3, 2, 1) if far != direct]
-
-
-def gather_order(mid, direct):
-    lines = [[(far, 0) for far in relayed(direct) + [0, direct]]]
-    lines[0] += [(direct, middle) for middle in range(1, mid)]
-    lines += [[(far, middle) for far in relayed(direct) + [0]] for middle in range(1, mid)]
+def relayed(order):
+    return list(order[:2])
+
+
+def gather_order(mid, order):
+    lines = [[(far, 0) for far in relayed(order) + [0, order[2]]]]
+    lines[0] += [(order[2], middle) for middle in range(1, mid)]
+    lines += [[(far, middle) for far in relayed(order) + [0]] for middle in range(1, mid)]
     return [
         core + 2 * middle + 2 * mid * far
         for core in (0, 1)
@@ -44,12 +45,12 @@
     ]
 
 
-def reduce_order(mid, direct):
+def reduce_order(mid, order):
     return [
         core + 2 * middle + 2 * mid * far
         for core in (0, 1)
         for middle in range(mid)
-        for far in relayed(direct) + [0, direct]
+        for far in relayed(order) + [0, order[2]]
     ]
 
 
@@ -72,7 +73,7 @@
     live = (owners == mine) & first & (jnp.broadcast_to(valid[...], (rows, slots)) == 1)
     mask[...] = jnp.where(live, 1.0, 0.0)
     place = lax.broadcasted_iota(jnp.int32, pick.shape, 1)
-    orders = (gather_order(mid, GATHER_DIRECT), reduce_order(mid, REDUCE_DIRECT))
+    orders = (gather_order(mid, QUERY_ORDER), reduce_order(mid, REDUCE_ORDER))
     for out, order in zip((pick, spread), orders):
         named = request_at(place, order, own_rows)
         out[...] = jnp.where((named == mine) & first, 1.0, 0.0).astype(bf16)
@@ -241,7 +242,7 @@
         (((1,), (1,)), ((), ())),
         preferred_element_type=f32,
     )
-    for at, distance in enumerate(gather_order(mid, GATHER_DIRECT)):
+    for at, distance in enumerate(gather_order(mid, RESULT_ORDER)):
         owner = lax.bitwise_xor(lax.axis_index("kv"), distance)
         start = pl.multiple_of(owner * own_rows, own_rows)
         acc[pl.ds(start, own_rows), :] = product[at * own_rows : (at + 1) * own_rows]
@@ -312,13 +313,13 @@
             spec=lambda at: WHOLE if at < len(parts) else ANY,
         )
 
-    def gather(block, own, before, after):
-        outer = {far: kv_hop(block, 2 * mid * far) for far in (3, 2, 1)}
+    def gather(block, own, order, before, after, beside):
+        outer = {far: kv_hop(block, 2 * mid * far) for far in order}
         across = [
-            kv_hop(block, 2 * middle + 2 * mid * GATHER_DIRECT) for middle in range(1, mid)
+            kv_hop(block, 2 * middle + 2 * mid * order[2]) for middle in range(1, mid)
         ]
-        relay = pack([outer[far] for far in relayed(GATHER_DIRECT)] + [own], *before)
-        near = pack([relay, outer[GATHER_DIRECT], *across])
+        relay = pack([outer[far] for far in relayed(order)] + [own], *before)
+        near = pack([relay, outer[order[2]], *across], *beside)
         far = [kv_hop(relay, 2 * middle) for middle in range(1, mid)]
         if after:
             far = [pack(far, *after)]
@@ -343,7 +344,7 @@
         call(ready_kernel, shaped((8, LANES), f32), [], "ready", x, spec=lambda at: ANY)
         for x in (keys, values)
     ]
-    blocks = gather(queries, held, [ready[0]], [ready[1], pick, own_top])
+    blocks = gather(queries, held, QUERY_ORDER, [own_top], [ready[0], pick], [ready[1]])
     size = OUTER * own_rows
     outs = call(
         functools.partial(attend_kernel, len(blocks)),
@@ -371,11 +372,11 @@
     for middle in range(1, mid):
         relay, straight = merged([outs[middle], kv_hop(outs[mid + middle], 1)], 3, 1)
         relays.append(kv_hop(relay, 2 * middle))
-        ins.append(kv_hop(straight, 2 * middle + 2 * mid * REDUCE_DIRECT))
+        ins.append(kv_hop(straight, 2 * middle + 2 * mid * REDUCE_ORDER[2]))
     *pair, own, straight = merged([outs[0], kv_hop(outs[mid], 1)], 2, 1, 1)
     pair = merged(pair + relays, 1, 1)
-    ins += [own, *relays, kv_hop(straight, 2 * mid * REDUCE_DIRECT)]
-    ins += [kv_hop(x, 2 * mid * far) for x, far in zip(pair, relayed(REDUCE_DIRECT))]
+    ins += [own, *relays, kv_hop(straight, 2 * mid * REDUCE_ORDER[2])]
+    ins += [kv_hop(x, 2 * mid * far) for x, far in zip(pair, relayed(REDUCE_ORDER))]
     attended = call(
         functools.partial(last_kernel, len(ins)),
         shaped((own_rows, width), bf16),
@@ -386,7 +387,7 @@
         own_top,
     )
 
-    blocks = gather(attended, attended, [], [])
+    blocks = gather(attended, attended, RESULT_ORDER, [], [], [])
     columns = out_weight.shape[1]
     shape = (requests // tp_count, columns)
     kept, *sent = call(

time: 57 us -> 55.9 us (0.981)
  waiting for transfers between devices: 23.2 us -> 17.3 us
  starting transfers between devices: 25 us -> 27.5 us
  local copies, waits for them, and re-layouts: 2.71 us -> 4.99 us
    ppermute x22, waiting for transfers between devices: 23.2 us -> 17.3 us  [hop(): return lax.ppermute(x, axis, [(i, i ^ distance) for i in range(count)])]
    ppermute x22, starting transfers between devices: 25 us -> 27.5 us  [hop(): return lax.ppermute(x, axis, [(i, i ^ distance) for i in range(count)])]
    reshape x1, local copies, waits for them, and re-layouts: 0.01 us -> 0.84 us  [on_device(): slot_valid.reshape(1, slots)]
    unnamed x22 -> x18, local copies, waits for them, and re-layouts: 2.7 us -> 3.47 us
    reshape x1, local copies, waits for them, and re-layouts: 0.01 us -> 0.68 us  [on_device(): slot_request.reshape(1, slots)]
  transfers between devices with their start and end apart: 22 -> 22, of which waited for: 14 -> 13; matrix products, arithmetic and copies ran while one was open for 0% -> 3% of each run, Pallas kernels for 3% -> 3%
where the time goes in v5:
time: 55.9 us; the launch traced here: 55.6 us
  starting transfers between devices  27.5 us (49%)
  waiting for transfers between devices  17.3 us (31%)
  Pallas kernels  5.67 us (10%)
  local copies, waits for them, and re-layouts  4.99 us (9%)
    ppermute x22, starting transfers between devices, hop(): return lax.ppermute(x, axis, [(i, i ^ distance) for i in range(count)])  27.5 us
    ppermute x22, waiting for transfers between devices, hop(): return lax.ppermute(x, axis, [(i, i ^ distance) for i in range(count)])  17.3 us
    pallas_call x18, Pallas kernels, call(): pl.pallas_call(kernel, out_shape=shapes, in_specs=[spec(at) for at in ran...  5.67 us
    unnamed x18, local copies, waits for them, and re-layouts  3.47 us
  transfers between devices with their start and end apart: 22, of which 13 were waited for; matrix products, arithmetic and copies ran while one was open for 3% of the time, Pallas kernels for 3%

profile of v5, /device:TPU:0, one launch (start us, length us, event | category | flops | bytes accessed | tf_op | source)
XLA Modules:
  0.0 55.6 jit_solution(16123475348334735360)
XLA Ops:
  0.0 5.0 %collective-permute-start = (bf16[8,3584]{1,0:T(8,128)(2,1)}, bf16[8,3584]{1,0:T(8,128)(2,1)S(1)}, u32[]{:S(2)}, u32[]{:S(2)}) collective-permute-start(bf16[8,3584]{1,0:T(8,128)(2,1)} %queries.1), channel_id=1, source_target_pairs={{0,24},{2,26},{4,28},{6,30},{8,16},{10,18},{12,20},{14,22},{16,8},... | collective-permute-start | bytes 172040 | tf_op jit(solution)/shard_map/ppermute | solution.py:267
  5.1 0.0 collective-permute-start.1
  5.1 0.6 %collective-permute-start.2 = (bf16[8,3584]{1,0:T(8,128)(2,1)}, bf16[8,3584]{1,0:T(8,128)(2,1)S(1)}, u32[]{:S(2)}, u32[]{:S(2)}) collective-permute-start(bf16[8,3584]{1,0:T(8,128)(2,1)} %queries.1), channel_id=1, source_target_pairs={{0,8},{2,10},{4,12},{6,14},{8,0},{10,2},{12,4},{14,6},{16,24},{18,... | collective-permute-start | bytes 172040 | tf_op jit(solution)/shard_map/ppermute | solution.py:267
  5.7 2.3 %collective-permute-start.3 = (bf16[8,3584]{1,0:T(8,128)(2,1)}, bf16[8,3584]{1,0:T(8,128)(2,1)S(1)}, u32[]{:S(2)}, u32[]{:S(2)}) collective-permute-start(bf16[8,3584]{1,0:T(8,128)(2,1)} %queries.1), channel_id=1, source_target_pairs={{0,12},{2,14},{4,8},{6,10},{8,4},{10,6},{12,0},{14,2},{16,28},{18,... | collective-permute-start | bytes 172040 | tf_op jit(solution)/shard_map/ppermute | solution.py:267
  8.0 0.9 %copy-done.6 = bf16[8,3584]{1,0:T(8,128)(2,1)S(1)} copy-done((bf16[8,3584]{1,0:T(8,128)(2,1)S(1)}, bf16[8,3584]{1,0:T(8,128)(2,1)}, u32[]{:S(2)}) %copy-start.6) | copy-done | bytes 57368
  8.9 0.8 %copy-done.7 = bf16[8,3584]{1,0:T(8,128)(2,1)S(1)} copy-done((bf16[8,3584]{1,0:T(8,128)(2,1)S(1)}, bf16[8,3584]{1,0:T(8,128)(2,1)}, u32[]{:S(2)}) %copy-start.7) | copy-done | bytes 57368
  9.7 0.1 own.1.refs_3_.refs_7_
  9.8 0.5 collective-permute-done.1.refs_1_
  10.4 1.6 %collective-permute-start.4 = (bf16[24,3584]{1,0:T(8,128)(2,1)S(1)}, bf16[24,3584]{1,0:T(8,128)(2,1)S(1)}, u32[]{:S(2)}, u32[]{:S(2)}) collective-permute-start(bf16[24,3584]{1,0:T(8,128)(2,1)S(1)} %pack.5.refs_0_), channel_id=1, source_target_pairs={{0,4},{2,6},{4,0},{6,2},{8,12},{10,14},{12,8},{14,10},{16,20},{18,... | collective-permute-start | bytes 516104 | tf_op jit(solution)/shard_map/ppermute | solution.py:267
  11.9 1.8 %copy-done.1 = bf16[384,3584]{1,0:T(8,128)(2,1)S(1)} copy-done((bf16[384,3584]{1,0:T(8,128)(2,1)S(1)}, bf16[384,3584]{1,0:T(8,128)(2,1)}, u32[]{:S(2)}) %copy-start.1) | copy-done | bytes 2752536
  13.7 0.1 collective-permute-start.5
  13.8 0.8 %reshape.10.valid = s32[1,384]{1,0:T(1,128)S(1)} reshape(s32[384]{0:T(512)} %param.16) | data formatting | bytes 3072 | tf_op jit(solution)/shard_map/reshape | solution.py:339
  14.7 0.7 %reshape.9.request = s32[1,384]{1,0:T(1,128)S(1)} reshape(s32[384]{0:T(512)} %param.15) | data formatting | bytes 3072 | tf_op jit(solution)/shard_map/reshape | solution.py:338
  15.3 0.1 prep.1
  15.4 0.6 %collective-permute-done.4.refs_0_ = bf16[24,3584]{1,0:T(8,128)(2,1)S(1)} collective-permute-done((bf16[24,3584]{1,0:T(8,128)(2,1)S(1)}, bf16[24,3584]{1,0:T(8,128)(2,1)S(1)}, u32[]{:S(2)}, u32[]{:S(2)}) %collective-permute-start.4) | collective-permute-done | bytes 172064 | tf_op jit(solution)/shard_map/ppermute | solution.py:267
  16.0 0.1 collective-permute-start.6
  16.1 1.4 %collective-permute-done.6.refs_3_ = bf16[24,3584]{1,0:T(8,128)(2,1)S(1)} collective-permute-done((bf16[24,3584]{1,0:T(8,128)(2,1)S(1)}, bf16[24,3584]{1,0:T(8,128)(2,1)S(1)}, u32[]{:S(2)}, u32[]{:S(2)}) %collective-permute-start.6) | collective-permute-done | bytes 172064 | tf_op jit(solution)/shard_map/ppermute | solution.py:267
  17.5 2.0 %attend.1 = (bf16[32,3712]{1,0:T(8,128)(2,1)S(1)}, bf16[32,3712]{1,0:T(8,128)(2,1)S(1)}, bf16[32,3712]{1,0:T(8,128)(2,1)S(1)}, bf16[32,3712]{1,0:T(8,128)(2,1)S(1)}) custom-call(bf16[32,128]{1,0:T(8,128)(2,1)S(1)} %get-tuple-element.21.refs_2_.pick, bf16[32,128]{1,0:T(8,128)(2,1)S(1)} %get-tuple-element.22.spread_to, f32[32,384]{1,0:T(8,128)S(1)} %get-tuple-element.23.mask, ...), custom_call_target="tpu_custom_call" | custom-call | tf_op jit(solution)/shard_map/attend/pallas_call | solution.py:295
  19.5 0.2 collective-permute-start.7
  19.7 0.4 collective-permute-start.9
  20.1 1.0 %collective-permute-done.7.refs_1_ = bf16[32,3712]{1,0:T(8,128)(2,1)S(1)} collective-permute-done((bf16[32,3712]{1,0:T(8,128)(2,1)S(1)}, bf16[32,3712]{1,0:T(8,128)(2,1)S(1)}, u32[]{:S(2)}, u32[]{:S(2)}) %collective-permute-start.7) | collective-permute-done | bytes 237600 | tf_op jit(solution)/shard_map/ppermute | solution.py:267
  21.1 0.4 merge.3
  21.5 1.5 %collective-permute-start.10 = (bf16[24,3712]{1,0:T(8,128)(2,1)S(1)}, bf16[24,3712]{1,0:T(8,128)(2,1)S(1)}, u32[]{:S(2)}, u32[]{:S(2)}) collective-permute-start(bf16[24,3712]{1,0:T(8,128)(2,1)S(1)} %get-tuple-element.30), channel_id=1, source_target_pairs={{0,4},{2,6},{4,0},{6,2},{8,12},{10,14},{12,8},{14,10},{16,20},{18,... | collective-permute-start | bytes 534536 | tf_op jit(solution)/shard_map/ppermute | solution.py:267
  23.0 0.4 merge.4
  23.4 2.6 %collective-permute-start.11 = (bf16[8,3712]{1,0:T(8,128)(2,1)S(1)}, bf16[8,3712]{1,0:T(8,128)(2,1)S(1)}, u32[]{:S(2)}, u32[]{:S(2)}) collective-permute-start(bf16[8,3712]{1,0:T(8,128)(2,1)S(1)} %get-tuple-element.31), channel_id=1, source_target_pairs={{0,24},{2,26},{4,28},{6,30},{8,16},{10,18},{12,20},{14,22},{16,8},... | collective-permute-start | bytes 178184 | tf_op jit(solution)/shard_map/ppermute | solution.py:267
  26.0 1.4 %collective-permute-start.8 = (bf16[8,3712]{1,0:T(8,128)(2,1)S(1)}, bf16[8,3712]{1,0:T(8,128)(2,1)S(1)}, u32[]{:S(2)}, u32[]{:S(2)}) collective-permute-start(bf16[8,3712]{1,0:T(8,128)(2,1)S(1)} %get-tuple-element.26), channel_id=1, source_target_pairs={{0,28},{2,30},{4,24},{6,26},{8,20},{10,22},{12,16},{14,18},{16,12}... | collective-permute-start | bytes 178184 | tf_op jit(solution)/shard_map/ppermute | solution.py:267
  27.4 0.7 %collective-permute-done.10.refs_1_.refs_2_ = bf16[24,3712]{1,0:T(8,128)(2,1)S(1)} collective-permute-done((bf16[24,3712]{1,0:T(8,128)(2,1)S(1)}, bf16[24,3712]{1,0:T(8,128)(2,1)S(1)}, u32[]{:S(2)}, u32[]{:S(2)}) %collective-permute-start.10) | collective-permute-done | bytes 178208 | tf_op jit(solution)/shard_map/ppermute | solution.py:267
  28.1 0.3 merge.5
  28.5 2.9 %collective-permute-start.12 = (bf16[8,3712]{1,0:T(8,128)(2,1)S(1)}, bf16[8,3712]{1,0:T(8,128)(2,1)S(1)}, u32[]{:S(2)}, u32[]{:S(2)}) collective-permute-start(bf16[8,3712]{1,0:T(8,128)(2,1)S(1)} %get-tuple-element.33), channel_id=1, source_target_pairs={{0,16},{2,18},{4,20},{6,22},{8,24},{10,26},{12,28},{14,30},{16,0},... | collective-permute-start | bytes 178184 | tf_op jit(solution)/shard_map/ppermute | solution.py:267
  31.4 0.3 collective-permute-start.13
  31.7 1.7 %collective-permute-done.8.refs_0_ = bf16[8,3712]{1,0:T(8,128)(2,1)S(1)} collective-permute-done((bf16[8,3712]{1,0:T(8,128)(2,1)S(1)}, bf16[8,3712]{1,0:T(8,128)(2,1)S(1)}, u32[]{:S(2)}, u32[]{:S(2)}) %collective-permute-start.8) | collective-permute-done | bytes 59424 | tf_op jit(solution)/shard_map/ppermute | solution.py:267
  33.4 1.1 %collective-permute-done.12.refs_4_ = bf16[8,3712]{1,0:T(8,128)(2,1)S(1)} collective-permute-done((bf16[8,3712]{1,0:T(8,128)(2,1)S(1)}, bf16[8,3712]{1,0:T(8,128)(2,1)S(1)}, u32[]{:S(2)}, u32[]{:S(2)}) %collective-permute-start.12) | collective-permute-done | bytes 59424 | tf_op jit(solution)/shard_map/ppermute | solution.py:267
  34.5 1.1 %collective-permute-done.13.refs_5_ = bf16[8,3712]{1,0:T(8,128)(2,1)S(1)} collective-permute-done((bf16[8,3712]{1,0:T(8,128)(2,1)S(1)}, bf16[8,3712]{1,0:T(8,128)(2,1)S(1)}, u32[]{:S(2)}, u32[]{:S(2)}) %collective-permute-start.13) | collective-permute-done | bytes 59424 | tf_op jit(solution)/shard_map/ppermute | solution.py:267
  35.6 0.4 last.1.refs_2_
  36.0 0.8 %collective-permute-start.14 = (bf16[8,3584]{1,0:T(8,128)(2,1)S(1)}, bf16[8,3584]{1,0:T(8,128)(2,1)S(1)}, u32[]{:S(2)}, u32[]{:S(2)}) collective-permute-start(bf16[8,3584]{1,0:T(8,128)(2,1)S(1)} %last.1.refs_2_), channel_id=1, source_target_pairs={{0,24},{2,26},{4,28},{6,30},{8,16},{10,18},{12,20},{14,22},{16,8},... | collective-permute-start | bytes 172040 | tf_op jit(solution)/shard_map/ppermute | solution.py:267
  36.8 1.3 %collective-permute-start.15 = (bf16[8,3584]{1,0:T(8,128)(2,1)S(1)}, bf16[8,3584]{1,0:T(8,128)(2,1)S(1)}, u32[]{:S(2)}, u32[]{:S(2)}) collective-permute-start(bf16[8,3584]{1,0:T(8,128)(2,1)S(1)} %last.1.refs_2_), channel_id=1, source_target_pairs={{0,16},{2,18},{4,20},{6,22},{8,24},{10,26},{12,28},{14,30},{16,0},... | collective-permute-start | bytes 172040 | tf_op jit(solution)/shard_map/ppermute | solution.py:267
  38.2 2.3 %collective-permute-start.16 = (bf16[8,3584]{1,0:T(8,128)(2,1)S(1)}, bf16[8,3584]{1,0:T(8,128)(2,1)S(1)}, u32[]{:S(2)}, u32[]{:S(2)}) collective-permute-start(bf16[8,3584]{1,0:T(8,128)(2,1)S(1)} %last.1.refs_2_), channel_id=1, source_target_pairs={{0,8},{2,10},{4,12},{6,14},{8,0},{10,2},{12,4},{14,6},{16,24},{18,... | collective-permute-start | bytes 172040 | tf_op jit(solution)/shard_map/ppermute | solution.py:267
  40.5 0.6 %collective-permute-start.17 = (bf16[8,3584]{1,0:T(8,128)(2,1)S(1)}, bf16[8,3584]{1,0:T(8,128)(2,1)S(1)}, u32[]{:S(2)}, u32[]{:S(2)}) collective-permute-start(bf16[8,3584]{1,0:T(8,128)(2,1)S(1)} %last.1.refs_2_), channel_id=1, source_target_pairs={{0,12},{2,14},{4,8},{6,10},{8,4},{10,6},{12,0},{14,2},{16,28},{18,... | collective-permute-start | bytes 172040 | tf_op jit(solution)/shard_map/ppermute | solution.py:267
  41.0 1.6 %collective-permute-done.14.refs_0_ = bf16[8,3584]{1,0:T(8,128)(2,1)S(1)} collective-permute-done((bf16[8,3584]{1,0:T(8,128)(2,1)S(1)}, bf16[8,3584]{1,0:T(8,128)(2,1)S(1)}, u32[]{:S(2)}, u32[]{:S(2)}) %collective-permute-start.14) | collective-permute-done | bytes 57376 | tf_op jit(solution)/shard_map/ppermute | solution.py:267
  42.7 1.9 %collective-permute-start.18 = (bf16[24,3584]{1,0:T(8,128)(2,1)S(1)}, bf16[24,3584]{1,0:T(8,128)(2,1)S(1)}, u32[]{:S(2)}, u32[]{:S(2)}) collective-permute-start(bf16[24,3584]{1,0:T(8,128)(2,1)S(1)} %pack.8.refs_0_), channel_id=1, source_target_pairs={{0,4},{2,6},{4,0},{6,2},{8,12},{10,14},{12,8},{14,10},{16,20},{18,... | collective-permute-start | bytes 516104 | tf_op jit(solution)/shard_map/ppermute | solution.py:267
  44.6 1.0 %collective-permute-done.17.refs_2_ = bf16[8,3584]{1,0:T(8,128)(2,1)S(1)} collective-permute-done((bf16[8,3584]{1,0:T(8,128)(2,1)S(1)}, bf16[8,3584]{1,0:T(8,128)(2,1)S(1)}, u32[]{:S(2)}, u32[]{:S(2)}) %collective-permute-start.17) | collective-permute-done | bytes 57376 | tf_op jit(solution)/shard_map/ppermute | solution.py:267
  45.6 0.1 collective-permute-start.19
  45.6 2.5 %collective-permute-done.18.refs_1_ = bf16[24,3584]{1,0:T(8,128)(2,1)S(1)} collective-permute-done((bf16[24,3584]{1,0:T(8,128)(2,1)S(1)}, bf16[24,3584]{1,0:T(8,128)(2,1)S(1)}, u32[]{:S(2)}, u32[]{:S(2)}) %collective-permute-start.18) | collective-permute-done | bytes 172064 | tf_op jit(solution)/shard_map/ppermute | solution.py:267
  48.1 1.4 %collective-permute-done.20.refs_3_ = bf16[24,3584]{1,0:T(8,128)(2,1)S(1)} collective-permute-done((bf16[24,3584]{1,0:T(8,128)(2,1)S(1)}, bf16[24,3584]{1,0:T(8,128)(2,1)S(1)}, u32[]{:S(2)}, u32[]{:S(2)}) %collective-permute-start.20) | collective-permute-done | bytes 172064 | tf_op jit(solution)/shard_map/ppermute | solution.py:267
  49.5 1.1 %project.1 = (f32[64,448]{1,0:T(8,128)S(1)}, bf16[64,448]{1,0:T(8,128)(2,1)S(1)}) custom-call(bf16[40,3584]{1,0:T(8,128)(2,1)S(1)} %pack.9.refs_0_, bf16[24,3584]{1,0:T(8,128)(2,1)S(1)} %collective-permute-done.18.refs_1_, bf16[40,3584]{1,0:T(8,128)(2,1)S(1)} %collective-permute-done.19.refs_2_, bf16[24,3584]{1,0:T(8,128)(2,1)S(1)} %collective-permute-done.20.refs_3_, ...), custom_call_target="tpu_custom_call" | custom-call | tf_op jit(solution)/shard_map/project/pallas_call | solution.py:295
  50.6 1.6 %collective-permute-start.21 = (bf16[64,448]{1,0:T(8,128)(2,1)S(1)}, bf16[64,448]{1,0:T(8,128)(2,1)S(1)}, u32[]{:S(2)}, u32[]{:S(2)}) collective-permute-start(bf16[64,448]{1,0:T(8,128)(2,1)S(1)} %get-tuple-element.36), channel_id=1, source_target_pairs={{0,1},{1,0},{2,3},{3,2},{4,5},{5,4},{6,7},{7,6},{8,9},{9,8},{10,11... | collective-permute-start | bytes 172040 | tf_op jit(solution)/shard_map/ppermute | solution.py:267
  52.3 2.7 %collective-permute-done.21.refs_0_ = bf16[64,448]{1,0:T(8,128)(2,1)S(1)} collective-permute-done((bf16[64,448]{1,0:T(8,128)(2,1)S(1)}, bf16[64,448]{1,0:T(8,128)(2,1)S(1)}, u32[]{:S(2)}, u32[]{:S(2)}) %collective-permute-start.21) | collective-permute-done | bytes 57376 | tf_op jit(solution)/shard_map/ppermute | solution.py:267
  55.0 0.6 %final.1 = bf16[64,448]{1,0:T(8,128)(2,1)} custom-call(f32[64,448]{1,0:T(8,128)S(1)} %base.1.total, bf16[64,448]{1,0:T(8,128)(2,1)S(1)} %collective-permute-done.21.refs_0_), custom_call_target="tpu_custom_call" | custom-call | tf_op jit(solution)/shard_map/final/pallas_call | solution.py:295
  (35 shorter events, 0.2 us)
Async XLA Ops:
  0.0 15.3 %copy-start = (bf16[384,3584]{1,0:T(8,128)(2,1)S(1)}, bf16[384,3584]{1,0:T(8,128)(2,1)}, u32[]{:S(2)}) copy-start(bf16[384,3584]{1,0:T(8,128)(2,1)} %keys.1) | copy-start | bytes 8257540
  0.0 9.8 %collective-permute-start = (bf16[8,3584]{1,0:T(8,128)(2,1)}, bf16[8,3584]{1,0:T(8,128)(2,1)S(1)}, u32[]{:S(2)}, u32[]{:S(2)}) collective-permute-start(bf16[8,3584]{1,0:T(8,128)(2,1)} %queries.1), channel_id=1, source_target_pairs={{0,24},{2,26},{4,28},{6,30},{8,16},{10,18},{12,20},{14,22},{16,8},... | collective-permute-start | bytes 172040 | tf_op jit(solution)/shard_map/ppermute | solution.py:267
  5.1 5.3 %collective-permute-start.1 = (bf16[8,3584]{1,0:T(8,128)(2,1)}, bf16[8,3584]{1,0:T(8,128)(2,1)S(1)}, u32[]{:S(2)}, u32[]{:S(2)}) collective-permute-start(bf16[8,3584]{1,0:T(8,128)(2,1)} %queries.1), channel_id=1, source_target_pairs={{0,16},{2,18},{4,20},{6,22},{8,24},{10,26},{12,28},{14,30},{16,0},... | collective-permute-start | bytes 172040 | tf_op jit(solution)/shard_map/ppermute | solution.py:267
  5.1 8.6 %collective-permute-start.2 = (bf16[8,3584]{1,0:T(8,128)(2,1)}, bf16[8,3584]{1,0:T(8,128)(2,1)S(1)}, u32[]{:S(2)}, u32[]{:S(2)}) collective-permute-start(bf16[8,3584]{1,0:T(8,128)(2,1)} %queries.1), channel_id=1, source_target_pairs={{0,8},{2,10},{4,12},{6,14},{8,0},{10,2},{12,4},{14,6},{16,24},{18,... | collective-permute-start | bytes 172040 | tf_op jit(solution)/shard_map/ppermute | solution.py:267
  5.7 8.0 %collective-permute-start.3 = (bf16[8,3584]{1,0:T(8,128)(2,1)}, bf16[8,3584]{1,0:T(8,128)(2,1)S(1)}, u32[]{:S(2)}, u32[]{:S(2)}) collective-permute-start(bf16[8,3584]{1,0:T(8,128)(2,1)} %queries.1), channel_id=1, source_target_pairs={{0,12},{2,14},{4,8},{6,10},{8,4},{10,6},{12,0},{14,2},{16,28},{18,... | collective-permute-start | bytes 172040 | tf_op jit(solution)/shard_map/ppermute | solution.py:267
  8.0 0.9 %copy-start.6 = (bf16[8,3584]{1,0:T(8,128)(2,1)S(1)}, bf16[8,3584]{1,0:T(8,128)(2,1)}, u32[]{:S(2)}) copy-start(bf16[8,3584]{1,0:T(8,128)(2,1)} %queries.1) | copy-start | bytes 172036
  8.9 0.8 %copy-start.7 = (bf16[8,3584]{1,0:T(8,128)(2,1)S(1)}, bf16[8,3584]{1,0:T(8,128)(2,1)}, u32[]{:S(2)}) copy-start(bf16[8,3584]{1,0:T(8,128)(2,1)} %new_keys.1) | copy-start | bytes 172036
  10.4 5.7 %collective-permute-start.4 = (bf16[24,3584]{1,0:T(8,128)(2,1)S(1)}, bf16[24,3584]{1,0:T(8,128)(2,1)S(1)}, u32[]{:S(2)}, u32[]{:S(2)}) collective-permute-start(bf16[24,3584]{1,0:T(8,128)(2,1)S(1)} %pack.5.refs_0_), channel_id=1, source_target_pairs={{0,4},{2,6},{4,0},{6,2},{8,12},{10,14},{12,8},{14,10},{16,20},{18,... | collective-permute-start | bytes 516104 | tf_op jit(solution)/shard_map/ppermute | solution.py:267
  11.9 1.8 %copy-start.1 = (bf16[384,3584]{1,0:T(8,128)(2,1)S(1)}, bf16[384,3584]{1,0:T(8,128)(2,1)}, u32[]{:S(2)}) copy-start(bf16[384,3584]{1,0:T(8,128)(2,1)} %values.1) | copy-start | bytes 8257540
  13.7 3.8 %copy-start.2 = (bf16[384,3584]{1,0:T(8,128)(2,1)S(1)}, bf16[384,3584]{1,0:T(8,128)(2,1)}, u32[]{:S(2)}) copy-start(bf16[384,3584]{1,0:T(8,128)(2,1)} %values.1) | copy-start | bytes 8257540
  13.7 2.4 %collective-permute-start.5 = (bf16[40,3584]{1,0:T(8,128)(2,1)S(1)}, bf16[40,3584]{1,0:T(8,128)(2,1)S(1)}, u32[]{:S(2)}, u32[]{:S(2)}) collective-permute-start(bf16[40,3584]{1,0:T(8,128)(2,1)S(1)} %pack.6.refs_0_), channel_id=1, source_target_pairs={{0,2},{2,0},{4,6},{6,4},{8,10},{10,8},{12,14},{14,12},{16,18},{18,... | collective-permute-start | bytes 860168 | tf_op jit(solution)/shard_map/ppermute | solution.py:267
  16.0 1.5 %collective-permute-start.6 = (bf16[24,3584]{1,0:T(8,128)(2,1)S(1)}, bf16[24,3584]{1,0:T(8,128)(2,1)S(1)}, u32[]{:S(2)}, u32[]{:S(2)}) collective-permute-start(bf16[24,3584]{1,0:T(8,128)(2,1)S(1)} %pack.7.refs_1_), channel_id=1, source_target_pairs={{0,2},{2,0},{4,6},{6,4},{8,10},{10,8},{12,14},{14,12},{16,18},{18,... | collective-permute-start | bytes 516104 | tf_op jit(solution)/shard_map/ppermute | solution.py:267
  17.5 18.1 %copy-start.5 = (bf16[8,3584]{1,0:T(8,128)(2,1)S(1)}, bf16[8,3584]{1,0:T(8,128)(2,1)}, u32[]{:S(2)}) copy-start(bf16[8,3584]{1,0:T(8,128)(2,1)} %refs_6_.1) | copy-start | bytes 172036
  17.5 32.0 %copy-start.3 = (bf16[3584,448]{0,1:T(8,128)(2,1)S(1)}, bf16[3584,448]{0,1:T(8,128)(2,1)}, u32[]{:S(2)}) copy-start(bf16[3584,448]{0,1:T(8,128)(2,1)} %param.17) | copy-start | bytes 9633796
  19.5 1.6 %collective-permute-start.7 = (bf16[32,3712]{1,0:T(8,128)(2,1)S(1)}, bf16[32,3712]{1,0:T(8,128)(2,1)S(1)}, u32[]{:S(2)}, u32[]{:S(2)}) collective-permute-start(bf16[32,3712]{1,0:T(8,128)(2,1)S(1)} %get-tuple-element.25), channel_id=1, source_target_pairs={{0,2},{2,0},{4,6},{6,4},{8,10},{10,8},{12,14},{14,12},{16,18},{18,... | collective-permute-start | bytes 712712 | tf_op jit(solution)/shard_map/ppermute | solution.py:267
  19.7 3.3 %collective-permute-start.9 = (bf16[32,3712]{1,0:T(8,128)(2,1)S(1)}, bf16[32,3712]{1,0:T(8,128)(2,1)S(1)}, u32[]{:S(2)}, u32[]{:S(2)}) collective-permute-start(bf16[32,3712]{1,0:T(8,128)(2,1)S(1)} %get-tuple-element.28), channel_id=1, source_target_pairs={{0,2},{2,0},{4,6},{6,4},{8,10},{10,8},{12,14},{14,12},{16,18},{18,... | collective-permute-start | bytes 712712 | tf_op jit(solution)/shard_map/ppermute | solution.py:267
  21.5 6.6 %collective-permute-start.10 = (bf16[24,3712]{1,0:T(8,128)(2,1)S(1)}, bf16[24,3712]{1,0:T(8,128)(2,1)S(1)}, u32[]{:S(2)}, u32[]{:S(2)}) collective-permute-start(bf16[24,3712]{1,0:T(8,128)(2,1)S(1)} %get-tuple-element.30), channel_id=1, source_target_pairs={{0,4},{2,6},{4,0},{6,2},{8,12},{10,14},{12,8},{14,10},{16,20},{18,... | collective-permute-start | bytes 534536 | tf_op jit(solution)/shard_map/ppermute | solution.py:267
  23.4 8.3 %collective-permute-start.11 = (bf16[8,3712]{1,0:T(8,128)(2,1)S(1)}, bf16[8,3712]{1,0:T(8,128)(2,1)S(1)}, u32[]{:S(2)}, u32[]{:S(2)}) collective-permute-start(bf16[8,3712]{1,0:T(8,128)(2,1)S(1)} %get-tuple-element.31), channel_id=1, source_target_pairs={{0,24},{2,26},{4,28},{6,30},{8,16},{10,18},{12,20},{14,22},{16,8},... | collective-permute-start | bytes 178184 | tf_op jit(solution)/shard_map/ppermute | solution.py:267
  26.0 7.4 %collective-permute-start.8 = (bf16[8,3712]{1,0:T(8,128)(2,1)S(1)}, bf16[8,3712]{1,0:T(8,128)(2,1)S(1)}, u32[]{:S(2)}, u32[]{:S(2)}) collective-permute-start(bf16[8,3712]{1,0:T(8,128)(2,1)S(1)} %get-tuple-element.26), channel_id=1, source_target_pairs={{0,28},{2,30},{4,24},{6,26},{8,20},{10,22},{12,16},{14,18},{16,12}... | collective-permute-start | bytes 178184 | tf_op jit(solution)/shard_map/ppermute | solution.py:267
  28.5 6.1 %collective-permute-start.12 = (bf16[8,3712]{1,0:T(8,128)(2,1)S(1)}, bf16[8,3712]{1,0:T(8,128)(2,1)S(1)}, u32[]{:S(2)}, u32[]{:S(2)}) collective-permute-start(bf16[8,3712]{1,0:T(8,128)(2,1)S(1)} %get-tuple-element.33), channel_id=1, source_target_pairs={{0,16},{2,18},{4,20},{6,22},{8,24},{10,26},{12,28},{14,30},{16,0},... | collective-permute-start | bytes 178184 | tf_op jit(solution)/shard_map/ppermute | solution.py:267
  31.4 4.2 %collective-permute-start.13 = (bf16[8,3712]{1,0:T(8,128)(2,1)S(1)}, bf16[8,3712]{1,0:T(8,128)(2,1)S(1)}, u32[]{:S(2)}, u32[]{:S(2)}) collective-permute-start(bf16[8,3712]{1,0:T(8,128)(2,1)S(1)} %get-tuple-element.34), channel_id=1, source_target_pairs={{0,8},{2,10},{4,12},{6,14},{8,0},{10,2},{12,4},{14,6},{16,24},{18,... | collective-permute-start | bytes 178184 | tf_op jit(solution)/shard_map/ppermute | solution.py:267
  35.6 16.6 %copy-start.8 = (bf16[448]{0:T(512)(128)(2,1)S(1)}, bf16[448]{0:T(512)(128)(2,1)}, u32[]{:S(2)}) copy-start(bf16[448]{0:T(512)(128)(2,1)} %param.18) | copy-start | bytes 2692
  35.6 16.6 %copy-start.4 = (bf16[64,448]{1,0:T(8,128)(2,1)S(1)}, bf16[64,448]{1,0:T(8,128)(2,1)}, u32[]{:S(2)}) copy-start(bf16[64,448]{1,0:T(8,128)(2,1)} %residual.1) | copy-start | bytes 172036
  36.0 6.6 %collective-permute-start.14 = (bf16[8,3584]{1,0:T(8,128)(2,1)S(1)}, bf16[8,3584]{1,0:T(8,128)(2,1)S(1)}, u32[]{:S(2)}, u32[]{:S(2)}) collective-permute-start(bf16[8,3584]{1,0:T(8,128)(2,1)S(1)} %last.1.refs_2_), channel_id=1, source_target_pairs={{0,24},{2,26},{4,28},{6,30},{8,16},{10,18},{12,20},{14,22},{16,8},... | collective-permute-start | bytes 172040 | tf_op jit(solution)/shard_map/ppermute | solution.py:267
  36.8 5.8 %collective-permute-start.15 = (bf16[8,3584]{1,0:T(8,128)(2,1)S(1)}, bf16[8,3584]{1,0:T(8,128)(2,1)S(1)}, u32[]{:S(2)}, u32[]{:S(2)}) collective-permute-start(bf16[8,3584]{1,0:T(8,128)(2,1)S(1)} %last.1.refs_2_), channel_id=1, source_target_pairs={{0,16},{2,18},{4,20},{6,22},{8,24},{10,26},{12,28},{14,30},{16,0},... | collective-permute-start | bytes 172040 | tf_op jit(solution)/shard_map/ppermute | solution.py:267
  38.2 6.4 %collective-permute-start.16 = (bf16[8,3584]{1,0:T(8,128)(2,1)S(1)}, bf16[8,3584]{1,0:T(8,128)(2,1)S(1)}, u32[]{:S(2)}, u32[]{:S(2)}) collective-permute-start(bf16[8,3584]{1,0:T(8,128)(2,1)S(1)} %last.1.refs_2_), channel_id=1, source_target_pairs={{0,8},{2,10},{4,12},{6,14},{8,0},{10,2},{12,4},{14,6},{16,24},{18,... | collective-permute-start | bytes 172040 | tf_op jit(solution)/shard_map/ppermute | solution.py:267
  40.5 5.1 %collective-permute-start.17 = (bf16[8,3584]{1,0:T(8,128)(2,1)S(1)}, bf16[8,3584]{1,0:T(8,128)(2,1)S(1)}, u32[]{:S(2)}, u32[]{:S(2)}) collective-permute-start(bf16[8,3584]{1,0:T(8,128)(2,1)S(1)} %last.1.refs_2_), channel_id=1, source_target_pairs={{0,12},{2,14},{4,8},{6,10},{8,4},{10,6},{12,0},{14,2},{16,28},{18,... | collective-permute-start | bytes 172040 | tf_op jit(solution)/shard_map/ppermute | solution.py:267
  42.7 5.5 %collective-permute-start.18 = (bf16[24,3584]{1,0:T(8,128)(2,1)S(1)}, bf16[24,3584]{1,0:T(8,128)(2,1)S(1)}, u32[]{:S(2)}, u32[]{:S(2)}) collective-permute-start(bf16[24,3584]{1,0:T(8,128)(2,1)S(1)} %pack.8.refs_0_), channel_id=1, source_target_pairs={{0,4},{2,6},{4,0},{6,2},{8,12},{10,14},{12,8},{14,10},{16,20},{18,... | collective-permute-start | bytes 516104 | tf_op jit(solution)/shard_map/ppermute | solution.py:267
  45.6 2.6 %collective-permute-start.19 = (bf16[40,3584]{1,0:T(8,128)(2,1)S(1)}, bf16[40,3584]{1,0:T(8,128)(2,1)S(1)}, u32[]{:S(2)}, u32[]{:S(2)}) collective-permute-start(bf16[40,3584]{1,0:T(8,128)(2,1)S(1)} %pack.9.refs_0_), channel_id=1, source_target_pairs={{0,2},{2,0},{4,6},{6,4},{8,10},{10,8},{12,14},{14,12},{16,18},{18,... | collective-permute-start | bytes 860168 | tf_op jit(solution)/shard_map/ppermute | solution.py:267
  48.1 1.4 %collective-permute-start.20 = (bf16[24,3584]{1,0:T(8,128)(2,1)S(1)}, bf16[24,3584]{1,0:T(8,128)(2,1)S(1)}, u32[]{:S(2)}, u32[]{:S(2)}) collective-permute-start(bf16[24,3584]{1,0:T(8,128)(2,1)S(1)} %collective-permute-done.18.refs_1_), channel_id=1, source_target_pairs={{0,2},{2,0},{4,6},{6,4},{8,10},{10,8},{12,14},{14,12},{16,18},{18,... | collective-permute-start | bytes 516104 | tf_op jit(solution)/shard_map/ppermute | solution.py:267
  50.6 4.3 %collective-permute-start.21 = (bf16[64,448]{1,0:T(8,128)(2,1)S(1)}, bf16[64,448]{1,0:T(8,128)(2,1)S(1)}, u32[]{:S(2)}, u32[]{:S(2)}) collective-permute-start(bf16[64,448]{1,0:T(8,128)(2,1)S(1)} %get-tuple-element.36), channel_id=1, source_target_pairs={{0,1},{1,0},{2,3},{3,2},{4,5},{5,4},{6,7},{7,6},{8,9},{9,8},{10,11... | collective-permute-start | bytes 172040 | tf_op jit(solution)/shard_map/ppermute | solution.py:267

commit v6 on v5

--- a/solution.py
+++ b/solution.py
@@ -12,6 +12,7 @@
 PAGE = 16
 OUTER = 4
 LANES = 128
+LAG = 3
 STAT = 32
 
 floor_score = -1e30
@@ -142,31 +143,39 @@
         ]
         return jnp.concatenate(bands, axis=0).astype(bf16)
 
-    scores = [
-        lax.dot_general(
+    def score_of(each, cut):
+        return lax.dot_general(
             diagonal(each), keys[:, cut], (((1,), (1,)), ((), ())), preferred_element_type=f32
         )
-        for each, cut in zip(sets, cuts)
-    ]
-    tops = jnp.zeros((rows, LANES), f32)
-    weights, denoms = [], []
-    for each, score in zip(sets, scores):
+
+    def weigh(each, score):
         wide = jnp.concatenate([live] * len(each), axis=0)
         score = jnp.where(wide, score * (1.0 / math.sqrt(HD)), floor_score)
         top = jnp.max(score, axis=1, keepdims=True)
         weight = jnp.where(wide, jnp.exp(score - top), 0.0).astype(bf16)
         denom = jnp.sum(weight.astype(f32), axis=1, keepdims=True)
         denom = jnp.where(denom > 0.0, denom, 1.0)
-        weights.append(weight)
-        denoms.append(denom)
-        for at, head in enumerate(each):
-            part = slice(at * rows, (at + 1) * rows)
-            tops = jnp.where(lane == head, top[part] + jnp.log(denom[part]), tops)
-    found = []
-    for each, cut, weight, denom in zip(sets, cuts, weights, denoms):
+        return weight, denom, top + jnp.log(denom)
+
+    def value_of(each, cut, weight, denom):
         numer = jnp.dot(weight, values[:, cut], preferred_element_type=f32) / denom
-        for at in range(len(each)):
-            found.append(numer[at * rows : (at + 1) * rows, at * HD : (at + 1) * HD])
+        return [
+            numer[at * rows : (at + 1) * rows, at * HD : (at + 1) * HD] for at in range(len(each))
+        ]
+
+    tops = jnp.zeros((rows, LANES), f32)
+    scores, weights, found = {}, {}, []
+    for step in range(len(sets) + 2 * LAG):
+        if step < len(sets):
+            scores[step] = score_of(sets[step], cuts[step])
+        at = step - LAG
+        if 0 <= at < len(sets):
+            *weights[at], top = weigh(sets[at], scores.pop(at))
+            for place, head in enumerate(sets[at]):
+                tops = jnp.where(lane == head, top[place * rows : (place + 1) * rows], tops)
+        at = step - 2 * LAG
+        if 0 <= at < len(sets):
+            found += value_of(sets[at], cuts[at], *weights.pop(at))
     spread = functools.partial(
         lax.dot_general, dimension_numbers=(((0,), (0,)), ((), ())), preferred_element_type=f32
     )
@@ -187,13 +196,14 @@
     best = functools.reduce(jnp.maximum, tops)
     weights = [jnp.exp(top - best) for top in tops]
     total = functools.reduce(jnp.add, weights)
-    shares = [weight / total for weight in weights]
+    shares = [weight / total for weight in weights[1:]]
 
     def head_of(head):
-        terms = [
-            share[:, head : head + 1] * part(head) for share, part in zip(shares, parts)
-        ]
-        return functools.reduce(jnp.add, terms)
+        first = parts[0](head)
+        value = first
+        for share, part in zip(shares, parts[1:]):
+            value = value + share[:, head : head + 1] * (part(head) - first)
+        return value
 
     return head_of, best + jnp.log(total)
 

time: 55.9 us -> 55.6 us (level)
  transfers between devices with their start and end apart: 22 -> 22, of which waited for: 13 -> 13; matrix products, arithmetic and copies ran while one was open for 3% -> 3% of each run, Pallas kernels for 3% -> 2%
where the time goes in v6:
time: 55.6 us; the launch traced here: 55.3 us
  starting transfers between devices  27.5 us (49%)
  waiting for transfers between devices  17.4 us (31%)
  Pallas kernels  5.23 us (9%)
  local copies, waits for them, and re-layouts  4.99 us (9%)
    ppermute x22, starting transfers between devices, hop(): return lax.ppermute(x, axis, [(i, i ^ distance) for i in range(count)])  27.5 us
    ppermute x22, waiting for transfers between devices, hop(): return lax.ppermute(x, axis, [(i, i ^ distance) for i in range(count)])  17.4 us
    pallas_call x18, Pallas kernels, call(): pl.pallas_call(kernel, out_shape=shapes, in_specs=[spec(at) for at in ran...  5.23 us
    unnamed x18, local copies, waits for them, and re-layouts  3.47 us
  transfers between devices with their start and end apart: 22, of which 13 were waited for; matrix products, arithmetic and copies ran while one was open for 3% of the time, Pallas kernels for 2%

profile of v6, /device:TPU:0, one launch (start us, length us, event | category | flops | bytes accessed | tf_op | source)
XLA Modules:
  0.0 55.3 jit_solution(8213653133255631907)
XLA Ops:
  0.0 5.0 %collective-permute-start = (bf16[8,3584]{1,0:T(8,128)(2,1)}, bf16[8,3584]{1,0:T(8,128)(2,1)S(1)}, u32[]{:S(2)}, u32[]{:S(2)}) collective-permute-start(bf16[8,3584]{1,0:T(8,128)(2,1)} %queries.1), channel_id=1, source_target_pairs={{0,24},{2,26},{4,28},{6,30},{8,16},{10,18},{12,20},{14,22},{16,8},... | collective-permute-start | bytes 172040 | tf_op jit(solution)/shard_map/ppermute | solution.py:277
  5.1 0.6 %collective-permute-start.2 = (bf16[8,3584]{1,0:T(8,128)(2,1)}, bf16[8,3584]{1,0:T(8,128)(2,1)S(1)}, u32[]{:S(2)}, u32[]{:S(2)}) collective-permute-start(bf16[8,3584]{1,0:T(8,128)(2,1)} %queries.1), channel_id=1, source_target_pairs={{0,8},{2,10},{4,12},{6,14},{8,0},{10,2},{12,4},{14,6},{16,24},{18,... | collective-permute-start | bytes 172040 | tf_op jit(solution)/shard_map/ppermute | solution.py:277
  5.7 2.3 %collective-permute-start.3 = (bf16[8,3584]{1,0:T(8,128)(2,1)}, bf16[8,3584]{1,0:T(8,128)(2,1)S(1)}, u32[]{:S(2)}, u32[]{:S(2)}) collective-permute-start(bf16[8,3584]{1,0:T(8,128)(2,1)} %queries.1), channel_id=1, source_target_pairs={{0,12},{2,14},{4,8},{6,10},{8,4},{10,6},{12,0},{14,2},{16,28},{18,... | collective-permute-start | bytes 172040 | tf_op jit(solution)/shard_map/ppermute | solution.py:277
  8.0 0.9 %copy-done.6 = bf16[8,3584]{1,0:T(8,128)(2,1)S(1)} copy-done((bf16[8,3584]{1,0:T(8,128)(2,1)S(1)}, bf16[8,3584]{1,0:T(8,128)(2,1)}, u32[]{:S(2)}) %copy-start.6) | copy-done | bytes 57368
  8.9 0.8 %copy-done.7 = bf16[8,3584]{1,0:T(8,128)(2,1)S(1)} copy-done((bf16[8,3584]{1,0:T(8,128)(2,1)S(1)}, bf16[8,3584]{1,0:T(8,128)(2,1)}, u32[]{:S(2)}) %copy-start.7) | copy-done | bytes 57368
  9.7 0.1 own.1.refs_3_.refs_7_
  9.8 0.0 collective-permute-done.refs_0_
  9.8 0.5 collective-permute-done.1.refs_1_
  10.4 1.6 %collective-permute-start.4 = (bf16[24,3584]{1,0:T(8,128)(2,1)S(1)}, bf16[24,3584]{1,0:T(8,128)(2,1)S(1)}, u32[]{:S(2)}, u32[]{:S(2)}) collective-permute-start(bf16[24,3584]{1,0:T(8,128)(2,1)S(1)} %pack.5.refs_0_), channel_id=1, source_target_pairs={{0,4},{2,6},{4,0},{6,2},{8,12},{10,14},{12,8},{14,10},{16,20},{18,... | collective-permute-start | bytes 516104 | tf_op jit(solution)/shard_map/ppermute | solution.py:277
  11.9 1.8 %copy-done.1 = bf16[384,3584]{1,0:T(8,128)(2,1)S(1)} copy-done((bf16[384,3584]{1,0:T(8,128)(2,1)S(1)}, bf16[384,3584]{1,0:T(8,128)(2,1)}, u32[]{:S(2)}) %copy-start.1) | copy-done | bytes 2752536
  13.7 0.1 collective-permute-start.5
  13.8 0.8 %reshape.10.valid = s32[1,384]{1,0:T(1,128)S(1)} reshape(s32[384]{0:T(512)} %param.16) | data formatting | bytes 3072 | tf_op jit(solution)/shard_map/reshape | solution.py:349
  14.7 0.7 %reshape.9.request = s32[1,384]{1,0:T(1,128)S(1)} reshape(s32[384]{0:T(512)} %param.15) | data formatting | bytes 3072 | tf_op jit(solution)/shard_map/reshape | solution.py:348
  15.3 0.1 prep.1
  15.4 0.6 %collective-permute-done.4.refs_0_ = bf16[24,3584]{1,0:T(8,128)(2,1)S(1)} collective-permute-done((bf16[24,3584]{1,0:T(8,128)(2,1)S(1)}, bf16[24,3584]{1,0:T(8,128)(2,1)S(1)}, u32[]{:S(2)}, u32[]{:S(2)}) %collective-permute-start.4) | collective-permute-done | bytes 172064 | tf_op jit(solution)/shard_map/ppermute | solution.py:277
  16.0 0.1 collective-permute-start.6
  16.1 1.4 %collective-permute-done.6.refs_3_ = bf16[24,3584]{1,0:T(8,128)(2,1)S(1)} collective-permute-done((bf16[24,3584]{1,0:T(8,128)(2,1)S(1)}, bf16[24,3584]{1,0:T(8,128)(2,1)S(1)}, u32[]{:S(2)}, u32[]{:S(2)}) %collective-permute-start.6) | collective-permute-done | bytes 172064 | tf_op jit(solution)/shard_map/ppermute | solution.py:277
  17.5 1.9 %attend.1 = (bf16[32,3712]{1,0:T(8,128)(2,1)S(1)}, bf16[32,3712]{1,0:T(8,128)(2,1)S(1)}, bf16[32,3712]{1,0:T(8,128)(2,1)S(1)}, bf16[32,3712]{1,0:T(8,128)(2,1)S(1)}) custom-call(bf16[32,128]{1,0:T(8,128)(2,1)S(1)} %get-tuple-element.21.refs_2_.pick, bf16[32,128]{1,0:T(8,128)(2,1)S(1)} %get-tuple-element.22.spread_to, f32[32,384]{1,0:T(8,128)S(1)} %get-tuple-element.23.mask, ...), custom_call_target="tpu_custom_call" | custom-call | tf_op jit(solution)/shard_map/attend/pallas_call | solution.py:305
  19.4 0.2 collective-permute-start.7
  19.6 0.4 collective-permute-start.9
  19.9 1.0 %collective-permute-done.7.refs_1_ = bf16[32,3712]{1,0:T(8,128)(2,1)S(1)} collective-permute-done((bf16[32,3712]{1,0:T(8,128)(2,1)S(1)}, bf16[32,3712]{1,0:T(8,128)(2,1)S(1)}, u32[]{:S(2)}, u32[]{:S(2)}) %collective-permute-start.7) | collective-permute-done | bytes 237600 | tf_op jit(solution)/shard_map/ppermute | solution.py:277
  20.9 0.3 merge.3
  21.3 1.5 %collective-permute-start.10 = (bf16[24,3712]{1,0:T(8,128)(2,1)S(1)}, bf16[24,3712]{1,0:T(8,128)(2,1)S(1)}, u32[]{:S(2)}, u32[]{:S(2)}) collective-permute-start(bf16[24,3712]{1,0:T(8,128)(2,1)S(1)} %get-tuple-element.30), channel_id=1, source_target_pairs={{0,4},{2,6},{4,0},{6,2},{8,12},{10,14},{12,8},{14,10},{16,20},{18,... | collective-permute-start | bytes 534536 | tf_op jit(solution)/shard_map/ppermute | solution.py:277
  22.7 0.3 merge.4
  23.1 2.6 %collective-permute-start.11 = (bf16[8,3712]{1,0:T(8,128)(2,1)S(1)}, bf16[8,3712]{1,0:T(8,128)(2,1)S(1)}, u32[]{:S(2)}, u32[]{:S(2)}) collective-permute-start(bf16[8,3712]{1,0:T(8,128)(2,1)S(1)} %get-tuple-element.31), channel_id=1, source_target_pairs={{0,24},{2,26},{4,28},{6,30},{8,16},{10,18},{12,20},{14,22},{16,8},... | collective-permute-start | bytes 178184 | tf_op jit(solution)/shard_map/ppermute | solution.py:277
  25.6 1.4 %collective-permute-start.8 = (bf16[8,3712]{1,0:T(8,128)(2,1)S(1)}, bf16[8,3712]{1,0:T(8,128)(2,1)S(1)}, u32[]{:S(2)}, u32[]{:S(2)}) collective-permute-start(bf16[8,3712]{1,0:T(8,128)(2,1)S(1)} %get-tuple-element.26), channel_id=1, source_target_pairs={{0,28},{2,30},{4,24},{6,26},{8,20},{10,22},{12,16},{14,18},{16,12}... | collective-permute-start | bytes 178184 | tf_op jit(solution)/shard_map/ppermute | solution.py:277
  27.0 0.9 %collective-permute-done.10.refs_1_.refs_2_ = bf16[24,3712]{1,0:T(8,128)(2,1)S(1)} collective-permute-done((bf16[24,3712]{1,0:T(8,128)(2,1)S(1)}, bf16[24,3712]{1,0:T(8,128)(2,1)S(1)}, u32[]{:S(2)}, u32[]{:S(2)}) %collective-permute-start.10) | collective-permute-done | bytes 178208 | tf_op jit(solution)/shard_map/ppermute | solution.py:277
  27.9 0.3 merge.5
  28.1 2.9 %collective-permute-start.12 = (bf16[8,3712]{1,0:T(8,128)(2,1)S(1)}, bf16[8,3712]{1,0:T(8,128)(2,1)S(1)}, u32[]{:S(2)}, u32[]{:S(2)}) collective-permute-start(bf16[8,3712]{1,0:T(8,128)(2,1)S(1)} %get-tuple-element.33), channel_id=1, source_target_pairs={{0,16},{2,18},{4,20},{6,22},{8,24},{10,26},{12,28},{14,30},{16,0},... | collective-permute-start | bytes 178184 | tf_op jit(solution)/shard_map/ppermute | solution.py:277
  31.1 0.3 collective-permute-start.13
  31.4 1.7 %collective-permute-done.8.refs_0_ = bf16[8,3712]{1,0:T(8,128)(2,1)S(1)} collective-permute-done((bf16[8,3712]{1,0:T(8,128)(2,1)S(1)}, bf16[8,3712]{1,0:T(8,128)(2,1)S(1)}, u32[]{:S(2)}, u32[]{:S(2)}) %collective-permute-start.8) | collective-permute-done | bytes 59424 | tf_op jit(solution)/shard_map/ppermute | solution.py:277
  33.1 1.1 %collective-permute-done.12.refs_4_ = bf16[8,3712]{1,0:T(8,128)(2,1)S(1)} collective-permute-done((bf16[8,3712]{1,0:T(8,128)(2,1)S(1)}, bf16[8,3712]{1,0:T(8,128)(2,1)S(1)}, u32[]{:S(2)}, u32[]{:S(2)}) %collective-permute-start.12) | collective-permute-done | bytes 59424 | tf_op jit(solution)/shard_map/ppermute | solution.py:277
  34.2 1.1 %collective-permute-done.13.refs_5_ = bf16[8,3712]{1,0:T(8,128)(2,1)S(1)} collective-permute-done((bf16[8,3712]{1,0:T(8,128)(2,1)S(1)}, bf16[8,3712]{1,0:T(8,128)(2,1)S(1)}, u32[]{:S(2)}, u32[]{:S(2)}) %collective-permute-start.13) | collective-permute-done | bytes 59424 | tf_op jit(solution)/shard_map/ppermute | solution.py:277
  35.3 0.4 last.1.refs_2_
  35.7 0.9 %collective-permute-start.14 = (bf16[8,3584]{1,0:T(8,128)(2,1)S(1)}, bf16[8,3584]{1,0:T(8,128)(2,1)S(1)}, u32[]{:S(2)}, u32[]{:S(2)}) collective-permute-start(bf16[8,3584]{1,0:T(8,128)(2,1)S(1)} %last.1.refs_2_), channel_id=1, source_target_pairs={{0,24},{2,26},{4,28},{6,30},{8,16},{10,18},{12,20},{14,22},{16,8},... | collective-permute-start | bytes 172040 | tf_op jit(solution)/shard_map/ppermute | solution.py:277
  36.5 1.3 %collective-permute-start.15 = (bf16[8,3584]{1,0:T(8,128)(2,1)S(1)}, bf16[8,3584]{1,0:T(8,128)(2,1)S(1)}, u32[]{:S(2)}, u32[]{:S(2)}) collective-permute-start(bf16[8,3584]{1,0:T(8,128)(2,1)S(1)} %last.1.refs_2_), channel_id=1, source_target_pairs={{0,16},{2,18},{4,20},{6,22},{8,24},{10,26},{12,28},{14,30},{16,0},... | collective-permute-start | bytes 172040 | tf_op jit(solution)/shard_map/ppermute | solution.py:277
  37.8 2.3 %collective-permute-start.16 = (bf16[8,3584]{1,0:T(8,128)(2,1)S(1)}, bf16[8,3584]{1,0:T(8,128)(2,1)S(1)}, u32[]{:S(2)}, u32[]{:S(2)}) collective-permute-start(bf16[8,3584]{1,0:T(8,128)(2,1)S(1)} %last.1.refs_2_), channel_id=1, source_target_pairs={{0,8},{2,10},{4,12},{6,14},{8,0},{10,2},{12,4},{14,6},{16,24},{18,... | collective-permute-start | bytes 172040 | tf_op jit(solution)/shard_map/ppermute | solution.py:277
  40.1 0.6 %collective-permute-start.17 = (bf16[8,3584]{1,0:T(8,128)(2,1)S(1)}, bf16[8,3584]{1,0:T(8,128)(2,1)S(1)}, u32[]{:S(2)}, u32[]{:S(2)}) collective-permute-start(bf16[8,3584]{1,0:T(8,128)(2,1)S(1)} %last.1.refs_2_), channel_id=1, source_target_pairs={{0,12},{2,14},{4,8},{6,10},{8,4},{10,6},{12,0},{14,2},{16,28},{18,... | collective-permute-start | bytes 172040 | tf_op jit(solution)/shard_map/ppermute | solution.py:277
  40.7 1.6 %collective-permute-done.14.refs_0_ = bf16[8,3584]{1,0:T(8,128)(2,1)S(1)} collective-permute-done((bf16[8,3584]{1,0:T(8,128)(2,1)S(1)}, bf16[8,3584]{1,0:T(8,128)(2,1)S(1)}, u32[]{:S(2)}, u32[]{:S(2)}) %collective-permute-start.14) | collective-permute-done | bytes 57376 | tf_op jit(solution)/shard_map/ppermute | solution.py:277
  42.3 1.9 %collective-permute-start.18 = (bf16[24,3584]{1,0:T(8,128)(2,1)S(1)}, bf16[24,3584]{1,0:T(8,128)(2,1)S(1)}, u32[]{:S(2)}, u32[]{:S(2)}) collective-permute-start(bf16[24,3584]{1,0:T(8,128)(2,1)S(1)} %pack.8.refs_0_), channel_id=1, source_target_pairs={{0,4},{2,6},{4,0},{6,2},{8,12},{10,14},{12,8},{14,10},{16,20},{18,... | collective-permute-start | bytes 516104 | tf_op jit(solution)/shard_map/ppermute | solution.py:277
  44.2 1.0 %collective-permute-done.17.refs_2_ = bf16[8,3584]{1,0:T(8,128)(2,1)S(1)} collective-permute-done((bf16[8,3584]{1,0:T(8,128)(2,1)S(1)}, bf16[8,3584]{1,0:T(8,128)(2,1)S(1)}, u32[]{:S(2)}, u32[]{:S(2)}) %collective-permute-start.17) | collective-permute-done | bytes 57376 | tf_op jit(solution)/shard_map/ppermute | solution.py:277
  45.2 0.1 collective-permute-start.19
  45.3 2.5 %collective-permute-done.18.refs_1_ = bf16[24,3584]{1,0:T(8,128)(2,1)S(1)} collective-permute-done((bf16[24,3584]{1,0:T(8,128)(2,1)S(1)}, bf16[24,3584]{1,0:T(8,128)(2,1)S(1)}, u32[]{:S(2)}, u32[]{:S(2)}) %collective-permute-start.18) | collective-permute-done | bytes 172064 | tf_op jit(solution)/shard_map/ppermute | solution.py:277
  47.8 1.4 %collective-permute-done.20.refs_3_ = bf16[24,3584]{1,0:T(8,128)(2,1)S(1)} collective-permute-done((bf16[24,3584]{1,0:T(8,128)(2,1)S(1)}, bf16[24,3584]{1,0:T(8,128)(2,1)S(1)}, u32[]{:S(2)}, u32[]{:S(2)}) %collective-permute-start.20) | collective-permute-done | bytes 172064 | tf_op jit(solution)/shard_map/ppermute | solution.py:277
  49.2 1.1 %project.1 = (f32[64,448]{1,0:T(8,128)S(1)}, bf16[64,448]{1,0:T(8,128)(2,1)S(1)}) custom-call(bf16[40,3584]{1,0:T(8,128)(2,1)S(1)} %pack.9.refs_0_, bf16[24,3584]{1,0:T(8,128)(2,1)S(1)} %collective-permute-done.18.refs_1_, bf16[40,3584]{1,0:T(8,128)(2,1)S(1)} %collective-permute-done.19.refs_2_, bf16[24,3584]{1,0:T(8,128)(2,1)S(1)} %collective-permute-done.20.refs_3_, ...), custom_call_target="tpu_custom_call" | custom-call | tf_op jit(solution)/shard_map/project/pallas_call | solution.py:305
  50.3 1.6 %collective-permute-start.21 = (bf16[64,448]{1,0:T(8,128)(2,1)S(1)}, bf16[64,448]{1,0:T(8,128)(2,1)S(1)}, u32[]{:S(2)}, u32[]{:S(2)}) collective-permute-start(bf16[64,448]{1,0:T(8,128)(2,1)S(1)} %get-tuple-element.36), channel_id=1, source_target_pairs={{0,1},{1,0},{2,3},{3,2},{4,5},{5,4},{6,7},{7,6},{8,9},{9,8},{10,11... | collective-permute-start | bytes 172040 | tf_op jit(solution)/shard_map/ppermute | solution.py:277
  52.0 2.7 %collective-permute-done.21.refs_0_ = bf16[64,448]{1,0:T(8,128)(2,1)S(1)} collective-permute-done((bf16[64,448]{1,0:T(8,128)(2,1)S(1)}, bf16[64,448]{1,0:T(8,128)(2,1)S(1)}, u32[]{:S(2)}, u32[]{:S(2)}) %collective-permute-start.21) | collective-permute-done | bytes 57376 | tf_op jit(solution)/shard_map/ppermute | solution.py:277
  54.7 0.6 %final.1 = bf16[64,448]{1,0:T(8,128)(2,1)} custom-call(f32[64,448]{1,0:T(8,128)S(1)} %base.1.total, bf16[64,448]{1,0:T(8,128)(2,1)S(1)} %collective-permute-done.21.refs_0_), custom_call_target="tpu_custom_call" | custom-call | tf_op jit(solution)/shard_map/final/pallas_call | solution.py:305
  (35 shorter events, 0.2 us)
Async XLA Ops:
  0.0 15.3 %copy-start = (bf16[384,3584]{1,0:T(8,128)(2,1)S(1)}, bf16[384,3584]{1,0:T(8,128)(2,1)}, u32[]{:S(2)}) copy-start(bf16[384,3584]{1,0:T(8,128)(2,1)} %keys.1) | copy-start | bytes 8257540
  0.0 9.8 %collective-permute-start = (bf16[8,3584]{1,0:T(8,128)(2,1)}, bf16[8,3584]{1,0:T(8,128)(2,1)S(1)}, u32[]{:S(2)}, u32[]{:S(2)}) collective-permute-start(bf16[8,3584]{1,0:T(8,128)(2,1)} %queries.1), channel_id=1, source_target_pairs={{0,24},{2,26},{4,28},{6,30},{8,16},{10,18},{12,20},{14,22},{16,8},... | collective-permute-start | bytes 172040 | tf_op jit(solution)/shard_map/ppermute | solution.py:277
  5.1 5.3 %collective-permute-start.1 = (bf16[8,3584]{1,0:T(8,128)(2,1)}, bf16[8,3584]{1,0:T(8,128)(2,1)S(1)}, u32[]{:S(2)}, u32[]{:S(2)}) collective-permute-start(bf16[8,3584]{1,0:T(8,128)(2,1)} %queries.1), channel_id=1, source_target_pairs={{0,16},{2,18},{4,20},{6,22},{8,24},{10,26},{12,28},{14,30},{16,0},... | collective-permute-start | bytes 172040 | tf_op jit(solution)/shard_map/ppermute | solution.py:277
  5.1 8.6 %collective-permute-start.2 = (bf16[8,3584]{1,0:T(8,128)(2,1)}, bf16[8,3584]{1,0:T(8,128)(2,1)S(1)}, u32[]{:S(2)}, u32[]{:S(2)}) collective-permute-start(bf16[8,3584]{1,0:T(8,128)(2,1)} %queries.1), channel_id=1, source_target_pairs={{0,8},{2,10},{4,12},{6,14},{8,0},{10,2},{12,4},{14,6},{16,24},{18,... | collective-permute-start | bytes 172040 | tf_op jit(solution)/shard_map/ppermute | solution.py:277
  5.7 8.0 %collective-permute-start.3 = (bf16[8,3584]{1,0:T(8,128)(2,1)}, bf16[8,3584]{1,0:T(8,128)(2,1)S(1)}, u32[]{:S(2)}, u32[]{:S(2)}) collective-permute-start(bf16[8,3584]{1,0:T(8,128)(2,1)} %queries.1), channel_id=1, source_target_pairs={{0,12},{2,14},{4,8},{6,10},{8,4},{10,6},{12,0},{14,2},{16,28},{18,... | collective-permute-start | bytes 172040 | tf_op jit(solution)/shard_map/ppermute | solution.py:277
  8.0 0.9 %copy-start.6 = (bf16[8,3584]{1,0:T(8,128)(2,1)S(1)}, bf16[8,3584]{1,0:T(8,128)(2,1)}, u32[]{:S(2)}) copy-start(bf16[8,3584]{1,0:T(8,128)(2,1)} %queries.1) | copy-start | bytes 172036
  8.9 0.8 %copy-start.7 = (bf16[8,3584]{1,0:T(8,128)(2,1)S(1)}, bf16[8,3584]{1,0:T(8,128)(2,1)}, u32[]{:S(2)}) copy-start(bf16[8,3584]{1,0:T(8,128)(2,1)} %new_keys.1) | copy-start | bytes 172036
  10.4 5.7 %collective-permute-start.4 = (bf16[24,3584]{1,0:T(8,128)(2,1)S(1)}, bf16[24,3584]{1,0:T(8,128)(2,1)S(1)}, u32[]{:S(2)}, u32[]{:S(2)}) collective-permute-start(bf16[24,3584]{1,0:T(8,128)(2,1)S(1)} %pack.5.refs_0_), channel_id=1, source_target_pairs={{0,4},{2,6},{4,0},{6,2},{8,12},{10,14},{12,8},{14,10},{16,20},{18,... | collective-permute-start | bytes 516104 | tf_op jit(solution)/shard_map/ppermute | solution.py:277
  11.9 1.8 %copy-start.1 = (bf16[384,3584]{1,0:T(8,128)(2,1)S(1)}, bf16[384,3584]{1,0:T(8,128)(2,1)}, u32[]{:S(2)}) copy-start(bf16[384,3584]{1,0:T(8,128)(2,1)} %values.1) | copy-start | bytes 8257540
  13.7 3.8 %copy-start.2 = (bf16[384,3584]{1,0:T(8,128)(2,1)S(1)}, bf16[384,3584]{1,0:T(8,128)(2,1)}, u32[]{:S(2)}) copy-start(bf16[384,3584]{1,0:T(8,128)(2,1)} %values.1) | copy-start | bytes 8257540
  13.7 2.4 %collective-permute-start.5 = (bf16[40,3584]{1,0:T(8,128)(2,1)S(1)}, bf16[40,3584]{1,0:T(8,128)(2,1)S(1)}, u32[]{:S(2)}, u32[]{:S(2)}) collective-permute-start(bf16[40,3584]{1,0:T(8,128)(2,1)S(1)} %pack.6.refs_0_), channel_id=1, source_target_pairs={{0,2},{2,0},{4,6},{6,4},{8,10},{10,8},{12,14},{14,12},{16,18},{18,... | collective-permute-start | bytes 860168 | tf_op jit(solution)/shard_map/ppermute | solution.py:277
  16.0 1.5 %collective-permute-start.6 = (bf16[24,3584]{1,0:T(8,128)(2,1)S(1)}, bf16[24,3584]{1,0:T(8,128)(2,1)S(1)}, u32[]{:S(2)}, u32[]{:S(2)}) collective-permute-start(bf16[24,3584]{1,0:T(8,128)(2,1)S(1)} %pack.7.refs_1_), channel_id=1, source_target_pairs={{0,2},{2,0},{4,6},{6,4},{8,10},{10,8},{12,14},{14,12},{16,18},{18,... | collective-permute-start | bytes 516104 | tf_op jit(solution)/shard_map/ppermute | solution.py:277
  17.5 17.8 %copy-start.5 = (bf16[8,3584]{1,0:T(8,128)(2,1)S(1)}, bf16[8,3584]{1,0:T(8,128)(2,1)}, u32[]{:S(2)}) copy-start(bf16[8,3584]{1,0:T(8,128)(2,1)} %refs_6_.1) | copy-start | bytes 172036
  17.5 31.7 %copy-start.3 = (bf16[3584,448]{0,1:T(8,128)(2,1)S(1)}, bf16[3584,448]{0,1:T(8,128)(2,1)}, u32[]{:S(2)}) copy-start(bf16[3584,448]{0,1:T(8,128)(2,1)} %param.17) | copy-start | bytes 9633796
  19.4 1.6 %collective-permute-start.7 = (bf16[32,3712]{1,0:T(8,128)(2,1)S(1)}, bf16[32,3712]{1,0:T(8,128)(2,1)S(1)}, u32[]{:S(2)}, u32[]{:S(2)}) collective-permute-start(bf16[32,3712]{1,0:T(8,128)(2,1)S(1)} %get-tuple-element.25), channel_id=1, source_target_pairs={{0,2},{2,0},{4,6},{6,4},{8,10},{10,8},{12,14},{14,12},{16,18},{18,... | collective-permute-start | bytes 712712 | tf_op jit(solution)/shard_map/ppermute | solution.py:277
  19.6 3.2 %collective-permute-start.9 = (bf16[32,3712]{1,0:T(8,128)(2,1)S(1)}, bf16[32,3712]{1,0:T(8,128)(2,1)S(1)}, u32[]{:S(2)}, u32[]{:S(2)}) collective-permute-start(bf16[32,3712]{1,0:T(8,128)(2,1)S(1)} %get-tuple-element.28), channel_id=1, source_target_pairs={{0,2},{2,0},{4,6},{6,4},{8,10},{10,8},{12,14},{14,12},{16,18},{18,... | collective-permute-start | bytes 712712 | tf_op jit(solution)/shard_map/ppermute | solution.py:277
  21.3 6.6 %collective-permute-start.10 = (bf16[24,3712]{1,0:T(8,128)(2,1)S(1)}, bf16[24,3712]{1,0:T(8,128)(2,1)S(1)}, u32[]{:S(2)}, u32[]{:S(2)}) collective-permute-start(bf16[24,3712]{1,0:T(8,128)(2,1)S(1)} %get-tuple-element.30), channel_id=1, source_target_pairs={{0,4},{2,6},{4,0},{6,2},{8,12},{10,14},{12,8},{14,10},{16,20},{18,... | collective-permute-start | bytes 534536 | tf_op jit(solution)/shard_map/ppermute | solution.py:277
  23.1 8.3 %collective-permute-start.11 = (bf16[8,3712]{1,0:T(8,128)(2,1)S(1)}, bf16[8,3712]{1,0:T(8,128)(2,1)S(1)}, u32[]{:S(2)}, u32[]{:S(2)}) collective-permute-start(bf16[8,3712]{1,0:T(8,128)(2,1)S(1)} %get-tuple-element.31), channel_id=1, source_target_pairs={{0,24},{2,26},{4,28},{6,30},{8,16},{10,18},{12,20},{14,22},{16,8},... | collective-permute-start | bytes 178184 | tf_op jit(solution)/shard_map/ppermute | solution.py:277
  25.6 7.5 %collective-permute-start.8 = (bf16[8,3712]{1,0:T(8,128)(2,1)S(1)}, bf16[8,3712]{1,0:T(8,128)(2,1)S(1)}, u32[]{:S(2)}, u32[]{:S(2)}) collective-permute-start(bf16[8,3712]{1,0:T(8,128)(2,1)S(1)} %get-tuple-element.26), channel_id=1, source_target_pairs={{0,28},{2,30},{4,24},{6,26},{8,20},{10,22},{12,16},{14,18},{16,12}... | collective-permute-start | bytes 178184 | tf_op jit(solution)/shard_map/ppermute | solution.py:277
  28.1 6.1 %collective-permute-start.12 = (bf16[8,3712]{1,0:T(8,128)(2,1)S(1)}, bf16[8,3712]{1,0:T(8,128)(2,1)S(1)}, u32[]{:S(2)}, u32[]{:S(2)}) collective-permute-start(bf16[8,3712]{1,0:T(8,128)(2,1)S(1)} %get-tuple-element.33), channel_id=1, source_target_pairs={{0,16},{2,18},{4,20},{6,22},{8,24},{10,26},{12,28},{14,30},{16,0},... | collective-permute-start | bytes 178184 | tf_op jit(solution)/shard_map/ppermute | solution.py:277
  31.1 4.2 %collective-permute-start.13 = (bf16[8,3712]{1,0:T(8,128)(2,1)S(1)}, bf16[8,3712]{1,0:T(8,128)(2,1)S(1)}, u32[]{:S(2)}, u32[]{:S(2)}) collective-permute-start(bf16[8,3712]{1,0:T(8,128)(2,1)S(1)} %get-tuple-element.34), channel_id=1, source_target_pairs={{0,8},{2,10},{4,12},{6,14},{8,0},{10,2},{12,4},{14,6},{16,24},{18,... | collective-permute-start | bytes 178184 | tf_op jit(solution)/shard_map/ppermute | solution.py:277
  35.3 16.7 %copy-start.8 = (bf16[448]{0:T(512)(128)(2,1)S(1)}, bf16[448]{0:T(512)(128)(2,1)}, u32[]{:S(2)}) copy-start(bf16[448]{0:T(512)(128)(2,1)} %param.18) | copy-start | bytes 2692
  35.3 16.7 %copy-start.4 = (bf16[64,448]{1,0:T(8,128)(2,1)S(1)}, bf16[64,448]{1,0:T(8,128)(2,1)}, u32[]{:S(2)}) copy-start(bf16[64,448]{1,0:T(8,128)(2,1)} %residual.1) | copy-start | bytes 172036
  35.7 6.6 %collective-permute-start.14 = (bf16[8,3584]{1,0:T(8,128)(2,1)S(1)}, bf16[8,3584]{1,0:T(8,128)(2,1)S(1)}, u32[]{:S(2)}, u32[]{:S(2)}) collective-permute-start(bf16[8,3584]{1,0:T(8,128)(2,1)S(1)} %last.1.refs_2_), channel_id=1, source_target_pairs={{0,24},{2,26},{4,28},{6,30},{8,16},{10,18},{12,20},{14,22},{16,8},... | collective-permute-start | bytes 172040 | tf_op jit(solution)/shard_map/ppermute | solution.py:277
  36.5 5.8 %collective-permute-start.15 = (bf16[8,3584]{1,0:T(8,128)(2,1)S(1)}, bf16[8,3584]{1,0:T(8,128)(2,1)S(1)}, u32[]{:S(2)}, u32[]{:S(2)}) collective-permute-start(bf16[8,3584]{1,0:T(8,128)(2,1)S(1)} %last.1.refs_2_), channel_id=1, source_target_pairs={{0,16},{2,18},{4,20},{6,22},{8,24},{10,26},{12,28},{14,30},{16,0},... | collective-permute-start | bytes 172040 | tf_op jit(solution)/shard_map/ppermute | solution.py:277
  37.8 6.4 %collective-permute-start.16 = (bf16[8,3584]{1,0:T(8,128)(2,1)S(1)}, bf16[8,3584]{1,0:T(8,128)(2,1)S(1)}, u32[]{:S(2)}, u32[]{:S(2)}) collective-permute-start(bf16[8,3584]{1,0:T(8,128)(2,1)S(1)} %last.1.refs_2_), channel_id=1, source_target_pairs={{0,8},{2,10},{4,12},{6,14},{8,0},{10,2},{12,4},{14,6},{16,24},{18,... | collective-permute-start | bytes 172040 | tf_op jit(solution)/shard_map/ppermute | solution.py:277
  40.1 5.1 %collective-permute-start.17 = (bf16[8,3584]{1,0:T(8,128)(2,1)S(1)}, bf16[8,3584]{1,0:T(8,128)(2,1)S(1)}, u32[]{:S(2)}, u32[]{:S(2)}) collective-permute-start(bf16[8,3584]{1,0:T(8,128)(2,1)S(1)} %last.1.refs_2_), channel_id=1, source_target_pairs={{0,12},{2,14},{4,8},{6,10},{8,4},{10,6},{12,0},{14,2},{16,28},{18,... | collective-permute-start | bytes 172040 | tf_op jit(solution)/shard_map/ppermute | solution.py:277
  42.3 5.5 %collective-permute-start.18 = (bf16[24,3584]{1,0:T(8,128)(2,1)S(1)}, bf16[24,3584]{1,0:T(8,128)(2,1)S(1)}, u32[]{:S(2)}, u32[]{:S(2)}) collective-permute-start(bf16[24,3584]{1,0:T(8,128)(2,1)S(1)} %pack.8.refs_0_), channel_id=1, source_target_pairs={{0,4},{2,6},{4,0},{6,2},{8,12},{10,14},{12,8},{14,10},{16,20},{18,... | collective-permute-start | bytes 516104 | tf_op jit(solution)/shard_map/ppermute | solution.py:277
  45.2 2.6 %collective-permute-start.19 = (bf16[40,3584]{1,0:T(8,128)(2,1)S(1)}, bf16[40,3584]{1,0:T(8,128)(2,1)S(1)}, u32[]{:S(2)}, u32[]{:S(2)}) collective-permute-start(bf16[40,3584]{1,0:T(8,128)(2,1)S(1)} %pack.9.refs_0_), channel_id=1, source_target_pairs={{0,2},{2,0},{4,6},{6,4},{8,10},{10,8},{12,14},{14,12},{16,18},{18,... | collective-permute-start | bytes 860168 | tf_op jit(solution)/shard_map/ppermute | solution.py:277
  47.8 1.4 %collective-permute-start.20 = (bf16[24,3584]{1,0:T(8,128)(2,1)S(1)}, bf16[24,3584]{1,0:T(8,128)(2,1)S(1)}, u32[]{:S(2)}, u32[]{:S(2)}) collective-permute-start(bf16[24,3584]{1,0:T(8,128)(2,1)S(1)} %collective-permute-done.18.refs_1_), channel_id=1, source_target_pairs={{0,2},{2,0},{4,6},{6,4},{8,10},{10,8},{12,14},{14,12},{16,18},{18,... | collective-permute-start | bytes 516104 | tf_op jit(solution)/shard_map/ppermute | solution.py:277
  50.3 4.3 %collective-permute-start.21 = (bf16[64,448]{1,0:T(8,128)(2,1)S(1)}, bf16[64,448]{1,0:T(8,128)(2,1)S(1)}, u32[]{:S(2)}, u32[]{:S(2)}) collective-permute-start(bf16[64,448]{1,0:T(8,128)(2,1)S(1)} %get-tuple-element.36), channel_id=1, source_target_pairs={{0,1},{1,0},{2,3},{3,2},{4,5},{5,4},{6,7},{7,6},{8,9},{9,8},{10,11... | collective-permute-start | bytes 172040 | tf_op jit(solution)/shard_map/ppermute | solution.py:277

commit v7 on v6

--- a/solution.py
+++ b/solution.py
@@ -152,7 +152,7 @@
         wide = jnp.concatenate([live] * len(each), axis=0)
         score = jnp.where(wide, score * (1.0 / math.sqrt(HD)), floor_score)
         top = jnp.max(score, axis=1, keepdims=True)
-        weight = jnp.where(wide, jnp.exp(score - top), 0.0).astype(bf16)
+        weight = jnp.exp(score - jnp.where(top > floor_score, top, 0.0)).astype(bf16)
         denom = jnp.sum(weight.astype(f32), axis=1, keepdims=True)
         denom = jnp.where(denom > 0.0, denom, 1.0)
         return weight, denom, top + jnp.log(denom)
@@ -232,15 +232,28 @@
             at += out.shape[0]
 
 
-def last_kernel(count, *refs):
+def early_kernel(count, *refs):
     ins = refs[:count]
     new_values, own_top, out = refs[count:]
     rows = out.shape[0]
-    head_of, _ = merge(
+    heads = new_values.shape[1] // HD
+    head_of, top = merge(
         [part_of(ref, ref.shape[0] - rows, rows) for ref in ins] + [part_of(new_values, 0, rows)],
         [top_of(ref, ref.shape[0] - rows, rows) for ref in ins] + [own_top[...]],
     )
-    for head in range(out.shape[1] // HD):
+    for head in range(heads):
+        out[:, head * HD : (head + 1) * HD] = head_of(head)
+    out[:, heads * HD :] = top
+
+
+def last_kernel(count, *refs):
+    ins, early, out = refs[:count], refs[count], refs[count + 1]
+    rows, width = out.shape
+    head_of, _ = merge(
+        [part_of(early, 0, rows)] + [part_of(ref, 0, rows) for ref in ins],
+        [early[:, width:]] + [top_of(ref, 0, rows) for ref in ins],
+    )
+    for head in range(width // HD):
         out[:, head * HD : (head + 1) * HD] = head_of(head).astype(bf16)
 
 
@@ -386,15 +399,23 @@
     *pair, own, straight = merged([outs[0], kv_hop(outs[mid], 1)], 2, 1, 1)
     pair = merged(pair + relays, 1, 1)
     ins += [own, *relays, kv_hop(straight, 2 * mid * REDUCE_ORDER[2])]
-    ins += [kv_hop(x, 2 * mid * far) for x, far in zip(pair, relayed(REDUCE_ORDER))]
+    early = call(
+        functools.partial(early_kernel, len(ins)),
+        shaped((own_rows, wide), f32),
+        [],
+        "early",
+        *ins,
+        new_values,
+        own_top,
+    )
+    ins = [kv_hop(x, 2 * mid * far) for x, far in zip(pair, relayed(REDUCE_ORDER))]
     attended = call(
         functools.partial(last_kernel, len(ins)),
         shaped((own_rows, width), bf16),
         [],
         "last",
         *ins,
-        new_values,
-        own_top,
+        early,
     )
 
     blocks = gather(attended, attended, RESULT_ORDER, [], [], [])

time: 55.6 us -> 55.4 us (level)
    pallas_call x18 -> x19, Pallas kernels: 5.23 us -> 5.42 us  [call(): pl.pallas_call(kernel, out_shape=shapes, in_specs=[spec(at) for at in ran...]
  transfers between devices with their start and end apart: 22 -> 22, of which waited for: 13 -> 13; matrix products, arithmetic and copies ran while one was open for 3% -> 3% of each run, Pallas kernels for 2% -> 3%
where the time goes in v7:
time: 55.4 us; the launch traced here: 55.2 us
  starting transfers between devices  27.5 us (50%)
  waiting for transfers between devices  17.1 us (31%)
  Pallas kernels  5.42 us (10%)
  local copies, waits for them, and re-layouts  5 us (9%)
    ppermute x22, starting transfers between devices, hop(): return lax.ppermute(x, axis, [(i, i ^ distance) for i in range(count)])  27.5 us
    ppermute x22, waiting for transfers between devices, hop(): return lax.ppermute(x, axis, [(i, i ^ distance) for i in range(count)])  17.1 us
    pallas_call x19, Pallas kernels, call(): pl.pallas_call(kernel, out_shape=shapes, in_specs=[spec(at) for at in ran...  5.42 us
    unnamed x18, local copies, waits for them, and re-layouts  3.47 us
  transfers between devices with their start and end apart: 22, of which 13 were waited for; matrix products, arithmetic and copies ran while one was open for 3% of the time, Pallas kernels for 3%

profile of v7, /device:TPU:0, one launch (start us, length us, event | category | flops | bytes accessed | tf_op | source)
XLA Modules:
  0.0 55.2 jit_solution(6605916211458639200)
XLA Ops:
  0.0 5.0 %collective-permute-start = (bf16[8,3584]{1,0:T(8,128)(2,1)}, bf16[8,3584]{1,0:T(8,128)(2,1)S(1)}, u32[]{:S(2)}, u32[]{:S(2)}) collective-permute-start(bf16[8,3584]{1,0:T(8,128)(2,1)} %queries.1), channel_id=1, source_target_pairs={{0,24},{2,26},{4,28},{6,30},{8,16},{10,18},{12,20},{14,22},{16,8},... | collective-permute-start | bytes 172040 | tf_op jit(solution)/shard_map/ppermute | solution.py:290
  5.1 0.6 %collective-permute-start.2 = (bf16[8,3584]{1,0:T(8,128)(2,1)}, bf16[8,3584]{1,0:T(8,128)(2,1)S(1)}, u32[]{:S(2)}, u32[]{:S(2)}) collective-permute-start(bf16[8,3584]{1,0:T(8,128)(2,1)} %queries.1), channel_id=1, source_target_pairs={{0,8},{2,10},{4,12},{6,14},{8,0},{10,2},{12,4},{14,6},{16,24},{18,... | collective-permute-start | bytes 172040 | tf_op jit(solution)/shard_map/ppermute | solution.py:290
  5.7 2.3 %collective-permute-start.3 = (bf16[8,3584]{1,0:T(8,128)(2,1)}, bf16[8,3584]{1,0:T(8,128)(2,1)S(1)}, u32[]{:S(2)}, u32[]{:S(2)}) collective-permute-start(bf16[8,3584]{1,0:T(8,128)(2,1)} %queries.1), channel_id=1, source_target_pairs={{0,12},{2,14},{4,8},{6,10},{8,4},{10,6},{12,0},{14,2},{16,28},{18,... | collective-permute-start | bytes 172040 | tf_op jit(solution)/shard_map/ppermute | solution.py:290
  8.0 0.9 %copy-done.6 = bf16[8,3584]{1,0:T(8,128)(2,1)S(1)} copy-done((bf16[8,3584]{1,0:T(8,128)(2,1)S(1)}, bf16[8,3584]{1,0:T(8,128)(2,1)}, u32[]{:S(2)}) %copy-start.6) | copy-done | bytes 57368
  8.9 0.8 %copy-done.7 = bf16[8,3584]{1,0:T(8,128)(2,1)S(1)} copy-done((bf16[8,3584]{1,0:T(8,128)(2,1)S(1)}, bf16[8,3584]{1,0:T(8,128)(2,1)}, u32[]{:S(2)}) %copy-start.7) | copy-done | bytes 57368
  9.7 0.1 own.1.refs_3_.refs_5_
  9.8 0.5 collective-permute-done.1.refs_1_
  10.4 1.6 %collective-permute-start.4 = (bf16[24,3584]{1,0:T(8,128)(2,1)S(1)}, bf16[24,3584]{1,0:T(8,128)(2,1)S(1)}, u32[]{:S(2)}, u32[]{:S(2)}) collective-permute-start(bf16[24,3584]{1,0:T(8,128)(2,1)S(1)} %pack.5.refs_0_), channel_id=1, source_target_pairs={{0,4},{2,6},{4,0},{6,2},{8,12},{10,14},{12,8},{14,10},{16,20},{18,... | collective-permute-start | bytes 516104 | tf_op jit(solution)/shard_map/ppermute | solution.py:290
  11.9 1.8 %copy-done.1 = bf16[384,3584]{1,0:T(8,128)(2,1)S(1)} copy-done((bf16[384,3584]{1,0:T(8,128)(2,1)S(1)}, bf16[384,3584]{1,0:T(8,128)(2,1)}, u32[]{:S(2)}) %copy-start.1) | copy-done | bytes 2752536
  13.7 0.1 collective-permute-start.5
  13.8 0.8 %reshape.10.valid = s32[1,384]{1,0:T(1,128)S(1)} reshape(s32[384]{0:T(512)} %param.16) | data formatting | bytes 3072 | tf_op jit(solution)/shard_map/reshape | solution.py:362
  14.7 0.7 %reshape.9.request = s32[1,384]{1,0:T(1,128)S(1)} reshape(s32[384]{0:T(512)} %param.15) | data formatting | bytes 3072 | tf_op jit(solution)/shard_map/reshape | solution.py:361
  15.3 0.1 prep.1
  15.4 0.6 %collective-permute-done.4.refs_0_ = bf16[24,3584]{1,0:T(8,128)(2,1)S(1)} collective-permute-done((bf16[24,3584]{1,0:T(8,128)(2,1)S(1)}, bf16[24,3584]{1,0:T(8,128)(2,1)S(1)}, u32[]{:S(2)}, u32[]{:S(2)}) %collective-permute-start.4) | collective-permute-done | bytes 172064 | tf_op jit(solution)/shard_map/ppermute | solution.py:290
  16.0 0.1 collective-permute-start.6
  16.1 1.4 %collective-permute-done.6.refs_3_ = bf16[24,3584]{1,0:T(8,128)(2,1)S(1)} collective-permute-done((bf16[24,3584]{1,0:T(8,128)(2,1)S(1)}, bf16[24,3584]{1,0:T(8,128)(2,1)S(1)}, u32[]{:S(2)}, u32[]{:S(2)}) %collective-permute-start.6) | collective-permute-done | bytes 172064 | tf_op jit(solution)/shard_map/ppermute | solution.py:290
  17.5 1.9 %attend.1 = (bf16[32,3712]{1,0:T(8,128)(2,1)S(1)}, bf16[32,3712]{1,0:T(8,128)(2,1)S(1)}, bf16[32,3712]{1,0:T(8,128)(2,1)S(1)}, bf16[32,3712]{1,0:T(8,128)(2,1)S(1)}) custom-call(bf16[32,128]{1,0:T(8,128)(2,1)S(1)} %get-tuple-element.21.refs_2_.pick, bf16[32,128]{1,0:T(8,128)(2,1)S(1)} %get-tuple-element.22.spread_to, f32[32,384]{1,0:T(8,128)S(1)} %get-tuple-element.23.mask, ...), custom_call_target="tpu_custom_call" | custom-call | tf_op jit(solution)/shard_map/attend/pallas_call | solution.py:318
  19.4 0.2 collective-permute-start.8
  19.6 0.4 collective-permute-start.7
  20.0 1.0 %collective-permute-done.8.refs_1_ = bf16[32,3712]{1,0:T(8,128)(2,1)S(1)} collective-permute-done((bf16[32,3712]{1,0:T(8,128)(2,1)S(1)}, bf16[32,3712]{1,0:T(8,128)(2,1)S(1)}, u32[]{:S(2)}, u32[]{:S(2)}) %collective-permute-start.8) | collective-permute-done | bytes 237600 | tf_op jit(solution)/shard_map/ppermute | solution.py:290
  20.9 0.3 merge.4
  21.3 1.4 %collective-permute-start.9 = (bf16[24,3712]{1,0:T(8,128)(2,1)S(1)}, bf16[24,3712]{1,0:T(8,128)(2,1)S(1)}, u32[]{:S(2)}, u32[]{:S(2)}) collective-permute-start(bf16[24,3712]{1,0:T(8,128)(2,1)S(1)} %get-tuple-element.29), channel_id=1, source_target_pairs={{0,4},{2,6},{4,0},{6,2},{8,12},{10,14},{12,8},{14,10},{16,20},{18,... | collective-permute-start | bytes 534536 | tf_op jit(solution)/shard_map/ppermute | solution.py:290
  22.7 0.3 merge.3
  23.1 2.6 %collective-permute-start.13 = (bf16[8,3712]{1,0:T(8,128)(2,1)S(1)}, bf16[8,3712]{1,0:T(8,128)(2,1)S(1)}, u32[]{:S(2)}, u32[]{:S(2)}) collective-permute-start(bf16[8,3712]{1,0:T(8,128)(2,1)S(1)} %get-tuple-element.34), channel_id=1, source_target_pairs={{0,24},{2,26},{4,28},{6,30},{8,16},{10,18},{12,20},{14,22},{16,8},... | collective-permute-start | bytes 178184 | tf_op jit(solution)/shard_map/ppermute | solution.py:290
  25.6 1.4 %collective-permute-start.12 = (bf16[8,3712]{1,0:T(8,128)(2,1)S(1)}, bf16[8,3712]{1,0:T(8,128)(2,1)S(1)}, u32[]{:S(2)}, u32[]{:S(2)}) collective-permute-start(bf16[8,3712]{1,0:T(8,128)(2,1)S(1)} %get-tuple-element.32), channel_id=1, source_target_pairs={{0,28},{2,30},{4,24},{6,26},{8,20},{10,22},{12,16},{14,18},{16,12}... | collective-permute-start | bytes 178184 | tf_op jit(solution)/shard_map/ppermute | solution.py:290
  27.0 0.9 %collective-permute-done.9.refs_1_.refs_2_ = bf16[24,3712]{1,0:T(8,128)(2,1)S(1)} collective-permute-done((bf16[24,3712]{1,0:T(8,128)(2,1)S(1)}, bf16[24,3712]{1,0:T(8,128)(2,1)S(1)}, u32[]{:S(2)}, u32[]{:S(2)}) %collective-permute-start.9) | collective-permute-done | bytes 178208 | tf_op jit(solution)/shard_map/ppermute | solution.py:290
  27.9 0.3 merge.5
  28.2 2.9 %collective-permute-start.10 = (bf16[8,3712]{1,0:T(8,128)(2,1)S(1)}, bf16[8,3712]{1,0:T(8,128)(2,1)S(1)}, u32[]{:S(2)}, u32[]{:S(2)}) collective-permute-start(bf16[8,3712]{1,0:T(8,128)(2,1)S(1)} %get-tuple-element.30), channel_id=1, source_target_pairs={{0,16},{2,18},{4,20},{6,22},{8,24},{10,26},{12,28},{14,30},{16,0},... | collective-permute-start | bytes 178184 | tf_op jit(solution)/shard_map/ppermute | solution.py:290
  31.1 0.3 collective-permute-start.11
  31.4 1.7 %collective-permute-done.12.refs_0_ = bf16[8,3712]{1,0:T(8,128)(2,1)S(1)} collective-permute-done((bf16[8,3712]{1,0:T(8,128)(2,1)S(1)}, bf16[8,3712]{1,0:T(8,128)(2,1)S(1)}, u32[]{:S(2)}, u32[]{:S(2)}) %collective-permute-start.12) | collective-permute-done | bytes 59424 | tf_op jit(solution)/shard_map/ppermute | solution.py:290
  33.1 0.3 early.1.refs_2_
  33.4 0.8 %collective-permute-done.10.refs_0_ = bf16[8,3712]{1,0:T(8,128)(2,1)S(1)} collective-permute-done((bf16[8,3712]{1,0:T(8,128)(2,1)S(1)}, bf16[8,3712]{1,0:T(8,128)(2,1)S(1)}, u32[]{:S(2)}, u32[]{:S(2)}) %collective-permute-start.10) | collective-permute-done | bytes 59424 | tf_op jit(solution)/shard_map/ppermute | solution.py:290
  34.2 1.1 %collective-permute-done.11.refs_1_ = bf16[8,3712]{1,0:T(8,128)(2,1)S(1)} collective-permute-done((bf16[8,3712]{1,0:T(8,128)(2,1)S(1)}, bf16[8,3712]{1,0:T(8,128)(2,1)S(1)}, u32[]{:S(2)}, u32[]{:S(2)}) %collective-permute-start.11) | collective-permute-done | bytes 59424 | tf_op jit(solution)/shard_map/ppermute | solution.py:290
  35.3 0.3 last.1.refs_2_
  35.5 0.8 %collective-permute-start.14 = (bf16[8,3584]{1,0:T(8,128)(2,1)S(1)}, bf16[8,3584]{1,0:T(8,128)(2,1)S(1)}, u32[]{:S(2)}, u32[]{:S(2)}) collective-permute-start(bf16[8,3584]{1,0:T(8,128)(2,1)S(1)} %last.1.refs_2_), channel_id=1, source_target_pairs={{0,24},{2,26},{4,28},{6,30},{8,16},{10,18},{12,20},{14,22},{16,8},... | collective-permute-start | bytes 172040 | tf_op jit(solution)/shard_map/ppermute | solution.py:290
  36.4 1.3 %collective-permute-start.15 = (bf16[8,3584]{1,0:T(8,128)(2,1)S(1)}, bf16[8,3584]{1,0:T(8,128)(2,1)S(1)}, u32[]{:S(2)}, u32[]{:S(2)}) collective-permute-start(bf16[8,3584]{1,0:T(8,128)(2,1)S(1)} %last.1.refs_2_), channel_id=1, source_target_pairs={{0,16},{2,18},{4,20},{6,22},{8,24},{10,26},{12,28},{14,30},{16,0},... | collective-permute-start | bytes 172040 | tf_op jit(solution)/shard_map/ppermute | solution.py:290
  37.7 2.3 %collective-permute-start.16 = (bf16[8,3584]{1,0:T(8,128)(2,1)S(1)}, bf16[8,3584]{1,0:T(8,128)(2,1)S(1)}, u32[]{:S(2)}, u32[]{:S(2)}) collective-permute-start(bf16[8,3584]{1,0:T(8,128)(2,1)S(1)} %last.1.refs_2_), channel_id=1, source_target_pairs={{0,8},{2,10},{4,12},{6,14},{8,0},{10,2},{12,4},{14,6},{16,24},{18,... | collective-permute-start | bytes 172040 | tf_op jit(solution)/shard_map/ppermute | solution.py:290
  40.0 0.6 %collective-permute-start.17 = (bf16[8,3584]{1,0:T(8,128)(2,1)S(1)}, bf16[8,3584]{1,0:T(8,128)(2,1)S(1)}, u32[]{:S(2)}, u32[]{:S(2)}) collective-permute-start(bf16[8,3584]{1,0:T(8,128)(2,1)S(1)} %last.1.refs_2_), channel_id=1, source_target_pairs={{0,12},{2,14},{4,8},{6,10},{8,4},{10,6},{12,0},{14,2},{16,28},{18,... | collective-permute-start | bytes 172040 | tf_op jit(solution)/shard_map/ppermute | solution.py:290
  40.6 1.6 %collective-permute-done.14.refs_0_ = bf16[8,3584]{1,0:T(8,128)(2,1)S(1)} collective-permute-done((bf16[8,3584]{1,0:T(8,128)(2,1)S(1)}, bf16[8,3584]{1,0:T(8,128)(2,1)S(1)}, u32[]{:S(2)}, u32[]{:S(2)}) %collective-permute-start.14) | collective-permute-done | bytes 57376 | tf_op jit(solution)/shard_map/ppermute | solution.py:290
  42.2 1.9 %collective-permute-start.18 = (bf16[24,3584]{1,0:T(8,128)(2,1)S(1)}, bf16[24,3584]{1,0:T(8,128)(2,1)S(1)}, u32[]{:S(2)}, u32[]{:S(2)}) collective-permute-start(bf16[24,3584]{1,0:T(8,128)(2,1)S(1)} %pack.8.refs_0_), channel_id=1, source_target_pairs={{0,4},{2,6},{4,0},{6,2},{8,12},{10,14},{12,8},{14,10},{16,20},{18,... | collective-permute-start | bytes 516104 | tf_op jit(solution)/shard_map/ppermute | solution.py:290
  44.1 1.0 %collective-permute-done.17.refs_2_ = bf16[8,3584]{1,0:T(8,128)(2,1)S(1)} collective-permute-done((bf16[8,3584]{1,0:T(8,128)(2,1)S(1)}, bf16[8,3584]{1,0:T(8,128)(2,1)S(1)}, u32[]{:S(2)}, u32[]{:S(2)}) %collective-permute-start.17) | collective-permute-done | bytes 57376 | tf_op jit(solution)/shard_map/ppermute | solution.py:290
  45.1 0.1 collective-permute-start.19
  45.2 2.5 %collective-permute-done.18.refs_1_ = bf16[24,3584]{1,0:T(8,128)(2,1)S(1)} collective-permute-done((bf16[24,3584]{1,0:T(8,128)(2,1)S(1)}, bf16[24,3584]{1,0:T(8,128)(2,1)S(1)}, u32[]{:S(2)}, u32[]{:S(2)}) %collective-permute-start.18) | collective-permute-done | bytes 172064 | tf_op jit(solution)/shard_map/ppermute | solution.py:290
  47.7 1.4 %collective-permute-done.20.refs_3_ = bf16[24,3584]{1,0:T(8,128)(2,1)S(1)} collective-permute-done((bf16[24,3584]{1,0:T(8,128)(2,1)S(1)}, bf16[24,3584]{1,0:T(8,128)(2,1)S(1)}, u32[]{:S(2)}, u32[]{:S(2)}) %collective-permute-start.20) | collective-permute-done | bytes 172064 | tf_op jit(solution)/shard_map/ppermute | solution.py:290
  49.1 1.1 %project.1 = (f32[64,448]{1,0:T(8,128)S(1)}, bf16[64,448]{1,0:T(8,128)(2,1)S(1)}) custom-call(bf16[40,3584]{1,0:T(8,128)(2,1)S(1)} %pack.9.refs_0_, bf16[24,3584]{1,0:T(8,128)(2,1)S(1)} %collective-permute-done.18.refs_1_, bf16[40,3584]{1,0:T(8,128)(2,1)S(1)} %collective-permute-done.19.refs_2_, bf16[24,3584]{1,0:T(8,128)(2,1)S(1)} %collective-permute-done.20.refs_3_, ...), custom_call_target="tpu_custom_call" | custom-call | tf_op jit(solution)/shard_map/project/pallas_call | solution.py:318
  50.2 1.6 %collective-permute-start.21 = (bf16[64,448]{1,0:T(8,128)(2,1)S(1)}, bf16[64,448]{1,0:T(8,128)(2,1)S(1)}, u32[]{:S(2)}, u32[]{:S(2)}) collective-permute-start(bf16[64,448]{1,0:T(8,128)(2,1)S(1)} %get-tuple-element.36), channel_id=1, source_target_pairs={{0,1},{1,0},{2,3},{3,2},{4,5},{5,4},{6,7},{7,6},{8,9},{9,8},{10,11... | collective-permute-start | bytes 172040 | tf_op jit(solution)/shard_map/ppermute | solution.py:290
  51.8 2.7 %collective-permute-done.21.refs_0_ = bf16[64,448]{1,0:T(8,128)(2,1)S(1)} collective-permute-done((bf16[64,448]{1,0:T(8,128)(2,1)S(1)}, bf16[64,448]{1,0:T(8,128)(2,1)S(1)}, u32[]{:S(2)}, u32[]{:S(2)}) %collective-permute-start.21) | collective-permute-done | bytes 57376 | tf_op jit(solution)/shard_map/ppermute | solution.py:290
  54.5 0.6 %final.1 = bf16[64,448]{1,0:T(8,128)(2,1)} custom-call(f32[64,448]{1,0:T(8,128)S(1)} %base.1.total, bf16[64,448]{1,0:T(8,128)(2,1)S(1)} %collective-permute-done.21.refs_0_), custom_call_target="tpu_custom_call" | custom-call | tf_op jit(solution)/shard_map/final/pallas_call | solution.py:318
  (36 shorter events, 0.2 us)
Async XLA Ops:
  0.0 15.3 %copy-start = (bf16[384,3584]{1,0:T(8,128)(2,1)S(1)}, bf16[384,3584]{1,0:T(8,128)(2,1)}, u32[]{:S(2)}) copy-start(bf16[384,3584]{1,0:T(8,128)(2,1)} %keys.1) | copy-start | bytes 8257540
  0.0 9.8 %collective-permute-start = (bf16[8,3584]{1,0:T(8,128)(2,1)}, bf16[8,3584]{1,0:T(8,128)(2,1)S(1)}, u32[]{:S(2)}, u32[]{:S(2)}) collective-permute-start(bf16[8,3584]{1,0:T(8,128)(2,1)} %queries.1), channel_id=1, source_target_pairs={{0,24},{2,26},{4,28},{6,30},{8,16},{10,18},{12,20},{14,22},{16,8},... | collective-permute-start | bytes 172040 | tf_op jit(solution)/shard_map/ppermute | solution.py:290
  5.1 5.3 %collective-permute-start.1 = (bf16[8,3584]{1,0:T(8,128)(2,1)}, bf16[8,3584]{1,0:T(8,128)(2,1)S(1)}, u32[]{:S(2)}, u32[]{:S(2)}) collective-permute-start(bf16[8,3584]{1,0:T(8,128)(2,1)} %queries.1), channel_id=1, source_target_pairs={{0,16},{2,18},{4,20},{6,22},{8,24},{10,26},{12,28},{14,30},{16,0},... | collective-permute-start | bytes 172040 | tf_op jit(solution)/shard_map/ppermute | solution.py:290
  5.1 8.6 %collective-permute-start.2 = (bf16[8,3584]{1,0:T(8,128)(2,1)}, bf16[8,3584]{1,0:T(8,128)(2,1)S(1)}, u32[]{:S(2)}, u32[]{:S(2)}) collective-permute-start(bf16[8,3584]{1,0:T(8,128)(2,1)} %queries.1), channel_id=1, source_target_pairs={{0,8},{2,10},{4,12},{6,14},{8,0},{10,2},{12,4},{14,6},{16,24},{18,... | collective-permute-start | bytes 172040 | tf_op jit(solution)/shard_map/ppermute | solution.py:290
  5.7 8.0 %collective-permute-start.3 = (bf16[8,3584]{1,0:T(8,128)(2,1)}, bf16[8,3584]{1,0:T(8,128)(2,1)S(1)}, u32[]{:S(2)}, u32[]{:S(2)}) collective-permute-start(bf16[8,3584]{1,0:T(8,128)(2,1)} %queries.1), channel_id=1, source_target_pairs={{0,12},{2,14},{4,8},{6,10},{8,4},{10,6},{12,0},{14,2},{16,28},{18,... | collective-permute-start | bytes 172040 | tf_op jit(solution)/shard_map/ppermute | solution.py:290
  8.0 0.9 %copy-start.6 = (bf16[8,3584]{1,0:T(8,128)(2,1)S(1)}, bf16[8,3584]{1,0:T(8,128)(2,1)}, u32[]{:S(2)}) copy-start(bf16[8,3584]{1,0:T(8,128)(2,1)} %queries.1) | copy-start | bytes 172036
  8.9 0.8 %copy-start.7 = (bf16[8,3584]{1,0:T(8,128)(2,1)S(1)}, bf16[8,3584]{1,0:T(8,128)(2,1)}, u32[]{:S(2)}) copy-start(bf16[8,3584]{1,0:T(8,128)(2,1)} %new_keys.1) | copy-start | bytes 172036
  10.4 5.7 %collective-permute-start.4 = (bf16[24,3584]{1,0:T(8,128)(2,1)S(1)}, bf16[24,3584]{1,0:T(8,128)(2,1)S(1)}, u32[]{:S(2)}, u32[]{:S(2)}) collective-permute-start(bf16[24,3584]{1,0:T(8,128)(2,1)S(1)} %pack.5.refs_0_), channel_id=1, source_target_pairs={{0,4},{2,6},{4,0},{6,2},{8,12},{10,14},{12,8},{14,10},{16,20},{18,... | collective-permute-start | bytes 516104 | tf_op jit(solution)/shard_map/ppermute | solution.py:290
  11.9 1.8 %copy-start.1 = (bf16[384,3584]{1,0:T(8,128)(2,1)S(1)}, bf16[384,3584]{1,0:T(8,128)(2,1)}, u32[]{:S(2)}) copy-start(bf16[384,3584]{1,0:T(8,128)(2,1)} %values.1) | copy-start | bytes 8257540
  13.7 3.8 %copy-start.2 = (bf16[384,3584]{1,0:T(8,128)(2,1)S(1)}, bf16[384,3584]{1,0:T(8,128)(2,1)}, u32[]{:S(2)}) copy-start(bf16[384,3584]{1,0:T(8,128)(2,1)} %values.1) | copy-start | bytes 8257540
  13.7 2.4 %collective-permute-start.5 = (bf16[40,3584]{1,0:T(8,128)(2,1)S(1)}, bf16[40,3584]{1,0:T(8,128)(2,1)S(1)}, u32[]{:S(2)}, u32[]{:S(2)}) collective-permute-start(bf16[40,3584]{1,0:T(8,128)(2,1)S(1)} %pack.6.refs_0_), channel_id=1, source_target_pairs={{0,2},{2,0},{4,6},{6,4},{8,10},{10,8},{12,14},{14,12},{16,18},{18,... | collective-permute-start | bytes 860168 | tf_op jit(solution)/shard_map/ppermute | solution.py:290
  16.0 1.5 %collective-permute-start.6 = (bf16[24,3584]{1,0:T(8,128)(2,1)S(1)}, bf16[24,3584]{1,0:T(8,128)(2,1)S(1)}, u32[]{:S(2)}, u32[]{:S(2)}) collective-permute-start(bf16[24,3584]{1,0:T(8,128)(2,1)S(1)} %pack.7.refs_1_), channel_id=1, source_target_pairs={{0,2},{2,0},{4,6},{6,4},{8,10},{10,8},{12,14},{14,12},{16,18},{18,... | collective-permute-start | bytes 516104 | tf_op jit(solution)/shard_map/ppermute | solution.py:290
  17.5 15.6 %copy-start.5 = (bf16[8,3584]{1,0:T(8,128)(2,1)S(1)}, bf16[8,3584]{1,0:T(8,128)(2,1)}, u32[]{:S(2)}) copy-start(bf16[8,3584]{1,0:T(8,128)(2,1)} %refs_4_.1) | copy-start | bytes 172036
  17.5 31.6 %copy-start.3 = (bf16[3584,448]{0,1:T(8,128)(2,1)S(1)}, bf16[3584,448]{0,1:T(8,128)(2,1)}, u32[]{:S(2)}) copy-start(bf16[3584,448]{0,1:T(8,128)(2,1)} %param.17) | copy-start | bytes 9633796
  19.4 1.6 %collective-permute-start.8 = (bf16[32,3712]{1,0:T(8,128)(2,1)S(1)}, bf16[32,3712]{1,0:T(8,128)(2,1)S(1)}, u32[]{:S(2)}, u32[]{:S(2)}) collective-permute-start(bf16[32,3712]{1,0:T(8,128)(2,1)S(1)} %get-tuple-element.28), channel_id=1, source_target_pairs={{0,2},{2,0},{4,6},{6,4},{8,10},{10,8},{12,14},{14,12},{16,18},{18,... | collective-permute-start | bytes 712712 | tf_op jit(solution)/shard_map/ppermute | solution.py:290
  19.6 3.1 %collective-permute-start.7 = (bf16[32,3712]{1,0:T(8,128)(2,1)S(1)}, bf16[32,3712]{1,0:T(8,128)(2,1)S(1)}, u32[]{:S(2)}, u32[]{:S(2)}) collective-permute-start(bf16[32,3712]{1,0:T(8,128)(2,1)S(1)} %get-tuple-element.25), channel_id=1, source_target_pairs={{0,2},{2,0},{4,6},{6,4},{8,10},{10,8},{12,14},{14,12},{16,18},{18,... | collective-permute-start | bytes 712712 | tf_op jit(solution)/shard_map/ppermute | solution.py:290
  21.3 6.6 %collective-permute-start.9 = (bf16[24,3712]{1,0:T(8,128)(2,1)S(1)}, bf16[24,3712]{1,0:T(8,128)(2,1)S(1)}, u32[]{:S(2)}, u32[]{:S(2)}) collective-permute-start(bf16[24,3712]{1,0:T(8,128)(2,1)S(1)} %get-tuple-element.29), channel_id=1, source_target_pairs={{0,4},{2,6},{4,0},{6,2},{8,12},{10,14},{12,8},{14,10},{16,20},{18,... | collective-permute-start | bytes 534536 | tf_op jit(solution)/shard_map/ppermute | solution.py:290
  23.1 8.3 %collective-permute-start.13 = (bf16[8,3712]{1,0:T(8,128)(2,1)S(1)}, bf16[8,3712]{1,0:T(8,128)(2,1)S(1)}, u32[]{:S(2)}, u32[]{:S(2)}) collective-permute-start(bf16[8,3712]{1,0:T(8,128)(2,1)S(1)} %get-tuple-element.34), channel_id=1, source_target_pairs={{0,24},{2,26},{4,28},{6,30},{8,16},{10,18},{12,20},{14,22},{16,8},... | collective-permute-start | bytes 178184 | tf_op jit(solution)/shard_map/ppermute | solution.py:290
  25.6 7.4 %collective-permute-start.12 = (bf16[8,3712]{1,0:T(8,128)(2,1)S(1)}, bf16[8,3712]{1,0:T(8,128)(2,1)S(1)}, u32[]{:S(2)}, u32[]{:S(2)}) collective-permute-start(bf16[8,3712]{1,0:T(8,128)(2,1)S(1)} %get-tuple-element.32), channel_id=1, source_target_pairs={{0,28},{2,30},{4,24},{6,26},{8,20},{10,22},{12,16},{14,18},{16,12}... | collective-permute-start | bytes 178184 | tf_op jit(solution)/shard_map/ppermute | solution.py:290
  28.2 6.1 %collective-permute-start.10 = (bf16[8,3712]{1,0:T(8,128)(2,1)S(1)}, bf16[8,3712]{1,0:T(8,128)(2,1)S(1)}, u32[]{:S(2)}, u32[]{:S(2)}) collective-permute-start(bf16[8,3712]{1,0:T(8,128)(2,1)S(1)} %get-tuple-element.30), channel_id=1, source_target_pairs={{0,16},{2,18},{4,20},{6,22},{8,24},{10,26},{12,28},{14,30},{16,0},... | collective-permute-start | bytes 178184 | tf_op jit(solution)/shard_map/ppermute | solution.py:290
  31.1 4.2 %collective-permute-start.11 = (bf16[8,3712]{1,0:T(8,128)(2,1)S(1)}, bf16[8,3712]{1,0:T(8,128)(2,1)S(1)}, u32[]{:S(2)}, u32[]{:S(2)}) collective-permute-start(bf16[8,3712]{1,0:T(8,128)(2,1)S(1)} %get-tuple-element.31), channel_id=1, source_target_pairs={{0,8},{2,10},{4,12},{6,14},{8,0},{10,2},{12,4},{14,6},{16,24},{18,... | collective-permute-start | bytes 178184 | tf_op jit(solution)/shard_map/ppermute | solution.py:290
  33.4 18.4 %copy-start.8 = (bf16[448]{0:T(512)(128)(2,1)S(1)}, bf16[448]{0:T(512)(128)(2,1)}, u32[]{:S(2)}) copy-start(bf16[448]{0:T(512)(128)(2,1)} %param.18) | copy-start | bytes 2692
  33.4 18.4 %copy-start.4 = (bf16[64,448]{1,0:T(8,128)(2,1)S(1)}, bf16[64,448]{1,0:T(8,128)(2,1)}, u32[]{:S(2)}) copy-start(bf16[64,448]{1,0:T(8,128)(2,1)} %residual.1) | copy-start | bytes 172036
  35.5 6.6 %collective-permute-start.14 = (bf16[8,3584]{1,0:T(8,128)(2,1)S(1)}, bf16[8,3584]{1,0:T(8,128)(2,1)S(1)}, u32[]{:S(2)}, u32[]{:S(2)}) collective-permute-start(bf16[8,3584]{1,0:T(8,128)(2,1)S(1)} %last.1.refs_2_), channel_id=1, source_target_pairs={{0,24},{2,26},{4,28},{6,30},{8,16},{10,18},{12,20},{14,22},{16,8},... | collective-permute-start | bytes 172040 | tf_op jit(solution)/shard_map/ppermute | solution.py:290
  36.4 5.8 %collective-permute-start.15 = (bf16[8,3584]{1,0:T(8,128)(2,1)S(1)}, bf16[8,3584]{1,0:T(8,128)(2,1)S(1)}, u32[]{:S(2)}, u32[]{:S(2)}) collective-permute-start(bf16[8,3584]{1,0:T(8,128)(2,1)S(1)} %last.1.refs_2_), channel_id=1, source_target_pairs={{0,16},{2,18},{4,20},{6,22},{8,24},{10,26},{12,28},{14,30},{16,0},... | collective-permute-start | bytes 172040 | tf_op jit(solution)/shard_map/ppermute | solution.py:290
  37.7 6.4 %collective-permute-start.16 = (bf16[8,3584]{1,0:T(8,128)(2,1)S(1)}, bf16[8,3584]{1,0:T(8,128)(2,1)S(1)}, u32[]{:S(2)}, u32[]{:S(2)}) collective-permute-start(bf16[8,3584]{1,0:T(8,128)(2,1)S(1)} %last.1.refs_2_), channel_id=1, source_target_pairs={{0,8},{2,10},{4,12},{6,14},{8,0},{10,2},{12,4},{14,6},{16,24},{18,... | collective-permute-start | bytes 172040 | tf_op jit(solution)/shard_map/ppermute | solution.py:290
  40.0 5.1 %collective-permute-start.17 = (bf16[8,3584]{1,0:T(8,128)(2,1)S(1)}, bf16[8,3584]{1,0:T(8,128)(2,1)S(1)}, u32[]{:S(2)}, u32[]{:S(2)}) collective-permute-start(bf16[8,3584]{1,0:T(8,128)(2,1)S(1)} %last.1.refs_2_), channel_id=1, source_target_pairs={{0,12},{2,14},{4,8},{6,10},{8,4},{10,6},{12,0},{14,2},{16,28},{18,... | collective-permute-start | bytes 172040 | tf_op jit(solution)/shard_map/ppermute | solution.py:290
  42.2 5.5 %collective-permute-start.18 = (bf16[24,3584]{1,0:T(8,128)(2,1)S(1)}, bf16[24,3584]{1,0:T(8,128)(2,1)S(1)}, u32[]{:S(2)}, u32[]{:S(2)}) collective-permute-start(bf16[24,3584]{1,0:T(8,128)(2,1)S(1)} %pack.8.refs_0_), channel_id=1, source_target_pairs={{0,4},{2,6},{4,0},{6,2},{8,12},{10,14},{12,8},{14,10},{16,20},{18,... | collective-permute-start | bytes 516104 | tf_op jit(solution)/shard_map/ppermute | solution.py:290
  45.1 2.6 %collective-permute-start.19 = (bf16[40,3584]{1,0:T(8,128)(2,1)S(1)}, bf16[40,3584]{1,0:T(8,128)(2,1)S(1)}, u32[]{:S(2)}, u32[]{:S(2)}) collective-permute-start(bf16[40,3584]{1,0:T(8,128)(2,1)S(1)} %pack.9.refs_0_), channel_id=1, source_target_pairs={{0,2},{2,0},{4,6},{6,4},{8,10},{10,8},{12,14},{14,12},{16,18},{18,... | collective-permute-start | bytes 860168 | tf_op jit(solution)/shard_map/ppermute | solution.py:290
  47.7 1.4 %collective-permute-start.20 = (bf16[24,3584]{1,0:T(8,128)(2,1)S(1)}, bf16[24,3584]{1,0:T(8,128)(2,1)S(1)}, u32[]{:S(2)}, u32[]{:S(2)}) collective-permute-start(bf16[24,3584]{1,0:T(8,128)(2,1)S(1)} %collective-permute-done.18.refs_1_), channel_id=1, source_target_pairs={{0,2},{2,0},{4,6},{6,4},{8,10},{10,8},{12,14},{14,12},{16,18},{18,... | collective-permute-start | bytes 516104 | tf_op jit(solution)/shard_map/ppermute | solution.py:290
  50.2 4.3 %collective-permute-start.21 = (bf16[64,448]{1,0:T(8,128)(2,1)S(1)}, bf16[64,448]{1,0:T(8,128)(2,1)S(1)}, u32[]{:S(2)}, u32[]{:S(2)}) collective-permute-start(bf16[64,448]{1,0:T(8,128)(2,1)S(1)} %get-tuple-element.36), channel_id=1, source_target_pairs={{0,1},{1,0},{2,3},{3,2},{4,5},{5,4},{6,7},{7,6},{8,9},{9,8},{10,11... | collective-permute-start | bytes 172040 | tf_op jit(solution)/shard_map/ppermute | solution.py:290

commit v8 on v7

--- a/solution.py
+++ b/solution.py
@@ -12,7 +12,7 @@
 PAGE = 16
 OUTER = 4
 LANES = 128
-LAG = 3
+LAG = 4
 STAT = 32
 
 floor_score = -1e30

time: 55.4 us -> 55.4 us (level)
  no operation moved by 1% of the time
where the time goes in v8:
time: 55.4 us; the launch traced here: 55.2 us
  starting transfers between devices  27.5 us (50%)
  waiting for transfers between devices  17.1 us (31%)
  Pallas kernels  5.42 us (10%)
  local copies, waits for them, and re-layouts  5 us (9%)
    ppermute x22, starting transfers between devices, hop(): return lax.ppermute(x, axis, [(i, i ^ distance) for i in range(count)])  27.5 us
    ppermute x22, waiting for transfers between devices, hop(): return lax.ppermute(x, axis, [(i, i ^ distance) for i in range(count)])  17.1 us
    pallas_call x19, Pallas kernels, call(): pl.pallas_call(kernel, out_shape=shapes, in_specs=[spec(at) for at in ran...  5.42 us
    unnamed x18, local copies, waits for them, and re-layouts  3.47 us
  transfers between devices with their start and end apart: 22, of which 13 were waited for; matrix products, arithmetic and copies ran while one was open for 3% of the time, Pallas kernels for 3%

profile of v8, /device:TPU:0, one launch (start us, length us, event | category | flops | bytes accessed | tf_op | source)
XLA Modules:
  0.0 55.2 jit_solution(2712363288514159828)
XLA Ops:
  0.0 5.0 %collective-permute-start = (bf16[8,3584]{1,0:T(8,128)(2,1)}, bf16[8,3584]{1,0:T(8,128)(2,1)S(1)}, u32[]{:S(2)}, u32[]{:S(2)}) collective-permute-start(bf16[8,3584]{1,0:T(8,128)(2,1)} %queries.1), channel_id=1, source_target_pairs={{0,24},{2,26},{4,28},{6,30},{8,16},{10,18},{12,20},{14,22},{16,8},... | collective-permute-start | bytes 172040 | tf_op jit(solution)/shard_map/ppermute | solution.py:290
  5.1 0.6 %collective-permute-start.2 = (bf16[8,3584]{1,0:T(8,128)(2,1)}, bf16[8,3584]{1,0:T(8,128)(2,1)S(1)}, u32[]{:S(2)}, u32[]{:S(2)}) collective-permute-start(bf16[8,3584]{1,0:T(8,128)(2,1)} %queries.1), channel_id=1, source_target_pairs={{0,8},{2,10},{4,12},{6,14},{8,0},{10,2},{12,4},{14,6},{16,24},{18,... | collective-permute-start | bytes 172040 | tf_op jit(solution)/shard_map/ppermute | solution.py:290
  5.7 2.3 %collective-permute-start.3 = (bf16[8,3584]{1,0:T(8,128)(2,1)}, bf16[8,3584]{1,0:T(8,128)(2,1)S(1)}, u32[]{:S(2)}, u32[]{:S(2)}) collective-permute-start(bf16[8,3584]{1,0:T(8,128)(2,1)} %queries.1), channel_id=1, source_target_pairs={{0,12},{2,14},{4,8},{6,10},{8,4},{10,6},{12,0},{14,2},{16,28},{18,... | collective-permute-start | bytes 172040 | tf_op jit(solution)/shard_map/ppermute | solution.py:290
  8.0 0.9 %copy-done.6 = bf16[8,3584]{1,0:T(8,128)(2,1)S(1)} copy-done((bf16[8,3584]{1,0:T(8,128)(2,1)S(1)}, bf16[8,3584]{1,0:T(8,128)(2,1)}, u32[]{:S(2)}) %copy-start.6) | copy-done | bytes 57368
  8.9 0.8 %copy-done.7 = bf16[8,3584]{1,0:T(8,128)(2,1)S(1)} copy-done((bf16[8,3584]{1,0:T(8,128)(2,1)S(1)}, bf16[8,3584]{1,0:T(8,128)(2,1)}, u32[]{:S(2)}) %copy-start.7) | copy-done | bytes 57368
  9.7 0.1 own.1.refs_3_.refs_5_
  9.8 0.5 collective-permute-done.1.refs_1_
  10.4 1.6 %collective-permute-start.4 = (bf16[24,3584]{1,0:T(8,128)(2,1)S(1)}, bf16[24,3584]{1,0:T(8,128)(2,1)S(1)}, u32[]{:S(2)}, u32[]{:S(2)}) collective-permute-start(bf16[24,3584]{1,0:T(8,128)(2,1)S(1)} %pack.5.refs_0_), channel_id=1, source_target_pairs={{0,4},{2,6},{4,0},{6,2},{8,12},{10,14},{12,8},{14,10},{16,20},{18,... | collective-permute-start | bytes 516104 | tf_op jit(solution)/shard_map/ppermute | solution.py:290
  11.9 1.8 %copy-done.1 = bf16[384,3584]{1,0:T(8,128)(2,1)S(1)} copy-done((bf16[384,3584]{1,0:T(8,128)(2,1)S(1)}, bf16[384,3584]{1,0:T(8,128)(2,1)}, u32[]{:S(2)}) %copy-start.1) | copy-done | bytes 2752536
  13.7 0.1 collective-permute-start.5
  13.8 0.8 %reshape.10.valid = s32[1,384]{1,0:T(1,128)S(1)} reshape(s32[384]{0:T(512)} %param.16) | data formatting | bytes 3072 | tf_op jit(solution)/shard_map/reshape | solution.py:362
  14.7 0.7 %reshape.9.request = s32[1,384]{1,0:T(1,128)S(1)} reshape(s32[384]{0:T(512)} %param.15) | data formatting | bytes 3072 | tf_op jit(solution)/shard_map/reshape | solution.py:361
  15.3 0.1 prep.1
  15.4 0.6 %collective-permute-done.4.refs_0_ = bf16[24,3584]{1,0:T(8,128)(2,1)S(1)} collective-permute-done((bf16[24,3584]{1,0:T(8,128)(2,1)S(1)}, bf16[24,3584]{1,0:T(8,128)(2,1)S(1)}, u32[]{:S(2)}, u32[]{:S(2)}) %collective-permute-start.4) | collective-permute-done | bytes 172064 | tf_op jit(solution)/shard_map/ppermute | solution.py:290
  16.0 0.1 collective-permute-start.6
  16.1 1.4 %collective-permute-done.6.refs_3_ = bf16[24,3584]{1,0:T(8,128)(2,1)S(1)} collective-permute-done((bf16[24,3584]{1,0:T(8,128)(2,1)S(1)}, bf16[24,3584]{1,0:T(8,128)(2,1)S(1)}, u32[]{:S(2)}, u32[]{:S(2)}) %collective-permute-start.6) | collective-permute-done | bytes 172064 | tf_op jit(solution)/shard_map/ppermute | solution.py:290
  17.5 1.9 %attend.1 = (bf16[32,3712]{1,0:T(8,128)(2,1)S(1)}, bf16[32,3712]{1,0:T(8,128)(2,1)S(1)}, bf16[32,3712]{1,0:T(8,128)(2,1)S(1)}, bf16[32,3712]{1,0:T(8,128)(2,1)S(1)}) custom-call(bf16[32,128]{1,0:T(8,128)(2,1)S(1)} %get-tuple-element.21.refs_2_.pick, bf16[32,128]{1,0:T(8,128)(2,1)S(1)} %get-tuple-element.22.spread_to, f32[32,384]{1,0:T(8,128)S(1)} %get-tuple-element.23.mask, ...), custom_call_target="tpu_custom_call" | custom-call | tf_op jit(solution)/shard_map/attend/pallas_call | solution.py:318
  19.4 0.2 collective-permute-start.8
  19.6 0.4 collective-permute-start.7
  19.9 1.0 %collective-permute-done.8.refs_1_ = bf16[32,3712]{1,0:T(8,128)(2,1)S(1)} collective-permute-done((bf16[32,3712]{1,0:T(8,128)(2,1)S(1)}, bf16[32,3712]{1,0:T(8,128)(2,1)S(1)}, u32[]{:S(2)}, u32[]{:S(2)}) %collective-permute-start.8) | collective-permute-done | bytes 237600 | tf_op jit(solution)/shard_map/ppermute | solution.py:290
  20.9 0.3 merge.4
  21.3 1.5 %collective-permute-start.9 = (bf16[24,3712]{1,0:T(8,128)(2,1)S(1)}, bf16[24,3712]{1,0:T(8,128)(2,1)S(1)}, u32[]{:S(2)}, u32[]{:S(2)}) collective-permute-start(bf16[24,3712]{1,0:T(8,128)(2,1)S(1)} %get-tuple-element.29), channel_id=1, source_target_pairs={{0,4},{2,6},{4,0},{6,2},{8,12},{10,14},{12,8},{14,10},{16,20},{18,... | collective-permute-start | bytes 534536 | tf_op jit(solution)/shard_map/ppermute | solution.py:290
  22.7 0.3 merge.3
  23.1 2.6 %collective-permute-start.13 = (bf16[8,3712]{1,0:T(8,128)(2,1)S(1)}, bf16[8,3712]{1,0:T(8,128)(2,1)S(1)}, u32[]{:S(2)}, u32[]{:S(2)}) collective-permute-start(bf16[8,3712]{1,0:T(8,128)(2,1)S(1)} %get-tuple-element.34), channel_id=1, source_target_pairs={{0,24},{2,26},{4,28},{6,30},{8,16},{10,18},{12,20},{14,22},{16,8},... | collective-permute-start | bytes 178184 | tf_op jit(solution)/shard_map/ppermute | solution.py:290
  25.6 1.4 %collective-permute-start.12 = (bf16[8,3712]{1,0:T(8,128)(2,1)S(1)}, bf16[8,3712]{1,0:T(8,128)(2,1)S(1)}, u32[]{:S(2)}, u32[]{:S(2)}) collective-permute-start(bf16[8,3712]{1,0:T(8,128)(2,1)S(1)} %get-tuple-element.32), channel_id=1, source_target_pairs={{0,28},{2,30},{4,24},{6,26},{8,20},{10,22},{12,16},{14,18},{16,12}... | collective-permute-start | bytes 178184 | tf_op jit(solution)/shard_map/ppermute | solution.py:290
  27.0 0.9 %collective-permute-done.9.refs_1_.refs_2_ = bf16[24,3712]{1,0:T(8,128)(2,1)S(1)} collective-permute-done((bf16[24,3712]{1,0:T(8,128)(2,1)S(1)}, bf16[24,3712]{1,0:T(8,128)(2,1)S(1)}, u32[]{:S(2)}, u32[]{:S(2)}) %collective-permute-start.9) | collective-permute-done | bytes 178208 | tf_op jit(solution)/shard_map/ppermute | solution.py:290
  27.9 0.3 merge.5
  28.1 2.9 %collective-permute-start.10 = (bf16[8,3712]{1,0:T(8,128)(2,1)S(1)}, bf16[8,3712]{1,0:T(8,128)(2,1)S(1)}, u32[]{:S(2)}, u32[]{:S(2)}) collective-permute-start(bf16[8,3712]{1,0:T(8,128)(2,1)S(1)} %get-tuple-element.30), channel_id=1, source_target_pairs={{0,16},{2,18},{4,20},{6,22},{8,24},{10,26},{12,28},{14,30},{16,0},... | collective-permute-start | bytes 178184 | tf_op jit(solution)/shard_map/ppermute | solution.py:290
  31.1 0.3 collective-permute-start.11
  31.4 1.7 %collective-permute-done.12.refs_0_ = bf16[8,3712]{1,0:T(8,128)(2,1)S(1)} collective-permute-done((bf16[8,3712]{1,0:T(8,128)(2,1)S(1)}, bf16[8,3712]{1,0:T(8,128)(2,1)S(1)}, u32[]{:S(2)}, u32[]{:S(2)}) %collective-permute-start.12) | collective-permute-done | bytes 59424 | tf_op jit(solution)/shard_map/ppermute | solution.py:290
  33.1 0.3 early.1.refs_2_
  33.4 0.8 %collective-permute-done.10.refs_0_ = bf16[8,3712]{1,0:T(8,128)(2,1)S(1)} collective-permute-done((bf16[8,3712]{1,0:T(8,128)(2,1)S(1)}, bf16[8,3712]{1,0:T(8,128)(2,1)S(1)}, u32[]{:S(2)}, u32[]{:S(2)}) %collective-permute-start.10) | collective-permute-done | bytes 59424 | tf_op jit(solution)/shard_map/ppermute | solution.py:290
  34.2 1.1 %collective-permute-done.11.refs_1_ = bf16[8,3712]{1,0:T(8,128)(2,1)S(1)} collective-permute-done((bf16[8,3712]{1,0:T(8,128)(2,1)S(1)}, bf16[8,3712]{1,0:T(8,128)(2,1)S(1)}, u32[]{:S(2)}, u32[]{:S(2)}) %collective-permute-start.11) | collective-permute-done | bytes 59424 | tf_op jit(solution)/shard_map/ppermute | solution.py:290
  35.3 0.3 last.1.refs_2_
  35.5 0.8 %collective-permute-start.14 = (bf16[8,3584]{1,0:T(8,128)(2,1)S(1)}, bf16[8,3584]{1,0:T(8,128)(2,1)S(1)}, u32[]{:S(2)}, u32[]{:S(2)}) collective-permute-start(bf16[8,3584]{1,0:T(8,128)(2,1)S(1)} %last.1.refs_2_), channel_id=1, source_target_pairs={{0,24},{2,26},{4,28},{6,30},{8,16},{10,18},{12,20},{14,22},{16,8},... | collective-permute-start | bytes 172040 | tf_op jit(solution)/shard_map/ppermute | solution.py:290
  36.4 1.3 %collective-permute-start.15 = (bf16[8,3584]{1,0:T(8,128)(2,1)S(1)}, bf16[8,3584]{1,0:T(8,128)(2,1)S(1)}, u32[]{:S(2)}, u32[]{:S(2)}) collective-permute-start(bf16[8,3584]{1,0:T(8,128)(2,1)S(1)} %last.1.refs_2_), channel_id=1, source_target_pairs={{0,16},{2,18},{4,20},{6,22},{8,24},{10,26},{12,28},{14,30},{16,0},... | collective-permute-start | bytes 172040 | tf_op jit(solution)/shard_map/ppermute | solution.py:290
  37.7 2.3 %collective-permute-start.16 = (bf16[8,3584]{1,0:T(8,128)(2,1)S(1)}, bf16[8,3584]{1,0:T(8,128)(2,1)S(1)}, u32[]{:S(2)}, u32[]{:S(2)}) collective-permute-start(bf16[8,3584]{1,0:T(8,128)(2,1)S(1)} %last.1.refs_2_), channel_id=1, source_target_pairs={{0,8},{2,10},{4,12},{6,14},{8,0},{10,2},{12,4},{14,6},{16,24},{18,... | collective-permute-start | bytes 172040 | tf_op jit(solution)/shard_map/ppermute | solution.py:290
  40.0 0.6 %collective-permute-start.17 = (bf16[8,3584]{1,0:T(8,128)(2,1)S(1)}, bf16[8,3584]{1,0:T(8,128)(2,1)S(1)}, u32[]{:S(2)}, u32[]{:S(2)}) collective-permute-start(bf16[8,3584]{1,0:T(8,128)(2,1)S(1)} %last.1.refs_2_), channel_id=1, source_target_pairs={{0,12},{2,14},{4,8},{6,10},{8,4},{10,6},{12,0},{14,2},{16,28},{18,... | collective-permute-start | bytes 172040 | tf_op jit(solution)/shard_map/ppermute | solution.py:290
  40.6 1.6 %collective-permute-done.14.refs_0_ = bf16[8,3584]{1,0:T(8,128)(2,1)S(1)} collective-permute-done((bf16[8,3584]{1,0:T(8,128)(2,1)S(1)}, bf16[8,3584]{1,0:T(8,128)(2,1)S(1)}, u32[]{:S(2)}, u32[]{:S(2)}) %collective-permute-start.14) | collective-permute-done | bytes 57376 | tf_op jit(solution)/shard_map/ppermute | solution.py:290
  42.2 1.9 %collective-permute-start.18 = (bf16[24,3584]{1,0:T(8,128)(2,1)S(1)}, bf16[24,3584]{1,0:T(8,128)(2,1)S(1)}, u32[]{:S(2)}, u32[]{:S(2)}) collective-permute-start(bf16[24,3584]{1,0:T(8,128)(2,1)S(1)} %pack.8.refs_0_), channel_id=1, source_target_pairs={{0,4},{2,6},{4,0},{6,2},{8,12},{10,14},{12,8},{14,10},{16,20},{18,... | collective-permute-start | bytes 516104 | tf_op jit(solution)/shard_map/ppermute | solution.py:290
  44.1 1.0 %collective-permute-done.17.refs_2_ = bf16[8,3584]{1,0:T(8,128)(2,1)S(1)} collective-permute-done((bf16[8,3584]{1,0:T(8,128)(2,1)S(1)}, bf16[8,3584]{1,0:T(8,128)(2,1)S(1)}, u32[]{:S(2)}, u32[]{:S(2)}) %collective-permute-start.17) | collective-permute-done | bytes 57376 | tf_op jit(solution)/shard_map/ppermute | solution.py:290
  45.1 0.1 collective-permute-start.19
  45.2 2.5 %collective-permute-done.18.refs_1_ = bf16[24,3584]{1,0:T(8,128)(2,1)S(1)} collective-permute-done((bf16[24,3584]{1,0:T(8,128)(2,1)S(1)}, bf16[24,3584]{1,0:T(8,128)(2,1)S(1)}, u32[]{:S(2)}, u32[]{:S(2)}) %collective-permute-start.18) | collective-permute-done | bytes 172064 | tf_op jit(solution)/shard_map/ppermute | solution.py:290
  47.7 1.4 %collective-permute-done.20.refs_3_ = bf16[24,3584]{1,0:T(8,128)(2,1)S(1)} collective-permute-done((bf16[24,3584]{1,0:T(8,128)(2,1)S(1)}, bf16[24,3584]{1,0:T(8,128)(2,1)S(1)}, u32[]{:S(2)}, u32[]{:S(2)}) %collective-permute-start.20) | collective-permute-done | bytes 172064 | tf_op jit(solution)/shard_map/ppermute | solution.py:290
  49.1 1.1 %project.1 = (f32[64,448]{1,0:T(8,128)S(1)}, bf16[64,448]{1,0:T(8,128)(2,1)S(1)}) custom-call(bf16[40,3584]{1,0:T(8,128)(2,1)S(1)} %pack.9.refs_0_, bf16[24,3584]{1,0:T(8,128)(2,1)S(1)} %collective-permute-done.18.refs_1_, bf16[40,3584]{1,0:T(8,128)(2,1)S(1)} %collective-permute-done.19.refs_2_, bf16[24,3584]{1,0:T(8,128)(2,1)S(1)} %collective-permute-done.20.refs_3_, ...), custom_call_target="tpu_custom_call" | custom-call | tf_op jit(solution)/shard_map/project/pallas_call | solution.py:318
  50.2 1.6 %collective-permute-start.21 = (bf16[64,448]{1,0:T(8,128)(2,1)S(1)}, bf16[64,448]{1,0:T(8,128)(2,1)S(1)}, u32[]{:S(2)}, u32[]{:S(2)}) collective-permute-start(bf16[64,448]{1,0:T(8,128)(2,1)S(1)} %get-tuple-element.36), channel_id=1, source_target_pairs={{0,1},{1,0},{2,3},{3,2},{4,5},{5,4},{6,7},{7,6},{8,9},{9,8},{10,11... | collective-permute-start | bytes 172040 | tf_op jit(solution)/shard_map/ppermute | solution.py:290
  51.8 2.7 %collective-permute-done.21.refs_0_ = bf16[64,448]{1,0:T(8,128)(2,1)S(1)} collective-permute-done((bf16[64,448]{1,0:T(8,128)(2,1)S(1)}, bf16[64,448]{1,0:T(8,128)(2,1)S(1)}, u32[]{:S(2)}, u32[]{:S(2)}) %collective-permute-start.21) | collective-permute-done | bytes 57376 | tf_op jit(solution)/shard_map/ppermute | solution.py:290
  54.5 0.6 %final.1 = bf16[64,448]{1,0:T(8,128)(2,1)} custom-call(f32[64,448]{1,0:T(8,128)S(1)} %base.1.total, bf16[64,448]{1,0:T(8,128)(2,1)S(1)} %collective-permute-done.21.refs_0_), custom_call_target="tpu_custom_call" | custom-call | tf_op jit(solution)/shard_map/final/pallas_call | solution.py:318
  (36 shorter events, 0.2 us)
Async XLA Ops:
  0.0 15.3 %copy-start = (bf16[384,3584]{1,0:T(8,128)(2,1)S(1)}, bf16[384,3584]{1,0:T(8,128)(2,1)}, u32[]{:S(2)}) copy-start(bf16[384,3584]{1,0:T(8,128)(2,1)} %keys.1) | copy-start | bytes 8257540
  0.0 9.8 %collective-permute-start = (bf16[8,3584]{1,0:T(8,128)(2,1)}, bf16[8,3584]{1,0:T(8,128)(2,1)S(1)}, u32[]{:S(2)}, u32[]{:S(2)}) collective-permute-start(bf16[8,3584]{1,0:T(8,128)(2,1)} %queries.1), channel_id=1, source_target_pairs={{0,24},{2,26},{4,28},{6,30},{8,16},{10,18},{12,20},{14,22},{16,8},... | collective-permute-start | bytes 172040 | tf_op jit(solution)/shard_map/ppermute | solution.py:290
  5.1 5.3 %collective-permute-start.1 = (bf16[8,3584]{1,0:T(8,128)(2,1)}, bf16[8,3584]{1,0:T(8,128)(2,1)S(1)}, u32[]{:S(2)}, u32[]{:S(2)}) collective-permute-start(bf16[8,3584]{1,0:T(8,128)(2,1)} %queries.1), channel_id=1, source_target_pairs={{0,16},{2,18},{4,20},{6,22},{8,24},{10,26},{12,28},{14,30},{16,0},... | collective-permute-start | bytes 172040 | tf_op jit(solution)/shard_map/ppermute | solution.py:290
  5.1 8.6 %collective-permute-start.2 = (bf16[8,3584]{1,0:T(8,128)(2,1)}, bf16[8,3584]{1,0:T(8,128)(2,1)S(1)}, u32[]{:S(2)}, u32[]{:S(2)}) collective-permute-start(bf16[8,3584]{1,0:T(8,128)(2,1)} %queries.1), channel_id=1, source_target_pairs={{0,8},{2,10},{4,12},{6,14},{8,0},{10,2},{12,4},{14,6},{16,24},{18,... | collective-permute-start | bytes 172040 | tf_op jit(solution)/shard_map/ppermute | solution.py:290
  5.7 8.0 %collective-permute-start.3 = (bf16[8,3584]{1,0:T(8,128)(2,1)}, bf16[8,3584]{1,0:T(8,128)(2,1)S(1)}, u32[]{:S(2)}, u32[]{:S(2)}) collective-permute-start(bf16[8,3584]{1,0:T(8,128)(2,1)} %queries.1), channel_id=1, source_target_pairs={{0,12},{2,14},{4,8},{6,10},{8,4},{10,6},{12,0},{14,2},{16,28},{18,... | collective-permute-start | bytes 172040 | tf_op jit(solution)/shard_map/ppermute | solution.py:290
  8.0 0.9 %copy-start.6 = (bf16[8,3584]{1,0:T(8,128)(2,1)S(1)}, bf16[8,3584]{1,0:T(8,128)(2,1)}, u32[]{:S(2)}) copy-start(bf16[8,3584]{1,0:T(8,128)(2,1)} %queries.1) | copy-start | bytes 172036
  8.9 0.8 %copy-start.7 = (bf16[8,3584]{1,0:T(8,128)(2,1)S(1)}, bf16[8,3584]{1,0:T(8,128)(2,1)}, u32[]{:S(2)}) copy-start(bf16[8,3584]{1,0:T(8,128)(2,1)} %new_keys.1) | copy-start | bytes 172036
  10.4 5.7 %collective-permute-start.4 = (bf16[24,3584]{1,0:T(8,128)(2,1)S(1)}, bf16[24,3584]{1,0:T(8,128)(2,1)S(1)}, u32[]{:S(2)}, u32[]{:S(2)}) collective-permute-start(bf16[24,3584]{1,0:T(8,128)(2,1)S(1)} %pack.5.refs_0_), channel_id=1, source_target_pairs={{0,4},{2,6},{4,0},{6,2},{8,12},{10,14},{12,8},{14,10},{16,20},{18,... | collective-permute-start | bytes 516104 | tf_op jit(solution)/shard_map/ppermute | solution.py:290
  11.9 1.8 %copy-start.1 = (bf16[384,3584]{1,0:T(8,128)(2,1)S(1)}, bf16[384,3584]{1,0:T(8,128)(2,1)}, u32[]{:S(2)}) copy-start(bf16[384,3584]{1,0:T(8,128)(2,1)} %values.1) | copy-start | bytes 8257540
  13.7 3.8 %copy-start.2 = (bf16[384,3584]{1,0:T(8,128)(2,1)S(1)}, bf16[384,3584]{1,0:T(8,128)(2,1)}, u32[]{:S(2)}) copy-start(bf16[384,3584]{1,0:T(8,128)(2,1)} %values.1) | copy-start | bytes 8257540
  13.7 2.4 %collective-permute-start.5 = (bf16[40,3584]{1,0:T(8,128)(2,1)S(1)}, bf16[40,3584]{1,0:T(8,128)(2,1)S(1)}, u32[]{:S(2)}, u32[]{:S(2)}) collective-permute-start(bf16[40,3584]{1,0:T(8,128)(2,1)S(1)} %pack.6.refs_0_), channel_id=1, source_target_pairs={{0,2},{2,0},{4,6},{6,4},{8,10},{10,8},{12,14},{14,12},{16,18},{18,... | collective-permute-start | bytes 860168 | tf_op jit(solution)/shard_map/ppermute | solution.py:290
  16.0 1.5 %collective-permute-start.6 = (bf16[24,3584]{1,0:T(8,128)(2,1)S(1)}, bf16[24,3584]{1,0:T(8,128)(2,1)S(1)}, u32[]{:S(2)}, u32[]{:S(2)}) collective-permute-start(bf16[24,3584]{1,0:T(8,128)(2,1)S(1)} %pack.7.refs_1_), channel_id=1, source_target_pairs={{0,2},{2,0},{4,6},{6,4},{8,10},{10,8},{12,14},{14,12},{16,18},{18,... | collective-permute-start | bytes 516104 | tf_op jit(solution)/shard_map/ppermute | solution.py:290
  17.5 15.6 %copy-start.5 = (bf16[8,3584]{1,0:T(8,128)(2,1)S(1)}, bf16[8,3584]{1,0:T(8,128)(2,1)}, u32[]{:S(2)}) copy-start(bf16[8,3584]{1,0:T(8,128)(2,1)} %refs_4_.1) | copy-start | bytes 172036
  17.5 31.6 %copy-start.3 = (bf16[3584,448]{0,1:T(8,128)(2,1)S(1)}, bf16[3584,448]{0,1:T(8,128)(2,1)}, u32[]{:S(2)}) copy-start(bf16[3584,448]{0,1:T(8,128)(2,1)} %param.17) | copy-start | bytes 9633796
  19.4 1.6 %collective-permute-start.8 = (bf16[32,3712]{1,0:T(8,128)(2,1)S(1)}, bf16[32,3712]{1,0:T(8,128)(2,1)S(1)}, u32[]{:S(2)}, u32[]{:S(2)}) collective-permute-start(bf16[32,3712]{1,0:T(8,128)(2,1)S(1)} %get-tuple-element.28), channel_id=1, source_target_pairs={{0,2},{2,0},{4,6},{6,4},{8,10},{10,8},{12,14},{14,12},{16,18},{18,... | collective-permute-start | bytes 712712 | tf_op jit(solution)/shard_map/ppermute | solution.py:290
  19.6 3.2 %collective-permute-start.7 = (bf16[32,3712]{1,0:T(8,128)(2,1)S(1)}, bf16[32,3712]{1,0:T(8,128)(2,1)S(1)}, u32[]{:S(2)}, u32[]{:S(2)}) collective-permute-start(bf16[32,3712]{1,0:T(8,128)(2,1)S(1)} %get-tuple-element.25), channel_id=1, source_target_pairs={{0,2},{2,0},{4,6},{6,4},{8,10},{10,8},{12,14},{14,12},{16,18},{18,... | collective-permute-start | bytes 712712 | tf_op jit(solution)/shard_map/ppermute | solution.py:290
  21.3 6.6 %collective-permute-start.9 = (bf16[24,3712]{1,0:T(8,128)(2,1)S(1)}, bf16[24,3712]{1,0:T(8,128)(2,1)S(1)}, u32[]{:S(2)}, u32[]{:S(2)}) collective-permute-start(bf16[24,3712]{1,0:T(8,128)(2,1)S(1)} %get-tuple-element.29), channel_id=1, source_target_pairs={{0,4},{2,6},{4,0},{6,2},{8,12},{10,14},{12,8},{14,10},{16,20},{18,... | collective-permute-start | bytes 534536 | tf_op jit(solution)/shard_map/ppermute | solution.py:290
  23.1 8.3 %collective-permute-start.13 = (bf16[8,3712]{1,0:T(8,128)(2,1)S(1)}, bf16[8,3712]{1,0:T(8,128)(2,1)S(1)}, u32[]{:S(2)}, u32[]{:S(2)}) collective-permute-start(bf16[8,3712]{1,0:T(8,128)(2,1)S(1)} %get-tuple-element.34), channel_id=1, source_target_pairs={{0,24},{2,26},{4,28},{6,30},{8,16},{10,18},{12,20},{14,22},{16,8},... | collective-permute-start | bytes 178184 | tf_op jit(solution)/shard_map/ppermute | solution.py:290
  25.6 7.4 %collective-permute-start.12 = (bf16[8,3712]{1,0:T(8,128)(2,1)S(1)}, bf16[8,3712]{1,0:T(8,128)(2,1)S(1)}, u32[]{:S(2)}, u32[]{:S(2)}) collective-permute-start(bf16[8,3712]{1,0:T(8,128)(2,1)S(1)} %get-tuple-element.32), channel_id=1, source_target_pairs={{0,28},{2,30},{4,24},{6,26},{8,20},{10,22},{12,16},{14,18},{16,12}... | collective-permute-start | bytes 178184 | tf_op jit(solution)/shard_map/ppermute | solution.py:290
  28.1 6.1 %collective-permute-start.10 = (bf16[8,3712]{1,0:T(8,128)(2,1)S(1)}, bf16[8,3712]{1,0:T(8,128)(2,1)S(1)}, u32[]{:S(2)}, u32[]{:S(2)}) collective-permute-start(bf16[8,3712]{1,0:T(8,128)(2,1)S(1)} %get-tuple-element.30), channel_id=1, source_target_pairs={{0,16},{2,18},{4,20},{6,22},{8,24},{10,26},{12,28},{14,30},{16,0},... | collective-permute-start | bytes 178184 | tf_op jit(solution)/shard_map/ppermute | solution.py:290
  31.1 4.2 %collective-permute-start.11 = (bf16[8,3712]{1,0:T(8,128)(2,1)S(1)}, bf16[8,3712]{1,0:T(8,128)(2,1)S(1)}, u32[]{:S(2)}, u32[]{:S(2)}) collective-permute-start(bf16[8,3712]{1,0:T(8,128)(2,1)S(1)} %get-tuple-element.31), channel_id=1, source_target_pairs={{0,8},{2,10},{4,12},{6,14},{8,0},{10,2},{12,4},{14,6},{16,24},{18,... | collective-permute-start | bytes 178184 | tf_op jit(solution)/shard_map/ppermute | solution.py:290
  33.4 18.4 %copy-start.8 = (bf16[448]{0:T(512)(128)(2,1)S(1)}, bf16[448]{0:T(512)(128)(2,1)}, u32[]{:S(2)}) copy-start(bf16[448]{0:T(512)(128)(2,1)} %param.18) | copy-start | bytes 2692
  33.4 18.3 %copy-start.4 = (bf16[64,448]{1,0:T(8,128)(2,1)S(1)}, bf16[64,448]{1,0:T(8,128)(2,1)}, u32[]{:S(2)}) copy-start(bf16[64,448]{1,0:T(8,128)(2,1)} %residual.1) | copy-start | bytes 172036
  35.5 6.6 %collective-permute-start.14 = (bf16[8,3584]{1,0:T(8,128)(2,1)S(1)}, bf16[8,3584]{1,0:T(8,128)(2,1)S(1)}, u32[]{:S(2)}, u32[]{:S(2)}) collective-permute-start(bf16[8,3584]{1,0:T(8,128)(2,1)S(1)} %last.1.refs_2_), channel_id=1, source_target_pairs={{0,24},{2,26},{4,28},{6,30},{8,16},{10,18},{12,20},{14,22},{16,8},... | collective-permute-start | bytes 172040 | tf_op jit(solution)/shard_map/ppermute | solution.py:290
  36.4 5.8 %collective-permute-start.15 = (bf16[8,3584]{1,0:T(8,128)(2,1)S(1)}, bf16[8,3584]{1,0:T(8,128)(2,1)S(1)}, u32[]{:S(2)}, u32[]{:S(2)}) collective-permute-start(bf16[8,3584]{1,0:T(8,128)(2,1)S(1)} %last.1.refs_2_), channel_id=1, source_target_pairs={{0,16},{2,18},{4,20},{6,22},{8,24},{10,26},{12,28},{14,30},{16,0},... | collective-permute-start | bytes 172040 | tf_op jit(solution)/shard_map/ppermute | solution.py:290
  37.7 6.4 %collective-permute-start.16 = (bf16[8,3584]{1,0:T(8,128)(2,1)S(1)}, bf16[8,3584]{1,0:T(8,128)(2,1)S(1)}, u32[]{:S(2)}, u32[]{:S(2)}) collective-permute-start(bf16[8,3584]{1,0:T(8,128)(2,1)S(1)} %last.1.refs_2_), channel_id=1, source_target_pairs={{0,8},{2,10},{4,12},{6,14},{8,0},{10,2},{12,4},{14,6},{16,24},{18,... | collective-permute-start | bytes 172040 | tf_op jit(solution)/shard_map/ppermute | solution.py:290
  40.0 5.1 %collective-permute-start.17 = (bf16[8,3584]{1,0:T(8,128)(2,1)S(1)}, bf16[8,3584]{1,0:T(8,128)(2,1)S(1)}, u32[]{:S(2)}, u32[]{:S(2)}) collective-permute-start(bf16[8,3584]{1,0:T(8,128)(2,1)S(1)} %last.1.refs_2_), channel_id=1, source_target_pairs={{0,12},{2,14},{4,8},{6,10},{8,4},{10,6},{12,0},{14,2},{16,28},{18,... | collective-permute-start | bytes 172040 | tf_op jit(solution)/shard_map/ppermute | solution.py:290
  42.2 5.5 %collective-permute-start.18 = (bf16[24,3584]{1,0:T(8,128)(2,1)S(1)}, bf16[24,3584]{1,0:T(8,128)(2,1)S(1)}, u32[]{:S(2)}, u32[]{:S(2)}) collective-permute-start(bf16[24,3584]{1,0:T(8,128)(2,1)S(1)} %pack.8.refs_0_), channel_id=1, source_target_pairs={{0,4},{2,6},{4,0},{6,2},{8,12},{10,14},{12,8},{14,10},{16,20},{18,... | collective-permute-start | bytes 516104 | tf_op jit(solution)/shard_map/ppermute | solution.py:290
  45.1 2.6 %collective-permute-start.19 = (bf16[40,3584]{1,0:T(8,128)(2,1)S(1)}, bf16[40,3584]{1,0:T(8,128)(2,1)S(1)}, u32[]{:S(2)}, u32[]{:S(2)}) collective-permute-start(bf16[40,3584]{1,0:T(8,128)(2,1)S(1)} %pack.9.refs_0_), channel_id=1, source_target_pairs={{0,2},{2,0},{4,6},{6,4},{8,10},{10,8},{12,14},{14,12},{16,18},{18,... | collective-permute-start | bytes 860168 | tf_op jit(solution)/shard_map/ppermute | solution.py:290
  47.7 1.4 %collective-permute-start.20 = (bf16[24,3584]{1,0:T(8,128)(2,1)S(1)}, bf16[24,3584]{1,0:T(8,128)(2,1)S(1)}, u32[]{:S(2)}, u32[]{:S(2)}) collective-permute-start(bf16[24,3584]{1,0:T(8,128)(2,1)S(1)} %collective-permute-done.18.refs_1_), channel_id=1, source_target_pairs={{0,2},{2,0},{4,6},{6,4},{8,10},{10,8},{12,14},{14,12},{16,18},{18,... | collective-permute-start | bytes 516104 | tf_op jit(solution)/shard_map/ppermute | solution.py:290
  50.2 4.3 %collective-permute-start.21 = (bf16[64,448]{1,0:T(8,128)(2,1)S(1)}, bf16[64,448]{1,0:T(8,128)(2,1)S(1)}, u32[]{:S(2)}, u32[]{:S(2)}) collective-permute-start(bf16[64,448]{1,0:T(8,128)(2,1)S(1)} %get-tuple-element.36), channel_id=1, source_target_pairs={{0,1},{1,0},{2,3},{3,2},{4,5},{5,4},{6,7},{7,6},{8,9},{9,8},{10,11... | collective-permute-start | bytes 172040 | tf_op jit(solution)/shard_map/ppermute | solution.py:290

commit v9 on v7

--- a/solution.py
+++ b/solution.py
@@ -308,7 +308,7 @@
     slots = keys.shape[0]
     mid = kv_count // (2 * OUTER)
     requests = kv_count * own_rows
-    rows = -(-(slots // PAGE) // 16) * 16
+    rows = slots // PAGE
     wide = width + LANES
     kv_hop = lambda x, distance: hop(x, "kv", kv_count, distance)
     shaped = jax.ShapeDtypeStruct

time: 55.4 us -> 55.4 us (level)
  no operation moved by 1% of the time
where the time goes in v9:
time: 55.4 us; the launch traced here: 55.2 us
  starting transfers between devices  27.5 us (50%)
  waiting for transfers between devices  17.1 us (31%)
  Pallas kernels  5.42 us (10%)
  local copies, waits for them, and re-layouts  5 us (9%)
    ppermute x22, starting transfers between devices, hop(): return lax.ppermute(x, axis, [(i, i ^ distance) for i in range(count)])  27.5 us
    ppermute x22, waiting for transfers between devices, hop(): return lax.ppermute(x, axis, [(i, i ^ distance) for i in range(count)])  17.1 us
    pallas_call x19, Pallas kernels, call(): pl.pallas_call(kernel, out_shape=shapes, in_specs=[spec(at) for at in ran...  5.42 us
    unnamed x18, local copies, waits for them, and re-layouts  3.47 us
  transfers between devices with their start and end apart: 22, of which 13 were waited for; matrix products, arithmetic and copies ran while one was open for 3% of the time, Pallas kernels for 3%

profile of v9, /device:TPU:0, one launch (start us, length us, event | category | flops | bytes accessed | tf_op | source)
XLA Modules:
  0.0 55.2 jit_solution(5584093374149049797)
XLA Ops:
  0.0 5.0 %collective-permute-start = (bf16[8,3584]{1,0:T(8,128)(2,1)}, bf16[8,3584]{1,0:T(8,128)(2,1)S(1)}, u32[]{:S(2)}, u32[]{:S(2)}) collective-permute-start(bf16[8,3584]{1,0:T(8,128)(2,1)} %queries.1), channel_id=1, source_target_pairs={{0,24},{2,26},{4,28},{6,30},{8,16},{10,18},{12,20},{14,22},{16,8},... | collective-permute-start | bytes 172040 | tf_op jit(solution)/shard_map/ppermute | solution.py:290
  5.1 0.6 %collective-permute-start.2 = (bf16[8,3584]{1,0:T(8,128)(2,1)}, bf16[8,3584]{1,0:T(8,128)(2,1)S(1)}, u32[]{:S(2)}, u32[]{:S(2)}) collective-permute-start(bf16[8,3584]{1,0:T(8,128)(2,1)} %queries.1), channel_id=1, source_target_pairs={{0,8},{2,10},{4,12},{6,14},{8,0},{10,2},{12,4},{14,6},{16,24},{18,... | collective-permute-start | bytes 172040 | tf_op jit(solution)/shard_map/ppermute | solution.py:290
  5.7 2.3 %collective-permute-start.3 = (bf16[8,3584]{1,0:T(8,128)(2,1)}, bf16[8,3584]{1,0:T(8,128)(2,1)S(1)}, u32[]{:S(2)}, u32[]{:S(2)}) collective-permute-start(bf16[8,3584]{1,0:T(8,128)(2,1)} %queries.1), channel_id=1, source_target_pairs={{0,12},{2,14},{4,8},{6,10},{8,4},{10,6},{12,0},{14,2},{16,28},{18,... | collective-permute-start | bytes 172040 | tf_op jit(solution)/shard_map/ppermute | solution.py:290
  8.0 0.9 %copy-done.6 = bf16[8,3584]{1,0:T(8,128)(2,1)S(1)} copy-done((bf16[8,3584]{1,0:T(8,128)(2,1)S(1)}, bf16[8,3584]{1,0:T(8,128)(2,1)}, u32[]{:S(2)}) %copy-start.6) | copy-done | bytes 57368
  8.9 0.8 %copy-done.7 = bf16[8,3584]{1,0:T(8,128)(2,1)S(1)} copy-done((bf16[8,3584]{1,0:T(8,128)(2,1)S(1)}, bf16[8,3584]{1,0:T(8,128)(2,1)}, u32[]{:S(2)}) %copy-start.7) | copy-done | bytes 57368
  9.7 0.1 own.1.refs_3_.refs_5_
  9.8 0.5 collective-permute-done.1.refs_1_
  10.4 1.6 %collective-permute-start.4 = (bf16[24,3584]{1,0:T(8,128)(2,1)S(1)}, bf16[24,3584]{1,0:T(8,128)(2,1)S(1)}, u32[]{:S(2)}, u32[]{:S(2)}) collective-permute-start(bf16[24,3584]{1,0:T(8,128)(2,1)S(1)} %pack.5.refs_0_), channel_id=1, source_target_pairs={{0,4},{2,6},{4,0},{6,2},{8,12},{10,14},{12,8},{14,10},{16,20},{18,... | collective-permute-start | bytes 516104 | tf_op jit(solution)/shard_map/ppermute | solution.py:290
  11.9 1.8 %copy-done.1 = bf16[384,3584]{1,0:T(8,128)(2,1)S(1)} copy-done((bf16[384,3584]{1,0:T(8,128)(2,1)S(1)}, bf16[384,3584]{1,0:T(8,128)(2,1)}, u32[]{:S(2)}) %copy-start.1) | copy-done | bytes 2752536
  13.7 0.1 collective-permute-start.5
  13.8 0.8 %reshape.10.valid = s32[1,384]{1,0:T(1,128)S(1)} reshape(s32[384]{0:T(512)} %param.16) | data formatting | bytes 3072 | tf_op jit(solution)/shard_map/reshape | solution.py:362
  14.7 0.7 %reshape.9.request = s32[1,384]{1,0:T(1,128)S(1)} reshape(s32[384]{0:T(512)} %param.15) | data formatting | bytes 3072 | tf_op jit(solution)/shard_map/reshape | solution.py:361
  15.3 0.1 prep.1
  15.4 0.6 %collective-permute-done.4.refs_0_ = bf16[24,3584]{1,0:T(8,128)(2,1)S(1)} collective-permute-done((bf16[24,3584]{1,0:T(8,128)(2,1)S(1)}, bf16[24,3584]{1,0:T(8,128)(2,1)S(1)}, u32[]{:S(2)}, u32[]{:S(2)}) %collective-permute-start.4) | collective-permute-done | bytes 172064 | tf_op jit(solution)/shard_map/ppermute | solution.py:290
  16.0 0.1 collective-permute-start.6
  16.1 1.4 %collective-permute-done.6.refs_3_ = bf16[24,3584]{1,0:T(8,128)(2,1)S(1)} collective-permute-done((bf16[24,3584]{1,0:T(8,128)(2,1)S(1)}, bf16[24,3584]{1,0:T(8,128)(2,1)S(1)}, u32[]{:S(2)}, u32[]{:S(2)}) %collective-permute-start.6) | collective-permute-done | bytes 172064 | tf_op jit(solution)/shard_map/ppermute | solution.py:290
  17.5 1.9 %attend.1 = (bf16[32,3712]{1,0:T(8,128)(2,1)S(1)}, bf16[32,3712]{1,0:T(8,128)(2,1)S(1)}, bf16[32,3712]{1,0:T(8,128)(2,1)S(1)}, bf16[32,3712]{1,0:T(8,128)(2,1)S(1)}) custom-call(bf16[24,128]{1,0:T(8,128)(2,1)S(1)} %get-tuple-element.21.refs_2_.pick, bf16[24,128]{1,0:T(8,128)(2,1)S(1)} %get-tuple-element.22.spread_to, f32[24,384]{1,0:T(8,128)S(1)} %get-tuple-element.23.mask, ...), custom_call_target="tpu_custom_call" | custom-call | tf_op jit(solution)/shard_map/attend/pallas_call | solution.py:318
  19.4 0.2 collective-permute-start.8
  19.6 0.4 collective-permute-start.7
  19.9 1.0 %collective-permute-done.8.refs_1_ = bf16[32,3712]{1,0:T(8,128)(2,1)S(1)} collective-permute-done((bf16[32,3712]{1,0:T(8,128)(2,1)S(1)}, bf16[32,3712]{1,0:T(8,128)(2,1)S(1)}, u32[]{:S(2)}, u32[]{:S(2)}) %collective-permute-start.8) | collective-permute-done | bytes 237600 | tf_op jit(solution)/shard_map/ppermute | solution.py:290
  20.9 0.3 merge.4
  21.3 1.4 %collective-permute-start.9 = (bf16[24,3712]{1,0:T(8,128)(2,1)S(1)}, bf16[24,3712]{1,0:T(8,128)(2,1)S(1)}, u32[]{:S(2)}, u32[]{:S(2)}) collective-permute-start(bf16[24,3712]{1,0:T(8,128)(2,1)S(1)} %get-tuple-element.29), channel_id=1, source_target_pairs={{0,4},{2,6},{4,0},{6,2},{8,12},{10,14},{12,8},{14,10},{16,20},{18,... | collective-permute-start | bytes 534536 | tf_op jit(solution)/shard_map/ppermute | solution.py:290
  22.7 0.3 merge.3
  23.1 2.6 %collective-permute-start.13 = (bf16[8,3712]{1,0:T(8,128)(2,1)S(1)}, bf16[8,3712]{1,0:T(8,128)(2,1)S(1)}, u32[]{:S(2)}, u32[]{:S(2)}) collective-permute-start(bf16[8,3712]{1,0:T(8,128)(2,1)S(1)} %get-tuple-element.34), channel_id=1, source_target_pairs={{0,24},{2,26},{4,28},{6,30},{8,16},{10,18},{12,20},{14,22},{16,8},... | collective-permute-start | bytes 178184 | tf_op jit(solution)/shard_map/ppermute | solution.py:290
  25.6 1.4 %collective-permute-start.12 = (bf16[8,3712]{1,0:T(8,128)(2,1)S(1)}, bf16[8,3712]{1,0:T(8,128)(2,1)S(1)}, u32[]{:S(2)}, u32[]{:S(2)}) collective-permute-start(bf16[8,3712]{1,0:T(8,128)(2,1)S(1)} %get-tuple-element.32), channel_id=1, source_target_pairs={{0,28},{2,30},{4,24},{6,26},{8,20},{10,22},{12,16},{14,18},{16,12}... | collective-permute-start | bytes 178184 | tf_op jit(solution)/shard_map/ppermute | solution.py:290
  27.0 0.9 %collective-permute-done.9.refs_1_.refs_2_ = bf16[24,3712]{1,0:T(8,128)(2,1)S(1)} collective-permute-done((bf16[24,3712]{1,0:T(8,128)(2,1)S(1)}, bf16[24,3712]{1,0:T(8,128)(2,1)S(1)}, u32[]{:S(2)}, u32[]{:S(2)}) %collective-permute-start.9) | collective-permute-done | bytes 178208 | tf_op jit(solution)/shard_map/ppermute | solution.py:290
  27.9 0.3 merge.5
  28.2 2.9 %collective-permute-start.10 = (bf16[8,3712]{1,0:T(8,128)(2,1)S(1)}, bf16[8,3712]{1,0:T(8,128)(2,1)S(1)}, u32[]{:S(2)}, u32[]{:S(2)}) collective-permute-start(bf16[8,3712]{1,0:T(8,128)(2,1)S(1)} %get-tuple-element.30), channel_id=1, source_target_pairs={{0,16},{2,18},{4,20},{6,22},{8,24},{10,26},{12,28},{14,30},{16,0},... | collective-permute-start | bytes 178184 | tf_op jit(solution)/shard_map/ppermute | solution.py:290
  31.1 0.3 collective-permute-start.11
  31.4 1.7 %collective-permute-done.12.refs_0_ = bf16[8,3712]{1,0:T(8,128)(2,1)S(1)} collective-permute-done((bf16[8,3712]{1,0:T(8,128)(2,1)S(1)}, bf16[8,3712]{1,0:T(8,128)(2,1)S(1)}, u32[]{:S(2)}, u32[]{:S(2)}) %collective-permute-start.12) | collective-permute-done | bytes 59424 | tf_op jit(solution)/shard_map/ppermute | solution.py:290
  33.1 0.3 early.1.refs_2_
  33.4 0.8 %collective-permute-done.10.refs_0_ = bf16[8,3712]{1,0:T(8,128)(2,1)S(1)} collective-permute-done((bf16[8,3712]{1,0:T(8,128)(2,1)S(1)}, bf16[8,3712]{1,0:T(8,128)(2,1)S(1)}, u32[]{:S(2)}, u32[]{:S(2)}) %collective-permute-start.10) | collective-permute-done | bytes 59424 | tf_op jit(solution)/shard_map/ppermute | solution.py:290
  34.2 1.1 %collective-permute-done.11.refs_1_ = bf16[8,3712]{1,0:T(8,128)(2,1)S(1)} collective-permute-done((bf16[8,3712]{1,0:T(8,128)(2,1)S(1)}, bf16[8,3712]{1,0:T(8,128)(2,1)S(1)}, u32[]{:S(2)}, u32[]{:S(2)}) %collective-permute-start.11) | collective-permute-done | bytes 59424 | tf_op jit(solution)/shard_map/ppermute | solution.py:290
  35.3 0.3 last.1.refs_2_
  35.5 0.8 %collective-permute-start.14 = (bf16[8,3584]{1,0:T(8,128)(2,1)S(1)}, bf16[8,3584]{1,0:T(8,128)(2,1)S(1)}, u32[]{:S(2)}, u32[]{:S(2)}) collective-permute-start(bf16[8,3584]{1,0:T(8,128)(2,1)S(1)} %last.1.refs_2_), channel_id=1, source_target_pairs={{0,24},{2,26},{4,28},{6,30},{8,16},{10,18},{12,20},{14,22},{16,8},... | collective-permute-start | bytes 172040 | tf_op jit(solution)/shard_map/ppermute | solution.py:290
  36.4 1.3 %collective-permute-start.15 = (bf16[8,3584]{1,0:T(8,128)(2,1)S(1)}, bf16[8,3584]{1,0:T(8,128)(2,1)S(1)}, u32[]{:S(2)}, u32[]{:S(2)}) collective-permute-start(bf16[8,3584]{1,0:T(8,128)(2,1)S(1)} %last.1.refs_2_), channel_id=1, source_target_pairs={{0,16},{2,18},{4,20},{6,22},{8,24},{10,26},{12,28},{14,30},{16,0},... | collective-permute-start | bytes 172040 | tf_op jit(solution)/shard_map/ppermute | solution.py:290
  37.7 2.3 %collective-permute-start.16 = (bf16[8,3584]{1,0:T(8,128)(2,1)S(1)}, bf16[8,3584]{1,0:T(8,128)(2,1)S(1)}, u32[]{:S(2)}, u32[]{:S(2)}) collective-permute-start(bf16[8,3584]{1,0:T(8,128)(2,1)S(1)} %last.1.refs_2_), channel_id=1, source_target_pairs={{0,8},{2,10},{4,12},{6,14},{8,0},{10,2},{12,4},{14,6},{16,24},{18,... | collective-permute-start | bytes 172040 | tf_op jit(solution)/shard_map/ppermute | solution.py:290
  40.0 0.6 %collective-permute-start.17 = (bf16[8,3584]{1,0:T(8,128)(2,1)S(1)}, bf16[8,3584]{1,0:T(8,128)(2,1)S(1)}, u32[]{:S(2)}, u32[]{:S(2)}) collective-permute-start(bf16[8,3584]{1,0:T(8,128)(2,1)S(1)} %last.1.refs_2_), channel_id=1, source_target_pairs={{0,12},{2,14},{4,8},{6,10},{8,4},{10,6},{12,0},{14,2},{16,28},{18,... | collective-permute-start | bytes 172040 | tf_op jit(solution)/shard_map/ppermute | solution.py:290
  40.6 1.6 %collective-permute-done.14.refs_0_ = bf16[8,3584]{1,0:T(8,128)(2,1)S(1)} collective-permute-done((bf16[8,3584]{1,0:T(8,128)(2,1)S(1)}, bf16[8,3584]{1,0:T(8,128)(2,1)S(1)}, u32[]{:S(2)}, u32[]{:S(2)}) %collective-permute-start.14) | collective-permute-done | bytes 57376 | tf_op jit(solution)/shard_map/ppermute | solution.py:290
  42.2 1.9 %collective-permute-start.18 = (bf16[24,3584]{1,0:T(8,128)(2,1)S(1)}, bf16[24,3584]{1,0:T(8,128)(2,1)S(1)}, u32[]{:S(2)}, u32[]{:S(2)}) collective-permute-start(bf16[24,3584]{1,0:T(8,128)(2,1)S(1)} %pack.8.refs_0_), channel_id=1, source_target_pairs={{0,4},{2,6},{4,0},{6,2},{8,12},{10,14},{12,8},{14,10},{16,20},{18,... | collective-permute-start | bytes 516104 | tf_op jit(solution)/shard_map/ppermute | solution.py:290
  44.1 1.0 %collective-permute-done.17.refs_2_ = bf16[8,3584]{1,0:T(8,128)(2,1)S(1)} collective-permute-done((bf16[8,3584]{1,0:T(8,128)(2,1)S(1)}, bf16[8,3584]{1,0:T(8,128)(2,1)S(1)}, u32[]{:S(2)}, u32[]{:S(2)}) %collective-permute-start.17) | collective-permute-done | bytes 57376 | tf_op jit(solution)/shard_map/ppermute | solution.py:290
  45.1 0.1 collective-permute-start.19
  45.2 2.5 %collective-permute-done.18.refs_1_ = bf16[24,3584]{1,0:T(8,128)(2,1)S(1)} collective-permute-done((bf16[24,3584]{1,0:T(8,128)(2,1)S(1)}, bf16[24,3584]{1,0:T(8,128)(2,1)S(1)}, u32[]{:S(2)}, u32[]{:S(2)}) %collective-permute-start.18) | collective-permute-done | bytes 172064 | tf_op jit(solution)/shard_map/ppermute | solution.py:290
  47.7 1.4 %collective-permute-done.20.refs_3_ = bf16[24,3584]{1,0:T(8,128)(2,1)S(1)} collective-permute-done((bf16[24,3584]{1,0:T(8,128)(2,1)S(1)}, bf16[24,3584]{1,0:T(8,128)(2,1)S(1)}, u32[]{:S(2)}, u32[]{:S(2)}) %collective-permute-start.20) | collective-permute-done | bytes 172064 | tf_op jit(solution)/shard_map/ppermute | solution.py:290
  49.1 1.1 %project.1 = (f32[64,448]{1,0:T(8,128)S(1)}, bf16[64,448]{1,0:T(8,128)(2,1)S(1)}) custom-call(bf16[40,3584]{1,0:T(8,128)(2,1)S(1)} %pack.9.refs_0_, bf16[24,3584]{1,0:T(8,128)(2,1)S(1)} %collective-permute-done.18.refs_1_, bf16[40,3584]{1,0:T(8,128)(2,1)S(1)} %collective-permute-done.19.refs_2_, bf16[24,3584]{1,0:T(8,128)(2,1)S(1)} %collective-permute-done.20.refs_3_, ...), custom_call_target="tpu_custom_call" | custom-call | tf_op jit(solution)/shard_map/project/pallas_call | solution.py:318
  50.2 1.6 %collective-permute-start.21 = (bf16[64,448]{1,0:T(8,128)(2,1)S(1)}, bf16[64,448]{1,0:T(8,128)(2,1)S(1)}, u32[]{:S(2)}, u32[]{:S(2)}) collective-permute-start(bf16[64,448]{1,0:T(8,128)(2,1)S(1)} %get-tuple-element.36), channel_id=1, source_target_pairs={{0,1},{1,0},{2,3},{3,2},{4,5},{5,4},{6,7},{7,6},{8,9},{9,8},{10,11... | collective-permute-start | bytes 172040 | tf_op jit(solution)/shard_map/ppermute | solution.py:290
  51.8 2.7 %collective-permute-done.21.refs_0_ = bf16[64,448]{1,0:T(8,128)(2,1)S(1)} collective-permute-done((bf16[64,448]{1,0:T(8,128)(2,1)S(1)}, bf16[64,448]{1,0:T(8,128)(2,1)S(1)}, u32[]{:S(2)}, u32[]{:S(2)}) %collective-permute-start.21) | collective-permute-done | bytes 57376 | tf_op jit(solution)/shard_map/ppermute | solution.py:290
  54.5 0.6 %final.1 = bf16[64,448]{1,0:T(8,128)(2,1)} custom-call(f32[64,448]{1,0:T(8,128)S(1)} %base.1.total, bf16[64,448]{1,0:T(8,128)(2,1)S(1)} %collective-permute-done.21.refs_0_), custom_call_target="tpu_custom_call" | custom-call | tf_op jit(solution)/shard_map/final/pallas_call | solution.py:318
  (36 shorter events, 0.2 us)
Async XLA Ops:
  0.0 15.3 %copy-start = (bf16[384,3584]{1,0:T(8,128)(2,1)S(1)}, bf16[384,3584]{1,0:T(8,128)(2,1)}, u32[]{:S(2)}) copy-start(bf16[384,3584]{1,0:T(8,128)(2,1)} %keys.1) | copy-start | bytes 8257540
  0.0 9.8 %collective-permute-start = (bf16[8,3584]{1,0:T(8,128)(2,1)}, bf16[8,3584]{1,0:T(8,128)(2,1)S(1)}, u32[]{:S(2)}, u32[]{:S(2)}) collective-permute-start(bf16[8,3584]{1,0:T(8,128)(2,1)} %queries.1), channel_id=1, source_target_pairs={{0,24},{2,26},{4,28},{6,30},{8,16},{10,18},{12,20},{14,22},{16,8},... | collective-permute-start | bytes 172040 | tf_op jit(solution)/shard_map/ppermute | solution.py:290
  5.1 5.3 %collective-permute-start.1 = (bf16[8,3584]{1,0:T(8,128)(2,1)}, bf16[8,3584]{1,0:T(8,128)(2,1)S(1)}, u32[]{:S(2)}, u32[]{:S(2)}) collective-permute-start(bf16[8,3584]{1,0:T(8,128)(2,1)} %queries.1), channel_id=1, source_target_pairs={{0,16},{2,18},{4,20},{6,22},{8,24},{10,26},{12,28},{14,30},{16,0},... | collective-permute-start | bytes 172040 | tf_op jit(solution)/shard_map/ppermute | solution.py:290
  5.1 8.6 %collective-permute-start.2 = (bf16[8,3584]{1,0:T(8,128)(2,1)}, bf16[8,3584]{1,0:T(8,128)(2,1)S(1)}, u32[]{:S(2)}, u32[]{:S(2)}) collective-permute-start(bf16[8,3584]{1,0:T(8,128)(2,1)} %queries.1), channel_id=1, source_target_pairs={{0,8},{2,10},{4,12},{6,14},{8,0},{10,2},{12,4},{14,6},{16,24},{18,... | collective-permute-start | bytes 172040 | tf_op jit(solution)/shard_map/ppermute | solution.py:290
  5.7 8.0 %collective-permute-start.3 = (bf16[8,3584]{1,0:T(8,128)(2,1)}, bf16[8,3584]{1,0:T(8,128)(2,1)S(1)}, u32[]{:S(2)}, u32[]{:S(2)}) collective-permute-start(bf16[8,3584]{1,0:T(8,128)(2,1)} %queries.1), channel_id=1, source_target_pairs={{0,12},{2,14},{4,8},{6,10},{8,4},{10,6},{12,0},{14,2},{16,28},{18,... | collective-permute-start | bytes 172040 | tf_op jit(solution)/shard_map/ppermute | solution.py:290
  8.0 0.9 %copy-start.6 = (bf16[8,3584]{1,0:T(8,128)(2,1)S(1)}, bf16[8,3584]{1,0:T(8,128)(2,1)}, u32[]{:S(2)}) copy-start(bf16[8,3584]{1,0:T(8,128)(2,1)} %queries.1) | copy-start | bytes 172036
  8.9 0.8 %copy-start.7 = (bf16[8,3584]{1,0:T(8,128)(2,1)S(1)}, bf16[8,3584]{1,0:T(8,128)(2,1)}, u32[]{:S(2)}) copy-start(bf16[8,3584]{1,0:T(8,128)(2,1)} %new_keys.1) | copy-start | bytes 172036
  10.4 5.7 %collective-permute-start.4 = (bf16[24,3584]{1,0:T(8,128)(2,1)S(1)}, bf16[24,3584]{1,0:T(8,128)(2,1)S(1)}, u32[]{:S(2)}, u32[]{:S(2)}) collective-permute-start(bf16[24,3584]{1,0:T(8,128)(2,1)S(1)} %pack.5.refs_0_), channel_id=1, source_target_pairs={{0,4},{2,6},{4,0},{6,2},{8,12},{10,14},{12,8},{14,10},{16,20},{18,... | collective-permute-start | bytes 516104 | tf_op jit(solution)/shard_map/ppermute | solution.py:290
  11.9 1.8 %copy-start.1 = (bf16[384,3584]{1,0:T(8,128)(2,1)S(1)}, bf16[384,3584]{1,0:T(8,128)(2,1)}, u32[]{:S(2)}) copy-start(bf16[384,3584]{1,0:T(8,128)(2,1)} %values.1) | copy-start | bytes 8257540
  13.7 3.8 %copy-start.2 = (bf16[384,3584]{1,0:T(8,128)(2,1)S(1)}, bf16[384,3584]{1,0:T(8,128)(2,1)}, u32[]{:S(2)}) copy-start(bf16[384,3584]{1,0:T(8,128)(2,1)} %values.1) | copy-start | bytes 8257540
  13.7 2.4 %collective-permute-start.5 = (bf16[40,3584]{1,0:T(8,128)(2,1)S(1)}, bf16[40,3584]{1,0:T(8,128)(2,1)S(1)}, u32[]{:S(2)}, u32[]{:S(2)}) collective-permute-start(bf16[40,3584]{1,0:T(8,128)(2,1)S(1)} %pack.6.refs_0_), channel_id=1, source_target_pairs={{0,2},{2,0},{4,6},{6,4},{8,10},{10,8},{12,14},{14,12},{16,18},{18,... | collective-permute-start | bytes 860168 | tf_op jit(solution)/shard_map/ppermute | solution.py:290
  16.0 1.5 %collective-permute-start.6 = (bf16[24,3584]{1,0:T(8,128)(2,1)S(1)}, bf16[24,3584]{1,0:T(8,128)(2,1)S(1)}, u32[]{:S(2)}, u32[]{:S(2)}) collective-permute-start(bf16[24,3584]{1,0:T(8,128)(2,1)S(1)} %pack.7.refs_1_), channel_id=1, source_target_pairs={{0,2},{2,0},{4,6},{6,4},{8,10},{10,8},{12,14},{14,12},{16,18},{18,... | collective-permute-start | bytes 516104 | tf_op jit(solution)/shard_map/ppermute | solution.py:290
  17.5 15.6 %copy-start.5 = (bf16[8,3584]{1,0:T(8,128)(2,1)S(1)}, bf16[8,3584]{1,0:T(8,128)(2,1)}, u32[]{:S(2)}) copy-start(bf16[8,3584]{1,0:T(8,128)(2,1)} %refs_4_.1) | copy-start | bytes 172036
  17.5 31.6 %copy-start.3 = (bf16[3584,448]{0,1:T(8,128)(2,1)S(1)}, bf16[3584,448]{0,1:T(8,128)(2,1)}, u32[]{:S(2)}) copy-start(bf16[3584,448]{0,1:T(8,128)(2,1)} %param.17) | copy-start | bytes 9633796
  19.4 1.6 %collective-permute-start.8 = (bf16[32,3712]{1,0:T(8,128)(2,1)S(1)}, bf16[32,3712]{1,0:T(8,128)(2,1)S(1)}, u32[]{:S(2)}, u32[]{:S(2)}) collective-permute-start(bf16[32,3712]{1,0:T(8,128)(2,1)S(1)} %get-tuple-element.28), channel_id=1, source_target_pairs={{0,2},{2,0},{4,6},{6,4},{8,10},{10,8},{12,14},{14,12},{16,18},{18,... | collective-permute-start | bytes 712712 | tf_op jit(solution)/shard_map/ppermute | solution.py:290
  19.6 3.1 %collective-permute-start.7 = (bf16[32,3712]{1,0:T(8,128)(2,1)S(1)}, bf16[32,3712]{1,0:T(8,128)(2,1)S(1)}, u32[]{:S(2)}, u32[]{:S(2)}) collective-permute-start(bf16[32,3712]{1,0:T(8,128)(2,1)S(1)} %get-tuple-element.25), channel_id=1, source_target_pairs={{0,2},{2,0},{4,6},{6,4},{8,10},{10,8},{12,14},{14,12},{16,18},{18,... | collective-permute-start | bytes 712712 | tf_op jit(solution)/shard_map/ppermute | solution.py:290
  21.3 6.6 %collective-permute-start.9 = (bf16[24,3712]{1,0:T(8,128)(2,1)S(1)}, bf16[24,3712]{1,0:T(8,128)(2,1)S(1)}, u32[]{:S(2)}, u32[]{:S(2)}) collective-permute-start(bf16[24,3712]{1,0:T(8,128)(2,1)S(1)} %get-tuple-element.29), channel_id=1, source_target_pairs={{0,4},{2,6},{4,0},{6,2},{8,12},{10,14},{12,8},{14,10},{16,20},{18,... | collective-permute-start | bytes 534536 | tf_op jit(solution)/shard_map/ppermute | solution.py:290
  23.1 8.3 %collective-permute-start.13 = (bf16[8,3712]{1,0:T(8,128)(2,1)S(1)}, bf16[8,3712]{1,0:T(8,128)(2,1)S(1)}, u32[]{:S(2)}, u32[]{:S(2)}) collective-permute-start(bf16[8,3712]{1,0:T(8,128)(2,1)S(1)} %get-tuple-element.34), channel_id=1, source_target_pairs={{0,24},{2,26},{4,28},{6,30},{8,16},{10,18},{12,20},{14,22},{16,8},... | collective-permute-start | bytes 178184 | tf_op jit(solution)/shard_map/ppermute | solution.py:290
  25.6 7.4 %collective-permute-start.12 = (bf16[8,3712]{1,0:T(8,128)(2,1)S(1)}, bf16[8,3712]{1,0:T(8,128)(2,1)S(1)}, u32[]{:S(2)}, u32[]{:S(2)}) collective-permute-start(bf16[8,3712]{1,0:T(8,128)(2,1)S(1)} %get-tuple-element.32), channel_id=1, source_target_pairs={{0,28},{2,30},{4,24},{6,26},{8,20},{10,22},{12,16},{14,18},{16,12}... | collective-permute-start | bytes 178184 | tf_op jit(solution)/shard_map/ppermute | solution.py:290
  28.2 6.1 %collective-permute-start.10 = (bf16[8,3712]{1,0:T(8,128)(2,1)S(1)}, bf16[8,3712]{1,0:T(8,128)(2,1)S(1)}, u32[]{:S(2)}, u32[]{:S(2)}) collective-permute-start(bf16[8,3712]{1,0:T(8,128)(2,1)S(1)} %get-tuple-element.30), channel_id=1, source_target_pairs={{0,16},{2,18},{4,20},{6,22},{8,24},{10,26},{12,28},{14,30},{16,0},... | collective-permute-start | bytes 178184 | tf_op jit(solution)/shard_map/ppermute | solution.py:290
  31.1 4.2 %collective-permute-start.11 = (bf16[8,3712]{1,0:T(8,128)(2,1)S(1)}, bf16[8,3712]{1,0:T(8,128)(2,1)S(1)}, u32[]{:S(2)}, u32[]{:S(2)}) collective-permute-start(bf16[8,3712]{1,0:T(8,128)(2,1)S(1)} %get-tuple-element.31), channel_id=1, source_target_pairs={{0,8},{2,10},{4,12},{6,14},{8,0},{10,2},{12,4},{14,6},{16,24},{18,... | collective-permute-start | bytes 178184 | tf_op jit(solution)/shard_map/ppermute | solution.py:290
  33.4 18.4 %copy-start.8 = (bf16[448]{0:T(512)(128)(2,1)S(1)}, bf16[448]{0:T(512)(128)(2,1)}, u32[]{:S(2)}) copy-start(bf16[448]{0:T(512)(128)(2,1)} %param.18) | copy-start | bytes 2692
  33.4 18.4 %copy-start.4 = (bf16[64,448]{1,0:T(8,128)(2,1)S(1)}, bf16[64,448]{1,0:T(8,128)(2,1)}, u32[]{:S(2)}) copy-start(bf16[64,448]{1,0:T(8,128)(2,1)} %residual.1) | copy-start | bytes 172036
  35.5 6.6 %collective-permute-start.14 = (bf16[8,3584]{1,0:T(8,128)(2,1)S(1)}, bf16[8,3584]{1,0:T(8,128)(2,1)S(1)}, u32[]{:S(2)}, u32[]{:S(2)}) collective-permute-start(bf16[8,3584]{1,0:T(8,128)(2,1)S(1)} %last.1.refs_2_), channel_id=1, source_target_pairs={{0,24},{2,26},{4,28},{6,30},{8,16},{10,18},{12,20},{14,22},{16,8},... | collective-permute-start | bytes 172040 | tf_op jit(solution)/shard_map/ppermute | solution.py:290
  36.4 5.8 %collective-permute-start.15 = (bf16[8,3584]{1,0:T(8,128)(2,1)S(1)}, bf16[8,3584]{1,0:T(8,128)(2,1)S(1)}, u32[]{:S(2)}, u32[]{:S(2)}) collective-permute-start(bf16[8,3584]{1,0:T(8,128)(2,1)S(1)} %last.1.refs_2_), channel_id=1, source_target_pairs={{0,16},{2,18},{4,20},{6,22},{8,24},{10,26},{12,28},{14,30},{16,0},... | collective-permute-start | bytes 172040 | tf_op jit(solution)/shard_map/ppermute | solution.py:290
  37.7 6.4 %collective-permute-start.16 = (bf16[8,3584]{1,0:T(8,128)(2,1)S(1)}, bf16[8,3584]{1,0:T(8,128)(2,1)S(1)}, u32[]{:S(2)}, u32[]{:S(2)}) collective-permute-start(bf16[8,3584]{1,0:T(8,128)(2,1)S(1)} %last.1.refs_2_), channel_id=1, source_target_pairs={{0,8},{2,10},{4,12},{6,14},{8,0},{10,2},{12,4},{14,6},{16,24},{18,... | collective-permute-start | bytes 172040 | tf_op jit(solution)/shard_map/ppermute | solution.py:290
  40.0 5.1 %collective-permute-start.17 = (bf16[8,3584]{1,0:T(8,128)(2,1)S(1)}, bf16[8,3584]{1,0:T(8,128)(2,1)S(1)}, u32[]{:S(2)}, u32[]{:S(2)}) collective-permute-start(bf16[8,3584]{1,0:T(8,128)(2,1)S(1)} %last.1.refs_2_), channel_id=1, source_target_pairs={{0,12},{2,14},{4,8},{6,10},{8,4},{10,6},{12,0},{14,2},{16,28},{18,... | collective-permute-start | bytes 172040 | tf_op jit(solution)/shard_map/ppermute | solution.py:290
  42.2 5.5 %collective-permute-start.18 = (bf16[24,3584]{1,0:T(8,128)(2,1)S(1)}, bf16[24,3584]{1,0:T(8,128)(2,1)S(1)}, u32[]{:S(2)}, u32[]{:S(2)}) collective-permute-start(bf16[24,3584]{1,0:T(8,128)(2,1)S(1)} %pack.8.refs_0_), channel_id=1, source_target_pairs={{0,4},{2,6},{4,0},{6,2},{8,12},{10,14},{12,8},{14,10},{16,20},{18,... | collective-permute-start | bytes 516104 | tf_op jit(solution)/shard_map/ppermute | solution.py:290
  45.1 2.6 %collective-permute-start.19 = (bf16[40,3584]{1,0:T(8,128)(2,1)S(1)}, bf16[40,3584]{1,0:T(8,128)(2,1)S(1)}, u32[]{:S(2)}, u32[]{:S(2)}) collective-permute-start(bf16[40,3584]{1,0:T(8,128)(2,1)S(1)} %pack.9.refs_0_), channel_id=1, source_target_pairs={{0,2},{2,0},{4,6},{6,4},{8,10},{10,8},{12,14},{14,12},{16,18},{18,... | collective-permute-start | bytes 860168 | tf_op jit(solution)/shard_map/ppermute | solution.py:290
  47.7 1.4 %collective-permute-start.20 = (bf16[24,3584]{1,0:T(8,128)(2,1)S(1)}, bf16[24,3584]{1,0:T(8,128)(2,1)S(1)}, u32[]{:S(2)}, u32[]{:S(2)}) collective-permute-start(bf16[24,3584]{1,0:T(8,128)(2,1)S(1)} %collective-permute-done.18.refs_1_), channel_id=1, source_target_pairs={{0,2},{2,0},{4,6},{6,4},{8,10},{10,8},{12,14},{14,12},{16,18},{18,... | collective-permute-start | bytes 516104 | tf_op jit(solution)/shard_map/ppermute | solution.py:290
  50.2 4.3 %collective-permute-start.21 = (bf16[64,448]{1,0:T(8,128)(2,1)S(1)}, bf16[64,448]{1,0:T(8,128)(2,1)S(1)}, u32[]{:S(2)}, u32[]{:S(2)}) collective-permute-start(bf16[64,448]{1,0:T(8,128)(2,1)S(1)} %get-tuple-element.36), channel_id=1, source_target_pairs={{0,1},{1,0},{2,3},{3,2},{4,5},{5,4},{6,7},{7,6},{8,9},{9,8},{10,11... | collective-permute-start | bytes 172040 | tf_op jit(solution)/shard_map/ppermute | solution.py:290
